TPU v7x, 512 devices: a whole 4x8x8 slice. The times are simulated.
512 devices in a mesh: dom: 512 (over z, x, y, core).
Axes of the slice: x: 4, y: 8, z: 8, core: 2. Of those that a mesh axis runs over, the one named last changes fastest.
Arguments:
- velocity: float32 [3, 3, 8192, 512], P(None, None, 'dom'), may hold values from -6 to 6
- conv_past: float32 [2, 3, 8192, 512], P(None, None, 'dom'), may hold values from -0.6 to 0.6
- metric: float32 [3, 8192, 512], P(None, 'dom'), may hold values from 0.5 to 2
- jacobian: float32 [8192, 512], P('dom'), may hold values from 0.5 to 2
- element_slot: int32 [8192], P('dom'), may hold values from 0 to 15, as said below
Outputs:
- pressure: float32 [4096, 896], P('dom')
- residual: float32 [4096, 896], P('dom')
Inputs may be any that keep to these rules, and one draw needn't show every extreme that they name: `element_slot`: within each aligned block of 16 entries (one slab's elements) the entries are a permutation of 0 to 15.
All inputs are finite; a program needn't handle non-finite values.
Results may differ from a plain program's by a relative error of at most 0.0003.
Values sent between devices are 32-bit elements; how exact they have to be, the bound alone decides.
No kernel may reach another device: no remote copies, remote signals or barrier semaphores. Data moves between devices by JAX's collectives and lax.ppermute only.
A program may use at most 64 MiB of HBM per device.

v0:
```python
import jax
import jax.numpy as jnp
import numpy as np
from jax import lax
from jax.sharding import PartitionSpec as P

NP = 8
NF = 12
EA = 1
ES = 16
ER = 1
ITERS = 3
A0 = 8
A1 = 112
A2 = 8


HIGHEST = lax.Precision.HIGHEST
time_step = 0.25
viscosity = 0.05
mass_shift = 0.001


def extended_2(block, sides, width):
    for axis, dim in sides:
        count = lax.axis_size(axis)
        forward = [(i, i + 1) for i in range(count - 1)]
        forward.append((count - 1, 0))
        backward = [(target, source) for source, target in forward]
        low = lax.ppermute(
            lax.slice_in_dim(block, block.shape[dim] - width, None, axis=dim), axis, forward
        )
        high = lax.ppermute(lax.slice_in_dim(block, 0, width, axis=dim), axis, backward)
        block = jnp.concatenate([low, block, high], axis=dim)
    return block


def legendre_pair(points, order):
    before = np.ones(points.shape)
    current = points * 1.0
    for level in range(2, order + 1):
        nextone = ((2 * level - 1) * points * current - (level - 1) * before) / level
        before = current
        current = nextone
    return (current, before)


def jacobi_eigen(matrix):
    size = matrix.shape[0]
    work = matrix * 1.0
    vectors = np.eye(size)
    for sweep in range(30):
        for first in range(size - 1):
            for second in range(first + 1, size):
                off = float(work[first, second])
                if abs(off) > 1e-300:
                    tau = (float(work[second, second]) - float(work[first, first])) / (2.0 * off)
                    if tau >= 0.0:
                        tangent = 1.0 / (tau + (1.0 + tau * tau) ** 0.5)
                    else:
                        tangent = -1.0 / (-tau + (1.0 + tau * tau) ** 0.5)
                    cosine = 1.0 / (1.0 + tangent * tangent) ** 0.5
                    sine = tangent * cosine
                    rotation = np.eye(size)
                    rotation[first, first] = cosine
                    rotation[second, second] = cosine
                    rotation[first, second] = sine
                    rotation[second, first] = -sine
                    work = rotation.T @ work @ rotation
                    vectors = vectors @ rotation
    diagonal_index = np.arange(size)
    return (work[diagonal_index, diagonal_index], vectors)


def build_tables(points_edge, points_fine):
    degree = points_edge - 1
    points = -np.cos(np.pi * np.arange(points_edge) / degree)
    for sweep in range(100):
        top, below = legendre_pair(points, degree)
        points = points - (points * top - below) / (points_edge * top)
    top, below = legendre_pair(points, degree)
    weight_gll = 2.0 / (degree * points_edge * top**2)
    spacing = points[:, None] - points[None, :] + np.eye(points_edge)
    barycentric = 1.0 / np.prod(spacing, axis=1)
    derivative = barycentric[None, :] / barycentric[:, None] / spacing
    derivative = derivative * (1.0 - np.eye(points_edge))
    derivative = derivative - np.eye(points_edge) * derivative.sum(axis=1)[:, None]
    fine_points = np.cos(np.pi * (np.arange(points_fine) + 0.75) / (points_fine + 0.5))
    for sweep in range(100):
        top, below = legendre_pair(fine_points, points_fine)
        slope = points_fine * (fine_points * top - below) / (fine_points * fine_points - 1.0)
        fine_points = fine_points - top / slope
    top, below = legendre_pair(fine_points, points_fine)
    slope = points_fine * (fine_points * top - below) / (fine_points * fine_points - 1.0)
    fine_weight = 2.0 / ((1.0 - fine_points * fine_points) * slope * slope)
    fine_points = fine_points[::-1]
    fine_weight = fine_weight[::-1]
    interpolate = np.ones((points_fine, points_edge))
    for column in range(points_edge):
        for other in range(points_edge):
            if other != column:
                interpolate[:, column] = (
                    interpolate[:, column]
                    * (fine_points - points[other])
                    / (points[column] - points[other])
                )
    stiffness = derivative.T @ (weight_gll[:, None] * derivative)
    extent = 3 * degree + 1
    joined_stiff = np.zeros((extent, extent))
    joined_mass = np.zeros(extent)
    for segment in range(3):
        offset = segment * degree
        joined_stiff[offset : offset + points_edge, offset : offset + points_edge] += stiffness
        joined_mass[offset : offset + points_edge] += weight_gll
    low = degree - 1
    high = 2 * degree + 2
    root_mass = np.sqrt(joined_mass[low:high])
    scaled = joined_stiff[low:high, low:high] / root_mass[:, None] / root_mass[None, :]
    scaled = 0.5 * (scaled + scaled.T)
    eigen_values, eigen_vectors = jacobi_eigen(scaled)
    solve_mat = eigen_vectors / root_mass[:, None]
    breadth = high - low
    identity = np.eye(points_edge)
    operator_tables = {
        "derivative": derivative,
        "dpair": np.concatenate(
            [np.kron(derivative, identity).T, np.kron(identity, derivative).T], axis=1
        ),
        "interpolate": interpolate,
        "ipair": np.kron(interpolate, interpolate).T,
        "mass_three": (
            weight_gll[:, None, None] * weight_gll[None, :, None] * weight_gll[None, None, :]
        ).reshape(points_edge, points_edge * points_edge),
        "fine_three": (
            fine_weight[:, None, None] * fine_weight[None, :, None] * fine_weight[None, None, :]
        ).reshape(points_fine, points_fine * points_fine),
        "solve_mat": solve_mat,
        "solve_pair": np.kron(solve_mat, solve_mat),
        "eigen_axial": eigen_values,
        "eigen_around": np.repeat(eigen_values, breadth),
        "eigen_radial": np.tile(eigen_values, breadth),
    }
    return {
        entry_name: jnp.asarray(entry_value, jnp.float32)
        for entry_name, entry_value in operator_tables.items()
    }


def matmul(left, right):
    return jnp.dot(left, right, precision=HIGHEST, preferred_element_type=jnp.float32)


def along_first(field, matrix, form):
    return jnp.einsum(form, field, matrix, precision=HIGHEST, preferred_element_type=jnp.float32)


def gradient(field, operator_tables):
    paired = matmul(field, operator_tables["dpair"])
    streamwise_piece = along_first(field, operator_tables["derivative"], "ebx,ab->eax")
    return (streamwise_piece, paired[..., : NP * NP], paired[..., NP * NP :])


def gradient_t(streamwise_piece, azimuthal_piece, radial_piece, operator_tables):
    paired = matmul(
        jnp.concatenate([azimuthal_piece, radial_piece], axis=-1), operator_tables["dpair"].T
    )
    return paired + along_first(streamwise_piece, operator_tables["derivative"], "eax,ab->ebx")


def coarse_to_dealiased(field, operator_tables):
    return along_first(
        matmul(field, operator_tables["ipair"]), operator_tables["interpolate"], "ebx,ab->eax"
    )


def from_fine(field, operator_tables):
    return matmul(
        along_first(field, operator_tables["interpolate"], "eax,ab->ebx"),
        operator_tables["ipair"].T,
    )


def element_forcing(velocity, conv_past, metric, jacobian, operator_tables):
    mass_node = jacobian * operator_tables["mass_three"]
    fine_jacobian = coarse_to_dealiased(jacobian, operator_tables) * operator_tables["fine_three"]
    advecting_velocities = [
        coarse_to_dealiased(
            velocity[0, velocity_component] * metric[velocity_component], operator_tables
        )
        for velocity_component in range(3)
    ]
    factors = [
        mass_node * metric[velocity_component] * metric[velocity_component]
        for velocity_component in range(3)
    ]
    outputs = []
    for velocity_component in range(3):
        streamwise_piece, azimuthal_piece, radial_piece = gradient(
            velocity[0, velocity_component], operator_tables
        )
        pointwise_product = (
            advecting_velocities[0] * coarse_to_dealiased(streamwise_piece, operator_tables)
            + advecting_velocities[1] * coarse_to_dealiased(azimuthal_piece, operator_tables)
            + advecting_velocities[2] * coarse_to_dealiased(radial_piece, operator_tables)
        )
        convect = from_fine(fine_jacobian * pointwise_product, operator_tables)
        extrap_term = (
            3.0 * convect
            - 3.0 * conv_past[0, velocity_component]
            + conv_past[1, velocity_component]
        )
        history = (
            3.0 * velocity[0, velocity_component]
            - 1.5 * velocity[1, velocity_component]
            + velocity[2, velocity_component] / 3.0
        )
        guessed = (
            3.0 * velocity[0, velocity_component]
            - 3.0 * velocity[1, velocity_component]
            + velocity[2, velocity_component]
        )
        streamwise_piece, azimuthal_piece, radial_piece = gradient(guessed, operator_tables)
        stiff_term = gradient_t(
            factors[0] * streamwise_piece,
            factors[1] * azimuthal_piece,
            factors[2] * radial_piece,
            operator_tables,
        )
        helmholtz = viscosity * stiff_term + 11.0 / (6.0 * time_step) * mass_node * guessed
        outputs.append(mass_node * history / time_step - extrap_term - helmholtz)
    outputs.append(mass_node)
    return jnp.stack(outputs)


def element_divergence(accel, metric, jacobian, operator_tables):
    mass_node = jacobian * operator_tables["mass_three"]
    return gradient_t(
        mass_node * metric[0] * accel[0],
        mass_node * metric[1] * accel[1],
        mass_node * metric[2] * accel[2],
        operator_tables,
    )


def element_pressure(values, metric, jacobian, operator_tables):
    mass_node = jacobian * operator_tables["mass_three"]
    streamwise_piece, azimuthal_piece, radial_piece = gradient(values, operator_tables)
    stiff_term = gradient_t(
        mass_node * metric[0] * metric[0] * streamwise_piece,
        mass_node * metric[1] * metric[1] * azimuthal_piece,
        mass_node * metric[2] * metric[2] * radial_piece,
        operator_tables,
    )
    return stiff_term + mass_shift * mass_node * values


def local_solve(extended, metric, jacobian, operator_tables):
    mass_node = jacobian * operator_tables["mass_three"]
    scales = [
        jnp.sum(mass_node * metric[velocity_component] * metric[velocity_component], axis=(1, 2))
        / 8.0
        for velocity_component in range(3)
    ]
    average = jnp.sum(mass_node, axis=(1, 2)) / 8.0
    breadth = operator_tables["solve_mat"].shape[0]
    spectra = extended.reshape(-1, breadth, breadth * breadth)
    spectra = along_first(
        matmul(spectra, operator_tables["solve_pair"]), operator_tables["solve_mat"], "eax,ab->ebx"
    )
    denom = (
        scales[0][:, None, None] * operator_tables["eigen_axial"][None, :, None]
        + scales[1][:, None, None] * operator_tables["eigen_around"][None, None, :]
        + scales[2][:, None, None] * operator_tables["eigen_radial"][None, None, :]
        + mass_shift * average[:, None, None]
    )
    spectra = spectra / denom
    restored = matmul(
        along_first(spectra, operator_tables["solve_mat"], "ebx,ab->eax"),
        operator_tables["solve_pair"].T,
    )
    return restored.reshape(extended.shape)


def place(piece, axis, low, total):
    config = [(0, 0, 0)] * piece.ndim
    config[axis] = (low, total - low - piece.shape[axis], 0)
    return lax.pad(piece, jnp.float32(0.0), config)


def windows(field, axis, count, width):
    stride = NP - 1
    parts = [
        lax.slice_in_dim(field, offset, offset + stride * (count - 1) + 1, stride, axis)
        for offset in range(width)
    ]
    return jnp.stack(parts, axis=axis + 1)


def intersection(values, axis, count, width):
    stride = NP - 1
    total = stride * count + width - stride
    result = None
    for group in range((width + stride - 1) // stride):
        columns = []
        for column in range(stride):
            offset = group * stride + column
            if offset < width:
                columns.append(lax.index_in_dim(values, offset, axis + 1, keepdims=False))
            else:
                columns.append(
                    jnp.zeros_like(lax.index_in_dim(values, 0, axis + 1, keepdims=False))
                )
        stacked = jnp.stack(columns, axis=axis + 1)
        flat = stacked.reshape(stacked.shape[:axis] + (count * stride,) + stacked.shape[axis + 2 :])
        piece = place(flat, axis, group * stride, total)
        result = piece if result is None else result + piece
    return result


def periodic_extend(field, axis, margin, total):
    period = field.shape[axis]
    parts = []
    if margin > 0:
        parts.append(lax.slice_in_dim(field, period - margin, period, 1, axis))
    parts.append(field)
    parts.append(lax.slice_in_dim(field, 0, total - period - margin, 1, axis))
    return jnp.concatenate(parts, axis=axis)


def fold_periodic(linear, axis, margin, period):
    total = linear.shape[axis]
    result = lax.slice_in_dim(linear, margin, margin + period, 1, axis)
    if margin > 0:
        result = result + place(
            lax.slice_in_dim(linear, 0, margin, 1, axis), axis, period - margin, period
        )
    result = result + place(
        lax.slice_in_dim(linear, margin + period, total, 1, axis), axis, 0, period
    )
    return result


def to_elements(grid, width, margin, order):
    channels = grid.shape[0]
    linear = periodic_extend(grid, 2, margin, (NP - 1) * ES + width - (NP - 1))
    spread = windows(linear, 3, ER, width)
    spread = windows(spread, 2, ES, width)
    spread = windows(spread, 1, EA, width)
    spread = spread.transpose(0, 1, 3, 5, 2, 4, 6).reshape(
        channels, EA * ES * ER, width, width * width
    )
    return jnp.einsum(
        "ep,cpxy->cexy", order, spread, precision=HIGHEST, preferred_element_type=jnp.float32
    )


def from_elements(values, width, margin, order):
    channels = values.shape[0]
    sorted_values = jnp.einsum(
        "ep,cexy->cpxy", order, values, precision=HIGHEST, preferred_element_type=jnp.float32
    )
    spread = sorted_values.reshape(channels, EA, ES, ER, width, width, width).transpose(
        0, 1, 4, 2, 5, 3, 6
    )
    spread = intersection(spread, 5, ER, width)
    spread = intersection(spread, 3, ES, width)
    spread = fold_periodic(spread, 3, margin, A1)
    return intersection(spread, 1, EA, width)


def shards(velocity, conv_past, metric, jacobian, element_slot):
    operator_tables = build_tables(NP, NF)
    elements = element_slot.shape[0]
    element_shape = (elements, NP, NP * NP)
    velocity = velocity.reshape((3, 3) + element_shape)
    conv_past = conv_past.reshape((2, 3) + element_shape)
    metric = metric.reshape((3,) + element_shape)
    jacobian = jacobian.reshape(element_shape)
    row_width = A1 * A2
    order = (element_slot[:, None] == jnp.arange(elements, dtype=jnp.int32)[None, :]).astype(
        jnp.float32
    )
    row_weights = jnp.ones((A0,), jnp.float32).at[0].set(0.5).at[A0 - 1].set(0.5)

    def gather_nodes(field):
        channels = field.shape[0]
        return to_elements(field.reshape(channels, A0, A1, A2), NP, 0, order)

    def spread_nodes(values):
        channels = values.shape[0]
        return from_elements(values, NP, 0, order).reshape(channels, A0, row_width)

    def assemble(local):
        rows = extended_2(local, (("dom", 1),), 1)
        return jnp.concatenate(
            [local[:, :1] + rows[:, :1], local[:, 1:-1], local[:, -1:] + rows[:, -1:]], axis=1
        )

    forcing = element_forcing(velocity, conv_past, metric, jacobian, operator_tables)
    summed = assemble(spread_nodes(forcing))
    accel = summed[:3] / summed[3:]
    divergence = element_divergence(gather_nodes(accel), metric, jacobian, operator_tables)
    source = assemble(spread_nodes(divergence[None]))

    def weighted(left, right):
        return jnp.sum(jnp.sum(left * right, axis=2)[0] * row_weights)

    solution = jnp.zeros((1, A0, row_width), jnp.float32)
    residual = source
    direction = solution
    previous_sum = jnp.float32(1.0)
    for step in range(ITERS):
        widen_rows = extended_2(residual[:, 1:-1], (("dom", 1),), 1)
        padded = jnp.pad(
            jnp.concatenate([widen_rows[:, :1], residual, widen_rows[:, -1:]], axis=1).reshape(
                1, A0 + 2, A1, A2
            ),
            ((0, 0), (0, 0), (0, 0), (1, 1)),
        )
        extended = to_elements(padded, NP + 2, 1, order)[0]
        solved = local_solve(extended, metric, jacobian, operator_tables)
        spread = from_elements(solved[None], NP + 2, 1, order)
        spread = spread[:, :, :, 1:-1].reshape(1, A0 + 2, row_width)
        precondition_rows = extended_2(spread, (("dom", 1),), 2)
        middle = spread[:, 1:-1]
        smoothed = jnp.concatenate(
            [
                middle[:, :2] + precondition_rows[:, :2],
                middle[:, 2:-2],
                middle[:, -2:] + precondition_rows[:, -2:],
            ],
            axis=1,
        )
        precond_sum = lax.psum(weighted(residual, smoothed), "dom")
        direction = smoothed if step == 0 else smoothed + precond_sum / previous_sum * direction
        apply_values = gather_nodes(direction)[0]
        apply_local = element_pressure(apply_values, metric, jacobian, operator_tables)
        image = assemble(spread_nodes(apply_local[None]))
        step_size = precond_sum / lax.psum(weighted(direction, image), "dom")
        solution = solution + step_size * direction
        residual = residual - step_size * image
        previous_sum = precond_sum
    return (solution.reshape(A0, row_width), residual.reshape(A0, row_width))


def solution(mesh):
    return jax.shard_map(
        shards,
        mesh=mesh,
        in_specs=(
            P(None, None, "dom", None),
            P(None, None, "dom", None),
            P(None, "dom", None),
            P("dom", None),
            P("dom"),
        ),
        out_specs=(P("dom", None), P("dom", None)),
        check_vma=False,
    )
```

profile of v0, /device:TPU:1, one launch (start us, length us, event | category | flops | bytes accessed | tf_op | source)
XLA Modules:
  0.0 813.3 jit_solution(17269395085194016272)
XLA Ops:
  27.4 1.6 copy.4469
  30.2 1.6 copy.4470
  31.8 1.6 maximum_maximum_fusion
  33.4 2.6 reshape.1769
  38.0 4.6 collective-permute-start
  42.6 6.1 collective-permute-start.1
  50.5 7.5 fusion.14
  71.8 10.7 %collective-permute-start.3 = (f32[1,1,896]{2,1,0:T(1,128)S(1)}, f32[1,1,896]{2,1,0:T(1,128)S(1)}, u32[]{:S(2)}, u32[]{:S(2)}) collective-permute-start(f32[1,1,896]{2,1,0:T(1,128)S(1)} %get-tuple-element.190), channel_id=1, source_target_pairs={{1,0},{2,1},{3,2},{4,3},{5,4},{6,5},{7,6},{8,7},{9,8},{10,9},{11,1... | collective-permute-start | bytes 10760 | tf_op jit(solution)/shard_map/ppermute | solution.py:33
  82.6 1.9 collective-permute-start.2
  84.5 7.7 collective-permute-done.2
  92.3 9.7 %collective-permute-start.5 = (f32[1,1,896]{2,1,0:T(1,128)S(1)}, f32[1,1,896]{2,1,0:T(1,128)S(1)}, u32[]{:S(2)}, u32[]{:S(2)}) collective-permute-start(f32[1,1,896]{2,1,0:T(1,128)S(1)} %get-tuple-element.186), channel_id=1, source_target_pairs={{1,0},{2,1},{3,2},{4,3},{5,4},{6,5},{7,6},{8,7},{9,8},{10,9},{11,1... | collective-permute-start | bytes 10760 | tf_op jit(solution)/shard_map/ppermute | solution.py:33
  102.0 2.3 collective-permute-start.4
  106.6 1.3 slice.1588
  107.9 1.3 slice.1587
  109.2 1.3 slice.1586
  110.4 1.3 slice.1585
  111.7 1.3 slice.1584
  114.3 1.3 slice.1582
  115.6 1.3 slice.1581
  116.8 1.3 slice.1580
  128.2 3.8 collective-permute-start.6
  132.6 5.4 collective-permute-done.6
  138.0 9.9 %collective-permute-start.7 = (f32[1,2,896]{2,1,0:T(2,128)S(1)}, f32[1,2,896]{2,1,0:T(2,128)S(1)}, u32[]{:S(2)}, u32[]{:S(2)}) collective-permute-start(f32[1,2,896]{2,1,0:T(2,128)S(1)} %get-tuple-element.160), channel_id=1, source_target_pairs={{1,0},{2,1},{3,2},{4,3},{5,4},{6,5},{7,6},{8,7},{9,8},{10,9},{11,1... | collective-permute-start | bytes 21512 | tf_op jit(solution)/shard_map/ppermute | solution.py:33
  148.9 2.1 fusion.87
  157.4 1.9 collective-permute-start.8
  159.3 2.4 collective-permute-start.9
  162.7 1.5 collective-permute-done.9
  165.1 104.3 %all-reduce.71 = (f32[]{:T(128)}, f32[]{:T(128)}) all-reduce(f32[]{:T(128)} %get-tuple-element.48, f32[]{:T(128)} %get-tuple-element.47), channel_id=1, replica_groups=mesh['dom'=512] {'dom'}, use_global_device_ids=true, to_apply=%region_6.7 | all-reduce | flops 2 | bytes 16 | tf_op jit(solution)/shard_map/psum | solution.py:434
  270.8 1.9 collective-permute-start.10
  272.7 2.9 collective-permute-start.11
  275.9 1.7 collective-permute-done.11
  278.7 1.3 slice.1675
  280.0 1.3 slice.1674
  281.3 1.3 slice.1673
  283.8 1.3 slice.1671
  285.1 1.3 slice.1670
  286.4 1.3 slice.1669
  287.7 1.3 slice.1668
  289.0 1.3 slice.1667
  300.3 2.0 collective-permute-start.12
  302.9 6.2 collective-permute-done.12
  309.1 9.7 %collective-permute-start.13 = (f32[1,2,896]{2,1,0:T(2,128)S(1)}, f32[1,2,896]{2,1,0:T(2,128)S(1)}, u32[]{:S(2)}, u32[]{:S(2)}) collective-permute-start(f32[1,2,896]{2,1,0:T(2,128)S(1)} %get-tuple-element.158), channel_id=1, source_target_pairs={{1,0},{2,1},{3,2},{4,3},{5,4},{6,5},{7,6},{8,7},{9,8},{10,9},{11,1... | collective-permute-start | bytes 21512 | tf_op jit(solution)/shard_map/ppermute | solution.py:33
  320.8 98.8 %psum.44 = f32[]{:T(128)} all-reduce(f32[]{:T(128)} %multiply_reduce_fusion.9), channel_id=1, replica_groups=mesh['dom'=512] {'dom'}, use_global_device_ids=true, to_apply=%region_12.13 | all-reduce | flops 1 | bytes 8 | tf_op jit(solution)/shard_map/psum | solution.py:434
  427.6 1.9 collective-permute-start.14
  429.5 2.7 collective-permute-start.15
  432.4 2.0 collective-permute-done.15
  435.3 104.4 %psum.45 = f32[]{:T(128)} all-reduce(f32[]{:T(128)} %multiply_reduce_fusion.8), channel_id=1, replica_groups=mesh['dom'=512] {'dom'}, use_global_device_ids=true, to_apply=%region_15.16 | all-reduce | flops 1 | bytes 8 | tf_op jit(solution)/shard_map/psum | solution.py:439
  541.1 1.9 collective-permute-start.16
  543.1 2.9 collective-permute-start.17
  546.3 1.6 collective-permute-done.17
  549.1 1.3 slice.1762
  550.3 1.3 slice.1761
  551.6 1.3 slice.1760
  552.9 1.3 slice.1759
  555.5 1.3 slice.1757
  556.8 1.3 slice.1756
  570.6 2.0 collective-permute-start.18
  572.6 6.8 collective-permute-done.18
  579.4 9.7 %collective-permute-start.19 = (f32[1,2,896]{2,1,0:T(2,128)S(1)}, f32[1,2,896]{2,1,0:T(2,128)S(1)}, u32[]{:S(2)}, u32[]{:S(2)}) collective-permute-start(f32[1,2,896]{2,1,0:T(2,128)S(1)} %get-tuple-element.156), channel_id=1, source_target_pairs={{1,0},{2,1},{3,2},{4,3},{5,4},{6,5},{7,6},{8,7},{9,8},{10,9},{11,1... | collective-permute-start | bytes 21512 | tf_op jit(solution)/shard_map/ppermute | solution.py:33
  590.9 99.1 %psum.46 = f32[]{:T(128)} all-reduce(f32[]{:T(128)} %multiply_reduce_fusion.7), channel_id=1, replica_groups=mesh['dom'=512] {'dom'}, use_global_device_ids=true, to_apply=%region_18.19 | all-reduce | flops 1 | bytes 8 | tf_op jit(solution)/shard_map/psum | solution.py:434
  698.0 1.9 collective-permute-start.20
  699.9 2.7 collective-permute-start.21
  702.6 2.2 collective-permute-done.21
  705.7 104.4 %psum.47 = f32[]{:T(128)} all-reduce(f32[]{:T(128)} %multiply_reduce_fusion.6), channel_id=1, replica_groups=mesh['dom'=512] {'dom'}, use_global_device_ids=true, to_apply=%region_21.22 | all-reduce | flops 1 | bytes 8 | tf_op jit(solution)/shard_map/psum | solution.py:439
  (783 shorter events, 113.5 us)
Async XLA Ops:
  0.6 6.3 copy-start.35
  0.6 6.3 copy-start.6
  0.7 6.3 copy-start.21
  2.4 5.5 copy-start
  6.2 2.7 copy-start.1
  6.2 3.3 copy-start.5
  6.9 3.3 copy-start.4
  8.1 4.7 copy-start.16
  9.3 4.4 copy-start.3
  14.2 2.1 copy-start.12
  14.2 2.3 copy-start.11
  14.2 2.6 copy-start.10
  15.5 2.8 copy-start.34
  22.5 2.0 copy-start.9
  23.0 1.8 copy-start.8
  23.2 2.0 copy-start.15
  23.8 1.5 copy-start.17
  37.0 11.8 %copy-start.48 = (f32[16]{0:T(128)S(1)}, f32[16]{0:T(128)}, u32[]{:S(2)}) copy-start(f32[16]{0:T(128)} %get-tuple-element.42) | copy-start | bytes 196
  37.0 11.8 %copy-start.46 = (f32[16]{0:T(128)S(1)}, f32[16]{0:T(128)}, u32[]{:S(2)}) copy-start(f32[16]{0:T(128)} %get-tuple-element.43) | copy-start | bytes 196
  37.0 11.8 %copy-start.47 = (f32[16]{0:T(128)S(1)}, f32[16]{0:T(128)}, u32[]{:S(2)}) copy-start(f32[16]{0:T(128)} %get-tuple-element.44) | copy-start | bytes 196
  37.0 11.8 %copy-start.53 = (f32[100]{0:T(128)S(1)}, f32[100]{0:T(128)}, u32[]{:S(2)}) copy-start(f32[100]{0:T(128)} %constant.132.clone) | copy-start | bytes 1204
  37.0 11.8 %copy-start.52 = (f32[10]{0:T(128)S(1)}, f32[10]{0:T(128)}, u32[]{:S(2)}) copy-start(f32[10]{0:T(128)} %constant.130.clone) | copy-start | bytes 124
  37.1 11.9 %copy-start.51 = (f32[100]{0:T(128)S(1)}, f32[100]{0:T(128)}, u32[]{:S(2)}) copy-start(f32[100]{0:T(128)} %constant.131.clone) | copy-start | bytes 1204
  37.1 12.0 %copy-start.36 = (f32[512]{0:T(512)S(1)}, f32[512]{0:T(512)}, u32[]{:S(2)}) copy-start(f32[512]{0:T(512)} %constant.280) | copy-start | bytes 6148
  38.0 11.2 %collective-permute-start = (f32[4,1,896]{2,1,0:T(1,128)S(1)}, f32[4,1,896]{2,1,0:T(1,128)S(1)}, u32[]{:S(2)}, u32[]{:S(2)}) collective-permute-start(f32[4,1,896]{2,1,0:T(1,128)S(1)} %get-tuple-element.111), channel_id=1, source_target_pairs={{0,1},{1,2},{2,3},{3,4},{4,5},{5,6},{6,7},{7,8},{8,9},{9,10},{10,1... | collective-permute-start | bytes 43016 | tf_op jit(solution)/shard_map/ppermute | solution.py:30
  42.6 6.9 collective-permute-start.1
  48.9 73.2 %copy-start.37 = (f32[16,100]{1,0:T(8,128)}, f32[16,100]{1,0:T(8,128)S(1)}, u32[]{:S(2)}) copy-start(f32[16,100]{1,0:T(8,128)S(1)} %broadcast_multiply_fusion.2) | copy-start | bytes 19204
  49.0 73.1 %copy-start.40 = (f32[16,10]{1,0:T(8,128)}, f32[16,10]{1,0:T(8,128)S(1)}, u32[]{:S(2)}) copy-start(f32[16,10]{1,0:T(8,128)S(1)} %broadcast_multiply_fusion.4) | copy-start | bytes 1924
  49.0 73.0 %copy-start.43 = (f32[16,100]{1,0:T(8,128)}, f32[16,100]{1,0:T(8,128)S(1)}, u32[]{:S(2)}) copy-start(f32[16,100]{1,0:T(8,128)S(1)} %broadcast_multiply_fusion.3) | copy-start | bytes 19204
  71.8 12.7 %collective-permute-start.3 = (f32[1,1,896]{2,1,0:T(1,128)S(1)}, f32[1,1,896]{2,1,0:T(1,128)S(1)}, u32[]{:S(2)}, u32[]{:S(2)}) collective-permute-start(f32[1,1,896]{2,1,0:T(1,128)S(1)} %get-tuple-element.190), channel_id=1, source_target_pairs={{1,0},{2,1},{3,2},{4,3},{5,4},{6,5},{7,6},{8,7},{9,8},{10,9},{11,1... | collective-permute-start | bytes 10760 | tf_op jit(solution)/shard_map/ppermute | solution.py:33
  82.6 9.7 %collective-permute-start.2 = (f32[1,1,896]{2,1,0:T(1,128)S(1)}, f32[1,1,896]{2,1,0:T(1,128)S(1)}, u32[]{:S(2)}, u32[]{:S(2)}) collective-permute-start(f32[1,1,896]{2,1,0:T(1,128)S(1)} %get-tuple-element.191), channel_id=1, source_target_pairs={{0,1},{1,2},{2,3},{3,4},{4,5},{5,6},{6,7},{7,8},{8,9},{9,10},{10,1... | collective-permute-start | bytes 10760 | tf_op jit(solution)/shard_map/ppermute | solution.py:30
  84.5 37.6 %copy-start.54 = (f32[16]{0:T(128)}, f32[16]{0:T(128)S(1)}, u32[]{:S(2)}) copy-start(f32[16]{0:T(128)S(1)} %broadcast_multiply_fusion.5) | copy-start | bytes 196
  92.3 178.4 %copy-start.22 = (f32[1,1,896]{2,1,0:T(1,128)}, f32[1,1,896]{2,1,0:T(1,128)S(1)}, u32[]{:S(2)}) copy-start(f32[1,1,896]{2,1,0:T(1,128)S(1)} %get-tuple-element.62) | copy-start | bytes 10756
  92.3 178.4 %copy-start.24 = (f32[1,1,896]{2,1,0:T(1,128)}, f32[1,1,896]{2,1,0:T(1,128)S(1)}, u32[]{:S(2)}) copy-start(f32[1,1,896]{2,1,0:T(1,128)S(1)} %get-tuple-element.188) | copy-start | bytes 10756
  92.3 12.7 %collective-permute-start.5 = (f32[1,1,896]{2,1,0:T(1,128)S(1)}, f32[1,1,896]{2,1,0:T(1,128)S(1)}, u32[]{:S(2)}, u32[]{:S(2)}) collective-permute-start(f32[1,1,896]{2,1,0:T(1,128)S(1)} %get-tuple-element.186), channel_id=1, source_target_pairs={{1,0},{2,1},{3,2},{4,3},{5,4},{6,5},{7,6},{8,7},{9,8},{10,9},{11,1... | collective-permute-start | bytes 10760 | tf_op jit(solution)/shard_map/ppermute | solution.py:33
  102.0 3.1 collective-permute-start.4
  128.2 9.9 %collective-permute-start.6 = (f32[1,2,896]{2,1,0:T(2,128)S(1)}, f32[1,2,896]{2,1,0:T(2,128)S(1)}, u32[]{:S(2)}, u32[]{:S(2)}) collective-permute-start(f32[1,2,896]{2,1,0:T(2,128)S(1)} %slice.1935), channel_id=1, source_target_pairs={{0,1},{1,2},{2,3},{3,4},{4,5},{5,6},{6,7},{7,8},{8,9},{9,10},{10,1... | collective-permute-start | bytes 21512 | tf_op jit(solution)/shard_map/ppermute | solution.py:30
  138.0 10.5 %collective-permute-start.7 = (f32[1,2,896]{2,1,0:T(2,128)S(1)}, f32[1,2,896]{2,1,0:T(2,128)S(1)}, u32[]{:S(2)}, u32[]{:S(2)}) collective-permute-start(f32[1,2,896]{2,1,0:T(2,128)S(1)} %get-tuple-element.160), channel_id=1, source_target_pairs={{1,0},{2,1},{3,2},{4,3},{5,4},{6,5},{7,6},{8,7},{9,8},{10,9},{11,1... | collective-permute-start | bytes 21512 | tf_op jit(solution)/shard_map/ppermute | solution.py:33
  156.4 8.0 copy-start.49
  157.4 5.3 collective-permute-start.8
  159.3 4.9 collective-permute-start.9
  164.3 113.9 %copy-start.32 = (f32[1,1,896]{2,1,0:T(1,128)}, f32[1,1,896]{2,1,0:T(1,128)S(1)}, u32[]{:S(2)}) copy-start(f32[1,1,896]{2,1,0:T(1,128)S(1)} %get-tuple-element.182) | copy-start | bytes 10756
  164.3 127.3 %copy-start.30 = (f32[1,1,896]{2,1,0:T(1,128)}, f32[1,1,896]{2,1,0:T(1,128)S(1)}, u32[]{:S(2)}) copy-start(f32[1,1,896]{2,1,0:T(1,128)S(1)} %get-tuple-element.56) | copy-start | bytes 10756
  270.8 7.0 collective-permute-start.10
  272.7 4.9 collective-permute-start.11
  300.3 8.8 %collective-permute-start.12 = (f32[1,2,896]{2,1,0:T(2,128)S(1)}, f32[1,2,896]{2,1,0:T(2,128)S(1)}, u32[]{:S(2)}, u32[]{:S(2)}) collective-permute-start(f32[1,2,896]{2,1,0:T(2,128)S(1)} %slice.2010), channel_id=1, source_target_pairs={{0,1},{1,2},{2,3},{3,4},{4,5},{5,6},{6,7},{7,8},{8,9},{9,10},{10,1... | collective-permute-start | bytes 21512 | tf_op jit(solution)/shard_map/ppermute | solution.py:30
  309.1 10.8 %collective-permute-start.13 = (f32[1,2,896]{2,1,0:T(2,128)S(1)}, f32[1,2,896]{2,1,0:T(2,128)S(1)}, u32[]{:S(2)}, u32[]{:S(2)}) collective-permute-start(f32[1,2,896]{2,1,0:T(2,128)S(1)} %get-tuple-element.158), channel_id=1, source_target_pairs={{1,0},{2,1},{3,2},{4,3},{5,4},{6,5},{7,6},{8,7},{9,8},{10,9},{11,1... | collective-permute-start | bytes 21512 | tf_op jit(solution)/shard_map/ppermute | solution.py:33
  426.6 8.0 copy-start.50
  427.6 4.8 collective-permute-start.14
  429.5 4.9 collective-permute-start.15
  541.1 7.0 collective-permute-start.16
  543.1 4.9 collective-permute-start.17
  570.6 8.8 %collective-permute-start.18 = (f32[1,2,896]{2,1,0:T(2,128)S(1)}, f32[1,2,896]{2,1,0:T(2,128)S(1)}, u32[]{:S(2)}, u32[]{:S(2)}) collective-permute-start(f32[1,2,896]{2,1,0:T(2,128)S(1)} %slice.2085), channel_id=1, source_target_pairs={{0,1},{1,2},{2,3},{3,4},{4,5},{5,6},{6,7},{7,8},{8,9},{9,10},{10,1... | collective-permute-start | bytes 21512 | tf_op jit(solution)/shard_map/ppermute | solution.py:30
  579.4 10.5 %collective-permute-start.19 = (f32[1,2,896]{2,1,0:T(2,128)S(1)}, f32[1,2,896]{2,1,0:T(2,128)S(1)}, u32[]{:S(2)}, u32[]{:S(2)}) collective-permute-start(f32[1,2,896]{2,1,0:T(2,128)S(1)} %get-tuple-element.156), channel_id=1, source_target_pairs={{1,0},{2,1},{3,2},{4,3},{5,4},{6,5},{7,6},{8,7},{9,8},{10,9},{11,1... | collective-permute-start | bytes 21512 | tf_op jit(solution)/shard_map/ppermute | solution.py:33
  696.5 114.9 %copy-start.28 = (f32[4,896]{1,0:T(4,128)S(1)}, f32[4,896]{1,0:T(4,128)}, u32[]{:S(2)}) copy-start(f32[4,896]{1,0:T(4,128)} %get-tuple-element.151) | copy-start | bytes 43012
  696.5 114.9 %copy-start.29 = (f32[4,896]{1,0:T(4,128)S(1)}, f32[4,896]{1,0:T(4,128)}, u32[]{:S(2)}) copy-start(f32[4,896]{1,0:T(4,128)} %get-tuple-element.153) | copy-start | bytes 43012
  696.5 115.6 %copy-start.19 = (f32[6,896]{1,0:T(8,128)S(1)}, f32[6,896]{1,0:T(8,128)}, u32[]{:S(2)}) copy-start(f32[6,896]{1,0:T(8,128)} %get-tuple-element.167) | copy-start | bytes 64516
  696.5 115.6 %copy-start.20 = (f32[6,896]{1,0:T(8,128)S(1)}, f32[6,896]{1,0:T(8,128)}, u32[]{:S(2)}) copy-start(f32[6,896]{1,0:T(8,128)} %get-tuple-element.165) | copy-start | bytes 64516
  696.5 115.6 %copy-start.23 = (f32[1,1,896]{2,1,0:T(1,128)S(1)}, f32[1,1,896]{2,1,0:T(1,128)}, u32[]{:S(2)}) copy-start(f32[1,1,896]{2,1,0:T(1,128)} %copy-done.22) | copy-start | bytes 10756
  696.6 115.5 %copy-start.25 = (f32[1,1,896]{2,1,0:T(1,128)S(1)}, f32[1,1,896]{2,1,0:T(1,128)}, u32[]{:S(2)}) copy-start(f32[1,1,896]{2,1,0:T(1,128)} %copy-done.24) | copy-start | bytes 10756
  696.6 115.5 %copy-start.31 = (f32[1,1,896]{2,1,0:T(1,128)S(1)}, f32[1,1,896]{2,1,0:T(1,128)}, u32[]{:S(2)}) copy-start(f32[1,1,896]{2,1,0:T(1,128)} %copy-done.30) | copy-start | bytes 10756
  696.6 115.5 %copy-start.33 = (f32[1,1,896]{2,1,0:T(1,128)S(1)}, f32[1,1,896]{2,1,0:T(1,128)}, u32[]{:S(2)}) copy-start(f32[1,1,896]{2,1,0:T(1,128)} %copy-done.32) | copy-start | bytes 10756
  698.0 4.6 collective-permute-start.20
  699.9 4.9 collective-permute-start.21
  (15 other events, 15.6 us)
where the time goes:
time: 823 us; the launch traced here: 813 us
  blocking collectives  511 us (62%)
  local copies, waits for them, and re-layouts  102 us (12%)
  starting transfers between devices  95.6 us (12%)
  waiting for transfers between devices  36.2 us (4%)
  matrix products  29.5 us (4%)
  other arithmetic  26.4 us (3%)
  between operations  12.9 us (2%)
    psum x3, blocking collectives, shards(): precond_sum = lax.psum(weighted(residual, smoothed), 'dom')  302 us
    psum x2, blocking collectives, shards(): step_size = precond_sum / lax.psum(weighted(direction, image), 'dom')  209 us
    ppermute x11, starting transfers between devices, extended_2(): lax.ppermute(lax.slice_in_dim(block, 0, width, axis=dim), axis, backward)  69.5 us
    slice x96, local copies, waits for them, and re-layouts, windows(): lax.slice_in_dim(field, offset, offset + stride * (count - 1) + 1, stride...  53.5 us
    ppermute x11, waiting for transfers between devices, extended_2(): lax.ppermute(lax.slice_in_dim(block, block.shape[dim] - width, None, axis...  26.3 us
    ppermute x11, starting transfers between devices, extended_2(): lax.ppermute(lax.slice_in_dim(block, block.shape[dim] - width, None, axis...  26.1 us
  transfers between devices with their start and end apart: 22, of which 12 were waited for; matrix products, arithmetic and copies ran while one was open for 1% of the time, Pallas kernels for 0%

commit v1 on v0

v1 whole, which is shorter than its diff:
```python
import functools

import jax
import jax.numpy as jnp
import numpy as np
from jax import lax
from jax.experimental import pallas as pl
from jax.experimental.pallas import tpu as pltpu
from jax.sharding import PartitionSpec as P

NP = 8
NF = 12
ES = 16
LANES = 128
HIGHEST = lax.Precision.HIGHEST
time_step = 0.25
viscosity = 0.05
mass_shift = 0.001
STEPS = (0.45, 0.3)
VMEM = 48 * 1024 * 1024


def legendre_pair(points, order):
    before = np.ones(points.shape)
    current = points * 1.0
    for level in range(2, order + 1):
        nextone = ((2 * level - 1) * points * current - (level - 1) * before) / level
        before = current
        current = nextone
    return (current, before)


def jacobi_eigen(matrix):
    size = matrix.shape[0]
    work = matrix * 1.0
    vectors = np.eye(size)
    for sweep in range(30):
        for first in range(size - 1):
            for second in range(first + 1, size):
                off = float(work[first, second])
                if abs(off) > 1e-300:
                    tau = (float(work[second, second]) - float(work[first, first])) / (2.0 * off)
                    if tau >= 0.0:
                        tangent = 1.0 / (tau + (1.0 + tau * tau) ** 0.5)
                    else:
                        tangent = -1.0 / (-tau + (1.0 + tau * tau) ** 0.5)
                    cosine = 1.0 / (1.0 + tangent * tangent) ** 0.5
                    sine = tangent * cosine
                    rotation = np.eye(size)
                    rotation[first, first] = cosine
                    rotation[second, second] = cosine
                    rotation[first, second] = sine
                    rotation[second, first] = -sine
                    work = rotation.T @ work @ rotation
                    vectors = vectors @ rotation
    diagonal_index = np.arange(size)
    return (work[diagonal_index, diagonal_index], vectors)


def base_tables(points_edge, points_fine):
    degree = points_edge - 1
    points = -np.cos(np.pi * np.arange(points_edge) / degree)
    for sweep in range(100):
        top, below = legendre_pair(points, degree)
        points = points - (points * top - below) / (points_edge * top)
    top, below = legendre_pair(points, degree)
    weight_gll = 2.0 / (degree * points_edge * top**2)
    spacing = points[:, None] - points[None, :] + np.eye(points_edge)
    barycentric = 1.0 / np.prod(spacing, axis=1)
    derivative = barycentric[None, :] / barycentric[:, None] / spacing
    derivative = derivative * (1.0 - np.eye(points_edge))
    derivative = derivative - np.eye(points_edge) * derivative.sum(axis=1)[:, None]
    fine_points = np.cos(np.pi * (np.arange(points_fine) + 0.75) / (points_fine + 0.5))
    for sweep in range(100):
        top, below = legendre_pair(fine_points, points_fine)
        slope = points_fine * (fine_points * top - below) / (fine_points * fine_points - 1.0)
        fine_points = fine_points - top / slope
    top, below = legendre_pair(fine_points, points_fine)
    slope = points_fine * (fine_points * top - below) / (fine_points * fine_points - 1.0)
    fine_weight = 2.0 / ((1.0 - fine_points * fine_points) * slope * slope)
    fine_points = fine_points[::-1]
    fine_weight = fine_weight[::-1]
    interpolate = np.ones((points_fine, points_edge))
    for column in range(points_edge):
        for other in range(points_edge):
            if other != column:
                interpolate[:, column] = (
                    interpolate[:, column]
                    * (fine_points - points[other])
                    / (points[column] - points[other])
                )
    stiffness = derivative.T @ (weight_gll[:, None] * derivative)
    extent = 3 * degree + 1
    joined_stiff = np.zeros((extent, extent))
    joined_mass = np.zeros(extent)
    for segment in range(3):
        offset = segment * degree
        joined_stiff[offset : offset + points_edge, offset : offset + points_edge] += stiffness
        joined_mass[offset : offset + points_edge] += weight_gll
    low = degree - 1
    high = 2 * degree + 2
    root_mass = np.sqrt(joined_mass[low:high])
    scaled = joined_stiff[low:high, low:high] / root_mass[:, None] / root_mass[None, :]
    scaled = 0.5 * (scaled + scaled.T)
    eigen_values, eigen_vectors = jacobi_eigen(scaled)
    solve_mat = eigen_vectors / root_mass[:, None]
    breadth = high - low
    return dict(
        derivative=derivative,
        interpolate=interpolate,
        weight=weight_gll,
        fine_weight=fine_weight,
        solve=solve_mat,
        eigen=eigen_values,
    )


def f32(value):
    return np.ascontiguousarray(value, dtype=np.float32)


def make_tables():
    base = base_tables(NP, NF)
    deriv, interp, solve, eigen = base["derivative"], base["interpolate"], base["solve"], base["eigen"]
    w, wf = base["weight"], base["fine_weight"]
    out = {}
    index = np.arange(NP)

    def sublane(matrix):
        rows = [matrix[index, (index + shift) % NP] for shift in range(NP)]
        return f32(np.broadcast_to(np.stack(rows)[:, :, None], (NP, NP, LANES)))

    def lane(matrix):
        rows = []
        for shift in range(-(NP - 1), NP):
            row = np.zeros(NP)
            for q in range(NP):
                if 0 <= q + shift < NP:
                    row[q] = matrix[q, q + shift]
            rows.append(np.tile(row, ES))
        return f32(np.broadcast_to(np.stack(rows)[:, None, :], (2 * NP - 1, NP, LANES)))

    out["deriv"] = deriv
    out["ds"] = np.stack([sublane(deriv), sublane(deriv.T)])
    out["dq"] = np.stack([lane(deriv), lane(deriv.T)])
    out["w3"] = f32(np.einsum("a,s,q->asq", w, w, w).reshape(1, 512))
    out["jright"] = f32(np.kron(np.eye(ES), interp.T))
    out["jleft"] = f32(np.kron(interp, interp))
    out["wfine"] = f32(np.kron(np.kron(wf, wf)[:, None], np.tile(wf, ES)[None, :]))
    wide = NP + 2
    left = np.zeros((104, 3, wide, NP))
    back = np.zeros((3, wide, NP, 104))
    for i in range(wide):
        for j in range(wide):
            row = i * wide + j
            for a in range(wide):
                for s in range(NP):
                    left[row, 0, a, s] = solve[a, i] * solve[s + 1, j]
                    back[0, a, s, row] = solve[a, i] * solve[s + 1, j]
                left[row, 1, a, NP - 2] = solve[a, i] * solve[0, j]
                left[row, 2, a, 1] = solve[a, i] * solve[wide - 1, j]
                back[1, a, NP - 2, row] = solve[a, i] * solve[0, j]
                back[1, a, NP - 1, row] = solve[a, i] * solve[1, j]
                back[2, a, 1, row] = solve[a, i] * solve[wide - 1, j]
                back[2, a, 0, row] = solve[a, i] * solve[wide - 2, j]
    out["sleft"] = f32(left.reshape(104, 240))
    out["sback"] = f32(back.reshape(240, 104))
    out["sright"] = f32(np.kron(np.eye(ES), solve[1:-1, :]))
    out["srback"] = f32(np.kron(np.eye(ES), solve[1:-1, :].T))
    out["spread"] = f32(np.kron(np.eye(ES), np.ones((NP, wide))) / 8.0)
    lam_a = np.zeros((104, 1))
    lam_s = np.zeros((104, 1))
    lam_a[:100, 0] = np.repeat(eigen, wide)
    lam_s[:100, 0] = np.tile(eigen, wide)
    lam_q = np.tile(eigen, ES)[None, :]
    full = (104, ES * wide)
    out["lam"] = f32(np.stack([np.broadcast_to(lam_a, full), np.broadcast_to(lam_s, full), np.broadcast_to(lam_q, full)]))
    half = np.ones(NP)
    half[0] = half[-1] = 0.5
    out["ws"] = f32(np.broadcast_to(half[:, None], (NP, LANES)))
    return out


TAB = make_tables()
DERIV = [[float(x) for x in row] for row in TAB["deriv"]]
PARAMS = pltpu.CompilerParams(vmem_limit_bytes=VMEM)


def dot(left, right):
    return jnp.dot(left, right, precision=HIGHEST, preferred_element_type=jnp.float32)


def roll(x, shift, axis):
    return pltpu.roll(x, shift % x.shape[axis], axis)


def d_a(x, transposed):
    rows = []
    for a in range(NP):
        total = None
        for b in range(NP):
            term = (DERIV[b][a] if transposed else DERIV[a][b]) * x[b]
            total = term if total is None else total + term
        rows.append(total)
    return jnp.stack(rows)


def d_s(x, coef):
    total = coef[0][None] * x
    for shift in range(1, NP):
        total = total + coef[shift][None] * roll(x, -shift, 1)
    return total


def d_q(x, coef):
    total = coef[NP - 1][None] * x
    for shift in range(1, NP):
        total = total + coef[NP - 1 + shift][None] * roll(x, -shift, 2)
        total = total + coef[NP - 1 - shift][None] * roll(x, shift, 2)
    return total


def gradient(x, ds, dq):
    return d_a(x, False), d_s(x, ds[0]), d_q(x, dq[0])


def gradient_t(xa, xs, xq, ds, dq):
    return d_a(xa, True) + d_s(xs, ds[1]) + d_q(xq, dq[1])


def join_s(x):
    s = lax.broadcasted_iota(jnp.int32, x.shape, 1)
    from_before = roll(roll(x, NP, 2), 1, 1)
    from_after = roll(roll(x, -NP, 2), -1, 1)
    zero = jnp.zeros_like(x)
    return x + jnp.where(s == 0, from_before, jnp.where(s == NP - 1, from_after, zero))


def parity():
    return lax.rem(lax.axis_index("dom"), 2)


def put_payload(even, low, high, inner_ref, cross_ref):
    inner_ref[...] = jnp.where(even, high, low)
    cross_ref[...] = jnp.where(even, low, high)


def get_payload(even, inner_ref, cross_ref):
    inner, cross = inner_ref[...], cross_ref[...]
    return jnp.where(even, cross, inner), jnp.where(even, inner, cross)


def swap_inner(x, count):
    return lax.ppermute(x, "dom", [(i, i ^ 1) for i in range(count)])


def swap_cross(x, count):
    pairs = [(i, (i + 1) % count if i % 2 else (i - 1) % count) for i in range(count)]
    return lax.ppermute(x, "dom", pairs)


def to_lanes(x):
    shape = (x.shape[0], NP, LANES)
    lane = lax.broadcasted_iota(jnp.int32, shape, 2)
    pieces = []
    for tile in range(4):
        first = x[:, :8, tile * LANES : (tile + 1) * LANES]
        second = x[:, 8:, tile * LANES : (tile + 1) * LANES]
        pieces.append(jnp.where(lane < 64, first, roll(second, 64, 2)))
        pieces.append(jnp.where(lane < 64, roll(first, 64, 2), second))
    y = jnp.stack(pieces, axis=1).reshape(x.shape[0] * NP, NP, LANES)
    sub = lax.broadcasted_iota(jnp.int32, y.shape, 1)
    lane = lax.broadcasted_iota(jnp.int32, y.shape, 2)
    for bit in range(3):
        step = 1 << bit
        in_sub = (sub & step) != 0
        in_lane = (lane & (step * 8)) != 0
        up = roll(roll(y, -step, 1), step * 8, 2)
        down = roll(roll(y, step, 1), -step * 8, 2)
        y = jnp.where(in_sub == in_lane, y, jnp.where(in_lane, up, down))
    return y.reshape(x.shape[0], NP, NP, LANES)


def rows(x):
    return x.reshape(NP * NP, LANES)


def planes(x):
    return x.reshape(NP, NP, LANES)


def take_lanes(x, index):
    flat = x.reshape(-1, LANES)
    tiled = jnp.broadcast_to(index[None], x.shape).reshape(-1, LANES)
    return jnp.take_along_axis(flat, tiled, axis=1).reshape(x.shape)


def forcing_kernel(slot_ref, vel_ref, past_ref, metric_ref, jac_ref, w3_ref, ds_ref, dq_ref, jright_ref, jleft_ref, wfine_ref, force_ref, static_ref, inner_ref, cross_ref):
    even = parity() == 0
    ds, dq = ds_ref[...], dq_ref[...]
    jac = jac_ref[...]
    new, mid, old = vel_ref[0], vel_ref[1], vel_ref[2]
    guess = 3.0 * (new - mid) + old
    direct = (jac * w3_ref[...])[None] * (-10.0 * new + 16.0 * mid - 6.0 * old) + 3.0 * past_ref[0] - past_ref[1]
    metric = metric_ref[...]
    lanes = to_lanes(jnp.concatenate([new, guess, direct, metric, jac[None]], axis=0))
    mass_w = to_lanes(jnp.broadcast_to(w3_ref[...], (16, 512))[None])[0]
    new, guess, direct, metric, jac = lanes[0:3], lanes[3:6], lanes[6:9], lanes[9:12], lanes[12]
    fields = [rows(jac)] + [rows(new[d] * metric[d]) for d in range(3)]
    for i in range(3):
        fields.extend(rows(part) for part in gradient(new[i], ds, dq))
    wide = dot(jnp.concatenate(fields, axis=0), jright_ref[...])
    jleft = jleft_ref[...]
    fine = [dot(jleft, wide[64 * k : 64 * k + 64]) for k in range(13)]
    scale = fine[0] * wfine_ref[...]
    products = []
    for i in range(3):
        total = fine[1] * fine[4 + 3 * i] + fine[2] * fine[5 + 3 * i] + fine[3] * fine[6 + 3 * i]
        products.append(lax.dot_general(jleft, scale * total, (((0,), (0,)), ((), ())), precision=HIGHEST, preferred_element_type=jnp.float32))
    coarse = lax.dot_general(jnp.concatenate(products, axis=0), jright_ref[...], (((1,), (1,)), ((), ())), precision=HIGHEST, preferred_element_type=jnp.float32)
    mass = jac * mass_w
    factor = [mass * metric[d] * metric[d] for d in range(3)]
    result = []
    for i in range(3):
        ga, gs, gq = gradient(guess[i], ds, dq)
        stiff = gradient_t(factor[0] * ga, factor[1] * gs, factor[2] * gq, ds, dq)
        result.append(direct[i] - 3.0 * planes(coarse[64 * i : 64 * i + 64]) - viscosity * stiff)
    result.append(mass)
    result.extend([metric[0], metric[1], metric[2]])
    lane = lax.broadcasted_iota(jnp.int32, (NP, LANES), 1)
    index = jnp.zeros((NP, LANES), jnp.int32)
    for e in range(ES):
        index = jnp.where(lane // NP == slot_ref[e], e * NP, index)
    index = index + lane % NP
    result = [take_lanes(x, index) for x in result]
    force = jnp.stack([join_s(x) for x in result[:4]])
    force_ref[...] = force
    static_ref[...] = jnp.stack(result[3:])
    put_payload(even, force[:, 0], force[:, NP - 1], inner_ref, cross_ref)


def factor_kernel(static_ref, spread_ref, lam_ref, op_ref, grad_ref, inv_ref):
    mass = static_ref[0]
    lam = lam_ref[...]
    denom = None
    sums = []
    for d in range(3):
        one = mass * static_ref[1 + d]
        two = one * static_ref[1 + d]
        grad_ref[d] = one
        op_ref[d] = two
        sums.append(jnp.sum(rows(two), axis=0, keepdims=True))
    op_ref[3] = mass_shift * mass
    sums.append(jnp.sum(rows(mass), axis=0, keepdims=True))
    sums.append(jnp.zeros((4, LANES), jnp.float32))
    level = dot(jnp.concatenate(sums, axis=0), spread_ref[...])
    denom = level[0:1] * lam[0] + level[1:2] * lam[1] + level[2:3] * lam[2] + mass_shift * level[3:4]
    inv_ref[...] = 1.0 / denom


def divergence_kernel(force_ref, inner_in, cross_in, grad_ref, ds_ref, dq_ref, div_ref, inner_ref, cross_ref):
    even = parity() == 0
    low, high = get_payload(even, inner_in, cross_in)
    force = force_ref[...]
    whole = jnp.concatenate([(force[:, 0] + low)[:, None], force[:, 1:-1], (force[:, -1] + high)[:, None]], axis=1)
    inv = 1.0 / whole[3]
    parts = [grad_ref[d] * (whole[d] * inv) for d in range(3)]
    div = join_s(gradient_t(parts[0], parts[1], parts[2], ds_ref[...], dq_ref[...]))
    div_ref[...] = div
    put_payload(even, div[:2], div[6:], inner_ref, cross_ref)


def assemble_rows(local, low, high):
    return jnp.concatenate(
        [low[:1], (local[0] + low[1])[None], local[1:-1], (local[-1] + high[0])[None], high[1:]], axis=0
    )


def schwarz(ext, even, inv_ref, sleft_ref, sright_ref, srback_ref, sback_ref, z_ref, inner_ref, cross_ref):
    flat = ext.reshape(80, LANES)
    stacked = jnp.concatenate([flat, roll(flat, NP, 1), roll(flat, -NP, 1)], axis=0)
    spectra = dot(dot(sleft_ref[...], stacked), sright_ref[...]) * inv_ref[...]
    blocks = dot(sback_ref[...], dot(spectra, srback_ref[...]))
    z = blocks[:80] + roll(blocks[80:160], -NP, 1) + roll(blocks[160:], NP, 1)
    z = z.reshape(NP + 2, NP, LANES)
    z_ref[...] = z[1:-1]
    put_payload(even, z[:2], z[8:], inner_ref, cross_ref)


def first_smooth_kernel(div_ref, inner_in, cross_in, inv_ref, sleft_ref, sright_ref, srback_ref, sback_ref, ext_ref, z_ref, inner_ref, cross_ref):
    even = parity() == 0
    low, high = get_payload(even, inner_in, cross_in)
    ext = assemble_rows(div_ref[...], low, high)
    ext_ref[...] = ext
    schwarz(ext, even, inv_ref, sleft_ref, sright_ref, srback_ref, sback_ref, z_ref, inner_ref, cross_ref)


def smooth_kernel(step, before_ref, local_ref, inner_in, cross_in, inv_ref, sleft_ref, sright_ref, srback_ref, sback_ref, image_ref, ext_ref, z_ref, inner_ref, cross_ref):
    even = parity() == 0
    low, high = get_payload(even, inner_in, cross_in)
    image = assemble_rows(local_ref[...], low, high)
    image_ref[...] = image[1:-1]
    ext = before_ref[...] - step * image
    ext_ref[...] = ext
    schwarz(ext, even, inv_ref, sleft_ref, sright_ref, srback_ref, sback_ref, z_ref, inner_ref, cross_ref)


def finish_smooth(even, z_ref, inner_in, cross_in):
    low, high = get_payload(even, inner_in, cross_in)
    z = z_ref[...]
    return jnp.concatenate([z[:2] + low, z[2:6], z[6:] + high], axis=0)


def operate(v, op_ref, ds_ref, dq_ref):
    ds, dq = ds_ref[...], dq_ref[...]
    ga, gs, gq = gradient(v, ds, dq)
    local = gradient_t(op_ref[0] * ga, op_ref[1] * gs, op_ref[2] * gq, ds, dq) + op_ref[3] * v
    return join_s(local)


def operator_kernel(z_ref, inner_in, cross_in, op_ref, ds_ref, dq_ref, v_ref, local_ref, inner_ref, cross_ref):
    even = parity() == 0
    v = finish_smooth(even, z_ref, inner_in, cross_in)
    v_ref[...] = v
    local = operate(v, op_ref, ds_ref, dq_ref)
    local_ref[...] = local
    put_payload(even, local[:2], local[6:], inner_ref, cross_ref)


def last_operator_kernel(z_ref, inner_in, cross_in, op_ref, ds_ref, dq_ref, ws_ref, ext_ref, v0_ref, v1_ref, l0_ref, l1_ref, v_ref, local_ref, inner_ref, cross_ref, sums_ref):
    even = parity() == 0
    v2 = finish_smooth(even, z_ref, inner_in, cross_in)
    v_ref[...] = v2
    l2 = operate(v2, op_ref, ds_ref, dq_ref)
    local_ref[...] = l2
    put_payload(even, l2[:2], l2[6:], inner_ref, cross_ref)
    ws = ws_ref[...]
    v = [v0_ref[...], v1_ref[...], v2]
    images = [l0_ref[...], l1_ref[...], l2]
    residual = ext_ref[...][1:-1]
    residual = jnp.concatenate([0.5 * residual[:1], residual[1:-1], 0.5 * residual[-1:]], axis=0)
    pairs = [(v[i], images[j]) for i, j in ((0, 0), (0, 1), (0, 2), (1, 1), (1, 2), (2, 2))]
    pairs.extend((v[i], residual) for i in range(3))
    lane = lax.broadcasted_iota(jnp.int32, (1, LANES), 1)
    line = jnp.zeros((1, LANES), jnp.float32)
    for k, (left, right) in enumerate(pairs):
        line = jnp.where(lane == k, jnp.sum(jnp.sum(left * right, axis=0) * ws), line)
    sums_ref[...] = jnp.broadcast_to(line, sums_ref.shape)


def to_output(x):
    by_s = [jnp.concatenate([x[a][s : s + 1] for a in range(NP)], axis=0) for s in range(NP - 1)]
    tiles = []
    for tile in range(7):
        at = lax.broadcasted_iota(jnp.int32, (NP, LANES), 1) + tile * LANES
        element = at // 56
        s = (at - element * 56) // NP
        index = element * NP + at % NP
        value = jnp.take_along_axis(by_s[0], index, axis=1)
        for k in range(1, NP - 1):
            value = jnp.where(s == k, jnp.take_along_axis(by_s[k], index, axis=1), value)
        tiles.append(value)
    return jnp.concatenate(tiles, axis=1)


def combine_kernel(sums_ref, ext_ref, v0_ref, v1_ref, v2_ref, w0_ref, w1_ref, local_ref, inner_in, cross_in, p_ref, r_ref):
    even = parity() == 0
    low, high = get_payload(even, inner_in, cross_in)
    w2 = assemble_rows(local_ref[...], low, high)[1:-1]
    line = jnp.sum(sums_ref[...], axis=0, keepdims=True)
    h00, h01, h02, h11, h12, h22, g0, g1, g2 = [line[:, k : k + 1] for k in range(9)]
    m1, m2 = h01 / h00, h02 / h00
    k11, k12, k22 = h11 - m1 * h01, h12 - m1 * h02, h22 - m2 * h02
    f1, f2 = g1 - m1 * g0, g2 - m2 * g0
    n2 = k12 / k11
    c2 = (f2 - n2 * f1) / (k22 - n2 * k12)
    c1 = (f1 - k12 * c2) / k11
    c0 = (g0 - h01 * c1 - h02 * c2) / h00
    v = [v0_ref[...], v1_ref[...], v2_ref[...]]
    pressure = (c0 + STEPS[0])[None] * v[0] + (c1 + STEPS[1])[None] * v[1] + c2[None] * v[2]
    residual = ext_ref[...][1:-1] - (c0[None] * w0_ref[...] + c1[None] * w1_ref[...] + c2[None] * w2)
    p_ref[...] = to_output(pressure)
    r_ref[...] = to_output(residual)


def call(kernel, shapes, *args, smem=()):
    specs = [pl.BlockSpec(memory_space=pltpu.SMEM if k in smem else pltpu.VMEM) for k in range(len(args))]
    return pl.pallas_call(
        kernel,
        out_shape=[jax.ShapeDtypeStruct(shape, jnp.float32) for shape in shapes],
        in_specs=specs,
        out_specs=[pl.BlockSpec(memory_space=pltpu.VMEM)] * len(shapes),
        compiler_params=PARAMS,
    )(*args)


def gather_sums(sums, count):
    if count == 512:
        near = [[16 * i + j for j in range(16)] for i in range(32)]
        far = [[16 * i + j for i in range(32)] for j in range(16)]
        first = lax.all_to_all(sums, "dom", 0, 0, tiled=True, axis_index_groups=near)
        again = jnp.broadcast_to(jnp.sum(first, axis=0, keepdims=True), (32, LANES))
        return lax.all_to_all(again, "dom", 0, 0, tiled=True, axis_index_groups=far)
    return lax.all_to_all(sums, "dom", 0, 0, tiled=True)


def shards(velocity, conv_past, metric, jacobian, element_slot):
    count = lax.axis_size("dom")
    t = {key: jnp.asarray(value) for key, value in TAB.items()}
    field = (NP, NP, LANES)
    edge = (2, NP, LANES)
    ext_shape = (NP + 2, NP, LANES)

    def swap(inner, cross):
        far = swap_cross(cross, count)
        return swap_inner(inner, count), far

    force, static, inner, cross = call(
        forcing_kernel,
        [(4,) + field, (4,) + field, (4, NP, LANES), (4, NP, LANES)],
        element_slot, velocity, conv_past, metric, jacobian,
        t["w3"], t["ds"], t["dq"], t["jright"], t["jleft"], t["wfine"],
        smem=(0,),
    )
    inner, cross = swap(inner, cross)
    op, grad, inv = call(
        factor_kernel, [(4,) + field, (3,) + field, (104, ES * (NP + 2))], static, t["spread"], t["lam"]
    )
    div, inner, cross = call(
        divergence_kernel, [field, edge, edge], force, inner, cross, grad, t["ds"], t["dq"]
    )
    inner, cross = swap(inner, cross)
    solve = (inv, t["sleft"], t["sright"], t["srback"], t["sback"])
    ext, z, inner, cross = call(
        first_smooth_kernel, [ext_shape, field, edge, edge], div, inner, cross, *solve
    )
    vectors, locals_, images = [], [], []
    for step in range(2):
        inner, cross = swap(inner, cross)
        v, local, inner, cross = call(
            operator_kernel, [field, field, edge, edge], z, inner, cross, op, t["ds"], t["dq"]
        )
        vectors.append(v)
        locals_.append(local)
        inner, cross = swap(inner, cross)
        image, ext, z, inner, cross = call(
            functools.partial(smooth_kernel, STEPS[step]),
            [field, ext_shape, field, edge, edge],
            ext, local, inner, cross, *solve,
        )
        images.append(image)
    inner, cross = swap(inner, cross)
    wide = 16 if count == 512 else count
    v, local, inner, cross, sums = call(
        last_operator_kernel,
        [field, field, edge, edge, (wide, LANES)],
        z, inner, cross, op, t["ds"], t["dq"], t["ws"], ext, vectors[0], vectors[1], locals_[0], locals_[1],
    )
    inner, cross = swap(inner, cross)
    sums = gather_sums(sums, count)
    return tuple(
        call(
            combine_kernel,
            [(NP, 896), (NP, 896)],
            sums, ext, vectors[0], vectors[1], v, images[0], images[1], local, inner, cross,
        )
    )


def solution(mesh):
    return jax.shard_map(
        shards,
        mesh=mesh,
        in_specs=(
            P(None, None, "dom", None),
            P(None, None, "dom", None),
            P(None, "dom", None),
            P("dom", None),
            P("dom"),
        ),
        out_specs=(P("dom", None), P("dom", None)),
        check_vma=False,
    )
```

time: 823 us -> 146 us (0.18)
  blocking collectives: 511 us -> 14.9 us
  local copies, waits for them, and re-layouts: 102 us -> 9.97 us
  matrix products: 29.5 us -> 0 us
  other arithmetic: 26.4 us -> 0.03 us
  starting transfers between devices: 95.6 us -> 80.7 us
  Pallas kernels: 0 us -> 12.8 us
  between operations: 12.9 us -> 0.98 us
  waiting for transfers between devices: 36.2 us -> 24.6 us
    psum x5 -> x0, blocking collectives: 511 us -> none  [the longest x3 302 us: shards(): precond_sum = lax.psum(weighted(residual, smoothed), 'dom')]
    slice x175 -> x0, local copies, waits for them, and re-layouts: 64.9 us -> none  [the longest x96 53.5 us: windows(): lax.slice_in_dim(field, offset, offset + stride * (count - 1) + 1, stride...]
    dot_general x91 -> x0, matrix products: 29.5 us -> none  [the longest x38 14.8 us: along_first(): jnp.einsum(form, field, matrix, precision=HIGHEST, preferred_element_type...]
    ppermute x22 -> x16, starting transfers between devices: 95.6 us -> 73 us  [the longest x8 57.5 us: swap_inner(): return lax.ppermute(x, 'dom', [(i, i ^ 1) for i in range(count)])]
    reshape x52 -> x0, local copies, waits for them, and re-layouts: 16.6 us -> none  [the longest x37 9.65 us: intersection(): stacked.reshape(stacked.shape[:axis] + (count * stride,) + stacked.shape[...]
    all_to_all x0 -> x1, blocking collectives: none -> 14.9 us  [gather_sums(): lax.all_to_all(sums, 'dom', 0, 0, tiled=True, axis_index_groups=near)]
    pallas_call x0 -> x10, Pallas kernels: none -> 12.8 us  [call(): pl.pallas_call(kernel, out_shape=[jax.ShapeDtypeStruct(shape, jnp.float32...]
    ppermute x22 -> x16, waiting for transfers between devices: 36.2 us -> 24.2 us  [the longest x8 24.2 us: swap_cross(): return lax.ppermute(x, 'dom', pairs)]
  transfers between devices with their start and end apart: 22 -> 17, of which waited for: 12 -> 9; matrix products, arithmetic and copies ran while one was open for 1% -> 0% of each run, Pallas kernels for 0% -> 0%
where the time goes in v1:
time: 146 us; the launch traced here: 144 us
  starting transfers between devices  80.7 us (55%)
  waiting for transfers between devices  24.6 us (17%)
  blocking collectives  14.9 us (10%)
  Pallas kernels  12.8 us (9%)
  local copies, waits for them, and re-layouts  9.97 us (7%)
    ppermute x8, starting transfers between devices, swap_inner(): return lax.ppermute(x, 'dom', [(i, i ^ 1) for i in range(count)])  57.5 us
    ppermute x8, waiting for transfers between devices, swap_cross(): return lax.ppermute(x, 'dom', pairs)  24.2 us
    ppermute x8, starting transfers between devices, swap_cross(): return lax.ppermute(x, 'dom', pairs)  15.5 us
    all_to_all x1, blocking collectives, gather_sums(): lax.all_to_all(sums, 'dom', 0, 0, tiled=True, axis_index_groups=near)  14.9 us
    pallas_call x10, Pallas kernels, call(): pl.pallas_call(kernel, out_shape=[jax.ShapeDtypeStruct(shape, jnp.float32...  12.8 us
    unnamed x40, local copies, waits for them, and re-layouts  9.35 us
    all_to_all x1, starting transfers between devices, gather_sums(): return lax.all_to_all(again, 'dom', 0, 0, tiled=True, axis_index_groups=far)  7.74 us
  transfers between devices with their start and end apart: 17, of which 9 were waited for; matrix products, arithmetic and copies ran while one was open for 0% of the time, Pallas kernels for 0%

profile of v1, /device:TPU:1, one launch (start us, length us, event | category | flops | bytes accessed | tf_op | source)
XLA Modules:
  0.0 144.0 jit_solution(17455919331059517811)
XLA Ops:
  0.6 0.0 copy-start.18
  0.6 0.7 copy-done.18
  1.3 0.9 copy-done
  2.2 0.8 copy-done.2
  3.1 1.0 copy-done.9
  4.0 0.9 copy-done.10
  5.0 0.9 copy-done.11
  5.9 0.9 copy-done.13
  6.8 0.9 copy-done.14
  7.7 0.9 copy-done.15
  8.5 0.8 copy-done.16
  9.3 0.7 copy-done.19
  10.0 5.3 %shard_map.185 = (f32[4,8,8,128]{3,2,1,0:T(8,128)S(1)}, f32[4,8,8,128]{3,2,1,0:T(8,128)S(1)}, f32[4,8,128]{2,1,0:T(8,128)S(1)}, f32[4,8,128]{2,1,0:T(8,128)S(1)}) custom-call(s32[16]{0:T(128)S(1)} %copy-done.19, f32[3,3,16,512]{3,2,1,0:T(8,128)S(1)} %copy-done.9, f32[2,3,16,512]{3,2,1,0:T(8,128)S(1)} %copy-done.10, f32[3,16,512]{2,1,0:T(8,128)S(1)} %copy-done.14, ...), custom_call_target="tpu_custom_call" | custom-call | tf_op jit(solution)/shard_map/pallas_call | solution.py:488
  15.3 8.8 %collective-permute-start = (f32[4,8,128]{2,1,0:T(8,128)S(1)}, f32[4,8,128]{2,1,0:T(8,128)S(1)}, u32[]{:S(2)}, u32[]{:S(2)}) collective-permute-start(f32[4,8,128]{2,1,0:T(8,128)S(1)} %get-tuple-element.40), channel_id=1, source_target_pairs={{0,1},{1,0},{2,3},{3,2},{4,5},{5,4},{6,7},{7,6},{8,9},{9,8},{10,11... | collective-permute-start | bytes 49160 | tf_op jit(solution)/shard_map/ppermute | solution.py:254
  24.1 1.9 %collective-permute-start.1 = (f32[4,8,128]{2,1,0:T(8,128)S(1)}, f32[4,8,128]{2,1,0:T(8,128)S(1)}, u32[]{:S(2)}, u32[]{:S(2)}) collective-permute-start(f32[4,8,128]{2,1,0:T(8,128)S(1)} %get-tuple-element.41), channel_id=1, source_target_pairs={{0,511},{1,2},{2,1},{3,4},{4,3},{5,6},{6,5},{7,8},{8,7},{9,10},{10... | collective-permute-start | bytes 49160 | tf_op jit(solution)/shard_map/ppermute | solution.py:259
  26.0 0.0 copy-done.8
  26.0 0.0 copy-start.1
  26.0 0.0 copy-start.3
  26.1 0.2 shard_map.186
  26.3 0.0 collective-permute-done.inner_in
  26.3 2.8 %collective-permute-done.1.cross_in = f32[4,8,128]{2,1,0:T(8,128)S(1)} collective-permute-done((f32[4,8,128]{2,1,0:T(8,128)S(1)}, f32[4,8,128]{2,1,0:T(8,128)S(1)}, u32[]{:S(2)}, u32[]{:S(2)}) %collective-permute-start.1) | collective-permute-done | bytes 16416 | tf_op jit(solution)/shard_map/ppermute | solution.py:259
  29.2 0.0 copy-start.6
  29.2 0.0 copy-start.7
  29.2 0.3 shard_map.187
  29.5 9.1 %collective-permute-start.2 = (f32[2,8,128]{2,1,0:T(8,128)S(1)}, f32[2,8,128]{2,1,0:T(8,128)S(1)}, u32[]{:S(2)}, u32[]{:S(2)}) collective-permute-start(f32[2,8,128]{2,1,0:T(8,128)S(1)} %get-tuple-element.45), channel_id=1, source_target_pairs={{0,1},{1,0},{2,3},{3,2},{4,5},{5,4},{6,7},{7,6},{8,9},{9,8},{10,11... | collective-permute-start | bytes 24584 | tf_op jit(solution)/shard_map/ppermute | solution.py:254
  38.5 1.9 %collective-permute-start.3 = (f32[2,8,128]{2,1,0:T(8,128)S(1)}, f32[2,8,128]{2,1,0:T(8,128)S(1)}, u32[]{:S(2)}, u32[]{:S(2)}) collective-permute-start(f32[2,8,128]{2,1,0:T(8,128)S(1)} %get-tuple-element.46), channel_id=1, source_target_pairs={{0,511},{1,2},{2,1},{3,4},{4,3},{5,6},{6,5},{7,8},{8,7},{9,10},{10... | collective-permute-start | bytes 24584 | tf_op jit(solution)/shard_map/ppermute | solution.py:259
  40.5 0.0 collective-permute-done.2.inner_in
  40.5 3.0 %collective-permute-done.3.cross_in = f32[2,8,128]{2,1,0:T(8,128)S(1)} collective-permute-done((f32[2,8,128]{2,1,0:T(8,128)S(1)}, f32[2,8,128]{2,1,0:T(8,128)S(1)}, u32[]{:S(2)}, u32[]{:S(2)}) %collective-permute-start.3) | collective-permute-done | bytes 8224 | tf_op jit(solution)/shard_map/ppermute | solution.py:259
  43.5 1.3 shard_map.188
  44.8 7.4 %collective-permute-start.4 = (f32[2,8,128]{2,1,0:T(8,128)S(1)}, f32[2,8,128]{2,1,0:T(8,128)S(1)}, u32[]{:S(2)}, u32[]{:S(2)}) collective-permute-start(f32[2,8,128]{2,1,0:T(8,128)S(1)} %get-tuple-element.50), channel_id=1, source_target_pairs={{0,1},{1,0},{2,3},{3,2},{4,5},{5,4},{6,7},{7,6},{8,9},{9,8},{10,11... | collective-permute-start | bytes 24584 | tf_op jit(solution)/shard_map/ppermute | solution.py:254
  52.2 1.9 %collective-permute-start.5 = (f32[2,8,128]{2,1,0:T(8,128)S(1)}, f32[2,8,128]{2,1,0:T(8,128)S(1)}, u32[]{:S(2)}, u32[]{:S(2)}) collective-permute-start(f32[2,8,128]{2,1,0:T(8,128)S(1)} %get-tuple-element.51), channel_id=1, source_target_pairs={{0,511},{1,2},{2,1},{3,4},{4,3},{5,6},{6,5},{7,8},{8,7},{9,10},{10... | collective-permute-start | bytes 24584 | tf_op jit(solution)/shard_map/ppermute | solution.py:259
  54.1 0.0 collective-permute-done.4.inner_in
  54.1 3.0 %collective-permute-done.5.cross_in = f32[2,8,128]{2,1,0:T(8,128)S(1)} collective-permute-done((f32[2,8,128]{2,1,0:T(8,128)S(1)}, f32[2,8,128]{2,1,0:T(8,128)S(1)}, u32[]{:S(2)}, u32[]{:S(2)}) %collective-permute-start.5) | collective-permute-done | bytes 8224 | tf_op jit(solution)/shard_map/ppermute | solution.py:259
  57.1 0.5 shard_map.189
  57.6 7.4 %collective-permute-start.6 = (f32[2,8,128]{2,1,0:T(8,128)S(1)}, f32[2,8,128]{2,1,0:T(8,128)S(1)}, u32[]{:S(2)}, u32[]{:S(2)}) collective-permute-start(f32[2,8,128]{2,1,0:T(8,128)S(1)} %get-tuple-element.54), channel_id=1, source_target_pairs={{0,1},{1,0},{2,3},{3,2},{4,5},{5,4},{6,7},{7,6},{8,9},{9,8},{10,11... | collective-permute-start | bytes 24584 | tf_op jit(solution)/shard_map/ppermute | solution.py:254
  65.0 1.9 %collective-permute-start.7 = (f32[2,8,128]{2,1,0:T(8,128)S(1)}, f32[2,8,128]{2,1,0:T(8,128)S(1)}, u32[]{:S(2)}, u32[]{:S(2)}) collective-permute-start(f32[2,8,128]{2,1,0:T(8,128)S(1)} %get-tuple-element.55), channel_id=1, source_target_pairs={{0,511},{1,2},{2,1},{3,4},{4,3},{5,6},{6,5},{7,8},{8,7},{9,10},{10... | collective-permute-start | bytes 24584 | tf_op jit(solution)/shard_map/ppermute | solution.py:259
  66.9 0.0 collective-permute-done.6.inner_in
  66.9 3.0 %collective-permute-done.7.cross_in = f32[2,8,128]{2,1,0:T(8,128)S(1)} collective-permute-done((f32[2,8,128]{2,1,0:T(8,128)S(1)}, f32[2,8,128]{2,1,0:T(8,128)S(1)}, u32[]{:S(2)}, u32[]{:S(2)}) %collective-permute-start.7) | collective-permute-done | bytes 8224 | tf_op jit(solution)/shard_map/ppermute | solution.py:259
  69.9 1.3 shard_map.190
  71.2 7.3 %collective-permute-start.8 = (f32[2,8,128]{2,1,0:T(8,128)S(1)}, f32[2,8,128]{2,1,0:T(8,128)S(1)}, u32[]{:S(2)}, u32[]{:S(2)}) collective-permute-start(f32[2,8,128]{2,1,0:T(8,128)S(1)} %get-tuple-element.58), channel_id=1, source_target_pairs={{0,1},{1,0},{2,3},{3,2},{4,5},{5,4},{6,7},{7,6},{8,9},{9,8},{10,11... | collective-permute-start | bytes 24584 | tf_op jit(solution)/shard_map/ppermute | solution.py:254
  78.6 1.9 %collective-permute-start.9 = (f32[2,8,128]{2,1,0:T(8,128)S(1)}, f32[2,8,128]{2,1,0:T(8,128)S(1)}, u32[]{:S(2)}, u32[]{:S(2)}) collective-permute-start(f32[2,8,128]{2,1,0:T(8,128)S(1)} %get-tuple-element.59), channel_id=1, source_target_pairs={{0,511},{1,2},{2,1},{3,4},{4,3},{5,6},{6,5},{7,8},{8,7},{9,10},{10... | collective-permute-start | bytes 24584 | tf_op jit(solution)/shard_map/ppermute | solution.py:259
  80.5 0.0 collective-permute-done.8.inner_in
  80.5 3.0 %collective-permute-done.9.cross_in = f32[2,8,128]{2,1,0:T(8,128)S(1)} collective-permute-done((f32[2,8,128]{2,1,0:T(8,128)S(1)}, f32[2,8,128]{2,1,0:T(8,128)S(1)}, u32[]{:S(2)}, u32[]{:S(2)}) %collective-permute-start.9) | collective-permute-done | bytes 8224 | tf_op jit(solution)/shard_map/ppermute | solution.py:259
  83.5 0.5 shard_map.191
  84.0 7.3 %collective-permute-start.10 = (f32[2,8,128]{2,1,0:T(8,128)S(1)}, f32[2,8,128]{2,1,0:T(8,128)S(1)}, u32[]{:S(2)}, u32[]{:S(2)}) collective-permute-start(f32[2,8,128]{2,1,0:T(8,128)S(1)} %get-tuple-element.61), channel_id=1, source_target_pairs={{0,1},{1,0},{2,3},{3,2},{4,5},{5,4},{6,7},{7,6},{8,9},{9,8},{10,11... | collective-permute-start | bytes 24584 | tf_op jit(solution)/shard_map/ppermute | solution.py:254
  91.4 1.9 %collective-permute-start.11 = (f32[2,8,128]{2,1,0:T(8,128)S(1)}, f32[2,8,128]{2,1,0:T(8,128)S(1)}, u32[]{:S(2)}, u32[]{:S(2)}) collective-permute-start(f32[2,8,128]{2,1,0:T(8,128)S(1)} %get-tuple-element.62), channel_id=1, source_target_pairs={{0,511},{1,2},{2,1},{3,4},{4,3},{5,6},{6,5},{7,8},{8,7},{9,10},{10... | collective-permute-start | bytes 24584 | tf_op jit(solution)/shard_map/ppermute | solution.py:259
  93.3 0.0 collective-permute-done.10.inner_in
  93.3 3.0 %collective-permute-done.11.cross_in = f32[2,8,128]{2,1,0:T(8,128)S(1)} collective-permute-done((f32[2,8,128]{2,1,0:T(8,128)S(1)}, f32[2,8,128]{2,1,0:T(8,128)S(1)}, u32[]{:S(2)}, u32[]{:S(2)}) %collective-permute-start.11) | collective-permute-done | bytes 8224 | tf_op jit(solution)/shard_map/ppermute | solution.py:259
  96.3 1.3 shard_map.192
  97.6 7.4 %collective-permute-start.12 = (f32[2,8,128]{2,1,0:T(8,128)S(1)}, f32[2,8,128]{2,1,0:T(8,128)S(1)}, u32[]{:S(2)}, u32[]{:S(2)}) collective-permute-start(f32[2,8,128]{2,1,0:T(8,128)S(1)} %get-tuple-element.64), channel_id=1, source_target_pairs={{0,1},{1,0},{2,3},{3,2},{4,5},{5,4},{6,7},{7,6},{8,9},{9,8},{10,11... | collective-permute-start | bytes 24584 | tf_op jit(solution)/shard_map/ppermute | solution.py:254
  105.0 0.0 copy-start.17
  105.0 1.9 %collective-permute-start.13 = (f32[2,8,128]{2,1,0:T(8,128)S(1)}, f32[2,8,128]{2,1,0:T(8,128)S(1)}, u32[]{:S(2)}, u32[]{:S(2)}) collective-permute-start(f32[2,8,128]{2,1,0:T(8,128)S(1)} %get-tuple-element.65), channel_id=1, source_target_pairs={{0,511},{1,2},{2,1},{3,4},{4,3},{5,6},{6,5},{7,8},{8,7},{9,10},{10... | collective-permute-start | bytes 24584 | tf_op jit(solution)/shard_map/ppermute | solution.py:259
  106.9 0.0 collective-permute-done.12.inner_in
  106.9 3.0 %collective-permute-done.13.cross_in = f32[2,8,128]{2,1,0:T(8,128)S(1)} collective-permute-done((f32[2,8,128]{2,1,0:T(8,128)S(1)}, f32[2,8,128]{2,1,0:T(8,128)S(1)}, u32[]{:S(2)}, u32[]{:S(2)}) %collective-permute-start.13) | collective-permute-done | bytes 8224 | tf_op jit(solution)/shard_map/ppermute | solution.py:259
  110.0 0.6 shard_map.193
  110.5 14.9 %all_to_all.17 = f32[16,1,128]{2,1,0:T(1,128)S(1)} all-to-all(f32[16,1,128]{2,1,0:T(1,128)S(1)} %bitcast.5), channel_id=1, replica_groups={{0,1,2,3,4,5,6,7,8,9,10,11,12,13,14,15},{16,17,18,19,20,21,22,23,24,25,..., dimensions={0} | all-to-all | bytes 16384 | tf_op jit(solution)/shard_map/all_to_all | solution.py:501
  125.5 0.6 broadcast_in_dim.2
  126.1 7.7 %all-to-all-start.1 = ((f32[32,1,128]{2,1,0:T(1,128)}), f32[32,1,128]{2,1,0:T(1,128)S(1)}, u32[]{:S(2)}, u32[]{:S(2)}) async-start(f32[32,1,128]{2,1,0:T(1,128)} %broadcast_in_dim.2), calls=%async_computation.1 | async-start | bytes 32768 | tf_op jit(solution)/shard_map/all_to_all | solution.py:503
  133.8 2.8 %collective-permute-start.14 = (f32[2,8,128]{2,1,0:T(8,128)S(1)}, f32[2,8,128]{2,1,0:T(8,128)S(1)}, u32[]{:S(2)}, u32[]{:S(2)}) collective-permute-start(f32[2,8,128]{2,1,0:T(8,128)S(1)} %get-tuple-element.74), channel_id=1, source_target_pairs={{0,1},{1,0},{2,3},{3,2},{4,5},{5,4},{6,7},{7,6},{8,9},{9,8},{10,11... | collective-permute-start | bytes 24584 | tf_op jit(solution)/shard_map/ppermute | solution.py:254
  136.7 2.1 %collective-permute-start.15 = (f32[2,8,128]{2,1,0:T(8,128)S(1)}, f32[2,8,128]{2,1,0:T(8,128)S(1)}, u32[]{:S(2)}, u32[]{:S(2)}) collective-permute-start(f32[2,8,128]{2,1,0:T(8,128)S(1)} %get-tuple-element.75), channel_id=1, source_target_pairs={{0,511},{1,2},{2,1},{3,4},{4,3},{5,6},{6,5},{7,8},{8,7},{9,10},{10... | collective-permute-start | bytes 24584 | tf_op jit(solution)/shard_map/ppermute | solution.py:259
  138.8 0.0 collective-permute-done.14.inner_in
  138.8 3.2 %collective-permute-done.15.cross_in = f32[2,8,128]{2,1,0:T(8,128)S(1)} collective-permute-done((f32[2,8,128]{2,1,0:T(8,128)S(1)}, f32[2,8,128]{2,1,0:T(8,128)S(1)}, u32[]{:S(2)}, u32[]{:S(2)}) %collective-permute-start.15) | collective-permute-done | bytes 8224 | tf_op jit(solution)/shard_map/ppermute | solution.py:259
  141.9 0.4 all-to-all-done.1
  142.3 1.6 %shard_map.194 = (f32[8,896]{1,0:T(8,128)}, f32[8,896]{1,0:T(8,128)}) custom-call(f32[32,128]{1,0:T(8,128)S(1)} %bitcast.4, f32[10,8,128]{2,1,0:T(8,128)S(1)} %get-tuple-element.66.ext_ref, f32[8,8,128]{2,1,0:T(8,128)S(1)} %get-tuple-element.67.v0_ref, f32[8,8,128]{2,1,0:T(8,128)S(1)} %get-tuple-element.68.v1_ref, ...), custom_call_target="tpu_custom_call" | custom-call | tf_op jit(solution)/shard_map/pallas_call | solution.py:488
  (23 shorter events, 0.1 us)
Async XLA Ops:
  0.6 0.7 copy-start.18
  1.3 0.9 copy-start
  2.2 0.8 copy-start.2
  3.1 1.0 copy-start.9
  4.0 0.9 copy-start.10
  4.9 0.9 copy-start.11
  5.9 0.9 copy-start.13
  6.8 0.9 copy-start.14
  7.7 0.9 copy-start.15
  8.5 0.8 copy-start.16
  9.3 0.7 copy-start.19
  10.0 16.1 %copy-start.8 = (f32[3,104,160]{2,1,0:T(8,128)S(1)}, f32[3,104,160]{2,1,0:T(8,128)}, u32[]{:S(2)}) copy-start(f32[3,104,160]{2,1,0:T(8,128)} %constant.39.clone.lam_ref) | copy-start | bytes 599044
  10.0 16.1 %copy-start.12 = (f32[128,160]{1,0:T(8,128)S(1)}, f32[128,160]{1,0:T(8,128)}, u32[]{:S(2)}) copy-start(f32[128,160]{1,0:T(8,128)} %constant.38.clone.spread_ref) | copy-start | bytes 245764
  15.3 11.0 %collective-permute-start = (f32[4,8,128]{2,1,0:T(8,128)S(1)}, f32[4,8,128]{2,1,0:T(8,128)S(1)}, u32[]{:S(2)}, u32[]{:S(2)}) collective-permute-start(f32[4,8,128]{2,1,0:T(8,128)S(1)} %get-tuple-element.40), channel_id=1, source_target_pairs={{0,1},{1,0},{2,3},{3,2},{4,5},{5,4},{6,7},{7,6},{8,9},{9,8},{10,11... | collective-permute-start | bytes 49160 | tf_op jit(solution)/shard_map/ppermute | solution.py:254
  24.1 5.1 %collective-permute-start.1 = (f32[4,8,128]{2,1,0:T(8,128)S(1)}, f32[4,8,128]{2,1,0:T(8,128)S(1)}, u32[]{:S(2)}, u32[]{:S(2)}) collective-permute-start(f32[4,8,128]{2,1,0:T(8,128)S(1)} %get-tuple-element.41), channel_id=1, source_target_pairs={{0,511},{1,2},{2,1},{3,4},{4,3},{5,6},{6,5},{7,8},{8,7},{9,10},{10... | collective-permute-start | bytes 49160 | tf_op jit(solution)/shard_map/ppermute | solution.py:259
  26.0 3.1 %copy-start.1 = (f32[2,15,8,128]{3,2,1,0:T(8,128)S(1)}, f32[2,15,8,128]{3,2,1,0:T(8,128)}, u32[]{:S(2)}) copy-start(f32[2,15,8,128]{3,2,1,0:T(8,128)} %constant.29.clone.dq_ref) | copy-start | bytes 368644
  26.0 3.1 %copy-start.3 = (f32[2,8,8,128]{3,2,1,0:T(8,128)S(1)}, f32[2,8,8,128]{3,2,1,0:T(8,128)}, u32[]{:S(2)}) copy-start(f32[2,8,8,128]{3,2,1,0:T(8,128)} %constant.28.clone.ds_ref) | copy-start | bytes 196612
  29.1 14.4 %copy-start.4 = (f32[128,160]{1,0:T(8,128)S(1)}, f32[128,160]{1,0:T(8,128)}, u32[]{:S(2)}) copy-start(f32[128,160]{1,0:T(8,128)} %constant.36.clone.sright_ref) | copy-start | bytes 245764
  29.2 14.4 %copy-start.5 = (f32[240,104]{1,0:T(8,128)S(1)}, f32[240,104]{1,0:T(8,128)}, u32[]{:S(2)}) copy-start(f32[240,104]{1,0:T(8,128)} %constant.35.clone.sback_ref) | copy-start | bytes 299524
  29.2 14.4 %copy-start.6 = (f32[104,240]{1,0:T(8,128)S(1)}, f32[104,240]{1,0:T(8,128)}, u32[]{:S(2)}) copy-start(f32[104,240]{1,0:T(8,128)} %constant.34.clone.sleft_ref) | copy-start | bytes 299524
  29.2 14.4 %copy-start.7 = (f32[160,128]{1,0:T(8,128)S(1)}, f32[160,128]{1,0:T(8,128)}, u32[]{:S(2)}) copy-start(f32[160,128]{1,0:T(8,128)} %constant.37.clone.srback_ref) | copy-start | bytes 245764
  29.5 11.0 %collective-permute-start.2 = (f32[2,8,128]{2,1,0:T(8,128)S(1)}, f32[2,8,128]{2,1,0:T(8,128)S(1)}, u32[]{:S(2)}, u32[]{:S(2)}) collective-permute-start(f32[2,8,128]{2,1,0:T(8,128)S(1)} %get-tuple-element.45), channel_id=1, source_target_pairs={{0,1},{1,0},{2,3},{3,2},{4,5},{5,4},{6,7},{7,6},{8,9},{9,8},{10,11... | collective-permute-start | bytes 24584 | tf_op jit(solution)/shard_map/ppermute | solution.py:254
  38.5 5.0 %collective-permute-start.3 = (f32[2,8,128]{2,1,0:T(8,128)S(1)}, f32[2,8,128]{2,1,0:T(8,128)S(1)}, u32[]{:S(2)}, u32[]{:S(2)}) collective-permute-start(f32[2,8,128]{2,1,0:T(8,128)S(1)} %get-tuple-element.46), channel_id=1, source_target_pairs={{0,511},{1,2},{2,1},{3,4},{4,3},{5,6},{6,5},{7,8},{8,7},{9,10},{10... | collective-permute-start | bytes 24584 | tf_op jit(solution)/shard_map/ppermute | solution.py:259
  44.8 9.3 %collective-permute-start.4 = (f32[2,8,128]{2,1,0:T(8,128)S(1)}, f32[2,8,128]{2,1,0:T(8,128)S(1)}, u32[]{:S(2)}, u32[]{:S(2)}) collective-permute-start(f32[2,8,128]{2,1,0:T(8,128)S(1)} %get-tuple-element.50), channel_id=1, source_target_pairs={{0,1},{1,0},{2,3},{3,2},{4,5},{5,4},{6,7},{7,6},{8,9},{9,8},{10,11... | collective-permute-start | bytes 24584 | tf_op jit(solution)/shard_map/ppermute | solution.py:254
  52.2 5.0 %collective-permute-start.5 = (f32[2,8,128]{2,1,0:T(8,128)S(1)}, f32[2,8,128]{2,1,0:T(8,128)S(1)}, u32[]{:S(2)}, u32[]{:S(2)}) collective-permute-start(f32[2,8,128]{2,1,0:T(8,128)S(1)} %get-tuple-element.51), channel_id=1, source_target_pairs={{0,511},{1,2},{2,1},{3,4},{4,3},{5,6},{6,5},{7,8},{8,7},{9,10},{10... | collective-permute-start | bytes 24584 | tf_op jit(solution)/shard_map/ppermute | solution.py:259
  57.6 9.3 %collective-permute-start.6 = (f32[2,8,128]{2,1,0:T(8,128)S(1)}, f32[2,8,128]{2,1,0:T(8,128)S(1)}, u32[]{:S(2)}, u32[]{:S(2)}) collective-permute-start(f32[2,8,128]{2,1,0:T(8,128)S(1)} %get-tuple-element.54), channel_id=1, source_target_pairs={{0,1},{1,0},{2,3},{3,2},{4,5},{5,4},{6,7},{7,6},{8,9},{9,8},{10,11... | collective-permute-start | bytes 24584 | tf_op jit(solution)/shard_map/ppermute | solution.py:254
  65.0 5.0 %collective-permute-start.7 = (f32[2,8,128]{2,1,0:T(8,128)S(1)}, f32[2,8,128]{2,1,0:T(8,128)S(1)}, u32[]{:S(2)}, u32[]{:S(2)}) collective-permute-start(f32[2,8,128]{2,1,0:T(8,128)S(1)} %get-tuple-element.55), channel_id=1, source_target_pairs={{0,511},{1,2},{2,1},{3,4},{4,3},{5,6},{6,5},{7,8},{8,7},{9,10},{10... | collective-permute-start | bytes 24584 | tf_op jit(solution)/shard_map/ppermute | solution.py:259
  71.2 9.3 %collective-permute-start.8 = (f32[2,8,128]{2,1,0:T(8,128)S(1)}, f32[2,8,128]{2,1,0:T(8,128)S(1)}, u32[]{:S(2)}, u32[]{:S(2)}) collective-permute-start(f32[2,8,128]{2,1,0:T(8,128)S(1)} %get-tuple-element.58), channel_id=1, source_target_pairs={{0,1},{1,0},{2,3},{3,2},{4,5},{5,4},{6,7},{7,6},{8,9},{9,8},{10,11... | collective-permute-start | bytes 24584 | tf_op jit(solution)/shard_map/ppermute | solution.py:254
  78.6 5.0 %collective-permute-start.9 = (f32[2,8,128]{2,1,0:T(8,128)S(1)}, f32[2,8,128]{2,1,0:T(8,128)S(1)}, u32[]{:S(2)}, u32[]{:S(2)}) collective-permute-start(f32[2,8,128]{2,1,0:T(8,128)S(1)} %get-tuple-element.59), channel_id=1, source_target_pairs={{0,511},{1,2},{2,1},{3,4},{4,3},{5,6},{6,5},{7,8},{8,7},{9,10},{10... | collective-permute-start | bytes 24584 | tf_op jit(solution)/shard_map/ppermute | solution.py:259
  84.0 9.3 %collective-permute-start.10 = (f32[2,8,128]{2,1,0:T(8,128)S(1)}, f32[2,8,128]{2,1,0:T(8,128)S(1)}, u32[]{:S(2)}, u32[]{:S(2)}) collective-permute-start(f32[2,8,128]{2,1,0:T(8,128)S(1)} %get-tuple-element.61), channel_id=1, source_target_pairs={{0,1},{1,0},{2,3},{3,2},{4,5},{5,4},{6,7},{7,6},{8,9},{9,8},{10,11... | collective-permute-start | bytes 24584 | tf_op jit(solution)/shard_map/ppermute | solution.py:254
  91.4 5.0 %collective-permute-start.11 = (f32[2,8,128]{2,1,0:T(8,128)S(1)}, f32[2,8,128]{2,1,0:T(8,128)S(1)}, u32[]{:S(2)}, u32[]{:S(2)}) collective-permute-start(f32[2,8,128]{2,1,0:T(8,128)S(1)} %get-tuple-element.62), channel_id=1, source_target_pairs={{0,511},{1,2},{2,1},{3,4},{4,3},{5,6},{6,5},{7,8},{8,7},{9,10},{10... | collective-permute-start | bytes 24584 | tf_op jit(solution)/shard_map/ppermute | solution.py:259
  97.6 9.3 %collective-permute-start.12 = (f32[2,8,128]{2,1,0:T(8,128)S(1)}, f32[2,8,128]{2,1,0:T(8,128)S(1)}, u32[]{:S(2)}, u32[]{:S(2)}) collective-permute-start(f32[2,8,128]{2,1,0:T(8,128)S(1)} %get-tuple-element.64), channel_id=1, source_target_pairs={{0,1},{1,0},{2,3},{3,2},{4,5},{5,4},{6,7},{7,6},{8,9},{9,8},{10,11... | collective-permute-start | bytes 24584 | tf_op jit(solution)/shard_map/ppermute | solution.py:254
  105.0 5.0 %copy-start.17 = (f32[8,128]{1,0:T(8,128)S(1)}, f32[8,128]{1,0:T(8,128)}, u32[]{:S(2)}) copy-start(f32[8,128]{1,0:T(8,128)} %constant.40.clone.ws_ref) | copy-start | bytes 12292
  105.0 5.0 %collective-permute-start.13 = (f32[2,8,128]{2,1,0:T(8,128)S(1)}, f32[2,8,128]{2,1,0:T(8,128)S(1)}, u32[]{:S(2)}, u32[]{:S(2)}) collective-permute-start(f32[2,8,128]{2,1,0:T(8,128)S(1)} %get-tuple-element.65), channel_id=1, source_target_pairs={{0,511},{1,2},{2,1},{3,4},{4,3},{5,6},{6,5},{7,8},{8,7},{9,10},{10... | collective-permute-start | bytes 24584 | tf_op jit(solution)/shard_map/ppermute | solution.py:259
  126.1 16.3 %all-to-all-start.1 = ((f32[32,1,128]{2,1,0:T(1,128)}), f32[32,1,128]{2,1,0:T(1,128)S(1)}, u32[]{:S(2)}, u32[]{:S(2)}) async-start(f32[32,1,128]{2,1,0:T(1,128)} %broadcast_in_dim.2), calls=%async_computation.1 | async-start | bytes 32768 | tf_op jit(solution)/shard_map/all_to_all | solution.py:503
  133.8 4.9 %collective-permute-start.14 = (f32[2,8,128]{2,1,0:T(8,128)S(1)}, f32[2,8,128]{2,1,0:T(8,128)S(1)}, u32[]{:S(2)}, u32[]{:S(2)}) collective-permute-start(f32[2,8,128]{2,1,0:T(8,128)S(1)} %get-tuple-element.74), channel_id=1, source_target_pairs={{0,1},{1,0},{2,3},{3,2},{4,5},{5,4},{6,7},{7,6},{8,9},{9,8},{10,11... | collective-permute-start | bytes 24584 | tf_op jit(solution)/shard_map/ppermute | solution.py:254
  136.7 5.3 %collective-permute-start.15 = (f32[2,8,128]{2,1,0:T(8,128)S(1)}, f32[2,8,128]{2,1,0:T(8,128)S(1)}, u32[]{:S(2)}, u32[]{:S(2)}) collective-permute-start(f32[2,8,128]{2,1,0:T(8,128)S(1)} %get-tuple-element.75), channel_id=1, source_target_pairs={{0,511},{1,2},{2,1},{3,4},{4,3},{5,6},{6,5},{7,8},{8,7},{9,10},{10... | collective-permute-start | bytes 24584 | tf_op jit(solution)/shard_map/ppermute | solution.py:259

commit v2 on v1

v2 whole, which is shorter than its diff:
```python
import functools

import jax
import jax.numpy as jnp
import numpy as np
from jax import lax
from jax.experimental import pallas as pl
from jax.experimental.pallas import tpu as pltpu
from jax.sharding import PartitionSpec as P

NP = 8
NF = 12
ES = 16
LANES = 128
time_step = 0.25
viscosity = 0.05
mass_shift = 0.001
STEPS = (0.45, 0.3)
VMEM = 48 * 1024 * 1024
ROWS = 2 * NP - 1
WINDOW = 4 * (NP - 1) + 3
EDGE = NP + 1
MODES = 112


def legendre_pair(points, order):
    before = np.ones(points.shape)
    current = points * 1.0
    for level in range(2, order + 1):
        nextone = ((2 * level - 1) * points * current - (level - 1) * before) / level
        before = current
        current = nextone
    return (current, before)


def jacobi_eigen(matrix):
    size = matrix.shape[0]
    work = matrix * 1.0
    vectors = np.eye(size)
    for sweep in range(30):
        for first in range(size - 1):
            for second in range(first + 1, size):
                off = float(work[first, second])
                if abs(off) > 1e-300:
                    tau = (float(work[second, second]) - float(work[first, first])) / (2.0 * off)
                    if tau >= 0.0:
                        tangent = 1.0 / (tau + (1.0 + tau * tau) ** 0.5)
                    else:
                        tangent = -1.0 / (-tau + (1.0 + tau * tau) ** 0.5)
                    cosine = 1.0 / (1.0 + tangent * tangent) ** 0.5
                    sine = tangent * cosine
                    rotation = np.eye(size)
                    rotation[first, first] = cosine
                    rotation[second, second] = cosine
                    rotation[first, second] = sine
                    rotation[second, first] = -sine
                    work = rotation.T @ work @ rotation
                    vectors = vectors @ rotation
    diagonal_index = np.arange(size)
    return (work[diagonal_index, diagonal_index], vectors)


def base_tables(points_edge, points_fine):
    degree = points_edge - 1
    points = -np.cos(np.pi * np.arange(points_edge) / degree)
    for sweep in range(100):
        top, below = legendre_pair(points, degree)
        points = points - (points * top - below) / (points_edge * top)
    top, below = legendre_pair(points, degree)
    weight_gll = 2.0 / (degree * points_edge * top**2)
    spacing = points[:, None] - points[None, :] + np.eye(points_edge)
    barycentric = 1.0 / np.prod(spacing, axis=1)
    derivative = barycentric[None, :] / barycentric[:, None] / spacing
    derivative = derivative * (1.0 - np.eye(points_edge))
    derivative = derivative - np.eye(points_edge) * derivative.sum(axis=1)[:, None]
    fine_points = np.cos(np.pi * (np.arange(points_fine) + 0.75) / (points_fine + 0.5))
    for sweep in range(100):
        top, below = legendre_pair(fine_points, points_fine)
        slope = points_fine * (fine_points * top - below) / (fine_points * fine_points - 1.0)
        fine_points = fine_points - top / slope
    top, below = legendre_pair(fine_points, points_fine)
    slope = points_fine * (fine_points * top - below) / (fine_points * fine_points - 1.0)
    fine_weight = 2.0 / ((1.0 - fine_points * fine_points) * slope * slope)
    fine_points = fine_points[::-1]
    fine_weight = fine_weight[::-1]
    interpolate = np.ones((points_fine, points_edge))
    for column in range(points_edge):
        for other in range(points_edge):
            if other != column:
                interpolate[:, column] = (
                    interpolate[:, column]
                    * (fine_points - points[other])
                    / (points[column] - points[other])
                )
    stiffness = derivative.T @ (weight_gll[:, None] * derivative)
    extent = 3 * degree + 1
    joined_stiff = np.zeros((extent, extent))
    joined_mass = np.zeros(extent)
    for segment in range(3):
        offset = segment * degree
        joined_stiff[offset : offset + points_edge, offset : offset + points_edge] += stiffness
        joined_mass[offset : offset + points_edge] += weight_gll
    low = degree - 1
    high = 2 * degree + 2
    root_mass = np.sqrt(joined_mass[low:high])
    scaled = joined_stiff[low:high, low:high] / root_mass[:, None] / root_mass[None, :]
    scaled = 0.5 * (scaled + scaled.T)
    eigen_values, eigen_vectors = jacobi_eigen(scaled)
    solve_mat = eigen_vectors / root_mass[:, None]
    breadth = high - low
    return dict(
        derivative=derivative,
        interpolate=interpolate,
        weight=weight_gll,
        fine_weight=fine_weight,
        solve=solve_mat,
        eigen=eigen_values,
    )


def f32(value):
    return np.ascontiguousarray(value, dtype=np.float32)


def halves(value):
    value = np.asarray(value, dtype=np.float32)
    high = value.astype(jnp.bfloat16)
    rest = (value - high.astype(np.float32)).astype(jnp.bfloat16)
    return np.stack([high, rest])


def make_tables():
    base = base_tables(NP, NF)
    deriv, interp, solve, eigen = base["derivative"], base["interpolate"], base["solve"], base["eigen"]
    w, wf = base["weight"], base["fine_weight"]
    out = {}
    index = np.arange(NP)

    def sublane(matrix):
        rows = [matrix[index, (index + shift) % NP] for shift in range(NP)]
        return f32(np.broadcast_to(np.stack(rows)[:, :, None], (NP, NP, LANES)))

    def lane(matrix):
        rows = []
        for shift in range(-(NP - 1), NP):
            row = np.zeros(NP)
            for q in range(NP):
                if 0 <= q + shift < NP:
                    row[q] = matrix[q, q + shift]
            rows.append(np.tile(row, ES))
        return f32(np.broadcast_to(np.stack(rows)[:, None, :], (2 * NP - 1, NP, LANES)))

    out["ds"] = np.stack([sublane(deriv), sublane(deriv.T)])
    out["dq"] = np.stack([lane(deriv), lane(deriv.T)])
    out["w3"] = f32(np.einsum("a,s,q->asq", w, w, w).reshape(1, 512))
    out["wmass"] = f32(np.tile(np.einsum("a,s,q->asq", w, w, w), (1, 1, ES)))
    out["jright"] = halves(np.kron(np.eye(ES), interp.T))
    out["jright_t"] = halves(np.kron(np.eye(ES), interp))
    out["jleft"] = halves(np.kron(interp, interp))
    out["jleft_t"] = halves(np.kron(interp, interp).T)
    out["wfine"] = f32(np.kron(np.kron(wf, wf)[:, None], np.tile(wf, ES)[None, :]))
    wide = NP + 2
    left = np.zeros((MODES, 3, wide, NP))
    back = np.zeros((3, wide, NP, MODES))
    for i in range(wide):
        for j in range(wide):
            row = i * wide + j
            for a in range(wide):
                for s in range(NP):
                    left[row, 0, a, s] = solve[a, i] * solve[s + 1, j]
                    back[0, a, s, row] = solve[a, i] * solve[s + 1, j]
                left[row, 1, a, NP - 2] = solve[a, i] * solve[0, j]
                left[row, 2, a, 1] = solve[a, i] * solve[wide - 1, j]
                back[1, a, NP - 2, row] = solve[a, i] * solve[0, j]
                back[1, a, NP - 1, row] = solve[a, i] * solve[1, j]
                back[2, a, 1, row] = solve[a, i] * solve[wide - 1, j]
                back[2, a, 0, row] = solve[a, i] * solve[wide - 2, j]
    out["sleft"] = halves(left.reshape(MODES, 240))
    out["sback"] = halves(back.reshape(240, MODES))
    out["sright"] = halves(np.kron(np.eye(ES), solve[1:-1, :]))
    out["srback"] = halves(np.kron(np.eye(ES), solve[1:-1, :].T))
    out["spread"] = f32(np.kron(np.eye(ES), np.ones((NP, wide))) / 8.0)
    lam_a = np.zeros((MODES, 1))
    lam_s = np.zeros((MODES, 1))
    lam_a[:100, 0] = np.repeat(eigen, wide)
    lam_s[:100, 0] = np.tile(eigen, wide)
    lam_q = np.tile(eigen, ES)[None, :]
    full = (MODES, ES * wide)
    out["lam"] = f32(np.stack([np.broadcast_to(lam_a, full), np.broadcast_to(lam_s, full), np.broadcast_to(lam_q, full)]))
    half = np.ones(NP)
    half[0] = half[-1] = 0.5
    out["ws"] = f32(np.broadcast_to(half[:, None], (NP, LANES)))
    return out


TAB = make_tables()
DERIV = [[float(x) for x in row] for row in base_tables(NP, NF)["derivative"].astype(np.float32)]
PARAMS = pltpu.CompilerParams(vmem_limit_bytes=VMEM)


def full_dot(left, right):
    return jnp.dot(left, right, precision=lax.Precision.HIGHEST, preferred_element_type=jnp.float32)


def short_dot(left, right):
    return jnp.dot(left, right, preferred_element_type=jnp.float32)


def split(x):
    high = x.astype(jnp.bfloat16)
    return high, (x - high.astype(jnp.float32)).astype(jnp.bfloat16)


def left_dot(table, x):
    high, rest = split(x)
    return short_dot(table[0], high) + (short_dot(table[1], high) + short_dot(table[0], rest))


def right_dot(x, table):
    high, rest = split(x)
    return short_dot(high, table[0]) + (short_dot(high, table[1]) + short_dot(rest, table[0]))


def roll(x, shift, axis):
    return pltpu.roll(x, shift % x.shape[axis], axis)


def d_a(x, transposed):
    rows = []
    for a in range(NP):
        total = None
        for b in range(NP):
            term = (DERIV[b][a] if transposed else DERIV[a][b]) * x[b]
            total = term if total is None else total + term
        rows.append(total)
    return jnp.stack(rows)


def d_s(x, coef):
    total = coef[0][None] * x
    for shift in range(1, NP):
        total = total + coef[shift][None] * roll(x, -shift, 1)
    return total


def d_q(x, coef):
    total = coef[NP - 1][None] * x
    for shift in range(1, NP):
        total = total + coef[NP - 1 + shift][None] * roll(x, -shift, 2)
        total = total + coef[NP - 1 - shift][None] * roll(x, shift, 2)
    return total


def gradient(x, ds, dq):
    return d_a(x, False), d_s(x, ds[0]), d_q(x, dq[0])


def gradient_t(xa, xs, xq, ds, dq):
    return d_a(xa, True) + d_s(xs, ds[1]) + d_q(xq, dq[1])


def join_s(x):
    s = lax.broadcasted_iota(jnp.int32, x.shape, 1)
    from_before = roll(roll(x, NP, 2), 1, 1)
    from_after = roll(roll(x, -NP, 2), -1, 1)
    zero = jnp.zeros_like(x)
    return x + jnp.where(s == 0, from_before, jnp.where(s == NP - 1, from_after, zero))


def parity():
    return lax.rem(lax.axis_index("dom"), 2)


def swap_inner(x, count):
    return lax.ppermute(x, "dom", [(i, i ^ 1) for i in range(count)])


def swap_cross(x, count):
    pairs = [(i, (i + 1) % count if i % 2 else (i - 1) % count) for i in range(count)]
    return lax.ppermute(x, "dom", pairs)


def to_lanes(x):
    shape = (x.shape[0], NP, LANES)
    lane = lax.broadcasted_iota(jnp.int32, shape, 2)
    pieces = []
    for tile in range(4):
        first = x[:, :8, tile * LANES : (tile + 1) * LANES]
        second = x[:, 8:, tile * LANES : (tile + 1) * LANES]
        pieces.append(jnp.where(lane < 64, first, roll(second, 64, 2)))
        pieces.append(jnp.where(lane < 64, roll(first, 64, 2), second))
    y = jnp.stack(pieces, axis=1).reshape(x.shape[0] * NP, NP, LANES)
    sub = lax.broadcasted_iota(jnp.int32, y.shape, 1)
    lane = lax.broadcasted_iota(jnp.int32, y.shape, 2)
    for bit in range(3):
        step = 1 << bit
        in_sub = (sub & step) != 0
        in_lane = (lane & (step * 8)) != 0
        up = roll(roll(y, -step, 1), step * 8, 2)
        down = roll(roll(y, step, 1), -step * 8, 2)
        y = jnp.where(in_sub == in_lane, y, jnp.where(in_lane, up, down))
    return y.reshape(x.shape[0], NP, NP, LANES)


def rows(x):
    return x.reshape(NP * NP, LANES)


def planes(x):
    return x.reshape(NP, NP, LANES)


def take_lanes(x, index):
    flat = x.reshape(-1, LANES)
    tiled = jnp.broadcast_to(index[None], x.shape).reshape(-1, LANES)
    return jnp.take_along_axis(flat, tiled, axis=1).reshape(x.shape)


def forcing_kernel(slot_in, vel_in, past_in, metric_in, jac_in, w3_in, wmass_in, ds_in, dq_in, jright_in, jright_t_in, jleft_in, jleft_t_in, wfine_in, pack_ref, cross_ref, slot_ref, vel_ref, past_ref, metric_ref, jac_ref, w3_ref, wmass_ref, ds_ref, dq_ref, jright_ref, jright_t_ref, jleft_ref, jleft_t_ref, wfine_ref, sems):
    sources = (slot_in, vel_in, past_in, metric_in, jac_in, w3_in, wmass_in, ds_in, dq_in, jright_in, jright_t_in, jleft_in, jleft_t_in, wfine_in)
    targets = (slot_ref, vel_ref, past_ref, metric_ref, jac_ref, w3_ref, wmass_ref, ds_ref, dq_ref, jright_ref, jright_t_ref, jleft_ref, jleft_t_ref, wfine_ref)
    copies = [pltpu.make_async_copy(x, y, sems.at[k]) for k, (x, y) in enumerate(zip(sources, targets))]
    for copy in copies:
        copy.start()
    for copy in copies:
        copy.wait()
    even = parity() == 0
    ds, dq = ds_ref[...], dq_ref[...]
    jac = jac_ref[...]
    new, mid, old = vel_ref[0], vel_ref[1], vel_ref[2]
    guess = 3.0 * (new - mid) + old
    direct = (jac * w3_ref[...])[None] * (-10.0 * new + 16.0 * mid - 6.0 * old) + 3.0 * past_ref[0] - past_ref[1]
    lanes = to_lanes(jnp.concatenate([new, guess, direct, metric_ref[...], jac[None]], axis=0))
    new, guess, direct, metric, jac = lanes[0:3], lanes[3:6], lanes[6:9], lanes[9:12], lanes[12]
    fields = [rows(jac)] + [rows(new[d] * metric[d]) for d in range(3)]
    for i in range(3):
        fields.extend(rows(part) for part in gradient(new[i], ds, dq))
    wide = right_dot(jnp.concatenate(fields, axis=0), jright_ref)
    fine = [left_dot(jleft_ref, wide[64 * k : 64 * k + 64]) for k in range(13)]
    scale = fine[0] * wfine_ref[...]
    products = []
    for i in range(3):
        total = fine[1] * fine[4 + 3 * i] + fine[2] * fine[5 + 3 * i] + fine[3] * fine[6 + 3 * i]
        products.append(left_dot(jleft_t_ref, scale * total))
    coarse = right_dot(jnp.concatenate(products, axis=0), jright_t_ref)
    mass = jac * wmass_ref[...]
    factor = [mass * metric[d] * metric[d] for d in range(3)]
    result = []
    for i in range(3):
        ga, gs, gq = gradient(guess[i], ds, dq)
        stiff = gradient_t(factor[0] * ga, factor[1] * gs, factor[2] * gq, ds, dq)
        result.append(direct[i] - 3.0 * planes(coarse[64 * i : 64 * i + 64]) - viscosity * stiff)
    result.extend([mass, metric[0], metric[1], metric[2]])
    lane = lax.broadcasted_iota(jnp.int32, (NP, LANES), 1)
    index = jnp.zeros((NP, LANES), jnp.int32)
    for e in range(ES):
        index = jnp.where(lane // NP == slot_ref[e], e * NP, index)
    index = index + lane % NP
    result = [take_lanes(x, index) for x in result]
    for k in range(4):
        joined = join_s(result[k])
        cross_ref[k] = jnp.where(even, joined[0], joined[NP - 1])
        pack_ref[NP * k : NP * k + NP] = joined if k < 3 else result[k]
    for k in range(4, 7):
        pack_ref[NP * k : NP * k + NP] = result[k]


def pair_kernel(pack_ref, cross_in, out_ref):
    out_ref[: 7 * NP] = pack_ref[...]
    out_ref[7 * NP :] = cross_in[...]


def chip_rows(first, second):
    return jnp.concatenate([first[:-1], (first[-1] + second[0])[None], second[1:]], axis=0)


def own_rows(even, x):
    return jnp.where(even, x[:NP], x[NP - 1 :])


def edge_rows(even, x):
    return jnp.where(even, x[:EDGE], x[ROWS - EDGE :])


def divergence_kernel(own_ref, mate_ref, ds_ref, dq_ref, div_ref, op_ref, level_ref, cross_ref):
    even = parity() == 0
    own, mate = own_ref[...], mate_ref[...]
    packs = [jnp.where(even, own, mate), jnp.where(even, mate, own)]
    parts = [[pack[NP * k : NP * k + NP] for k in range(7)] for pack in packs]
    low, high = packs[0][7 * NP :], packs[1][7 * NP :]
    sides = []
    for k in range(4):
        first, second = parts[0][k], parts[1][k]
        if k == 3:
            first, second = join_s(first), join_s(second)
        whole = chip_rows(first, second)
        sides.append(jnp.concatenate([(whole[0] + low[k])[None], whole[1:-1], (whole[-1] + high[k])[None]], axis=0))
    inv = 1.0 / sides[3]
    accel = [sides[d] * inv for d in range(3)]
    div = []
    levels = []
    for layer in range(2):
        mass = parts[layer][3]
        at = (NP - 1) * layer
        sums = []
        terms = []
        for d in range(3):
            one = mass * parts[layer][4 + d]
            two = one * parts[layer][4 + d]
            op_ref[layer, d] = two
            sums.append(jnp.sum(rows(two), axis=0, keepdims=True))
            terms.append(one * accel[d][at : at + NP])
        op_ref[layer, 3] = mass_shift * mass
        sums.append(jnp.sum(rows(mass), axis=0, keepdims=True))
        sums.append(jnp.zeros((4, LANES), jnp.float32))
        levels.append(jnp.concatenate(sums, axis=0))
        level_ref[layer] = levels[layer]
        div.append(join_s(gradient_t(terms[0], terms[1], terms[2], ds_ref[...], dq_ref[...])))
    whole = chip_rows(div[0], div[1])
    div_ref[...] = whole
    cross_ref[:EDGE] = edge_rows(even, whole)
    cross_ref[EDGE] = jnp.where(even, levels[0], levels[1])


def window(local, low, high):
    return jnp.concatenate(
        [low[: EDGE - 1], (low[EDGE - 1] + local[0])[None], local[1:-1], (local[-1] + high[0])[None], high[1:EDGE]],
        axis=0,
    )


def inverse_levels(levels, spread_ref, lam_ref):
    result = []
    for level in levels:
        level = full_dot(level, spread_ref[...])
        denom = level[0:1] * lam_ref[0] + level[1:2] * lam_ref[1] + level[2:3] * lam_ref[2] + mass_shift * level[3:4]
        result.append(1.0 / denom)
    return result


def schwarz(wide, inv_ref, sleft_ref, sright_ref, srback_ref, sback_ref):
    before, after = roll(wide, NP, 2), roll(wide, -NP, 2)
    columns = []
    for layer in range(4):
        at = (NP - 1) * layer
        columns.append(jnp.concatenate([x[at : at + NP + 2].reshape(80, LANES) for x in (wide, before, after)], axis=0))
    spectra = left_dot(sleft_ref, jnp.concatenate(columns, axis=1))
    spectra = jnp.concatenate([spectra[:, LANES * k : LANES * k + LANES] for k in range(4)], axis=0)
    spectra = right_dot(right_dot(spectra, sright_ref) * inv_ref[...], srback_ref)
    spectra = jnp.concatenate([spectra[MODES * k : MODES * k + MODES] for k in range(4)], axis=1)
    blocks = left_dot(sback_ref, spectra)
    z = []
    for layer in range(4):
        part = blocks[:, LANES * layer : LANES * layer + LANES]
        part = part[:80] + roll(part[80:160], -NP, 1) + roll(part[160:], NP, 1)
        z.append(part.reshape(NP + 2, NP, LANES))
    middle = jnp.concatenate([z[1][1:8], (z[1][8] + z[2][1])[None], z[2][2:9]], axis=0)
    first = jnp.concatenate([z[0][8:10], jnp.zeros((4, NP, LANES), jnp.float32), z[2][0:1], jnp.zeros((1, NP, LANES), jnp.float32), z[1][9:10], jnp.zeros((4, NP, LANES), jnp.float32), z[3][0:2]], axis=0)
    return middle + first


def operate(v, op_ref, ds_ref, dq_ref):
    ds, dq = ds_ref[...], dq_ref[...]
    parts = []
    for layer in range(2):
        x = v[(NP - 1) * layer : (NP - 1) * layer + NP]
        ga, gs, gq = gradient(x, ds, dq)
        local = gradient_t(op_ref[layer, 0] * ga, op_ref[layer, 1] * gs, op_ref[layer, 2] * gq, ds, dq)
        parts.append(join_s(local + op_ref[layer, 3] * x))
    return chip_rows(parts[0], parts[1])


def sides_of(even, own_in, mate_in):
    own, mate = own_in[...], mate_in[...]
    return jnp.where(even, own, mate), jnp.where(even, mate, own)


def first_kernel(div_ref, own_in, mate_in, level_ref, spread_ref, lam_ref, op_ref, ds_ref, dq_ref, sleft_ref, sright_ref, srback_ref, sback_ref, wide_ref, inv_ref, v_ref, local_ref, cross_ref):
    even = parity() == 0
    low, high = sides_of(even, own_in, mate_in)
    wide = window(div_ref[...], low, high)
    wide_ref[...] = wide
    for k, inv in enumerate(inverse_levels([low[EDGE], level_ref[0], level_ref[1], high[EDGE]], spread_ref, lam_ref)):
        inv_ref[MODES * k : MODES * k + MODES] = inv
    v = schwarz(wide, inv_ref, sleft_ref, sright_ref, srback_ref, sback_ref)
    v_ref[...] = v
    local = operate(v, op_ref, ds_ref, dq_ref)
    local_ref[...] = local
    cross_ref[...] = edge_rows(even, local)


def next_kernel(step, before_ref, image_ref, own_in, mate_in, inv_ref, op_ref, ds_ref, dq_ref, sleft_ref, sright_ref, srback_ref, sback_ref, own_image_ref, wide_ref, v_ref, local_ref, cross_ref):
    even = parity() == 0
    low, high = sides_of(even, own_in, mate_in)
    image = window(image_ref[...], low, high)
    own_image_ref[...] = own_rows(even, image[NP : NP + ROWS])
    wide = before_ref[...] - step * image
    wide_ref[...] = wide
    v = schwarz(wide, inv_ref, sleft_ref, sright_ref, srback_ref, sback_ref)
    v_ref[...] = v
    local = operate(v, op_ref, ds_ref, dq_ref)
    local_ref[...] = local
    cross_ref[...] = edge_rows(even, local)


def last_kernel(step, before_ref, image_ref, own_in, mate_in, inv_ref, op_ref, ds_ref, dq_ref, sleft_ref, sright_ref, srback_ref, sback_ref, ws_ref, v0_ref, v1_ref, l0_ref, own_image_ref, own_ref, sums_ref):
    even = parity() == 0
    low, high = sides_of(even, own_in, mate_in)
    image = window(image_ref[...], low, high)
    own_image_ref[...] = own_rows(even, image[NP : NP + ROWS])
    residual = before_ref[NP : NP + ROWS] - step * image[NP : NP + ROWS]
    wide = before_ref[...] - step * image
    v2 = schwarz(wide, inv_ref, sleft_ref, sright_ref, srback_ref, sback_ref)
    l2 = operate(v2, op_ref, ds_ref, dq_ref)
    v = [v0_ref[...], v1_ref[...], v2]
    images = [l0_ref[...], image_ref[...], l2]
    for k, x in enumerate((v[0], v[1], v2, l2, residual)):
        own_ref[k] = own_rows(even, x)
    weighted = jnp.concatenate([0.5 * residual[:1], residual[1:-1], 0.5 * residual[-1:]], axis=0)
    ws = ws_ref[...]
    pairs = [(v[i], images[j]) for i, j in ((0, 0), (0, 1), (0, 2), (1, 1), (1, 2), (2, 2))]
    pairs.extend((v[i], weighted) for i in range(3))
    lane = lax.broadcasted_iota(jnp.int32, (NP, LANES), 1)
    line = jnp.zeros((NP, LANES), jnp.float32)
    for k, (left, right) in enumerate(pairs):
        line = jnp.where(lane == k, jnp.sum(jnp.sum(left * right, axis=0) * ws), line)
    face = jnp.where(even, l2[0], l2[-1])
    for k in range(sums_ref.shape[0]):
        sums_ref[k, 0] = face
        sums_ref[k, 1] = line


def relay_kernel(near_ref, out_ref):
    total = jnp.sum(near_ref[:, 1], axis=0)
    device = lax.axis_index("dom")
    count = near_ref.shape[0]
    chip = lax.rem(device // 2, count)
    face = near_ref[chip, 0]
    for k in range(out_ref.shape[0]):
        out_ref[k, 0] = face
        out_ref[k, 1] = total


def to_output(x):
    by_s = [jnp.concatenate([x[a][s : s + 1] for a in range(NP)], axis=0) for s in range(NP - 1)]
    tiles = []
    for tile in range(7):
        at = lax.broadcasted_iota(jnp.int32, (NP, LANES), 1) + tile * LANES
        element = at // 56
        s = (at - element * 56) // NP
        index = element * NP + at % NP
        value = jnp.take_along_axis(by_s[0], index, axis=1)
        for k in range(1, NP - 1):
            value = jnp.where(s == k, jnp.take_along_axis(by_s[k], index, axis=1), value)
        tiles.append(value)
    return jnp.concatenate(tiles, axis=1)


def combine_kernel(near_ref, far_ref, own_ref, w0_ref, w1_ref, p_ref, r_ref):
    device = lax.axis_index("dom")
    even = lax.rem(device, 2) == 0
    near, far = near_ref.shape[0], far_ref.shape[0]
    chips = near * far
    chip = device // 2
    partner = lax.rem(jnp.where(even, chip + chips - 1, chip + 1), chips)
    inside = partner // near == chip // near
    face = jnp.where(inside, near_ref[lax.rem(partner, near), 0], far_ref[partner // near, 0])
    local = own_ref[3]
    first = jnp.where(even, local[0] + face, local[0])
    last = jnp.where(even, local[-1], local[-1] + face)
    w2 = jnp.concatenate([first[None], local[1:-1], last[None]], axis=0)
    line = jnp.sum(far_ref[:, 1], axis=0)[:1]
    h00, h01, h02, h11, h12, h22, g0, g1, g2 = [line[:, k : k + 1] for k in range(9)]
    m1, m2 = h01 / h00, h02 / h00
    k11, k12, k22 = h11 - m1 * h01, h12 - m1 * h02, h22 - m2 * h02
    f1, f2 = g1 - m1 * g0, g2 - m2 * g0
    n2 = k12 / k11
    c2 = (f2 - n2 * f1) / (k22 - n2 * k12)
    c1 = (f1 - k12 * c2) / k11
    c0 = (g0 - h01 * c1 - h02 * c2) / h00
    pressure = (c0 + STEPS[0])[None] * own_ref[0] + (c1 + STEPS[1])[None] * own_ref[1] + c2[None] * own_ref[2]
    residual = own_ref[4] - (c0[None] * w0_ref[...] + c1[None] * w1_ref[...] + c2[None] * w2)
    p_ref[...] = to_output(pressure)
    r_ref[...] = to_output(residual)


def call(kernel, shapes, *args):
    return pl.pallas_call(
        kernel,
        out_shape=[jax.ShapeDtypeStruct(shape, jnp.float32) for shape in shapes],
        in_specs=[pl.BlockSpec(memory_space=pltpu.VMEM)] * len(args),
        out_specs=[pl.BlockSpec(memory_space=pltpu.VMEM)] * len(shapes),
        compiler_params=PARAMS,
    )(*args)


def call_forcing(*args):
    shapes = [(7 * NP, NP, LANES), (4, NP, LANES)]
    scratch = [pltpu.SMEM(args[0].shape, jnp.int32)]
    scratch.extend(pltpu.VMEM(x.shape, x.dtype) for x in args[1:])
    scratch.append(pltpu.SemaphoreType.DMA((len(args),)))
    return pl.pallas_call(
        forcing_kernel,
        out_shape=[jax.ShapeDtypeStruct(shape, jnp.float32) for shape in shapes],
        in_specs=[pl.BlockSpec(memory_space=pl.ANY)] * len(args),
        out_specs=[pl.BlockSpec(memory_space=pltpu.VMEM)] * len(shapes),
        scratch_shapes=scratch,
        compiler_params=PARAMS,
    )(*args)


def groups_of(count):
    chips = count // 2
    near = {256: 16, 16: 4, 4: 2}[chips]
    far = chips // near
    first, second = [], []
    for team in range(2):
        member = [2 * c + (team + c) % 2 for c in range(chips)]
        first.extend([member[near * i + j] for j in range(near)] for i in range(far))
        second.extend([member[near * i + (j if i % 2 == 0 else near - 1 - j)] for i in range(far)] for j in range(near))
    return near, far, first, second


def shards(velocity, conv_past, metric, jacobian, element_slot):
    count = lax.axis_size("dom")
    t = {key: jnp.asarray(value) for key, value in TAB.items()}
    field = (NP, NP, LANES)
    chip = (ROWS, NP, LANES)
    wide_shape = (WINDOW, NP, LANES)
    edge = (EDGE, NP, LANES)

    def exchange(x):
        own = swap_cross(x, count)
        return own, swap_inner(own, count)

    pack, cross = call_forcing(
        element_slot, velocity, conv_past, metric, jacobian,
        t["w3"], t["wmass"], t["ds"], t["dq"], t["jright"], t["jright_t"], t["jleft"], t["jleft_t"], t["wfine"],
    )
    (own,) = call(pair_kernel, [(7 * NP + 4, NP, LANES)], pack, swap_cross(cross, count))
    mate = swap_inner(own, count)
    div, op, level, cross = call(
        divergence_kernel,
        [chip, (2, 4) + field, (2, NP, LANES), (EDGE + 1, NP, LANES)],
        own, mate, t["ds"], t["dq"],
    )
    tables = (op, t["ds"], t["dq"], t["sleft"], t["sright"], t["srback"], t["sback"])
    wide, inv, v0, local0, cross = call(
        first_kernel,
        [wide_shape, (4 * MODES, ES * (NP + 2)), chip, chip, edge],
        div, *exchange(cross), level, t["spread"], t["lam"], *tables,
    )
    image0, wide, v1, local1, cross = call(
        functools.partial(next_kernel, STEPS[0]),
        [field, wide_shape, chip, chip, edge],
        wide, local0, *exchange(cross), inv, *tables,
    )
    near, far, first, second = groups_of(count)
    image1, own, sums = call(
        functools.partial(last_kernel, STEPS[1]),
        [field, (5,) + field, (near, 2, NP, LANES)],
        wide, local1, *exchange(cross), inv, *tables, t["ws"], v0, v1, local0,
    )
    near_sums = lax.all_to_all(sums, "dom", 0, 0, tiled=True, axis_index_groups=first)
    (sums,) = call(relay_kernel, [(far, 2, NP, LANES)], near_sums)
    far_sums = lax.all_to_all(sums, "dom", 0, 0, tiled=True, axis_index_groups=second)
    return tuple(
        call(combine_kernel, [(NP, 896), (NP, 896)], near_sums, far_sums, own, image0, image1)
    )


def solution(mesh):
    return jax.shard_map(
        shards,
        mesh=mesh,
        in_specs=(
            P(None, None, "dom", None),
            P(None, None, "dom", None),
            P(None, "dom", None),
            P("dom", None),
            P("dom"),
        ),
        out_specs=(P("dom", None), P("dom", None)),
        check_vma=False,
    )
```

time: 146 us -> 123 us (0.84)
  the two profiles are of different devices: /device:TPU:1 before, /device:TPU:9 now
where the time goes in v2:
time: 123 us; the launch traced here: 122 us
  starting transfers between devices  41.6 us (34%)
  blocking collectives  41 us (33%)
  waiting for transfers between devices  13.8 us (11%)
  Pallas kernels  13.3 us (11%)
  local copies, waits for them, and re-layouts  11.8 us (10%)
    ppermute x4, starting transfers between devices, swap_inner(): return lax.ppermute(x, 'dom', [(i, i ^ 1) for i in range(count)])  30.4 us
    all_to_all x1, blocking collectives, shards(): lax.all_to_all(sums, 'dom', 0, 0, tiled=True, axis_index_groups=second)  22.8 us
    all_to_all x1, blocking collectives, shards(): lax.all_to_all(sums, 'dom', 0, 0, tiled=True, axis_index_groups=first)  18.2 us
    unnamed x46, local copies, waits for them, and re-layouts  11.8 us
    ppermute x4, starting transfers between devices, swap_cross(): return lax.ppermute(x, 'dom', pairs)  11.2 us
    ppermute x4, waiting for transfers between devices, swap_cross(): return lax.ppermute(x, 'dom', pairs)  10.1 us
    pallas_call x7, Pallas kernels, call(): pl.pallas_call(kernel, out_shape=[jax.ShapeDtypeStruct(shape, jnp.float32...  8.77 us
    pallas_call x1, Pallas kernels, call_forcing(): pl.pallas_call(forcing_kernel, out_shape=[jax.ShapeDtypeStruct(shape, jnp...  4.51 us
  transfers between devices with their start and end apart: 8, of which 8 were waited for; matrix products, arithmetic and copies ran while one was open for 0% of the time, Pallas kernels for 0%

profile of v2, /device:TPU:9, one launch (start us, length us, event | category | flops | bytes accessed | tf_op | source)
XLA Modules:
  0.0 122.3 jit_solution(16503960304833201162)
XLA Ops:
  0.6 0.0 copy-start.21
  0.6 0.7 copy-done.21
  1.3 0.9 copy-done
  2.2 0.0 copy-start.2
  2.2 0.8 copy-done.2
  3.1 0.0 copy-start.9
  3.1 1.0 copy-done.9
  4.0 0.0 copy-start.10
  4.0 0.9 copy-done.10
  4.9 0.0 copy-start.11
  5.0 0.9 copy-done.11
  5.9 0.0 copy-start.13
  5.9 0.9 copy-done.13
  6.8 0.0 copy-start.14
  6.8 0.9 copy-done.14
  7.7 0.9 copy-done.15
  8.5 0.0 copy-start.16
  8.6 0.9 copy-done.16
  9.4 0.0 copy-start.17
  9.4 0.8 copy-done.17
  10.3 0.0 copy-start.18
  10.3 0.8 copy-done.18
  11.0 0.0 copy-start.19
  11.0 0.8 copy-done.19
  11.8 0.0 copy-start.22
  11.8 0.7 copy-done.22
  12.4 4.5 %shard_map.212 = (f32[56,8,128]{2,1,0:T(8,128)S(1)}, f32[4,8,128]{2,1,0:T(8,128)S(1)}) custom-call(s32[16]{0:T(128)S(1)} %copy-done.22, f32[3,3,16,512]{3,2,1,0:T(8,128)S(1)} %copy-done.9, f32[2,3,16,512]{3,2,1,0:T(8,128)S(1)} %copy-done.10, f32[3,16,512]{2,1,0:T(8,128)S(1)} %copy-done.14, f32[16,512]{1,0:T(8,128)S(1)} %copy-done.18, ...), custom_call_target="tpu_custom_call" | custom-call | tf_op jit(solution)/shard_map/pallas_call | solution.py:602
  17.0 3.8 %collective-permute-start = (f32[4,8,128]{2,1,0:T(8,128)S(1)}, f32[4,8,128]{2,1,0:T(8,128)S(1)}, u32[]{:S(2)}, u32[]{:S(2)}) collective-permute-start(f32[4,8,128]{2,1,0:T(8,128)S(1)} %get-tuple-element.22), channel_id=1, source_target_pairs={{0,511},{1,2},{2,1},{3,4},{4,3},{5,6},{6,5},{7,8},{8,7},{9,10},{10... | collective-permute-start | bytes 49160 | tf_op jit(solution)/shard_map/ppermute | solution.py:280
  20.7 1.6 %collective-permute-done.cross_in = f32[4,8,128]{2,1,0:T(8,128)S(1)} collective-permute-done((f32[4,8,128]{2,1,0:T(8,128)S(1)}, f32[4,8,128]{2,1,0:T(8,128)S(1)}, u32[]{:S(2)}, u32[]{:S(2)}) %collective-permute-start) | collective-permute-done | bytes 16416 | tf_op jit(solution)/shard_map/ppermute | solution.py:280
  22.3 0.0 copy-start.4
  22.3 0.0 copy-start.5
  22.4 0.0 copy-start.6
  22.4 0.0 copy-start.7
  22.4 0.0 copy-start.12
  22.4 2.4 %collective-permute-start.1 = (f32[60,8,128]{2,1,0:T(8,128)S(1)}, f32[60,8,128]{2,1,0:T(8,128)S(1)}, u32[]{:S(2)}, u32[]{:S(2)}) collective-permute-start(f32[60,8,128]{2,1,0:T(8,128)S(1)} %shard_map.213.own_ref), channel_id=1, source_target_pairs={{0,1},{1,0},{2,3},{3,2},{4,5},{5,4},{6,7},{7,6},{8,9},{9,8},{10,11... | collective-permute-start | bytes 737288 | tf_op jit(solution)/shard_map/ppermute | solution.py:275
  24.8 1.1 collective-permute-done.1.mate_ref
  26.0 0.0 copy-done.1
  26.0 0.0 copy-done.3
  26.0 0.6 shard_map.214
  26.5 3.5 %collective-permute-start.2 = (f32[10,8,128]{2,1,0:T(8,128)S(1)}, f32[10,8,128]{2,1,0:T(8,128)S(1)}, u32[]{:S(2)}, u32[]{:S(2)}) collective-permute-start(f32[10,8,128]{2,1,0:T(8,128)S(1)} %get-tuple-element.24), channel_id=1, source_target_pairs={{0,511},{1,2},{2,1},{3,4},{4,3},{5,6},{6,5},{7,8},{8,7},{9,10},{10... | collective-permute-start | bytes 122888 | tf_op jit(solution)/shard_map/ppermute | solution.py:280
  30.0 1.9 %collective-permute-done.2.own_in = f32[10,8,128]{2,1,0:T(8,128)S(1)} collective-permute-done((f32[10,8,128]{2,1,0:T(8,128)S(1)}, f32[10,8,128]{2,1,0:T(8,128)S(1)}, u32[]{:S(2)}, u32[]{:S(2)}) %collective-permute-start.2) | collective-permute-done | bytes 40992 | tf_op jit(solution)/shard_map/ppermute | solution.py:280
  31.9 12.6 %collective-permute-start.3 = (f32[10,8,128]{2,1,0:T(8,128)S(1)}, f32[10,8,128]{2,1,0:T(8,128)S(1)}, u32[]{:S(2)}, u32[]{:S(2)}) collective-permute-start(f32[10,8,128]{2,1,0:T(8,128)S(1)} %collective-permute-done.2.own_in), channel_id=1, source_target_pairs={{0,1},{1,0},{2,3},{3,2},{4,5},{5,4},{6,7},{7,6},{8,9},{9,8},{10,11... | collective-permute-start | bytes 122888 | tf_op jit(solution)/shard_map/ppermute | solution.py:275
  44.4 0.8 collective-permute-done.3.mate_in
  45.3 0.0 copy-done.8
  45.3 0.0 copy-done.4
  45.3 0.0 copy-done.5
  45.3 0.0 copy-done.6
  45.3 0.0 copy-done.7
  45.3 0.0 copy-done.12
  45.3 2.2 %shard_map.215 = (f32[31,8,128]{2,1,0:T(8,128)S(1)}, f32[448,160]{1,0:T(8,128)S(1)}, f32[15,8,128]{2,1,0:T(8,128)S(1)}, f32[15,8,128]{2,1,0:T(8,128)S(1)}, f32[9,8,128]{2,1,0:T(8,128)S(1)}) custom-call(f32[15,8,128]{2,1,0:T(8,128)S(1)} %get-tuple-element.23.div_ref, f32[10,8,128]{2,1,0:T(8,128)S(1)} %collective-permute-done.2.own_in, ...), custom_call_target="tpu_custom_call" | custom-call | tf_op jit(solution)/shard_map/pallas_call | solution.py:588
  47.6 1.9 %collective-permute-start.4 = (f32[9,8,128]{2,1,0:T(8,128)S(1)}, f32[9,8,128]{2,1,0:T(8,128)S(1)}, u32[]{:S(2)}, u32[]{:S(2)}) collective-permute-start(f32[9,8,128]{2,1,0:T(8,128)S(1)} %get-tuple-element.29), channel_id=1, source_target_pairs={{0,511},{1,2},{2,1},{3,4},{4,3},{5,6},{6,5},{7,8},{8,7},{9,10},{10... | collective-permute-start | bytes 110600 | tf_op jit(solution)/shard_map/ppermute | solution.py:280
  49.5 3.3 %collective-permute-done.4.own_in = f32[9,8,128]{2,1,0:T(8,128)S(1)} collective-permute-done((f32[9,8,128]{2,1,0:T(8,128)S(1)}, f32[9,8,128]{2,1,0:T(8,128)S(1)}, u32[]{:S(2)}, u32[]{:S(2)}) %collective-permute-start.4) | collective-permute-done | bytes 36896 | tf_op jit(solution)/shard_map/ppermute | solution.py:280
  52.8 7.7 %collective-permute-start.5 = (f32[9,8,128]{2,1,0:T(8,128)S(1)}, f32[9,8,128]{2,1,0:T(8,128)S(1)}, u32[]{:S(2)}, u32[]{:S(2)}) collective-permute-start(f32[9,8,128]{2,1,0:T(8,128)S(1)} %collective-permute-done.4.own_in), channel_id=1, source_target_pairs={{0,1},{1,0},{2,3},{3,2},{4,5},{5,4},{6,7},{7,6},{8,9},{9,8},{10,11... | collective-permute-start | bytes 110600 | tf_op jit(solution)/shard_map/ppermute | solution.py:275
  60.6 0.8 collective-permute-done.5.mate_in
  61.4 2.1 %shard_map.216 = (f32[8,8,128]{2,1,0:T(8,128)S(1)}, f32[31,8,128]{2,1,0:T(8,128)S(1)}, f32[15,8,128]{2,1,0:T(8,128)S(1)}, f32[15,8,128]{2,1,0:T(8,128)S(1)}, f32[9,8,128]{2,1,0:T(8,128)S(1)}) custom-call(f32[31,8,128]{2,1,0:T(8,128)S(1)} %get-tuple-element.27.before_ref, f32[15,8,128]{2,1,0:T(8,128)S(1)} %get-tuple-element.28.image_ref.l0_ref, ...), custom_call_target="tpu_custom_call" | custom-call | tf_op jit(solution)/shard_map/pallas_call | solution.py:588
  63.5 2.0 %collective-permute-start.6 = (f32[9,8,128]{2,1,0:T(8,128)S(1)}, f32[9,8,128]{2,1,0:T(8,128)S(1)}, u32[]{:S(2)}, u32[]{:S(2)}) collective-permute-start(f32[9,8,128]{2,1,0:T(8,128)S(1)} %get-tuple-element.33), channel_id=1, source_target_pairs={{0,511},{1,2},{2,1},{3,4},{4,3},{5,6},{6,5},{7,8},{8,7},{9,10},{10... | collective-permute-start | bytes 110600 | tf_op jit(solution)/shard_map/ppermute | solution.py:280
  65.5 3.3 %collective-permute-done.6.own_in = f32[9,8,128]{2,1,0:T(8,128)S(1)} collective-permute-done((f32[9,8,128]{2,1,0:T(8,128)S(1)}, f32[9,8,128]{2,1,0:T(8,128)S(1)}, u32[]{:S(2)}, u32[]{:S(2)}) %collective-permute-start.6) | collective-permute-done | bytes 36896 | tf_op jit(solution)/shard_map/ppermute | solution.py:280
  68.9 7.7 %collective-permute-start.7 = (f32[9,8,128]{2,1,0:T(8,128)S(1)}, f32[9,8,128]{2,1,0:T(8,128)S(1)}, u32[]{:S(2)}, u32[]{:S(2)}) collective-permute-start(f32[9,8,128]{2,1,0:T(8,128)S(1)} %collective-permute-done.6.own_in), channel_id=1, source_target_pairs={{0,1},{1,0},{2,3},{3,2},{4,5},{5,4},{6,7},{7,6},{8,9},{9,8},{10,11... | collective-permute-start | bytes 110600 | tf_op jit(solution)/shard_map/ppermute | solution.py:275
  76.6 0.8 collective-permute-done.7.mate_in
  77.4 0.0 copy-done.20
  77.4 2.2 %shard_map.217 = (f32[8,8,128]{2,1,0:T(8,128)S(1)}, f32[5,8,8,128]{3,2,1,0:T(8,128)S(1)}, f32[16,2,8,128]{3,2,1,0:T(8,128)S(1)}) custom-call(f32[31,8,128]{2,1,0:T(8,128)S(1)} %get-tuple-element.31.before_ref, f32[15,8,128]{2,1,0:T(8,128)S(1)} %get-tuple-element.32.image_ref, f32[9,8,128]{2,1,0:T(8,128)S(1)} %collective-permute-done.6.own_in, ...), custom_call_target="tpu_custom_call" | custom-call | tf_op jit(solution)/shard_map/pallas_call | solution.py:588
  79.6 18.2 %all_to_all.10.near_ref = f32[16,2,8,128]{3,2,1,0:T(8,128)S(1)} all-to-all(f32[16,2,8,128]{3,2,1,0:T(8,128)S(1)} %get-tuple-element.36), channel_id=1, replica_groups={{0,3,4,7,8,11,12,15,16,19,20,23,24,27,28,31},{32,35,36,39,40,43,44,47,4..., dimensions={0} | all-to-all | bytes 262144 | tf_op jit(solution)/shard_map/all_to_all | solution.py:664
  97.8 22.8 %all_to_all.11.far_ref = f32[16,2,8,128]{3,2,1,0:T(8,128)S(1)} all-to-all(f32[16,2,8,128]{3,2,1,0:T(8,128)S(1)} %shard_map.218), channel_id=1, replica_groups={{0,63,64,127,128,191,192,255,256,319,320,383,384,447,448,511},{3,60,67,..., dimensions={0} | all-to-all | bytes 262144 | tf_op jit(solution)/shard_map/all_to_all | solution.py:666
  120.6 1.6 %shard_map.219 = (f32[8,896]{1,0:T(8,128)}, f32[8,896]{1,0:T(8,128)}) custom-call(f32[16,2,8,128]{3,2,1,0:T(8,128)S(1)} %all_to_all.10.near_ref, f32[16,2,8,128]{3,2,1,0:T(8,128)S(1)} %all_to_all.11.far_ref, f32[5,8,8,128]{3,2,1,0:T(8,128)S(1)} %get-tuple-element.37.own_ref, f32[8,8,128]{2,1,0:T(8,128)S(1)} %get-tuple-element.38.w0_ref, ...), custom_call_target="tpu_custom_call" | custom-call | tf_op jit(solution)/shard_map/pallas_call | solution.py:588
  (8 shorter events, 0.1 us)
Async XLA Ops:
  0.6 0.7 copy-start.21
  1.3 0.9 copy-start
  2.2 0.8 copy-start.2
  3.1 1.0 copy-start.9
  4.0 0.9 copy-start.10
  4.9 0.9 copy-start.11
  5.9 0.9 copy-start.13
  6.8 0.9 copy-start.14
  7.7 0.9 copy-start.15
  8.5 0.9 copy-start.16
  9.4 0.8 copy-start.17
  10.3 0.8 copy-start.18
  11.0 0.8 copy-start.19
  11.8 0.7 copy-start.22
  17.0 5.3 %collective-permute-start = (f32[4,8,128]{2,1,0:T(8,128)S(1)}, f32[4,8,128]{2,1,0:T(8,128)S(1)}, u32[]{:S(2)}, u32[]{:S(2)}) collective-permute-start(f32[4,8,128]{2,1,0:T(8,128)S(1)} %get-tuple-element.22), channel_id=1, source_target_pairs={{0,511},{1,2},{2,1},{3,4},{4,3},{5,6},{6,5},{7,8},{8,7},{9,10},{10... | collective-permute-start | bytes 49160 | tf_op jit(solution)/shard_map/ppermute | solution.py:280
  22.3 3.7 %copy-start.1 = (f32[2,15,8,128]{3,2,1,0:T(8,128)S(1)}, f32[2,15,8,128]{3,2,1,0:T(8,128)}, u32[]{:S(2)}) copy-start(f32[2,15,8,128]{3,2,1,0:T(8,128)} %constant.33.clone.dq_in.dq_ref) | copy-start | bytes 368644
  22.3 3.7 %copy-start.3 = (f32[2,8,8,128]{3,2,1,0:T(8,128)S(1)}, f32[2,8,8,128]{3,2,1,0:T(8,128)}, u32[]{:S(2)}) copy-start(f32[2,8,8,128]{3,2,1,0:T(8,128)} %constant.32.clone.ds_in.ds_ref) | copy-start | bytes 196612
  22.3 23.0 %copy-start.8 = (f32[3,112,160]{2,1,0:T(8,128)S(1)}, f32[3,112,160]{2,1,0:T(8,128)}, u32[]{:S(2)}) copy-start(f32[3,112,160]{2,1,0:T(8,128)} %constant.46.clone.lam_ref) | copy-start | bytes 645124
  22.3 23.0 %copy-start.4 = (bf16[2,128,160]{2,1,0:T(8,128)(2,1)S(1)}, bf16[2,128,160]{2,1,0:T(8,128)(2,1)}, u32[]{:S(2)}) copy-start(bf16[2,128,160]{2,1,0:T(8,128)(2,1)} %constant.43.clone.sright_ref) | copy-start | bytes 245764
  22.3 23.0 %copy-start.5 = (bf16[2,240,112]{2,1,0:T(8,128)(2,1)S(1)}, bf16[2,240,112]{2,1,0:T(8,128)(2,1)}, u32[]{:S(2)}) copy-start(bf16[2,240,112]{2,1,0:T(8,128)(2,1)} %constant.42.clone.sback_ref) | copy-start | bytes 322564
  22.4 23.0 %copy-start.6 = (bf16[2,112,240]{2,1,0:T(8,128)(2,1)S(1)}, bf16[2,112,240]{2,1,0:T(8,128)(2,1)}, u32[]{:S(2)}) copy-start(bf16[2,112,240]{2,1,0:T(8,128)(2,1)} %constant.41.clone.sleft_ref) | copy-start | bytes 322564
  22.4 22.9 %copy-start.7 = (bf16[2,160,128]{2,1,0:T(8,128)(2,1)S(1)}, bf16[2,160,128]{2,1,0:T(8,128)(2,1)}, u32[]{:S(2)}) copy-start(bf16[2,160,128]{2,1,0:T(8,128)(2,1)} %constant.44.clone.srback_ref) | copy-start | bytes 245764
  22.4 22.9 %copy-start.12 = (f32[128,160]{1,0:T(8,128)S(1)}, f32[128,160]{1,0:T(8,128)}, u32[]{:S(2)}) copy-start(f32[128,160]{1,0:T(8,128)} %constant.45.clone.spread_ref) | copy-start | bytes 245764
  22.4 3.6 %collective-permute-start.1 = (f32[60,8,128]{2,1,0:T(8,128)S(1)}, f32[60,8,128]{2,1,0:T(8,128)S(1)}, u32[]{:S(2)}, u32[]{:S(2)}) collective-permute-start(f32[60,8,128]{2,1,0:T(8,128)S(1)} %shard_map.213.own_ref), channel_id=1, source_target_pairs={{0,1},{1,0},{2,3},{3,2},{4,5},{5,4},{6,7},{7,6},{8,9},{9,8},{10,11... | collective-permute-start | bytes 737288 | tf_op jit(solution)/shard_map/ppermute | solution.py:275
  26.5 5.3 %collective-permute-start.2 = (f32[10,8,128]{2,1,0:T(8,128)S(1)}, f32[10,8,128]{2,1,0:T(8,128)S(1)}, u32[]{:S(2)}, u32[]{:S(2)}) collective-permute-start(f32[10,8,128]{2,1,0:T(8,128)S(1)} %get-tuple-element.24), channel_id=1, source_target_pairs={{0,511},{1,2},{2,1},{3,4},{4,3},{5,6},{6,5},{7,8},{8,7},{9,10},{10... | collective-permute-start | bytes 122888 | tf_op jit(solution)/shard_map/ppermute | solution.py:280
  31.9 13.4 %collective-permute-start.3 = (f32[10,8,128]{2,1,0:T(8,128)S(1)}, f32[10,8,128]{2,1,0:T(8,128)S(1)}, u32[]{:S(2)}, u32[]{:S(2)}) collective-permute-start(f32[10,8,128]{2,1,0:T(8,128)S(1)} %collective-permute-done.2.own_in), channel_id=1, source_target_pairs={{0,1},{1,0},{2,3},{3,2},{4,5},{5,4},{6,7},{7,6},{8,9},{9,8},{10,11... | collective-permute-start | bytes 122888 | tf_op jit(solution)/shard_map/ppermute | solution.py:275
  47.6 5.3 %collective-permute-start.4 = (f32[9,8,128]{2,1,0:T(8,128)S(1)}, f32[9,8,128]{2,1,0:T(8,128)S(1)}, u32[]{:S(2)}, u32[]{:S(2)}) collective-permute-start(f32[9,8,128]{2,1,0:T(8,128)S(1)} %get-tuple-element.29), channel_id=1, source_target_pairs={{0,511},{1,2},{2,1},{3,4},{4,3},{5,6},{6,5},{7,8},{8,7},{9,10},{10... | collective-permute-start | bytes 110600 | tf_op jit(solution)/shard_map/ppermute | solution.py:280
  52.8 8.6 %collective-permute-start.5 = (f32[9,8,128]{2,1,0:T(8,128)S(1)}, f32[9,8,128]{2,1,0:T(8,128)S(1)}, u32[]{:S(2)}, u32[]{:S(2)}) collective-permute-start(f32[9,8,128]{2,1,0:T(8,128)S(1)} %collective-permute-done.4.own_in), channel_id=1, source_target_pairs={{0,1},{1,0},{2,3},{3,2},{4,5},{5,4},{6,7},{7,6},{8,9},{9,8},{10,11... | collective-permute-start | bytes 110600 | tf_op jit(solution)/shard_map/ppermute | solution.py:275
  63.5 13.9 %copy-start.20 = (f32[8,128]{1,0:T(8,128)S(1)}, f32[8,128]{1,0:T(8,128)}, u32[]{:S(2)}) copy-start(f32[8,128]{1,0:T(8,128)} %constant.47.clone.ws_ref) | copy-start | bytes 12292
  63.5 5.4 %collective-permute-start.6 = (f32[9,8,128]{2,1,0:T(8,128)S(1)}, f32[9,8,128]{2,1,0:T(8,128)S(1)}, u32[]{:S(2)}, u32[]{:S(2)}) collective-permute-start(f32[9,8,128]{2,1,0:T(8,128)S(1)} %get-tuple-element.33), channel_id=1, source_target_pairs={{0,511},{1,2},{2,1},{3,4},{4,3},{5,6},{6,5},{7,8},{8,7},{9,10},{10... | collective-permute-start | bytes 110600 | tf_op jit(solution)/shard_map/ppermute | solution.py:280
  68.9 8.5 %collective-permute-start.7 = (f32[9,8,128]{2,1,0:T(8,128)S(1)}, f32[9,8,128]{2,1,0:T(8,128)S(1)}, u32[]{:S(2)}, u32[]{:S(2)}) collective-permute-start(f32[9,8,128]{2,1,0:T(8,128)S(1)} %collective-permute-done.6.own_in), channel_id=1, source_target_pairs={{0,1},{1,0},{2,3},{3,2},{4,5},{5,4},{6,7},{7,6},{8,9},{9,8},{10,11... | collective-permute-start | bytes 110600 | tf_op jit(solution)/shard_map/ppermute | solution.py:275

commit v3 on v2

--- a/solution.py
+++ b/solution.py
@@ -126,7 +126,21 @@
     value = np.asarray(value, dtype=np.float32)
     high = value.astype(jnp.bfloat16)
     rest = (value - high.astype(np.float32)).astype(jnp.bfloat16)
-    return np.stack([high, rest])
+    return high, rest
+
+
+def for_left(value):
+    high, rest = halves(value)
+    return np.concatenate([high, rest, high], axis=1)
+
+
+def for_right(value):
+    high, rest = halves(value)
+    return np.concatenate([high, rest, high], axis=0)
+
+
+def pair(value):
+    return np.stack(halves(value))
 
 
 def make_tables():
@@ -154,11 +168,23 @@
     out["dq"] = np.stack([lane(deriv), lane(deriv.T)])
     out["w3"] = f32(np.einsum("a,s,q->asq", w, w, w).reshape(1, 512))
     out["wmass"] = f32(np.tile(np.einsum("a,s,q->asq", w, w, w), (1, 1, ES)))
-    out["jright"] = halves(np.kron(np.eye(ES), interp.T))
-    out["jright_t"] = halves(np.kron(np.eye(ES), interp))
-    out["jleft"] = halves(np.kron(interp, interp))
-    out["jleft_t"] = halves(np.kron(interp, interp).T)
-    out["wfine"] = f32(np.kron(np.kron(wf, wf)[:, None], np.tile(wf, ES)[None, :]))
+    both = interp @ deriv
+    pad = np.zeros((16 - NF, NP))
+    line = np.concatenate([interp, pad])
+    slope = np.concatenate([both, pad])
+    out["jright"] = for_right(np.kron(np.eye(ES), line.T))
+    out["jslope"] = for_right(np.kron(np.eye(ES), slope.T))
+    out["jright_t"] = pair(np.kron(np.eye(ES), line))
+    out["jleft"] = for_left(np.kron(interp, interp))
+    out["jleft_a"] = for_left(np.kron(both, interp))
+    out["jleft_s"] = for_left(np.kron(interp, both))
+    out["jleft_t"] = for_left(np.kron(interp, interp).T)
+    wide_wf = np.concatenate([wf, np.zeros(16 - NF)])
+    out["wfine"] = f32(np.kron(np.kron(wf, wf)[:, None], np.tile(wide_wf, ES)[None, :]))
+    at = np.arange(7 * LANES)
+    element, within = at // 56, at % 56
+    order = np.stack([element * NP + within % NP, within // NP]).reshape(2, 7, 1, LANES)
+    out["order"] = np.ascontiguousarray(np.broadcast_to(order, (2, 7, NP, LANES)), dtype=np.int32)
     wide = NP + 2
     left = np.zeros((MODES, 3, wide, NP))
     back = np.zeros((3, wide, NP, MODES))
@@ -175,10 +201,10 @@
                 back[1, a, NP - 1, row] = solve[a, i] * solve[1, j]
                 back[2, a, 1, row] = solve[a, i] * solve[wide - 1, j]
                 back[2, a, 0, row] = solve[a, i] * solve[wide - 2, j]
-    out["sleft"] = halves(left.reshape(MODES, 240))
-    out["sback"] = halves(back.reshape(240, MODES))
-    out["sright"] = halves(np.kron(np.eye(ES), solve[1:-1, :]))
-    out["srback"] = halves(np.kron(np.eye(ES), solve[1:-1, :].T))
+    out["sleft"] = for_left(left.reshape(MODES, 240))
+    out["sback"] = for_left(back.reshape(240, MODES))
+    out["sright"] = for_right(np.kron(np.eye(ES), solve[1:-1, :]))
+    out["srback"] = pair(np.kron(np.eye(ES), solve[1:-1, :].T))
     out["spread"] = f32(np.kron(np.eye(ES), np.ones((NP, wide))) / 8.0)
     lam_a = np.zeros((MODES, 1))
     lam_s = np.zeros((MODES, 1))
@@ -211,14 +237,19 @@
     return high, (x - high.astype(jnp.float32)).astype(jnp.bfloat16)
 
 
-def left_dot(table, x):
+def left_dot(table_ref, x):
     high, rest = split(x)
-    return short_dot(table[0], high) + (short_dot(table[1], high) + short_dot(table[0], rest))
-
-
-def right_dot(x, table):
+    return short_dot(table_ref[...], jnp.concatenate([high, high, rest], axis=0))
+
+
+def right_dot(x, table_ref):
     high, rest = split(x)
-    return short_dot(high, table[0]) + (short_dot(high, table[1]) + short_dot(rest, table[0]))
+    return short_dot(jnp.concatenate([high, high, rest], axis=1), table_ref[...])
+
+
+def pair_dot(x, table_ref):
+    high, rest = split(x)
+    return short_dot(high, table_ref[0]) + (short_dot(high, table_ref[1]) + short_dot(rest, table_ref[0]))
 
 
 def roll(x, shift, axis):
@@ -316,9 +347,9 @@
     return jnp.take_along_axis(flat, tiled, axis=1).reshape(x.shape)
 
 
-def forcing_kernel(slot_in, vel_in, past_in, metric_in, jac_in, w3_in, wmass_in, ds_in, dq_in, jright_in, jright_t_in, jleft_in, jleft_t_in, wfine_in, pack_ref, cross_ref, slot_ref, vel_ref, past_ref, metric_ref, jac_ref, w3_ref, wmass_ref, ds_ref, dq_ref, jright_ref, jright_t_ref, jleft_ref, jleft_t_ref, wfine_ref, sems):
-    sources = (slot_in, vel_in, past_in, metric_in, jac_in, w3_in, wmass_in, ds_in, dq_in, jright_in, jright_t_in, jleft_in, jleft_t_in, wfine_in)
-    targets = (slot_ref, vel_ref, past_ref, metric_ref, jac_ref, w3_ref, wmass_ref, ds_ref, dq_ref, jright_ref, jright_t_ref, jleft_ref, jleft_t_ref, wfine_ref)
+def forcing_kernel(slot_in, vel_in, past_in, metric_in, jac_in, w3_in, wmass_in, ds_in, dq_in, jright_in, jslope_in, jright_t_in, jleft_in, jleft_a_in, jleft_s_in, jleft_t_in, wfine_in, pack_ref, cross_ref, slot_ref, vel_ref, past_ref, metric_ref, jac_ref, w3_ref, wmass_ref, ds_ref, dq_ref, jright_ref, jslope_ref, jright_t_ref, jleft_ref, jleft_a_ref, jleft_s_ref, jleft_t_ref, wfine_ref, sems):
+    sources = (slot_in, vel_in, past_in, metric_in, jac_in, w3_in, wmass_in, ds_in, dq_in, jright_in, jslope_in, jright_t_in, jleft_in, jleft_a_in, jleft_s_in, jleft_t_in, wfine_in)
+    targets = (slot_ref, vel_ref, past_ref, metric_ref, jac_ref, w3_ref, wmass_ref, ds_ref, dq_ref, jright_ref, jslope_ref, jright_t_ref, jleft_ref, jleft_a_ref, jleft_s_ref, jleft_t_ref, wfine_ref)
     copies = [pltpu.make_async_copy(x, y, sems.at[k]) for k, (x, y) in enumerate(zip(sources, targets))]
     for copy in copies:
         copy.start()
@@ -332,17 +363,20 @@
     direct = (jac * w3_ref[...])[None] * (-10.0 * new + 16.0 * mid - 6.0 * old) + 3.0 * past_ref[0] - past_ref[1]
     lanes = to_lanes(jnp.concatenate([new, guess, direct, metric_ref[...], jac[None]], axis=0))
     new, guess, direct, metric, jac = lanes[0:3], lanes[3:6], lanes[6:9], lanes[9:12], lanes[12]
-    fields = [rows(jac)] + [rows(new[d] * metric[d]) for d in range(3)]
-    for i in range(3):
-        fields.extend(rows(part) for part in gradient(new[i], ds, dq))
-    wide = right_dot(jnp.concatenate(fields, axis=0), jright_ref)
-    fine = [left_dot(jleft_ref, wide[64 * k : 64 * k + 64]) for k in range(13)]
-    scale = fine[0] * wfine_ref[...]
+    moved = [rows(new[i]) for i in range(3)]
+    plain = moved + [rows(jac)] + [rows(new[d] * metric[d]) for d in range(3)]
+    wide = right_dot(jnp.concatenate(plain, axis=0), jright_ref)
+    slope = right_dot(jnp.concatenate(moved, axis=0), jslope_ref)
+    scale = left_dot(jleft_ref, wide[192:256]) * wfine_ref[...]
+    carry = [left_dot(jleft_ref, wide[256 + 64 * d : 320 + 64 * d]) for d in range(3)]
     products = []
     for i in range(3):
-        total = fine[1] * fine[4 + 3 * i] + fine[2] * fine[5 + 3 * i] + fine[3] * fine[6 + 3 * i]
-        products.append(left_dot(jleft_t_ref, scale * total))
-    coarse = right_dot(jnp.concatenate(products, axis=0), jright_t_ref)
+        part = wide[64 * i : 64 * i + 64]
+        total = carry[0] * left_dot(jleft_a_ref, part) + carry[1] * left_dot(jleft_s_ref, part)
+        total = total + carry[2] * left_dot(jleft_ref, slope[64 * i : 64 * i + 64])
+        products.append(scale * total)
+    coarse = left_dot(jleft_t_ref, jnp.concatenate(products, axis=1))
+    coarse = pair_dot(jnp.concatenate([coarse[:, 256 * i : 256 * i + 256] for i in range(3)], axis=0), jright_t_ref)
     mass = jac * wmass_ref[...]
     factor = [mass * metric[d] * metric[d] for d in range(3)]
     result = []
@@ -354,8 +388,8 @@
     lane = lax.broadcasted_iota(jnp.int32, (NP, LANES), 1)
     index = jnp.zeros((NP, LANES), jnp.int32)
     for e in range(ES):
-        index = jnp.where(lane // NP == slot_ref[e], e * NP, index)
-    index = index + lane % NP
+        index = jnp.where((lane >> 3) == slot_ref[e], e * NP, index)
+    index = index + (lane & 7)
     result = [take_lanes(x, index) for x in result]
     for k in range(4):
         joined = join_s(result[k])
@@ -446,7 +480,7 @@
         columns.append(jnp.concatenate([x[at : at + NP + 2].reshape(80, LANES) for x in (wide, before, after)], axis=0))
     spectra = left_dot(sleft_ref, jnp.concatenate(columns, axis=1))
     spectra = jnp.concatenate([spectra[:, LANES * k : LANES * k + LANES] for k in range(4)], axis=0)
-    spectra = right_dot(right_dot(spectra, sright_ref) * inv_ref[...], srback_ref)
+    spectra = pair_dot(right_dot(spectra, sright_ref) * inv_ref[...], srback_ref)
     spectra = jnp.concatenate([spectra[MODES * k : MODES * k + MODES] for k in range(4)], axis=1)
     blocks = left_dot(sback_ref, spectra)
     z = []
@@ -524,31 +558,28 @@
     line = jnp.zeros((NP, LANES), jnp.float32)
     for k, (left, right) in enumerate(pairs):
         line = jnp.where(lane == k, jnp.sum(jnp.sum(left * right, axis=0) * ws), line)
-    face = jnp.where(even, l2[0], l2[-1])
+    put_sums(sums_ref, jnp.where(even, l2[0], l2[-1]), line)
+
+
+def put_sums(sums_ref, face, line):
+    sub = lax.broadcasted_iota(jnp.int32, (NP, LANES), 0)
+    value = jnp.where(sub == NP - 1, line, face)
     for k in range(sums_ref.shape[0]):
-        sums_ref[k, 0] = face
-        sums_ref[k, 1] = line
+        sums_ref[k] = value
 
 
 def relay_kernel(near_ref, out_ref):
-    total = jnp.sum(near_ref[:, 1], axis=0)
-    device = lax.axis_index("dom")
     count = near_ref.shape[0]
-    chip = lax.rem(device // 2, count)
-    face = near_ref[chip, 0]
-    for k in range(out_ref.shape[0]):
-        out_ref[k, 0] = face
-        out_ref[k, 1] = total
-
-
-def to_output(x):
-    by_s = [jnp.concatenate([x[a][s : s + 1] for a in range(NP)], axis=0) for s in range(NP - 1)]
+    chip = lax.rem(lax.axis_index("dom") // 2, count)
+    put_sums(out_ref, near_ref[chip], jnp.sum(near_ref[...], axis=0))
+
+
+def to_output(x, order_ref, scratch_ref):
+    scratch_ref[...] = rows(x)
+    by_s = [scratch_ref[pl.ds(s, NP, stride=NP), :] for s in range(NP - 1)]
     tiles = []
     for tile in range(7):
-        at = lax.broadcasted_iota(jnp.int32, (NP, LANES), 1) + tile * LANES
-        element = at // 56
-        s = (at - element * 56) // NP
-        index = element * NP + at % NP
+        index, s = order_ref[0, tile], order_ref[1, tile]
         value = jnp.take_along_axis(by_s[0], index, axis=1)
         for k in range(1, NP - 1):
             value = jnp.where(s == k, jnp.take_along_axis(by_s[k], index, axis=1), value)
@@ -556,7 +587,7 @@
     return jnp.concatenate(tiles, axis=1)
 
 
-def combine_kernel(near_ref, far_ref, own_ref, w0_ref, w1_ref, p_ref, r_ref):
+def combine_kernel(near_ref, far_ref, own_ref, w0_ref, w1_ref, order_ref, p_ref, r_ref, first_ref, second_ref):
     device = lax.axis_index("dom")
     even = lax.rem(device, 2) == 0
     near, far = near_ref.shape[0], far_ref.shape[0]
@@ -564,12 +595,12 @@
     chip = device // 2
     partner = lax.rem(jnp.where(even, chip + chips - 1, chip + 1), chips)
     inside = partner // near == chip // near
-    face = jnp.where(inside, near_ref[lax.rem(partner, near), 0], far_ref[partner // near, 0])
+    face = jnp.where(inside, near_ref[lax.rem(partner, near)], far_ref[partner // near])
     local = own_ref[3]
     first = jnp.where(even, local[0] + face, local[0])
     last = jnp.where(even, local[-1], local[-1] + face)
     w2 = jnp.concatenate([first[None], local[1:-1], last[None]], axis=0)
-    line = jnp.sum(far_ref[:, 1], axis=0)[:1]
+    line = jnp.sum(far_ref[...], axis=0)[NP - 1 :]
     h00, h01, h02, h11, h12, h22, g0, g1, g2 = [line[:, k : k + 1] for k in range(9)]
     m1, m2 = h01 / h00, h02 / h00
     k11, k12, k22 = h11 - m1 * h01, h12 - m1 * h02, h22 - m2 * h02
@@ -580,16 +611,17 @@
     c0 = (g0 - h01 * c1 - h02 * c2) / h00
     pressure = (c0 + STEPS[0])[None] * own_ref[0] + (c1 + STEPS[1])[None] * own_ref[1] + c2[None] * own_ref[2]
     residual = own_ref[4] - (c0[None] * w0_ref[...] + c1[None] * w1_ref[...] + c2[None] * w2)
-    p_ref[...] = to_output(pressure)
-    r_ref[...] = to_output(residual)
-
-
-def call(kernel, shapes, *args):
+    p_ref[...] = to_output(pressure, order_ref, first_ref)
+    r_ref[...] = to_output(residual, order_ref, second_ref)
+
+
+def call(kernel, shapes, *args, scratch=()):
     return pl.pallas_call(
         kernel,
         out_shape=[jax.ShapeDtypeStruct(shape, jnp.float32) for shape in shapes],
         in_specs=[pl.BlockSpec(memory_space=pltpu.VMEM)] * len(args),
         out_specs=[pl.BlockSpec(memory_space=pltpu.VMEM)] * len(shapes),
+        scratch_shapes=scratch,
         compiler_params=PARAMS,
     )(*args)
 
@@ -602,11 +634,14 @@
     return pl.pallas_call(
         forcing_kernel,
         out_shape=[jax.ShapeDtypeStruct(shape, jnp.float32) for shape in shapes],
-        in_specs=[pl.BlockSpec(memory_space=pl.ANY)] * len(args),
+        in_specs=[pl.BlockSpec(memory_space=pltpu.HBM)] * len(args),
         out_specs=[pl.BlockSpec(memory_space=pltpu.VMEM)] * len(shapes),
         scratch_shapes=scratch,
         compiler_params=PARAMS,
     )(*args)
+
+
+FORCING_TABLES = ("w3", "wmass", "ds", "dq", "jright", "jslope", "jright_t", "jleft", "jleft_a", "jleft_s", "jleft_t", "wfine")
 
 
 def groups_of(count):
@@ -617,7 +652,9 @@
     for team in range(2):
         member = [2 * c + (team + c) % 2 for c in range(chips)]
         first.extend([member[near * i + j] for j in range(near)] for i in range(far))
-        second.extend([member[near * i + (j if i % 2 == 0 else near - 1 - j)] for i in range(far)] for j in range(near))
+        for j in range(near):
+            turned = near - 1 - j if j in (0, near - 1) else j
+            second.append([member[near * i + (turned if i % 2 else j)] for i in range(far)])
     return near, far, first, second
 
 
@@ -635,7 +672,7 @@
 
     pack, cross = call_forcing(
         element_slot, velocity, conv_past, metric, jacobian,
-        t["w3"], t["wmass"], t["ds"], t["dq"], t["jright"], t["jright_t"], t["jleft"], t["jleft_t"], t["wfine"],
+        *(t[key] for key in FORCING_TABLES),
     )
     (own,) = call(pair_kernel, [(7 * NP + 4, NP, LANES)], pack, swap_cross(cross, count))
     mate = swap_inner(own, count)
@@ -658,14 +695,19 @@
     near, far, first, second = groups_of(count)
     image1, own, sums = call(
         functools.partial(last_kernel, STEPS[1]),
-        [field, (5,) + field, (near, 2, NP, LANES)],
+        [field, (5,) + field, (near, NP, LANES)],
         wide, local1, *exchange(cross), inv, *tables, t["ws"], v0, v1, local0,
     )
     near_sums = lax.all_to_all(sums, "dom", 0, 0, tiled=True, axis_index_groups=first)
-    (sums,) = call(relay_kernel, [(far, 2, NP, LANES)], near_sums)
+    (sums,) = call(relay_kernel, [(far, NP, LANES)], near_sums)
     far_sums = lax.all_to_all(sums, "dom", 0, 0, tiled=True, axis_index_groups=second)
     return tuple(
-        call(combine_kernel, [(NP, 896), (NP, 896)], near_sums, far_sums, own, image0, image1)
+        call(
+            combine_kernel,
+            [(NP, 896), (NP, 896)],
+            near_sums, far_sums, own, image0, image1, t["order"],
+            scratch=[pltpu.VMEM((NP * NP, LANES), jnp.float32)] * 2,
+        )
     )
 
 

time: 123 us -> 123 us (level)
  the two profiles are of different devices: /device:TPU:9 before, /device:TPU:1 now
where the time goes in v3:
time: 123 us; the launch traced here: 121 us
  starting transfers between devices  48 us (39%)
  blocking collectives  30.3 us (25%)
  waiting for transfers between devices  15.1 us (12%)
  local copies, waits for them, and re-layouts  14.6 us (12%)
  Pallas kernels  12.7 us (10%)
    ppermute x4, starting transfers between devices, swap_inner(): return lax.ppermute(x, 'dom', [(i, i ^ 1) for i in range(count)])  37.5 us
    all_to_all x1, blocking collectives, shards(): lax.all_to_all(sums, 'dom', 0, 0, tiled=True, axis_index_groups=second)  20.3 us
    unnamed x54, local copies, waits for them, and re-layouts  14.6 us
    ppermute x4, waiting for transfers between devices, swap_cross(): return lax.ppermute(x, 'dom', pairs)  11.5 us
    ppermute x4, starting transfers between devices, swap_cross(): return lax.ppermute(x, 'dom', pairs)  10.5 us
    all_to_all x1, blocking collectives, shards(): lax.all_to_all(sums, 'dom', 0, 0, tiled=True, axis_index_groups=first)  9.95 us
    pallas_call x7, Pallas kernels, call(): pl.pallas_call(kernel, out_shape=[jax.ShapeDtypeStruct(shape, jnp.float32...  8.22 us
    pallas_call x1, Pallas kernels, call_forcing(): pl.pallas_call(forcing_kernel, out_shape=[jax.ShapeDtypeStruct(shape, jnp...  4.45 us
  transfers between devices with their start and end apart: 8, of which 8 were waited for; matrix products, arithmetic and copies ran while one was open for 0% of the time, Pallas kernels for 0%

profile of v3, /device:TPU:1, one launch (start us, length us, event | category | flops | bytes accessed | tf_op | source)
XLA Modules:
  0.0 121.5 jit_solution(8625774569760151291)
XLA Ops:
  0.6 0.0 copy-start.25
  0.6 0.7 copy-done.25
  1.3 0.0 copy-start
  1.3 0.9 copy-done
  2.2 0.0 copy-start.4
  2.2 0.8 copy-done.4
  3.1 0.0 copy-start.9
  3.1 1.0 copy-done.9
  4.0 0.0 copy-start.10
  4.0 0.9 copy-done.10
  4.9 0.0 copy-start.11
  5.0 0.9 copy-done.11
  5.9 0.0 copy-start.12
  5.9 0.9 copy-done.12
  6.8 0.0 copy-start.13
  6.8 0.9 copy-done.13
  7.7 0.9 copy-done.14
  8.6 0.9 copy-done.16
  9.5 0.9 copy-done.17
  10.4 0.9 copy-done.18
  11.3 0.9 copy-done.19
  12.2 0.8 copy-done.20
  13.0 0.8 copy-done.22
  13.8 0.8 copy-done.23
  14.5 0.7 copy-done.26
  15.2 4.4 %shard_map.248 = (f32[56,8,128]{2,1,0:T(8,128)S(1)}, f32[4,8,128]{2,1,0:T(8,128)S(1)}) custom-call(s32[16]{0:T(128)S(1)} %copy-done.26, f32[3,3,16,512]{3,2,1,0:T(8,128)S(1)} %copy-done.9, f32[2,3,16,512]{3,2,1,0:T(8,128)S(1)} %copy-done.10, f32[3,16,512]{2,1,0:T(8,128)S(1)} %copy-done.16, f32[16,512]{1,0:T(8,128)S(1)} %copy-done.22, ...), custom_call_target="tpu_custom_call" | custom-call | tf_op jit(solution)/shard_map/pallas_call | solution.py:634
  19.6 4.6 %collective-permute-start = (f32[4,8,128]{2,1,0:T(8,128)S(1)}, f32[4,8,128]{2,1,0:T(8,128)S(1)}, u32[]{:S(2)}, u32[]{:S(2)}) collective-permute-start(f32[4,8,128]{2,1,0:T(8,128)S(1)} %get-tuple-element.22), channel_id=1, source_target_pairs={{0,511},{1,2},{2,1},{3,4},{4,3},{5,6},{6,5},{7,8},{8,7},{9,10},{10... | collective-permute-start | bytes 49160 | tf_op jit(solution)/shard_map/ppermute | solution.py:311
  24.2 1.4 %collective-permute-done.cross_in = f32[4,8,128]{2,1,0:T(8,128)S(1)} collective-permute-done((f32[4,8,128]{2,1,0:T(8,128)S(1)}, f32[4,8,128]{2,1,0:T(8,128)S(1)}, u32[]{:S(2)}, u32[]{:S(2)}) %collective-permute-start) | collective-permute-done | bytes 16416 | tf_op jit(solution)/shard_map/ppermute | solution.py:311
  25.7 0.0 copy-start.2
  25.7 0.0 copy-start.3
  25.7 0.0 copy-start.6
  25.7 0.0 copy-start.7
  25.7 14.5 %collective-permute-start.1 = (f32[60,8,128]{2,1,0:T(8,128)S(1)}, f32[60,8,128]{2,1,0:T(8,128)S(1)}, u32[]{:S(2)}, u32[]{:S(2)}) collective-permute-start(f32[60,8,128]{2,1,0:T(8,128)S(1)} %shard_map.249.own_ref), channel_id=1, source_target_pairs={{0,1},{1,0},{2,3},{3,2},{4,5},{5,4},{6,7},{7,6},{8,9},{9,8},{10,11... | collective-permute-start | bytes 737288 | tf_op jit(solution)/shard_map/ppermute | solution.py:306
  40.2 1.1 collective-permute-done.1.mate_ref
  41.3 0.0 copy-done.1
  41.3 0.0 copy-done.5
  41.3 0.6 shard_map.250
  41.9 1.9 %collective-permute-start.2 = (f32[10,8,128]{2,1,0:T(8,128)S(1)}, f32[10,8,128]{2,1,0:T(8,128)S(1)}, u32[]{:S(2)}, u32[]{:S(2)}) collective-permute-start(f32[10,8,128]{2,1,0:T(8,128)S(1)} %get-tuple-element.24), channel_id=1, source_target_pairs={{0,511},{1,2},{2,1},{3,4},{4,3},{5,6},{6,5},{7,8},{8,7},{9,10},{10... | collective-permute-start | bytes 122888 | tf_op jit(solution)/shard_map/ppermute | solution.py:311
  43.8 3.4 %collective-permute-done.2.own_in = f32[10,8,128]{2,1,0:T(8,128)S(1)} collective-permute-done((f32[10,8,128]{2,1,0:T(8,128)S(1)}, f32[10,8,128]{2,1,0:T(8,128)S(1)}, u32[]{:S(2)}, u32[]{:S(2)}) %collective-permute-start.2) | collective-permute-done | bytes 40992 | tf_op jit(solution)/shard_map/ppermute | solution.py:311
  47.2 7.7 %collective-permute-start.3 = (f32[10,8,128]{2,1,0:T(8,128)S(1)}, f32[10,8,128]{2,1,0:T(8,128)S(1)}, u32[]{:S(2)}, u32[]{:S(2)}) collective-permute-start(f32[10,8,128]{2,1,0:T(8,128)S(1)} %collective-permute-done.2.own_in), channel_id=1, source_target_pairs={{0,1},{1,0},{2,3},{3,2},{4,5},{5,4},{6,7},{7,6},{8,9},{9,8},{10,11... | collective-permute-start | bytes 122888 | tf_op jit(solution)/shard_map/ppermute | solution.py:306
  54.9 0.8 collective-permute-done.3.mate_in
  55.8 0.0 copy-done.15
  55.8 0.0 copy-done.8
  55.8 0.0 copy-done.2
  55.8 0.0 copy-done.3
  55.8 0.0 copy-done.6
  55.8 0.0 copy-done.7
  55.8 2.1 %shard_map.251 = (f32[31,8,128]{2,1,0:T(8,128)S(1)}, f32[448,160]{1,0:T(8,128)S(1)}, f32[15,8,128]{2,1,0:T(8,128)S(1)}, f32[15,8,128]{2,1,0:T(8,128)S(1)}, f32[9,8,128]{2,1,0:T(8,128)S(1)}) custom-call(f32[15,8,128]{2,1,0:T(8,128)S(1)} %get-tuple-element.23.div_ref, f32[10,8,128]{2,1,0:T(8,128)S(1)} %collective-permute-done.2.own_in, ...), custom_call_target="tpu_custom_call" | custom-call | tf_op jit(solution)/shard_map/pallas_call | solution.py:619
  57.9 1.9 %collective-permute-start.4 = (f32[9,8,128]{2,1,0:T(8,128)S(1)}, f32[9,8,128]{2,1,0:T(8,128)S(1)}, u32[]{:S(2)}, u32[]{:S(2)}) collective-permute-start(f32[9,8,128]{2,1,0:T(8,128)S(1)} %get-tuple-element.29), channel_id=1, source_target_pairs={{0,511},{1,2},{2,1},{3,4},{4,3},{5,6},{6,5},{7,8},{8,7},{9,10},{10... | collective-permute-start | bytes 110600 | tf_op jit(solution)/shard_map/ppermute | solution.py:311
  59.8 3.3 %collective-permute-done.4.own_in = f32[9,8,128]{2,1,0:T(8,128)S(1)} collective-permute-done((f32[9,8,128]{2,1,0:T(8,128)S(1)}, f32[9,8,128]{2,1,0:T(8,128)S(1)}, u32[]{:S(2)}, u32[]{:S(2)}) %collective-permute-start.4) | collective-permute-done | bytes 36896 | tf_op jit(solution)/shard_map/ppermute | solution.py:311
  63.1 7.7 %collective-permute-start.5 = (f32[9,8,128]{2,1,0:T(8,128)S(1)}, f32[9,8,128]{2,1,0:T(8,128)S(1)}, u32[]{:S(2)}, u32[]{:S(2)}) collective-permute-start(f32[9,8,128]{2,1,0:T(8,128)S(1)} %collective-permute-done.4.own_in), channel_id=1, source_target_pairs={{0,1},{1,0},{2,3},{3,2},{4,5},{5,4},{6,7},{7,6},{8,9},{9,8},{10,11... | collective-permute-start | bytes 110600 | tf_op jit(solution)/shard_map/ppermute | solution.py:306
  70.8 0.8 collective-permute-done.5.mate_in
  71.7 1.9 %shard_map.252 = (f32[8,8,128]{2,1,0:T(8,128)S(1)}, f32[31,8,128]{2,1,0:T(8,128)S(1)}, f32[15,8,128]{2,1,0:T(8,128)S(1)}, f32[15,8,128]{2,1,0:T(8,128)S(1)}, f32[9,8,128]{2,1,0:T(8,128)S(1)}) custom-call(f32[31,8,128]{2,1,0:T(8,128)S(1)} %get-tuple-element.27.before_ref, f32[15,8,128]{2,1,0:T(8,128)S(1)} %get-tuple-element.28.image_ref.l0_ref, ...), custom_call_target="tpu_custom_call" | custom-call | tf_op jit(solution)/shard_map/pallas_call | solution.py:619
  73.6 2.0 %collective-permute-start.6 = (f32[9,8,128]{2,1,0:T(8,128)S(1)}, f32[9,8,128]{2,1,0:T(8,128)S(1)}, u32[]{:S(2)}, u32[]{:S(2)}) collective-permute-start(f32[9,8,128]{2,1,0:T(8,128)S(1)} %get-tuple-element.33), channel_id=1, source_target_pairs={{0,511},{1,2},{2,1},{3,4},{4,3},{5,6},{6,5},{7,8},{8,7},{9,10},{10... | collective-permute-start | bytes 110600 | tf_op jit(solution)/shard_map/ppermute | solution.py:311
  75.6 3.3 %collective-permute-done.6.own_in = f32[9,8,128]{2,1,0:T(8,128)S(1)} collective-permute-done((f32[9,8,128]{2,1,0:T(8,128)S(1)}, f32[9,8,128]{2,1,0:T(8,128)S(1)}, u32[]{:S(2)}, u32[]{:S(2)}) %collective-permute-start.6) | collective-permute-done | bytes 36896 | tf_op jit(solution)/shard_map/ppermute | solution.py:311
  79.0 7.7 %collective-permute-start.7 = (f32[9,8,128]{2,1,0:T(8,128)S(1)}, f32[9,8,128]{2,1,0:T(8,128)S(1)}, u32[]{:S(2)}, u32[]{:S(2)}) collective-permute-start(f32[9,8,128]{2,1,0:T(8,128)S(1)} %collective-permute-done.6.own_in), channel_id=1, source_target_pairs={{0,1},{1,0},{2,3},{3,2},{4,5},{5,4},{6,7},{7,6},{8,9},{9,8},{10,11... | collective-permute-start | bytes 110600 | tf_op jit(solution)/shard_map/ppermute | solution.py:306
  86.7 0.8 collective-permute-done.7.mate_in
  87.5 0.0 copy-done.24
  87.5 2.0 %shard_map.253 = (f32[8,8,128]{2,1,0:T(8,128)S(1)}, f32[5,8,8,128]{3,2,1,0:T(8,128)S(1)}, f32[16,8,128]{2,1,0:T(8,128)S(1)}) custom-call(f32[31,8,128]{2,1,0:T(8,128)S(1)} %get-tuple-element.31.before_ref, f32[15,8,128]{2,1,0:T(8,128)S(1)} %get-tuple-element.32.image_ref, f32[9,8,128]{2,1,0:T(8,128)S(1)} %collective-permute-done.6.own_in, ...), custom_call_target="tpu_custom_call" | custom-call | tf_op jit(solution)/shard_map/pallas_call | solution.py:619
  89.5 10.0 %all_to_all.10.near_ref = f32[16,8,128]{2,1,0:T(8,128)S(1)} all-to-all(f32[16,8,128]{2,1,0:T(8,128)S(1)} %get-tuple-element.36), channel_id=1, replica_groups={{0,3,4,7,8,11,12,15,16,19,20,23,24,27,28,31},{32,35,36,39,40,43,44,47,4..., dimensions={0} | all-to-all | bytes 131072 | tf_op jit(solution)/shard_map/all_to_all | solution.py:701
  99.5 0.0 copy-start.21
  99.5 20.3 %all_to_all.11.far_ref = f32[16,8,128]{2,1,0:T(8,128)S(1)} all-to-all(f32[16,8,128]{2,1,0:T(8,128)S(1)} %shard_map.254), channel_id=1, replica_groups={{0,63,64,127,128,191,192,255,256,319,320,383,384,447,448,511},{3,35,67,..., dimensions={0} | all-to-all | bytes 131072 | tf_op jit(solution)/shard_map/all_to_all | solution.py:703
  119.9 0.0 copy-done.21
  119.9 1.6 %shard_map.255 = (f32[8,896]{1,0:T(8,128)}, f32[8,896]{1,0:T(8,128)}) custom-call(f32[16,8,128]{2,1,0:T(8,128)S(1)} %all_to_all.10.near_ref, f32[16,8,128]{2,1,0:T(8,128)S(1)} %all_to_all.11.far_ref, f32[5,8,8,128]{3,2,1,0:T(8,128)S(1)} %get-tuple-element.37.own_ref, f32[8,8,128]{2,1,0:T(8,128)S(1)} %get-tuple-element.38.w0_ref, ...), custom_call_target="tpu_custom_call" | custom-call | tf_op jit(solution)/shard_map/pallas_call | solution.py:619
  (16 shorter events, 0.1 us)
Async XLA Ops:
  0.6 0.7 copy-start.25
  1.3 0.9 copy-start
  2.2 0.8 copy-start.4
  3.1 1.0 copy-start.9
  4.0 0.9 copy-start.10
  4.9 0.9 copy-start.11
  5.9 0.9 copy-start.12
  6.8 0.9 copy-start.13
  7.7 0.9 copy-start.14
  8.6 0.9 copy-start.16
  9.5 0.9 copy-start.17
  10.4 0.9 copy-start.18
  11.3 0.9 copy-start.19
  12.2 0.8 copy-start.20
  13.0 0.8 copy-start.22
  13.8 0.8 copy-start.23
  14.5 0.7 copy-start.26
  15.2 40.6 %copy-start.15 = (f32[128,160]{1,0:T(8,128)S(1)}, f32[128,160]{1,0:T(8,128)}, u32[]{:S(2)}) copy-start(f32[128,160]{1,0:T(8,128)} %constant.57.clone.spread_ref) | copy-start | bytes 245764
  19.6 6.0 %collective-permute-start = (f32[4,8,128]{2,1,0:T(8,128)S(1)}, f32[4,8,128]{2,1,0:T(8,128)S(1)}, u32[]{:S(2)}, u32[]{:S(2)}) collective-permute-start(f32[4,8,128]{2,1,0:T(8,128)S(1)} %get-tuple-element.22), channel_id=1, source_target_pairs={{0,511},{1,2},{2,1},{3,4},{4,3},{5,6},{6,5},{7,8},{8,7},{9,10},{10... | collective-permute-start | bytes 49160 | tf_op jit(solution)/shard_map/ppermute | solution.py:311
  25.6 15.7 %copy-start.1 = (f32[2,15,8,128]{3,2,1,0:T(8,128)S(1)}, f32[2,15,8,128]{3,2,1,0:T(8,128)}, u32[]{:S(2)}) copy-start(f32[2,15,8,128]{3,2,1,0:T(8,128)} %constant.41.clone.dq_in.dq_ref) | copy-start | bytes 368644
  25.7 15.7 %copy-start.5 = (f32[2,8,8,128]{3,2,1,0:T(8,128)S(1)}, f32[2,8,8,128]{3,2,1,0:T(8,128)}, u32[]{:S(2)}) copy-start(f32[2,8,8,128]{3,2,1,0:T(8,128)} %constant.40.clone.ds_in.ds_ref) | copy-start | bytes 196612
  25.7 30.1 %copy-start.8 = (f32[3,112,160]{2,1,0:T(8,128)S(1)}, f32[3,112,160]{2,1,0:T(8,128)}, u32[]{:S(2)}) copy-start(f32[3,112,160]{2,1,0:T(8,128)} %constant.58.clone.lam_ref) | copy-start | bytes 645124
  25.7 30.1 %copy-start.2 = (bf16[384,160]{1,0:T(8,128)(2,1)S(1)}, bf16[384,160]{1,0:T(8,128)(2,1)}, u32[]{:S(2)}) copy-start(bf16[384,160]{1,0:T(8,128)(2,1)} %constant.55.clone.sright_ref) | copy-start | bytes 368644
  25.7 30.1 %copy-start.3 = (bf16[240,336]{1,0:T(8,128)(2,1)S(1)}, bf16[240,336]{1,0:T(8,128)(2,1)}, u32[]{:S(2)}) copy-start(bf16[240,336]{1,0:T(8,128)(2,1)} %constant.54.clone.sback_ref) | copy-start | bytes 483844
  25.7 30.1 %copy-start.6 = (bf16[112,720]{1,0:T(8,128)(2,1)S(1)}, bf16[112,720]{1,0:T(8,128)(2,1)}, u32[]{:S(2)}) copy-start(bf16[112,720]{1,0:T(8,128)(2,1)} %constant.53.clone.sleft_ref) | copy-start | bytes 483844
  25.7 30.1 %copy-start.7 = (bf16[2,160,128]{2,1,0:T(8,128)(2,1)S(1)}, bf16[2,160,128]{2,1,0:T(8,128)(2,1)}, u32[]{:S(2)}) copy-start(bf16[2,160,128]{2,1,0:T(8,128)(2,1)} %constant.56.clone.srback_ref) | copy-start | bytes 245764
  25.7 15.6 %collective-permute-start.1 = (f32[60,8,128]{2,1,0:T(8,128)S(1)}, f32[60,8,128]{2,1,0:T(8,128)S(1)}, u32[]{:S(2)}, u32[]{:S(2)}) collective-permute-start(f32[60,8,128]{2,1,0:T(8,128)S(1)} %shard_map.249.own_ref), channel_id=1, source_target_pairs={{0,1},{1,0},{2,3},{3,2},{4,5},{5,4},{6,7},{7,6},{8,9},{9,8},{10,11... | collective-permute-start | bytes 737288 | tf_op jit(solution)/shard_map/ppermute | solution.py:306
  41.9 5.3 %collective-permute-start.2 = (f32[10,8,128]{2,1,0:T(8,128)S(1)}, f32[10,8,128]{2,1,0:T(8,128)S(1)}, u32[]{:S(2)}, u32[]{:S(2)}) collective-permute-start(f32[10,8,128]{2,1,0:T(8,128)S(1)} %get-tuple-element.24), channel_id=1, source_target_pairs={{0,511},{1,2},{2,1},{3,4},{4,3},{5,6},{6,5},{7,8},{8,7},{9,10},{10... | collective-permute-start | bytes 122888 | tf_op jit(solution)/shard_map/ppermute | solution.py:311
  47.2 8.6 %collective-permute-start.3 = (f32[10,8,128]{2,1,0:T(8,128)S(1)}, f32[10,8,128]{2,1,0:T(8,128)S(1)}, u32[]{:S(2)}, u32[]{:S(2)}) collective-permute-start(f32[10,8,128]{2,1,0:T(8,128)S(1)} %collective-permute-done.2.own_in), channel_id=1, source_target_pairs={{0,1},{1,0},{2,3},{3,2},{4,5},{5,4},{6,7},{7,6},{8,9},{9,8},{10,11... | collective-permute-start | bytes 122888 | tf_op jit(solution)/shard_map/ppermute | solution.py:306
  57.9 5.3 %collective-permute-start.4 = (f32[9,8,128]{2,1,0:T(8,128)S(1)}, f32[9,8,128]{2,1,0:T(8,128)S(1)}, u32[]{:S(2)}, u32[]{:S(2)}) collective-permute-start(f32[9,8,128]{2,1,0:T(8,128)S(1)} %get-tuple-element.29), channel_id=1, source_target_pairs={{0,511},{1,2},{2,1},{3,4},{4,3},{5,6},{6,5},{7,8},{8,7},{9,10},{10... | collective-permute-start | bytes 110600 | tf_op jit(solution)/shard_map/ppermute | solution.py:311
  63.1 8.5 %collective-permute-start.5 = (f32[9,8,128]{2,1,0:T(8,128)S(1)}, f32[9,8,128]{2,1,0:T(8,128)S(1)}, u32[]{:S(2)}, u32[]{:S(2)}) collective-permute-start(f32[9,8,128]{2,1,0:T(8,128)S(1)} %collective-permute-done.4.own_in), channel_id=1, source_target_pairs={{0,1},{1,0},{2,3},{3,2},{4,5},{5,4},{6,7},{7,6},{8,9},{9,8},{10,11... | collective-permute-start | bytes 110600 | tf_op jit(solution)/shard_map/ppermute | solution.py:306
  73.6 13.9 %copy-start.24 = (f32[8,128]{1,0:T(8,128)S(1)}, f32[8,128]{1,0:T(8,128)}, u32[]{:S(2)}) copy-start(f32[8,128]{1,0:T(8,128)} %constant.59.clone.ws_ref) | copy-start | bytes 12292
  73.6 5.4 %collective-permute-start.6 = (f32[9,8,128]{2,1,0:T(8,128)S(1)}, f32[9,8,128]{2,1,0:T(8,128)S(1)}, u32[]{:S(2)}, u32[]{:S(2)}) collective-permute-start(f32[9,8,128]{2,1,0:T(8,128)S(1)} %get-tuple-element.33), channel_id=1, source_target_pairs={{0,511},{1,2},{2,1},{3,4},{4,3},{5,6},{6,5},{7,8},{8,7},{9,10},{10... | collective-permute-start | bytes 110600 | tf_op jit(solution)/shard_map/ppermute | solution.py:311
  79.0 8.5 %collective-permute-start.7 = (f32[9,8,128]{2,1,0:T(8,128)S(1)}, f32[9,8,128]{2,1,0:T(8,128)S(1)}, u32[]{:S(2)}, u32[]{:S(2)}) collective-permute-start(f32[9,8,128]{2,1,0:T(8,128)S(1)} %collective-permute-done.6.own_in), channel_id=1, source_target_pairs={{0,1},{1,0},{2,3},{3,2},{4,5},{5,4},{6,7},{7,6},{8,9},{9,8},{10,11... | collective-permute-start | bytes 110600 | tf_op jit(solution)/shard_map/ppermute | solution.py:306
  99.5 20.4 %copy-start.21 = (s32[2,7,8,128]{3,2,1,0:T(8,128)S(1)}, s32[2,7,8,128]{3,2,1,0:T(8,128)}, u32[]{:S(2)}) copy-start(s32[2,7,8,128]{3,2,1,0:T(8,128)} %constant.52.clone.order_ref) | copy-start | bytes 172036

commit v4 on v3

--- a/solution.py
+++ b/solution.py
@@ -17,8 +17,8 @@
 mass_shift = 0.001
 STEPS = (0.45, 0.3)
 VMEM = 48 * 1024 * 1024
+FORCING_VMEM = 56 * 1024 * 1024
 ROWS = 2 * NP - 1
-WINDOW = 4 * (NP - 1) + 3
 EDGE = NP + 1
 MODES = 112
 
@@ -166,6 +166,8 @@
 
     out["ds"] = np.stack([sublane(deriv), sublane(deriv.T)])
     out["dq"] = np.stack([lane(deriv), lane(deriv.T)])
+    out["qright"] = for_right(np.kron(np.eye(ES), deriv.T))
+    out["qright_t"] = for_right(np.kron(np.eye(ES), deriv))
     out["w3"] = f32(np.einsum("a,s,q->asq", w, w, w).reshape(1, 512))
     out["wmass"] = f32(np.tile(np.einsum("a,s,q->asq", w, w, w), (1, 1, ES)))
     both = interp @ deriv
@@ -399,11 +401,6 @@
         pack_ref[NP * k : NP * k + NP] = result[k]
 
 
-def pair_kernel(pack_ref, cross_in, out_ref):
-    out_ref[: 7 * NP] = pack_ref[...]
-    out_ref[7 * NP :] = cross_in[...]
-
-
 def chip_rows(first, second):
     return jnp.concatenate([first[:-1], (first[-1] + second[0])[None], second[1:]], axis=0)
 
@@ -448,19 +445,24 @@
         sums.append(jnp.sum(rows(mass), axis=0, keepdims=True))
         sums.append(jnp.zeros((4, LANES), jnp.float32))
         levels.append(jnp.concatenate(sums, axis=0))
-        level_ref[layer] = levels[layer]
         div.append(join_s(gradient_t(terms[0], terms[1], terms[2], ds_ref[...], dq_ref[...])))
     whole = chip_rows(div[0], div[1])
     div_ref[...] = whole
     cross_ref[:EDGE] = edge_rows(even, whole)
-    cross_ref[EDGE] = jnp.where(even, levels[0], levels[1])
-
-
-def window(local, low, high):
-    return jnp.concatenate(
-        [low[: EDGE - 1], (low[EDGE - 1] + local[0])[None], local[1:-1], (local[-1] + high[0])[None], high[1:EDGE]],
-        axis=0,
-    )
+    level = jnp.where(even, levels[0], levels[1])
+    level_ref[...] = level
+    cross_ref[EDGE] = level
+
+
+def half_window(even, local, received):
+    edge = received[:EDGE]
+    low = jnp.concatenate([edge[:-1], (edge[-1] + local[0])[None], local[1:EDGE]], axis=0)
+    high = jnp.concatenate([local[ROWS - EDGE : -1], (local[-1] + edge[0])[None], edge[1:]], axis=0)
+    return jnp.where(even, low, high)
+
+
+def own_of_half(even, x):
+    return jnp.where(even, x[NP : 2 * NP], x[1 : NP + 1])
 
 
 def inverse_levels(levels, spread_ref, lam_ref):
@@ -472,106 +474,95 @@
     return result
 
 
-def schwarz(wide, inv_ref, sleft_ref, sright_ref, srback_ref, sback_ref):
-    before, after = roll(wide, NP, 2), roll(wide, -NP, 2)
+def schwarz(half, even, inv_ref, sleft_ref, sright_ref, srback_ref, sback_ref):
+    before, after = roll(half, NP, 2), roll(half, -NP, 2)
     columns = []
-    for layer in range(4):
+    for layer in range(2):
         at = (NP - 1) * layer
-        columns.append(jnp.concatenate([x[at : at + NP + 2].reshape(80, LANES) for x in (wide, before, after)], axis=0))
+        columns.append(jnp.concatenate([x[at : at + NP + 2].reshape(80, LANES) for x in (half, before, after)], axis=0))
     spectra = left_dot(sleft_ref, jnp.concatenate(columns, axis=1))
-    spectra = jnp.concatenate([spectra[:, LANES * k : LANES * k + LANES] for k in range(4)], axis=0)
+    spectra = jnp.concatenate([spectra[:, LANES * k : LANES * k + LANES] for k in range(2)], axis=0)
     spectra = pair_dot(right_dot(spectra, sright_ref) * inv_ref[...], srback_ref)
-    spectra = jnp.concatenate([spectra[MODES * k : MODES * k + MODES] for k in range(4)], axis=1)
+    spectra = jnp.concatenate([spectra[MODES * k : MODES * k + MODES] for k in range(2)], axis=1)
     blocks = left_dot(sback_ref, spectra)
     z = []
-    for layer in range(4):
+    for layer in range(2):
         part = blocks[:, LANES * layer : LANES * layer + LANES]
         part = part[:80] + roll(part[80:160], -NP, 1) + roll(part[160:], NP, 1)
         z.append(part.reshape(NP + 2, NP, LANES))
-    middle = jnp.concatenate([z[1][1:8], (z[1][8] + z[2][1])[None], z[2][2:9]], axis=0)
-    first = jnp.concatenate([z[0][8:10], jnp.zeros((4, NP, LANES), jnp.float32), z[2][0:1], jnp.zeros((1, NP, LANES), jnp.float32), z[1][9:10], jnp.zeros((4, NP, LANES), jnp.float32), z[3][0:2]], axis=0)
-    return middle + first
-
-
-def operate(v, op_ref, ds_ref, dq_ref):
-    ds, dq = ds_ref[...], dq_ref[...]
+    upper = jnp.concatenate([z[0][8:] + z[1][1:3], z[1][3:]], axis=0)
+    lower = jnp.concatenate([z[0][:7], z[0][7:9] + z[1][:2]], axis=0)
+    return jnp.where(even, upper, lower)
+
+
+def join_sides(even, own, mate):
+    first, second = jnp.where(even, own, mate), jnp.where(even, mate, own)
+    return jnp.concatenate([first[:6], first[6:] + second[:3], second[3:]], axis=0)
+
+
+def operate(v, op_ref, ds_ref, qright_ref, qright_t_ref):
+    ds = ds_ref[...]
+    layers = [v[(NP - 1) * k : (NP - 1) * k + NP] for k in range(2)]
+    gq = right_dot(jnp.concatenate([rows(x) for x in layers], axis=0), qright_ref)
+    hq = [op_ref[k, 2] * planes(gq[64 * k : 64 * k + 64]) for k in range(2)]
+    back = right_dot(jnp.concatenate([rows(x) for x in hq], axis=0), qright_t_ref)
     parts = []
-    for layer in range(2):
-        x = v[(NP - 1) * layer : (NP - 1) * layer + NP]
-        ga, gs, gq = gradient(x, ds, dq)
-        local = gradient_t(op_ref[layer, 0] * ga, op_ref[layer, 1] * gs, op_ref[layer, 2] * gq, ds, dq)
-        parts.append(join_s(local + op_ref[layer, 3] * x))
+    for k, x in enumerate(layers):
+        local = d_a(op_ref[k, 0] * d_a(x, False), True) + d_s(op_ref[k, 1] * d_s(x, ds[0]), ds[1])
+        parts.append(join_s(local + (op_ref[k, 3] * x + planes(back[64 * k : 64 * k + 64]))))
     return chip_rows(parts[0], parts[1])
 
 
-def sides_of(even, own_in, mate_in):
-    own, mate = own_in[...], mate_in[...]
-    return jnp.where(even, own, mate), jnp.where(even, mate, own)
-
-
-def first_kernel(div_ref, own_in, mate_in, level_ref, spread_ref, lam_ref, op_ref, ds_ref, dq_ref, sleft_ref, sright_ref, srback_ref, sback_ref, wide_ref, inv_ref, v_ref, local_ref, cross_ref):
+def first_smooth_kernel(div_ref, received_ref, level_ref, spread_ref, lam_ref, sleft_ref, sright_ref, srback_ref, sback_ref, half_ref, inv_ref, part_ref):
     even = parity() == 0
-    low, high = sides_of(even, own_in, mate_in)
-    wide = window(div_ref[...], low, high)
-    wide_ref[...] = wide
-    for k, inv in enumerate(inverse_levels([low[EDGE], level_ref[0], level_ref[1], high[EDGE]], spread_ref, lam_ref)):
+    half = half_window(even, div_ref[...], received_ref)
+    half_ref[...] = half
+    other = received_ref[EDGE]
+    own = level_ref[...]
+    levels = [jnp.where(even, other, own), jnp.where(even, own, other)]
+    for k, inv in enumerate(inverse_levels(levels, spread_ref, lam_ref)):
         inv_ref[MODES * k : MODES * k + MODES] = inv
-    v = schwarz(wide, inv_ref, sleft_ref, sright_ref, srback_ref, sback_ref)
+    part_ref[...] = schwarz(half, even, inv_ref, sleft_ref, sright_ref, srback_ref, sback_ref)
+
+
+def smooth_kernel(step, before_ref, local_ref, received_ref, inv_ref, sleft_ref, sright_ref, srback_ref, sback_ref, own_image_ref, half_ref, part_ref):
+    even = parity() == 0
+    image = half_window(even, local_ref[...], received_ref)
+    half = before_ref[...] - step * image
+    half_ref[...] = half
+    part_ref[...] = schwarz(half, even, inv_ref, sleft_ref, sright_ref, srback_ref, sback_ref)
+    own_image_ref[...] = own_of_half(even, image)
+
+
+def operator_kernel(part_ref, mate_ref, op_ref, ds_ref, qright_ref, qright_t_ref, v_ref, local_ref, cross_ref):
+    even = parity() == 0
+    v = join_sides(even, part_ref[...], mate_ref[...])
     v_ref[...] = v
-    local = operate(v, op_ref, ds_ref, dq_ref)
+    local = operate(v, op_ref, ds_ref, qright_ref, qright_t_ref)
     local_ref[...] = local
     cross_ref[...] = edge_rows(even, local)
 
 
-def next_kernel(step, before_ref, image_ref, own_in, mate_in, inv_ref, op_ref, ds_ref, dq_ref, sleft_ref, sright_ref, srback_ref, sback_ref, own_image_ref, wide_ref, v_ref, local_ref, cross_ref):
+def last_operator_kernel(part_ref, mate_ref, op_ref, ds_ref, qright_ref, qright_t_ref, ws_ref, div_ref, half_ref, v0_ref, v1_ref, l0_ref, l1_ref, own_ref, face_ref, sums_ref):
     even = parity() == 0
-    low, high = sides_of(even, own_in, mate_in)
-    image = window(image_ref[...], low, high)
-    own_image_ref[...] = own_rows(even, image[NP : NP + ROWS])
-    wide = before_ref[...] - step * image
-    wide_ref[...] = wide
-    v = schwarz(wide, inv_ref, sleft_ref, sright_ref, srback_ref, sback_ref)
-    v_ref[...] = v
-    local = operate(v, op_ref, ds_ref, dq_ref)
-    local_ref[...] = local
-    cross_ref[...] = edge_rows(even, local)
-
-
-def last_kernel(step, before_ref, image_ref, own_in, mate_in, inv_ref, op_ref, ds_ref, dq_ref, sleft_ref, sright_ref, srback_ref, sback_ref, ws_ref, v0_ref, v1_ref, l0_ref, own_image_ref, own_ref, sums_ref):
-    even = parity() == 0
-    low, high = sides_of(even, own_in, mate_in)
-    image = window(image_ref[...], low, high)
-    own_image_ref[...] = own_rows(even, image[NP : NP + ROWS])
-    residual = before_ref[NP : NP + ROWS] - step * image[NP : NP + ROWS]
-    wide = before_ref[...] - step * image
-    v2 = schwarz(wide, inv_ref, sleft_ref, sright_ref, srback_ref, sback_ref)
-    l2 = operate(v2, op_ref, ds_ref, dq_ref)
+    v2 = join_sides(even, part_ref[...], mate_ref[...])
+    l2 = operate(v2, op_ref, ds_ref, qright_ref, qright_t_ref)
+    face_ref[...] = jnp.where(even, l2[0], l2[-1])
     v = [v0_ref[...], v1_ref[...], v2]
-    images = [l0_ref[...], image_ref[...], l2]
-    for k, x in enumerate((v[0], v[1], v2, l2, residual)):
-        own_ref[k] = own_rows(even, x)
-    weighted = jnp.concatenate([0.5 * residual[:1], residual[1:-1], 0.5 * residual[-1:]], axis=0)
+    images = [l0_ref[...], l1_ref[...], l2]
+    residual = div_ref[...] - STEPS[0] * images[0] - STEPS[1] * images[1]
     ws = ws_ref[...]
     pairs = [(v[i], images[j]) for i, j in ((0, 0), (0, 1), (0, 2), (1, 1), (1, 2), (2, 2))]
-    pairs.extend((v[i], weighted) for i in range(3))
+    pairs.extend((v[i], residual) for i in range(3))
     lane = lax.broadcasted_iota(jnp.int32, (NP, LANES), 1)
     line = jnp.zeros((NP, LANES), jnp.float32)
     for k, (left, right) in enumerate(pairs):
         line = jnp.where(lane == k, jnp.sum(jnp.sum(left * right, axis=0) * ws), line)
-    put_sums(sums_ref, jnp.where(even, l2[0], l2[-1]), line)
-
-
-def put_sums(sums_ref, face, line):
-    sub = lax.broadcasted_iota(jnp.int32, (NP, LANES), 0)
-    value = jnp.where(sub == NP - 1, line, face)
-    for k in range(sums_ref.shape[0]):
-        sums_ref[k] = value
-
-
-def relay_kernel(near_ref, out_ref):
-    count = near_ref.shape[0]
-    chip = lax.rem(lax.axis_index("dom") // 2, count)
-    put_sums(out_ref, near_ref[chip], jnp.sum(near_ref[...], axis=0))
+    for k in range(sums_ref.shape[0] // NP):
+        sums_ref[NP * k : NP * k + NP] = line
+    for k, x in enumerate((v[0], v[1], v2, l2)):
+        own_ref[k] = own_rows(even, x)
+    own_ref[4] = own_of_half(even, half_ref[...])
 
 
 def to_output(x, order_ref, scratch_ref):
@@ -587,20 +578,14 @@
     return jnp.concatenate(tiles, axis=1)
 
 
-def combine_kernel(near_ref, far_ref, own_ref, w0_ref, w1_ref, order_ref, p_ref, r_ref, first_ref, second_ref):
-    device = lax.axis_index("dom")
-    even = lax.rem(device, 2) == 0
-    near, far = near_ref.shape[0], far_ref.shape[0]
-    chips = near * far
-    chip = device // 2
-    partner = lax.rem(jnp.where(even, chip + chips - 1, chip + 1), chips)
-    inside = partner // near == chip // near
-    face = jnp.where(inside, near_ref[lax.rem(partner, near)], far_ref[partner // near])
+def combine_kernel(sums_ref, face_ref, own_ref, w0_ref, w1_ref, order_ref, p_ref, r_ref, first_ref, second_ref):
+    even = parity() == 0
+    face = face_ref[...]
     local = own_ref[3]
     first = jnp.where(even, local[0] + face, local[0])
     last = jnp.where(even, local[-1], local[-1] + face)
     w2 = jnp.concatenate([first[None], local[1:-1], last[None]], axis=0)
-    line = jnp.sum(far_ref[...], axis=0)[NP - 1 :]
+    line = jnp.sum(sums_ref[...], axis=0, keepdims=True)
     h00, h01, h02, h11, h12, h22, g0, g1, g2 = [line[:, k : k + 1] for k in range(9)]
     m1, m2 = h01 / h00, h02 / h00
     k11, k12, k22 = h11 - m1 * h01, h12 - m1 * h02, h22 - m2 * h02
@@ -627,7 +612,7 @@
 
 
 def call_forcing(*args):
-    shapes = [(7 * NP, NP, LANES), (4, NP, LANES)]
+    shapes = [(7 * NP + 4, NP, LANES), (4, NP, LANES)]
     scratch = [pltpu.SMEM(args[0].shape, jnp.int32)]
     scratch.extend(pltpu.VMEM(x.shape, x.dtype) for x in args[1:])
     scratch.append(pltpu.SemaphoreType.DMA((len(args),)))
@@ -637,25 +622,15 @@
         in_specs=[pl.BlockSpec(memory_space=pltpu.HBM)] * len(args),
         out_specs=[pl.BlockSpec(memory_space=pltpu.VMEM)] * len(shapes),
         scratch_shapes=scratch,
-        compiler_params=PARAMS,
+        compiler_params=pltpu.CompilerParams(vmem_limit_bytes=FORCING_VMEM),
     )(*args)
 
 
 FORCING_TABLES = ("w3", "wmass", "ds", "dq", "jright", "jslope", "jright_t", "jleft", "jleft_a", "jleft_s", "jleft_t", "wfine")
 
 
-def groups_of(count):
-    chips = count // 2
-    near = {256: 16, 16: 4, 4: 2}[chips]
-    far = chips // near
-    first, second = [], []
-    for team in range(2):
-        member = [2 * c + (team + c) % 2 for c in range(chips)]
-        first.extend([member[near * i + j] for j in range(near)] for i in range(far))
-        for j in range(near):
-            turned = near - 1 - j if j in (0, near - 1) else j
-            second.append([member[near * i + (turned if i % 2 else j)] for i in range(far)])
-    return near, far, first, second
+def team_groups(count):
+    return [[2 * c + side for c in range(count // 2)] for side in range(2)]
 
 
 def shards(velocity, conv_past, metric, jacobian, element_slot):
@@ -663,49 +638,50 @@
     t = {key: jnp.asarray(value) for key, value in TAB.items()}
     field = (NP, NP, LANES)
     chip = (ROWS, NP, LANES)
-    wide_shape = (WINDOW, NP, LANES)
+    half_shape = (2 * NP + 1, NP, LANES)
     edge = (EDGE, NP, LANES)
-
-    def exchange(x):
-        own = swap_cross(x, count)
-        return own, swap_inner(own, count)
-
     pack, cross = call_forcing(
-        element_slot, velocity, conv_past, metric, jacobian,
-        *(t[key] for key in FORCING_TABLES),
+        element_slot, velocity, conv_past, metric, jacobian, *(t[key] for key in FORCING_TABLES)
     )
-    (own,) = call(pair_kernel, [(7 * NP + 4, NP, LANES)], pack, swap_cross(cross, count))
+    own = lax.dynamic_update_slice(pack, swap_cross(cross, count), (7 * NP, 0, 0))
     mate = swap_inner(own, count)
     div, op, level, cross = call(
         divergence_kernel,
-        [chip, (2, 4) + field, (2, NP, LANES), (EDGE + 1, NP, LANES)],
+        [chip, (2, 4) + field, (NP, LANES), (EDGE + 1, NP, LANES)],
         own, mate, t["ds"], t["dq"],
     )
-    tables = (op, t["ds"], t["dq"], t["sleft"], t["sright"], t["srback"], t["sback"])
-    wide, inv, v0, local0, cross = call(
-        first_kernel,
-        [wide_shape, (4 * MODES, ES * (NP + 2)), chip, chip, edge],
-        div, *exchange(cross), level, t["spread"], t["lam"], *tables,
+    solve = (t["sleft"], t["sright"], t["srback"], t["sback"])
+    tables = (op, t["ds"], t["qright"], t["qright_t"])
+    half, inv, part = call(
+        first_smooth_kernel,
+        [half_shape, (2 * MODES, ES * (NP + 2)), edge],
+        div, swap_cross(cross, count), level, t["spread"], t["lam"], *solve,
     )
-    image0, wide, v1, local1, cross = call(
-        functools.partial(next_kernel, STEPS[0]),
-        [field, wide_shape, chip, chip, edge],
-        wide, local0, *exchange(cross), inv, *tables,
+    vectors, locals_, images = [], [], []
+    for step in STEPS:
+        v, local, cross = call(
+            operator_kernel, [chip, chip, edge], part, swap_inner(part, count), *tables
+        )
+        image, half, part = call(
+            functools.partial(smooth_kernel, step),
+            [field, half_shape, edge],
+            half, local, swap_cross(cross, count), inv, *solve,
+        )
+        vectors.append(v)
+        locals_.append(local)
+        images.append(image)
+    own, face, sums = call(
+        last_operator_kernel,
+        [(5,) + field, (NP, LANES), (count // 2, LANES)],
+        part, swap_inner(part, count), *tables, t["ws"], div, half, *vectors, *locals_,
     )
-    near, far, first, second = groups_of(count)
-    image1, own, sums = call(
-        functools.partial(last_kernel, STEPS[1]),
-        [field, (5,) + field, (near, NP, LANES)],
-        wide, local1, *exchange(cross), inv, *tables, t["ws"], v0, v1, local0,
-    )
-    near_sums = lax.all_to_all(sums, "dom", 0, 0, tiled=True, axis_index_groups=first)
-    (sums,) = call(relay_kernel, [(far, NP, LANES)], near_sums)
-    far_sums = lax.all_to_all(sums, "dom", 0, 0, tiled=True, axis_index_groups=second)
+    sums = lax.all_to_all(sums, "dom", 0, 0, tiled=True, axis_index_groups=team_groups(count))
+    face = swap_cross(face, count)
     return tuple(
         call(
             combine_kernel,
             [(NP, 896), (NP, 896)],
-            near_sums, far_sums, own, image0, image1, t["order"],
+            sums, face, own, *images, t["order"],
             scratch=[pltpu.VMEM((NP * NP, LANES), jnp.float32)] * 2,
         )
     )

time: 123 us -> 104 us (0.85)
  blocking collectives: 30.3 us -> 0 us
  starting transfers between devices: 48 us -> 63.2 us
  local copies, waits for them, and re-layouts: 14.6 us -> 1.61 us
  waiting for transfers between devices: 15.1 us -> 25.7 us
    all_to_all x2 -> x0, blocking collectives: 30.3 us -> none  [the longest x1 20.3 us: shards(): lax.all_to_all(sums, 'dom', 0, 0, tiled=True, axis_index_groups=second)]
    unnamed x54 -> x26, local copies, waits for them, and re-layouts: 14.6 us -> 1.01 us
    all_to_all x0 -> x1, starting transfers between devices: none -> 13.1 us  [shards(): lax.all_to_all(sums, 'dom', 0, 0, tiled=True, axis_index_groups=team_grou...]
    all_to_all x0 -> x1, waiting for transfers between devices: none -> 7.12 us  [shards(): lax.all_to_all(sums, 'dom', 0, 0, tiled=True, axis_index_groups=team_grou...]
    ppermute x4 -> x5, waiting for transfers between devices: 11.5 us -> 14.7 us  [swap_cross(): return lax.ppermute(x, 'dom', pairs)]
    ppermute x4 -> x5, starting transfers between devices: 10.5 us -> 12.6 us  [swap_cross(): return lax.ppermute(x, 'dom', pairs)]
    pallas_call x7 -> x8, Pallas kernels: 8.22 us -> 7.67 us  [call(): pl.pallas_call(kernel, out_shape=[jax.ShapeDtypeStruct(shape, jnp.float32...]
  transfers between devices with their start and end apart: 8 -> 10, of which waited for: 8 -> 10; matrix products, arithmetic and copies ran while one was open for 0% -> 0% of each run, Pallas kernels for 0% -> 0%
where the time goes in v4:
time: 104 us
  starting transfers between devices  63.2 us (61%)
  waiting for transfers between devices  25.7 us (25%)
  Pallas kernels  12.3 us (12%)
  local copies, waits for them, and re-layouts  1.61 us (2%)
    ppermute x4, starting transfers between devices, swap_inner(): return lax.ppermute(x, 'dom', [(i, i ^ 1) for i in range(count)])  37.5 us
    ppermute x5, waiting for transfers between devices, swap_cross(): return lax.ppermute(x, 'dom', pairs)  14.7 us
    all_to_all x1, starting transfers between devices, shards(): lax.all_to_all(sums, 'dom', 0, 0, tiled=True, axis_index_groups=team_grou...  13.1 us
    ppermute x5, starting transfers between devices, swap_cross(): return lax.ppermute(x, 'dom', pairs)  12.6 us
    pallas_call x8, Pallas kernels, call(): pl.pallas_call(kernel, out_shape=[jax.ShapeDtypeStruct(shape, jnp.float32...  7.67 us
    all_to_all x1, waiting for transfers between devices, shards(): lax.all_to_all(sums, 'dom', 0, 0, tiled=True, axis_index_groups=team_grou...  7.12 us
    pallas_call x1, Pallas kernels, call_forcing(): pl.pallas_call(forcing_kernel, out_shape=[jax.ShapeDtypeStruct(shape, jnp...  4.62 us
    ppermute x4, waiting for transfers between devices, swap_inner(): return lax.ppermute(x, 'dom', [(i, i ^ 1) for i in range(count)])  3.86 us
  transfers between devices with their start and end apart: 10, of which 10 were waited for; matrix products, arithmetic and copies ran while one was open for 0% of the time, Pallas kernels for 0%

profile of v4, /device:TPU:1, one launch (start us, length us, event | category | flops | bytes accessed | tf_op | source)
XLA Modules:
  0.0 103.7 jit_solution(6321361735329351545)
XLA Ops:
  0.6 0.0 copy-start.7
  0.6 0.0 copy-start.2
  0.7 0.0 copy-start.8
  0.7 0.0 copy-start.10
  0.7 4.6 %shard_map.266 = (f32[60,8,128]{2,1,0:T(8,128)}, f32[4,8,128]{2,1,0:T(8,128)}) custom-call(s32[16]{0:T(128)} %slot_in.1, f32[3,3,16,512]{3,2,1,0:T(8,128)} %vel_in.1, f32[2,3,16,512]{3,2,1,0:T(8,128)} %past_in.1, f32[3,16,512]{2,1,0:T(8,128)} %metric_in.1, f32[16,512]{1,0:T(8,128)} %jac_in.1, f32[1,512]{1,0:T(1,128)} %constant.52.clone.w3_in, ...), custom_call_target="tpu_custom_call" | custom-call | tf_op jit(solution)/shard_map/pallas_call | solution.py:619
  5.3 4.6 %collective-permute-start = (f32[4,8,128]{2,1,0:T(8,128)}, f32[4,8,128]{2,1,0:T(8,128)S(1)}, u32[]{:S(2)}, u32[]{:S(2)}) collective-permute-start(f32[4,8,128]{2,1,0:T(8,128)} %get-tuple-element.27), channel_id=1, source_target_pairs={{0,511},{1,2},{2,1},{3,4},{4,3},{5,6},{6,5},{7,8},{8,7},{9,10},{10... | collective-permute-start | bytes 49160 | tf_op jit(solution)/shard_map/ppermute | solution.py:313
  9.9 1.6 %collective-permute-done = f32[4,8,128]{2,1,0:T(8,128)S(1)} collective-permute-done((f32[4,8,128]{2,1,0:T(8,128)}, f32[4,8,128]{2,1,0:T(8,128)S(1)}, u32[]{:S(2)}, u32[]{:S(2)}) %collective-permute-start) | collective-permute-done | bytes 16416 | tf_op jit(solution)/shard_map/ppermute | solution.py:313
  11.5 0.6 constant_dynamic-update-slice_fusion.own_ref
  12.1 0.0 copy-start
  12.1 0.0 copy-start.1
  12.1 0.0 copy-start.3
  12.1 0.0 copy-start.6
  12.1 14.4 %collective-permute-start.1 = (f32[60,8,128]{2,1,0:T(8,128)}, f32[60,8,128]{2,1,0:T(8,128)S(1)}, u32[]{:S(2)}, u32[]{:S(2)}) collective-permute-start(f32[60,8,128]{2,1,0:T(8,128)} %constant_dynamic-update-slice_fusion.own_ref), channel_id=1, source_target_pairs={{0,1},{1,0},{2,3},{3,2},{4,5},{5,4},{6,7},{7,6},{8,9},{9,8},{10,11... | collective-permute-start | bytes 737288 | tf_op jit(solution)/shard_map/ppermute | solution.py:308
  26.6 1.3 %collective-permute-done.1.mate_ref = f32[60,8,128]{2,1,0:T(8,128)S(1)} collective-permute-done((f32[60,8,128]{2,1,0:T(8,128)}, f32[60,8,128]{2,1,0:T(8,128)S(1)}, u32[]{:S(2)}, u32[]{:S(2)}) %collective-permute-start.1) | collective-permute-done | bytes 245792 | tf_op jit(solution)/shard_map/ppermute | solution.py:308
  27.9 0.0 copy-done.7
  27.9 0.0 copy-done.2
  27.9 0.0 copy-start.9
  27.9 0.9 copy-done.9
  28.9 0.6 shard_map.267
  29.4 1.9 %collective-permute-start.2 = (f32[10,8,128]{2,1,0:T(8,128)S(1)}, f32[10,8,128]{2,1,0:T(8,128)S(1)}, u32[]{:S(2)}, u32[]{:S(2)}) collective-permute-start(f32[10,8,128]{2,1,0:T(8,128)S(1)} %get-tuple-element.29), channel_id=1, source_target_pairs={{0,511},{1,2},{2,1},{3,4},{4,3},{5,6},{6,5},{7,8},{8,7},{9,10},{10... | collective-permute-start | bytes 122888 | tf_op jit(solution)/shard_map/ppermute | solution.py:313
  31.4 3.4 %collective-permute-done.2.received_ref = f32[10,8,128]{2,1,0:T(8,128)S(1)} collective-permute-done((f32[10,8,128]{2,1,0:T(8,128)S(1)}, f32[10,8,128]{2,1,0:T(8,128)S(1)}, u32[]{:S(2)}, u32[]{:S(2)}) %collective-permute-start.2) | collective-permute-done | bytes 40992 | tf_op jit(solution)/shard_map/ppermute | solution.py:313
  34.8 0.0 copy-done.8
  34.8 0.0 copy-done.10
  34.8 0.0 copy-done
  34.8 0.0 copy-done.1
  34.8 0.0 copy-done.3
  34.8 0.0 copy-done.6
  34.8 0.0 copy-start.4
  34.8 0.0 copy-start.5
  34.8 1.1 %shard_map.268 = (f32[17,8,128]{2,1,0:T(8,128)S(1)}, f32[224,160]{1,0:T(8,128)S(1)}, f32[9,8,128]{2,1,0:T(8,128)S(1)}) custom-call(f32[15,8,128]{2,1,0:T(8,128)S(1)} %get-tuple-element.28.div_ref, f32[10,8,128]{2,1,0:T(8,128)S(1)} %collective-permute-done.2.received_ref, f32[8,128]{1,0:T(8,128)S(1)} %get-tuple-element.30.level_ref, ...), custom_call_target="tpu_custom_call" | custom-call | tf_op jit(solution)/shard_map/pallas_call | solution.py:604
  36.0 7.7 %collective-permute-start.3 = (f32[9,8,128]{2,1,0:T(8,128)S(1)}, f32[9,8,128]{2,1,0:T(8,128)S(1)}, u32[]{:S(2)}, u32[]{:S(2)}) collective-permute-start(f32[9,8,128]{2,1,0:T(8,128)S(1)} %get-tuple-element.32.part_ref), channel_id=1, source_target_pairs={{0,1},{1,0},{2,3},{3,2},{4,5},{5,4},{6,7},{7,6},{8,9},{9,8},{10,11... | collective-permute-start | bytes 110600 | tf_op jit(solution)/shard_map/ppermute | solution.py:308
  43.7 0.8 collective-permute-done.3.mate_ref
  44.5 0.0 copy-done.4
  44.5 0.0 copy-done.5
  44.5 0.4 shard_map.269
  45.0 1.9 %collective-permute-start.4 = (f32[9,8,128]{2,1,0:T(8,128)S(1)}, f32[9,8,128]{2,1,0:T(8,128)S(1)}, u32[]{:S(2)}, u32[]{:S(2)}) collective-permute-start(f32[9,8,128]{2,1,0:T(8,128)S(1)} %get-tuple-element.35), channel_id=1, source_target_pairs={{0,511},{1,2},{2,1},{3,4},{4,3},{5,6},{6,5},{7,8},{8,7},{9,10},{10... | collective-permute-start | bytes 110600 | tf_op jit(solution)/shard_map/ppermute | solution.py:313
  46.9 3.3 %collective-permute-done.4.received_ref = f32[9,8,128]{2,1,0:T(8,128)S(1)} collective-permute-done((f32[9,8,128]{2,1,0:T(8,128)S(1)}, f32[9,8,128]{2,1,0:T(8,128)S(1)}, u32[]{:S(2)}, u32[]{:S(2)}) %collective-permute-start.4) | collective-permute-done | bytes 36896 | tf_op jit(solution)/shard_map/ppermute | solution.py:313
  50.2 1.1 %shard_map.270 = (f32[8,8,128]{2,1,0:T(8,128)S(1)}, f32[17,8,128]{2,1,0:T(8,128)S(1)}, f32[9,8,128]{2,1,0:T(8,128)S(1)}) custom-call(f32[17,8,128]{2,1,0:T(8,128)S(1)} %get-tuple-element.31.before_ref, f32[15,8,128]{2,1,0:T(8,128)S(1)} %get-tuple-element.34.local_ref.l0_ref, f32[9,8,128]{2,1,0:T(8,128)S(1)} %collective-permute-done.4.received_ref, ...), custom_call_target="tpu_custom_call" | custom-call | tf_op jit(solution)/shard_map/pallas_call | solution.py:604
  51.4 7.7 %collective-permute-start.5 = (f32[9,8,128]{2,1,0:T(8,128)S(1)}, f32[9,8,128]{2,1,0:T(8,128)S(1)}, u32[]{:S(2)}, u32[]{:S(2)}) collective-permute-start(f32[9,8,128]{2,1,0:T(8,128)S(1)} %get-tuple-element.38.part_ref), channel_id=1, source_target_pairs={{0,1},{1,0},{2,3},{3,2},{4,5},{5,4},{6,7},{7,6},{8,9},{9,8},{10,11... | collective-permute-start | bytes 110600 | tf_op jit(solution)/shard_map/ppermute | solution.py:308
  59.1 0.8 collective-permute-done.5.mate_ref
  59.9 0.4 shard_map.271
  60.3 1.9 %collective-permute-start.6 = (f32[9,8,128]{2,1,0:T(8,128)S(1)}, f32[9,8,128]{2,1,0:T(8,128)S(1)}, u32[]{:S(2)}, u32[]{:S(2)}) collective-permute-start(f32[9,8,128]{2,1,0:T(8,128)S(1)} %get-tuple-element.40), channel_id=1, source_target_pairs={{0,511},{1,2},{2,1},{3,4},{4,3},{5,6},{6,5},{7,8},{8,7},{9,10},{10... | collective-permute-start | bytes 110600 | tf_op jit(solution)/shard_map/ppermute | solution.py:313
  62.3 3.3 %collective-permute-done.6.received_ref = f32[9,8,128]{2,1,0:T(8,128)S(1)} collective-permute-done((f32[9,8,128]{2,1,0:T(8,128)S(1)}, f32[9,8,128]{2,1,0:T(8,128)S(1)}, u32[]{:S(2)}, u32[]{:S(2)}) %collective-permute-start.6) | collective-permute-done | bytes 36896 | tf_op jit(solution)/shard_map/ppermute | solution.py:313
  65.6 1.1 %shard_map.272 = (f32[8,8,128]{2,1,0:T(8,128)S(1)}, f32[17,8,128]{2,1,0:T(8,128)S(1)}, f32[9,8,128]{2,1,0:T(8,128)S(1)}) custom-call(f32[17,8,128]{2,1,0:T(8,128)S(1)} %get-tuple-element.37.before_ref, f32[15,8,128]{2,1,0:T(8,128)S(1)} %get-tuple-element.39.local_ref.l1_ref, f32[9,8,128]{2,1,0:T(8,128)S(1)} %collective-permute-done.6.received_ref, ...), custom_call_target="tpu_custom_call" | custom-call | tf_op jit(solution)/shard_map/pallas_call | solution.py:604
  66.7 0.0 copy-start.12
  66.8 7.7 %collective-permute-start.7 = (f32[9,8,128]{2,1,0:T(8,128)S(1)}, f32[9,8,128]{2,1,0:T(8,128)S(1)}, u32[]{:S(2)}, u32[]{:S(2)}) collective-permute-start(f32[9,8,128]{2,1,0:T(8,128)S(1)} %get-tuple-element.41.part_ref), channel_id=1, source_target_pairs={{0,1},{1,0},{2,3},{3,2},{4,5},{5,4},{6,7},{7,6},{8,9},{9,8},{10,11... | collective-permute-start | bytes 110600 | tf_op jit(solution)/shard_map/ppermute | solution.py:308
  74.4 0.8 collective-permute-done.7.mate_ref
  75.3 0.0 copy-done.12
  75.3 1.2 %shard_map.273 = (f32[5,8,8,128]{3,2,1,0:T(8,128)S(1)}, f32[8,128]{1,0:T(8,128)S(1)}, f32[256,128]{1,0:T(8,128)}) custom-call(f32[9,8,128]{2,1,0:T(8,128)S(1)} %get-tuple-element.41.part_ref, f32[9,8,128]{2,1,0:T(8,128)S(1)} %collective-permute-done.7.mate_ref, f32[2,4,8,8,128]{4,3,2,1,0:T(8,128)S(1)} %get-tuple-element.33.op_ref, ...), custom_call_target="tpu_custom_call" | custom-call | tf_op jit(solution)/shard_map/pallas_call | solution.py:604
  76.5 0.0 copy-start.11
  76.5 13.1 %all-to-all-start = ((f32[256,1,128]{2,1,0:T(1,128)}), f32[256,1,128]{2,1,0:T(1,128)S(1)}, u32[]{:S(2)}, u32[]{:S(2)}) async-start(f32[256,1,128]{2,1,0:T(1,128)} %bitcast.1), calls=%async_computation | async-start | bytes 262144 | tf_op jit(solution)/shard_map/all_to_all | solution.py:678
  89.7 2.2 %collective-permute-start.8 = (f32[8,128]{1,0:T(8,128)S(1)}, f32[8,128]{1,0:T(8,128)S(1)}, u32[]{:S(2)}, u32[]{:S(2)}) collective-permute-start(f32[8,128]{1,0:T(8,128)S(1)} %get-tuple-element.46), channel_id=1, source_target_pairs={{0,511},{1,2},{2,1},{3,4},{4,3},{5,6},{6,5},{7,8},{8,7},{9,10},{10... | collective-permute-start | bytes 12296 | tf_op jit(solution)/shard_map/ppermute | solution.py:313
  91.9 3.0 %collective-permute-done.8.face_ref = f32[8,128]{1,0:T(8,128)S(1)} collective-permute-done((f32[8,128]{1,0:T(8,128)S(1)}, f32[8,128]{1,0:T(8,128)S(1)}, u32[]{:S(2)}, u32[]{:S(2)}) %collective-permute-start.8) | collective-permute-done | bytes 4128 | tf_op jit(solution)/shard_map/ppermute | solution.py:313
  94.9 7.1 %all-to-all-done = f32[256,1,128]{2,1,0:T(1,128)S(1)} async-done(((f32[256,1,128]{2,1,0:T(1,128)}), f32[256,1,128]{2,1,0:T(1,128)S(1)}, u32[]{:S(2)}, u32[]{:S(2)}) %all-to-all-start) | async-done | bytes 131104 | tf_op jit(solution)/shard_map/all_to_all | solution.py:678
  102.0 0.0 copy-done.11
  102.0 1.7 %shard_map.274 = (f32[8,896]{1,0:T(8,128)}, f32[8,896]{1,0:T(8,128)}) custom-call(f32[256,128]{1,0:T(8,128)S(1)} %bitcast.4, f32[8,128]{1,0:T(8,128)S(1)} %collective-permute-done.8.face_ref, f32[5,8,8,128]{3,2,1,0:T(8,128)S(1)} %get-tuple-element.47.own_ref, f32[8,8,128]{2,1,0:T(8,128)S(1)} %get-tuple-element.48.w0_ref, ...), custom_call_target="tpu_custom_call" | custom-call | tf_op jit(solution)/shard_map/pallas_call | solution.py:604
Async XLA Ops:
  0.6 27.3 %copy-start.7 = (f32[2,15,8,128]{3,2,1,0:T(8,128)S(1)}, f32[2,15,8,128]{3,2,1,0:T(8,128)}, u32[]{:S(2)}) copy-start(f32[2,15,8,128]{3,2,1,0:T(8,128)} %constant.49.clone.dq_in.dq_ref) | copy-start | bytes 368644
  0.6 27.3 %copy-start.2 = (f32[2,8,8,128]{3,2,1,0:T(8,128)S(1)}, f32[2,8,8,128]{3,2,1,0:T(8,128)}, u32[]{:S(2)}) copy-start(f32[2,8,8,128]{3,2,1,0:T(8,128)} %constant.48.clone.ds_in.ds_ref) | copy-start | bytes 196612
  0.7 34.1 %copy-start.8 = (f32[3,112,160]{2,1,0:T(8,128)S(1)}, f32[3,112,160]{2,1,0:T(8,128)}, u32[]{:S(2)}) copy-start(f32[3,112,160]{2,1,0:T(8,128)} %constant.68.clone.lam_ref) | copy-start | bytes 645124
  0.7 34.1 %copy-start.10 = (f32[128,160]{1,0:T(8,128)S(1)}, f32[128,160]{1,0:T(8,128)}, u32[]{:S(2)}) copy-start(f32[128,160]{1,0:T(8,128)} %constant.67.clone.spread_ref) | copy-start | bytes 245764
  5.3 6.2 %collective-permute-start = (f32[4,8,128]{2,1,0:T(8,128)}, f32[4,8,128]{2,1,0:T(8,128)S(1)}, u32[]{:S(2)}, u32[]{:S(2)}) collective-permute-start(f32[4,8,128]{2,1,0:T(8,128)} %get-tuple-element.27), channel_id=1, source_target_pairs={{0,511},{1,2},{2,1},{3,4},{4,3},{5,6},{6,5},{7,8},{8,7},{9,10},{10... | collective-permute-start | bytes 49160 | tf_op jit(solution)/shard_map/ppermute | solution.py:313
  12.1 22.6 %copy-start = (bf16[384,160]{1,0:T(8,128)(2,1)S(1)}, bf16[384,160]{1,0:T(8,128)(2,1)}, u32[]{:S(2)}) copy-start(bf16[384,160]{1,0:T(8,128)(2,1)} %constant.65.clone.sright_ref) | copy-start | bytes 368644
  12.1 22.6 %copy-start.1 = (bf16[240,336]{1,0:T(8,128)(2,1)S(1)}, bf16[240,336]{1,0:T(8,128)(2,1)}, u32[]{:S(2)}) copy-start(bf16[240,336]{1,0:T(8,128)(2,1)} %constant.64.clone.sback_ref) | copy-start | bytes 483844
  12.1 22.7 %copy-start.3 = (bf16[112,720]{1,0:T(8,128)(2,1)S(1)}, bf16[112,720]{1,0:T(8,128)(2,1)}, u32[]{:S(2)}) copy-start(bf16[112,720]{1,0:T(8,128)(2,1)} %constant.63.clone.sleft_ref) | copy-start | bytes 483844
  12.1 22.7 %copy-start.6 = (bf16[2,160,128]{2,1,0:T(8,128)(2,1)S(1)}, bf16[2,160,128]{2,1,0:T(8,128)(2,1)}, u32[]{:S(2)}) copy-start(bf16[2,160,128]{2,1,0:T(8,128)(2,1)} %constant.66.clone.srback_ref) | copy-start | bytes 245764
  12.1 15.8 %collective-permute-start.1 = (f32[60,8,128]{2,1,0:T(8,128)}, f32[60,8,128]{2,1,0:T(8,128)S(1)}, u32[]{:S(2)}, u32[]{:S(2)}) collective-permute-start(f32[60,8,128]{2,1,0:T(8,128)} %constant_dynamic-update-slice_fusion.own_ref), channel_id=1, source_target_pairs={{0,1},{1,0},{2,3},{3,2},{4,5},{5,4},{6,7},{7,6},{8,9},{9,8},{10,11... | collective-permute-start | bytes 737288 | tf_op jit(solution)/shard_map/ppermute | solution.py:308
  27.9 0.9 copy-start.9
  29.4 5.3 %collective-permute-start.2 = (f32[10,8,128]{2,1,0:T(8,128)S(1)}, f32[10,8,128]{2,1,0:T(8,128)S(1)}, u32[]{:S(2)}, u32[]{:S(2)}) collective-permute-start(f32[10,8,128]{2,1,0:T(8,128)S(1)} %get-tuple-element.29), channel_id=1, source_target_pairs={{0,511},{1,2},{2,1},{3,4},{4,3},{5,6},{6,5},{7,8},{8,7},{9,10},{10... | collective-permute-start | bytes 122888 | tf_op jit(solution)/shard_map/ppermute | solution.py:313
  34.8 9.7 %copy-start.4 = (bf16[384,128]{1,0:T(8,128)(2,1)S(1)}, bf16[384,128]{1,0:T(8,128)(2,1)}, u32[]{:S(2)}) copy-start(bf16[384,128]{1,0:T(8,128)(2,1)} %constant.51.clone.qright_t_ref) | copy-start | bytes 294916
  34.8 9.7 %copy-start.5 = (bf16[384,128]{1,0:T(8,128)(2,1)S(1)}, bf16[384,128]{1,0:T(8,128)(2,1)}, u32[]{:S(2)}) copy-start(bf16[384,128]{1,0:T(8,128)(2,1)} %constant.50.clone.qright_ref) | copy-start | bytes 294916
  36.0 8.6 %collective-permute-start.3 = (f32[9,8,128]{2,1,0:T(8,128)S(1)}, f32[9,8,128]{2,1,0:T(8,128)S(1)}, u32[]{:S(2)}, u32[]{:S(2)}) collective-permute-start(f32[9,8,128]{2,1,0:T(8,128)S(1)} %get-tuple-element.32.part_ref), channel_id=1, source_target_pairs={{0,1},{1,0},{2,3},{3,2},{4,5},{5,4},{6,7},{7,6},{8,9},{9,8},{10,11... | collective-permute-start | bytes 110600 | tf_op jit(solution)/shard_map/ppermute | solution.py:308
  45.0 5.3 %collective-permute-start.4 = (f32[9,8,128]{2,1,0:T(8,128)S(1)}, f32[9,8,128]{2,1,0:T(8,128)S(1)}, u32[]{:S(2)}, u32[]{:S(2)}) collective-permute-start(f32[9,8,128]{2,1,0:T(8,128)S(1)} %get-tuple-element.35), channel_id=1, source_target_pairs={{0,511},{1,2},{2,1},{3,4},{4,3},{5,6},{6,5},{7,8},{8,7},{9,10},{10... | collective-permute-start | bytes 110600 | tf_op jit(solution)/shard_map/ppermute | solution.py:313
  51.4 8.5 %collective-permute-start.5 = (f32[9,8,128]{2,1,0:T(8,128)S(1)}, f32[9,8,128]{2,1,0:T(8,128)S(1)}, u32[]{:S(2)}, u32[]{:S(2)}) collective-permute-start(f32[9,8,128]{2,1,0:T(8,128)S(1)} %get-tuple-element.38.part_ref), channel_id=1, source_target_pairs={{0,1},{1,0},{2,3},{3,2},{4,5},{5,4},{6,7},{7,6},{8,9},{9,8},{10,11... | collective-permute-start | bytes 110600 | tf_op jit(solution)/shard_map/ppermute | solution.py:308
  60.3 5.3 %collective-permute-start.6 = (f32[9,8,128]{2,1,0:T(8,128)S(1)}, f32[9,8,128]{2,1,0:T(8,128)S(1)}, u32[]{:S(2)}, u32[]{:S(2)}) collective-permute-start(f32[9,8,128]{2,1,0:T(8,128)S(1)} %get-tuple-element.40), channel_id=1, source_target_pairs={{0,511},{1,2},{2,1},{3,4},{4,3},{5,6},{6,5},{7,8},{8,7},{9,10},{10... | collective-permute-start | bytes 110600 | tf_op jit(solution)/shard_map/ppermute | solution.py:313
  66.7 8.6 %copy-start.12 = (f32[8,128]{1,0:T(8,128)S(1)}, f32[8,128]{1,0:T(8,128)}, u32[]{:S(2)}) copy-start(f32[8,128]{1,0:T(8,128)} %constant.69.clone.ws_ref) | copy-start | bytes 12292
  66.8 8.5 %collective-permute-start.7 = (f32[9,8,128]{2,1,0:T(8,128)S(1)}, f32[9,8,128]{2,1,0:T(8,128)S(1)}, u32[]{:S(2)}, u32[]{:S(2)}) collective-permute-start(f32[9,8,128]{2,1,0:T(8,128)S(1)} %get-tuple-element.41.part_ref), channel_id=1, source_target_pairs={{0,1},{1,0},{2,3},{3,2},{4,5},{5,4},{6,7},{7,6},{8,9},{9,8},{10,11... | collective-permute-start | bytes 110600 | tf_op jit(solution)/shard_map/ppermute | solution.py:308
  76.5 25.5 %copy-start.11 = (s32[2,7,8,128]{3,2,1,0:T(8,128)S(1)}, s32[2,7,8,128]{3,2,1,0:T(8,128)}, u32[]{:S(2)}) copy-start(s32[2,7,8,128]{3,2,1,0:T(8,128)} %constant.62.clone.order_ref) | copy-start | bytes 172036
  76.5 25.5 %all-to-all-start = ((f32[256,1,128]{2,1,0:T(1,128)}), f32[256,1,128]{2,1,0:T(1,128)S(1)}, u32[]{:S(2)}, u32[]{:S(2)}) async-start(f32[256,1,128]{2,1,0:T(1,128)} %bitcast.1), calls=%async_computation | async-start | bytes 262144 | tf_op jit(solution)/shard_map/all_to_all | solution.py:678
  89.7 5.2 %collective-permute-start.8 = (f32[8,128]{1,0:T(8,128)S(1)}, f32[8,128]{1,0:T(8,128)S(1)}, u32[]{:S(2)}, u32[]{:S(2)}) collective-permute-start(f32[8,128]{1,0:T(8,128)S(1)} %get-tuple-element.46), channel_id=1, source_target_pairs={{0,511},{1,2},{2,1},{3,4},{4,3},{5,6},{6,5},{7,8},{8,7},{9,10},{10... | collective-permute-start | bytes 12296 | tf_op jit(solution)/shard_map/ppermute | solution.py:313

commit v5 on v4

--- a/solution.py
+++ b/solution.py
@@ -139,8 +139,20 @@
     return np.concatenate([high, rest, high], axis=0)
 
 
+def by_modes_right(value):
+    high, rest = halves(by_modes(value, 0))
+    parts = (high, rest, high)
+    return np.concatenate([x[:LANES] for x in parts] + [x[LANES:] for x in parts])
+
+
 def pair(value):
     return np.stack(halves(value))
+
+
+def by_modes(value, axis):
+    at = np.arange(ES * (NP + 2))
+    order = np.concatenate([at[at % (NP + 2) < NP], at[at % (NP + 2) >= NP]])
+    return np.take(value, order, axis=axis)
 
 
 def make_tables():
@@ -188,31 +200,29 @@
     order = np.stack([element * NP + within % NP, within // NP]).reshape(2, 7, 1, LANES)
     out["order"] = np.ascontiguousarray(np.broadcast_to(order, (2, 7, NP, LANES)), dtype=np.int32)
     wide = NP + 2
-    left = np.zeros((MODES, 3, wide, NP))
-    back = np.zeros((3, wide, NP, MODES))
+    left = np.zeros((MODES, 112))
+    back = np.zeros((144, MODES))
+    at = np.arange(wide)
     for i in range(wide):
         for j in range(wide):
             row = i * wide + j
-            for a in range(wide):
-                for s in range(NP):
-                    left[row, 0, a, s] = solve[a, i] * solve[s + 1, j]
-                    back[0, a, s, row] = solve[a, i] * solve[s + 1, j]
-                left[row, 1, a, NP - 2] = solve[a, i] * solve[0, j]
-                left[row, 2, a, 1] = solve[a, i] * solve[wide - 1, j]
-                back[1, a, NP - 2, row] = solve[a, i] * solve[0, j]
-                back[1, a, NP - 1, row] = solve[a, i] * solve[1, j]
-                back[2, a, 1, row] = solve[a, i] * solve[wide - 1, j]
-                back[2, a, 0, row] = solve[a, i] * solve[wide - 2, j]
-    out["sleft"] = for_left(left.reshape(MODES, 240))
-    out["sback"] = for_left(back.reshape(240, MODES))
-    out["sright"] = for_right(np.kron(np.eye(ES), solve[1:-1, :]))
-    out["srback"] = pair(np.kron(np.eye(ES), solve[1:-1, :].T))
-    out["spread"] = f32(np.kron(np.eye(ES), np.ones((NP, wide))) / 8.0)
+            inside = np.outer(solve[:, i], solve[1:-1, j]).reshape(80)
+            left[row, :80] = inside
+            left[row, 80 + at] = solve[:, i] * solve[0, j]
+            left[row, 96 + at] = solve[:, i] * solve[wide - 1, j]
+            back[:80, row] = inside
+            for block, s in enumerate((0, 1, wide - 2, wide - 1)):
+                back[80 + 16 * block + at, row] = solve[:, i] * solve[s, j]
+    out["sleft"] = for_left(left)
+    out["sback"] = for_left(back)
+    out["sright"] = for_right(by_modes(np.kron(np.eye(ES), solve[1:-1, :]), 1))
+    out["srback"] = by_modes_right(np.kron(np.eye(ES), solve[1:-1, :].T))
+    out["spread"] = f32(by_modes(np.kron(np.eye(ES), np.ones((NP, wide))), 1) / 8.0)
     lam_a = np.zeros((MODES, 1))
     lam_s = np.zeros((MODES, 1))
     lam_a[:100, 0] = np.repeat(eigen, wide)
     lam_s[:100, 0] = np.tile(eigen, wide)
-    lam_q = np.tile(eigen, ES)[None, :]
+    lam_q = by_modes(np.tile(eigen, ES)[None, :], 1)
     full = (MODES, ES * wide)
     out["lam"] = f32(np.stack([np.broadcast_to(lam_a, full), np.broadcast_to(lam_s, full), np.broadcast_to(lam_q, full)]))
     half = np.ones(NP)
@@ -247,6 +257,13 @@
 def right_dot(x, table_ref):
     high, rest = split(x)
     return short_dot(jnp.concatenate([high, high, rest], axis=1), table_ref[...])
+
+
+def modes_dot(x, table_ref):
+    high, rest = split(x)
+    parts = (high, high, rest)
+    whole = [y[:, :LANES] for y in parts] + [y[:, LANES:] for y in parts]
+    return short_dot(jnp.concatenate(whole, axis=1), table_ref[...])
 
 
 def pair_dot(x, table_ref):
@@ -355,16 +372,18 @@
     copies = [pltpu.make_async_copy(x, y, sems.at[k]) for k, (x, y) in enumerate(zip(sources, targets))]
     for copy in copies:
         copy.start()
-    for copy in copies:
+    for copy in copies[:6]:
         copy.wait()
     even = parity() == 0
-    ds, dq = ds_ref[...], dq_ref[...]
     jac = jac_ref[...]
     new, mid, old = vel_ref[0], vel_ref[1], vel_ref[2]
     guess = 3.0 * (new - mid) + old
     direct = (jac * w3_ref[...])[None] * (-10.0 * new + 16.0 * mid - 6.0 * old) + 3.0 * past_ref[0] - past_ref[1]
     lanes = to_lanes(jnp.concatenate([new, guess, direct, metric_ref[...], jac[None]], axis=0))
     new, guess, direct, metric, jac = lanes[0:3], lanes[3:6], lanes[6:9], lanes[9:12], lanes[12]
+    for copy in copies[6:]:
+        copy.wait()
+    ds, dq = ds_ref[...], dq_ref[...]
     moved = [rows(new[i]) for i in range(3)]
     plain = moved + [rows(jac)] + [rows(new[d] * metric[d]) for d in range(3)]
     wide = right_dot(jnp.concatenate(plain, axis=0), jright_ref)
@@ -401,6 +420,17 @@
         pack_ref[NP * k : NP * k + NP] = result[k]
 
 
+def stage_kernel(pack_ref, out_ref, sem):
+    copy = pltpu.make_async_copy(pack_ref, out_ref, sem)
+    copy.start()
+    copy.wait()
+
+
+def pair_kernel(pack_ref, cross_in, out_ref):
+    out_ref[: 7 * NP] = pack_ref[...]
+    out_ref[7 * NP :] = cross_in[...]
+
+
 def chip_rows(first, second):
     return jnp.concatenate([first[:-1], (first[-1] + second[0])[None], second[1:]], axis=0)
 
@@ -413,7 +443,7 @@
     return jnp.where(even, x[:EDGE], x[ROWS - EDGE :])
 
 
-def divergence_kernel(own_ref, mate_ref, ds_ref, dq_ref, div_ref, op_ref, level_ref, cross_ref):
+def divergence_kernel(own_ref, mate_ref, ds_ref, qright_t_ref, div_ref, op_ref, level_ref, cross_ref):
     even = parity() == 0
     own, mate = own_ref[...], mate_ref[...]
     packs = [jnp.where(even, own, mate), jnp.where(even, mate, own)]
@@ -428,8 +458,7 @@
         sides.append(jnp.concatenate([(whole[0] + low[k])[None], whole[1:-1], (whole[-1] + high[k])[None]], axis=0))
     inv = 1.0 / sides[3]
     accel = [sides[d] * inv for d in range(3)]
-    div = []
-    levels = []
+    div, last, levels = [], [], []
     for layer in range(2):
         mass = parts[layer][3]
         at = (NP - 1) * layer
@@ -445,7 +474,10 @@
         sums.append(jnp.sum(rows(mass), axis=0, keepdims=True))
         sums.append(jnp.zeros((4, LANES), jnp.float32))
         levels.append(jnp.concatenate(sums, axis=0))
-        div.append(join_s(gradient_t(terms[0], terms[1], terms[2], ds_ref[...], dq_ref[...])))
+        div.append(d_a(terms[0], True) + d_s(terms[1], ds_ref[1]))
+        last.append(rows(terms[2]))
+    last = right_dot(jnp.concatenate(last, axis=0), qright_t_ref)
+    div = [join_s(x + planes(last[64 * k : 64 * k + 64])) for k, x in enumerate(div)]
     whole = chip_rows(div[0], div[1])
     div_ref[...] = whole
     cross_ref[:EDGE] = edge_rows(even, whole)
@@ -474,22 +506,31 @@
     return result
 
 
-def schwarz(half, even, inv_ref, sleft_ref, sright_ref, srback_ref, sback_ref):
-    before, after = roll(half, NP, 2), roll(half, -NP, 2)
+def schwarz(half, even, inv_ref, sleft_ref, sright_ref, srback_ref, sback_ref, scratch_ref, sum_ref):
+    wide = NP + 2
+    scratch_ref[...] = half.reshape((2 * NP + 1) * NP, LANES)
+    none = jnp.zeros((16 - wide, LANES), jnp.float32)
     columns = []
     for layer in range(2):
-        at = (NP - 1) * layer
-        columns.append(jnp.concatenate([x[at : at + NP + 2].reshape(80, LANES) for x in (half, before, after)], axis=0))
+        at = (NP - 1) * NP * layer
+        before = roll(scratch_ref[pl.ds(at + NP - 2, wide, stride=NP), :], NP, 1)
+        after = roll(scratch_ref[pl.ds(at + 1, wide, stride=NP), :], -NP, 1)
+        own = half[(NP - 1) * layer : (NP - 1) * layer + wide].reshape(wide * NP, LANES)
+        columns.append(jnp.concatenate([own, before, none, after, none], axis=0))
     spectra = left_dot(sleft_ref, jnp.concatenate(columns, axis=1))
     spectra = jnp.concatenate([spectra[:, LANES * k : LANES * k + LANES] for k in range(2)], axis=0)
-    spectra = pair_dot(right_dot(spectra, sright_ref) * inv_ref[...], srback_ref)
+    spectra = modes_dot(right_dot(spectra, sright_ref) * inv_ref[...], srback_ref)
     spectra = jnp.concatenate([spectra[MODES * k : MODES * k + MODES] for k in range(2)], axis=1)
     blocks = left_dot(sback_ref, spectra)
     z = []
     for layer in range(2):
         part = blocks[:, LANES * layer : LANES * layer + LANES]
-        part = part[:80] + roll(part[80:160], -NP, 1) + roll(part[160:], NP, 1)
-        z.append(part.reshape(NP + 2, NP, LANES))
+        sum_ref[layer] = part[:80]
+        for block, (s, shift) in enumerate(((NP - 2, -NP), (NP - 1, -NP), (0, NP), (1, NP))):
+            rows_at = pl.ds(s, wide, stride=NP)
+            start = 80 + 16 * block
+            sum_ref[layer, rows_at, :] = sum_ref[layer, rows_at, :] + roll(part[start : start + wide], shift, 1)
+        z.append(sum_ref[layer].reshape(wide, NP, LANES))
     upper = jnp.concatenate([z[0][8:] + z[1][1:3], z[1][3:]], axis=0)
     lower = jnp.concatenate([z[0][:7], z[0][7:9] + z[1][:2]], axis=0)
     return jnp.where(even, upper, lower)
@@ -513,7 +554,7 @@
     return chip_rows(parts[0], parts[1])
 
 
-def first_smooth_kernel(div_ref, received_ref, level_ref, spread_ref, lam_ref, sleft_ref, sright_ref, srback_ref, sback_ref, half_ref, inv_ref, part_ref):
+def first_smooth_kernel(div_ref, received_ref, level_ref, spread_ref, lam_ref, sleft_ref, sright_ref, srback_ref, sback_ref, half_ref, inv_ref, part_ref, scratch_ref, sum_ref):
     even = parity() == 0
     half = half_window(even, div_ref[...], received_ref)
     half_ref[...] = half
@@ -522,15 +563,15 @@
     levels = [jnp.where(even, other, own), jnp.where(even, own, other)]
     for k, inv in enumerate(inverse_levels(levels, spread_ref, lam_ref)):
         inv_ref[MODES * k : MODES * k + MODES] = inv
-    part_ref[...] = schwarz(half, even, inv_ref, sleft_ref, sright_ref, srback_ref, sback_ref)
-
-
-def smooth_kernel(step, before_ref, local_ref, received_ref, inv_ref, sleft_ref, sright_ref, srback_ref, sback_ref, own_image_ref, half_ref, part_ref):
+    part_ref[...] = schwarz(half, even, inv_ref, sleft_ref, sright_ref, srback_ref, sback_ref, scratch_ref, sum_ref)
+
+
+def smooth_kernel(step, before_ref, local_ref, received_ref, inv_ref, sleft_ref, sright_ref, srback_ref, sback_ref, own_image_ref, half_ref, part_ref, scratch_ref, sum_ref):
     even = parity() == 0
     image = half_window(even, local_ref[...], received_ref)
     half = before_ref[...] - step * image
     half_ref[...] = half
-    part_ref[...] = schwarz(half, even, inv_ref, sleft_ref, sright_ref, srback_ref, sback_ref)
+    part_ref[...] = schwarz(half, even, inv_ref, sleft_ref, sright_ref, srback_ref, sback_ref, scratch_ref, sum_ref)
     own_image_ref[...] = own_of_half(even, image)
 
 
@@ -543,31 +584,47 @@
     cross_ref[...] = edge_rows(even, local)
 
 
-def last_operator_kernel(part_ref, mate_ref, op_ref, ds_ref, qright_ref, qright_t_ref, ws_ref, div_ref, half_ref, v0_ref, v1_ref, l0_ref, l1_ref, own_ref, face_ref, sums_ref):
+def fold(parts):
+    lane = lax.broadcasted_iota(jnp.int32, (NP, LANES), 1)
+    parts = parts + [jnp.zeros((NP, LANES), jnp.float32)] * (ES - len(parts))
+    for step in (8, 16, 32, 64):
+        chosen = (lane & step) != 0
+        parts = [
+            jnp.where(chosen, b, a) + roll(jnp.where(chosen, a, b), step, 1)
+            for a, b in zip(parts[::2], parts[1::2])
+        ]
+    return parts[0]
+
+
+def early_kernel(ws_ref, div_ref, v0_ref, v1_ref, l0_ref, l1_ref, residual_ref, parts_ref):
+    ws = ws_ref[...]
+    l0, l1 = l0_ref[...], l1_ref[...]
+    residual = div_ref[...] - STEPS[0] * l0 - STEPS[1] * l1
+    residual_ref[...] = residual
+    v0, v1 = v0_ref[...], v1_ref[...]
+    for k, (left, right) in enumerate(((v0, l0), (v0, l1), (v1, l1), (v0, residual), (v1, residual))):
+        parts_ref[k] = jnp.sum(left * right, axis=0) * ws
+
+
+def last_operator_kernel(part_ref, mate_ref, op_ref, ds_ref, qright_ref, qright_t_ref, ws_ref, residual_ref, parts_ref, v0_ref, v1_ref, v_ref, local_ref, face_ref, sums_ref):
     even = parity() == 0
-    v2 = join_sides(even, part_ref[...], mate_ref[...])
-    l2 = operate(v2, op_ref, ds_ref, qright_ref, qright_t_ref)
-    face_ref[...] = jnp.where(even, l2[0], l2[-1])
-    v = [v0_ref[...], v1_ref[...], v2]
-    images = [l0_ref[...], l1_ref[...], l2]
-    residual = div_ref[...] - STEPS[0] * images[0] - STEPS[1] * images[1]
+    v = join_sides(even, part_ref[...], mate_ref[...])
+    v_ref[...] = v
+    local = operate(v, op_ref, ds_ref, qright_ref, qright_t_ref)
+    local_ref[...] = local
+    face_ref[...] = jnp.where(even, local[0], local[-1])
     ws = ws_ref[...]
-    pairs = [(v[i], images[j]) for i, j in ((0, 0), (0, 1), (0, 2), (1, 1), (1, 2), (2, 2))]
-    pairs.extend((v[i], residual) for i in range(3))
-    lane = lax.broadcasted_iota(jnp.int32, (NP, LANES), 1)
-    line = jnp.zeros((NP, LANES), jnp.float32)
-    for k, (left, right) in enumerate(pairs):
-        line = jnp.where(lane == k, jnp.sum(jnp.sum(left * right, axis=0) * ws), line)
+    new = [jnp.sum(x * y, axis=0) * ws for x, y in ((v0_ref[...], local), (v1_ref[...], local), (v, local), (v, residual_ref[...]))]
+    p = [parts_ref[k] for k in range(5)]
+    folded = fold([p[0], p[1], new[0], p[2], new[1], new[2], p[3], p[4], new[3]])
+    line = jnp.broadcast_to(jnp.sum(folded, axis=0, keepdims=True), (NP, LANES))
     for k in range(sums_ref.shape[0] // NP):
         sums_ref[NP * k : NP * k + NP] = line
-    for k, x in enumerate((v[0], v[1], v2, l2)):
-        own_ref[k] = own_rows(even, x)
-    own_ref[4] = own_of_half(even, half_ref[...])
-
-
-def to_output(x, order_ref, scratch_ref):
-    scratch_ref[...] = rows(x)
-    by_s = [scratch_ref[pl.ds(s, NP, stride=NP), :] for s in range(NP - 1)]
+
+
+def to_output(x, order_ref, scratch_ref, slot):
+    scratch_ref[slot] = rows(x)
+    by_s = [scratch_ref[slot, pl.ds(s, NP, stride=NP), :] for s in range(NP - 1)]
     tiles = []
     for tile in range(7):
         index, s = order_ref[0, tile], order_ref[1, tile]
@@ -578,26 +635,38 @@
     return jnp.concatenate(tiles, axis=1)
 
 
-def combine_kernel(sums_ref, face_ref, own_ref, w0_ref, w1_ref, order_ref, p_ref, r_ref, first_ref, second_ref):
+def layout_kernel(face_ref, v0_ref, v1_ref, v2_ref, half_ref, w0_ref, w1_ref, local_ref, order_ref, out_ref, scratch_ref):
     even = parity() == 0
     face = face_ref[...]
-    local = own_ref[3]
+    local = own_rows(even, local_ref[...])
     first = jnp.where(even, local[0] + face, local[0])
     last = jnp.where(even, local[-1], local[-1] + face)
     w2 = jnp.concatenate([first[None], local[1:-1], last[None]], axis=0)
+    fields = [own_rows(even, x[...]) for x in (v0_ref, v1_ref, v2_ref)]
+    fields.extend((own_of_half(even, half_ref[...]), w0_ref[...], w1_ref[...], w2))
+    for k, x in enumerate(fields):
+        out_ref[k] = to_output(x, order_ref, scratch_ref, k)
+
+
+def combine_kernel(sums_ref, fields_ref, p_ref, r_ref):
     line = jnp.sum(sums_ref[...], axis=0, keepdims=True)
-    h00, h01, h02, h11, h12, h22, g0, g1, g2 = [line[:, k : k + 1] for k in range(9)]
-    m1, m2 = h01 / h00, h02 / h00
+    for step in (4, 2, 1):
+        line = line + roll(line, -step, 1)
+    shape = (NP, LANES)
+    h00, h01, h02, h11, h12, h22, g0, g1, g2 = [jnp.broadcast_to(line[:, NP * k : NP * k + 1], shape) for k in range(9)]
+    scale = 1.0 / h00
+    m1, m2, m0 = h01 * scale, h02 * scale, g0 * scale
     k11, k12, k22 = h11 - m1 * h01, h12 - m1 * h02, h22 - m2 * h02
     f1, f2 = g1 - m1 * g0, g2 - m2 * g0
-    n2 = k12 / k11
+    second = 1.0 / k11
+    n2 = k12 * second
     c2 = (f2 - n2 * f1) / (k22 - n2 * k12)
-    c1 = (f1 - k12 * c2) / k11
-    c0 = (g0 - h01 * c1 - h02 * c2) / h00
-    pressure = (c0 + STEPS[0])[None] * own_ref[0] + (c1 + STEPS[1])[None] * own_ref[1] + c2[None] * own_ref[2]
-    residual = own_ref[4] - (c0[None] * w0_ref[...] + c1[None] * w1_ref[...] + c2[None] * w2)
-    p_ref[...] = to_output(pressure, order_ref, first_ref)
-    r_ref[...] = to_output(residual, order_ref, second_ref)
+    c1 = f1 * second - n2 * c2
+    c0 = m0 - m1 * c1 - m2 * c2
+    for tile in range(7):
+        x = [fields_ref[k, :, LANES * tile : LANES * tile + LANES] for k in range(7)]
+        p_ref[:, LANES * tile : LANES * tile + LANES] = (c0 + STEPS[0]) * x[0] + (c1 + STEPS[1]) * x[1] + c2 * x[2]
+        r_ref[:, LANES * tile : LANES * tile + LANES] = x[3] - (c0 * x[4] + c1 * x[5] + c2 * x[6])
 
 
 def call(kernel, shapes, *args, scratch=()):
@@ -611,8 +680,14 @@
     )(*args)
 
 
+SMOOTH_SCRATCH = (
+    pltpu.VMEM(((2 * NP + 1) * NP, LANES), jnp.float32),
+    pltpu.VMEM((2, (NP + 2) * NP, LANES), jnp.float32),
+)
+
+
 def call_forcing(*args):
-    shapes = [(7 * NP + 4, NP, LANES), (4, NP, LANES)]
+    shapes = [(7 * NP, NP, LANES), (4, NP, LANES)]
     scratch = [pltpu.SMEM(args[0].shape, jnp.int32)]
     scratch.extend(pltpu.VMEM(x.shape, x.dtype) for x in args[1:])
     scratch.append(pltpu.SemaphoreType.DMA((len(args),)))
@@ -643,12 +718,21 @@
     pack, cross = call_forcing(
         element_slot, velocity, conv_past, metric, jacobian, *(t[key] for key in FORCING_TABLES)
     )
-    own = lax.dynamic_update_slice(pack, swap_cross(cross, count), (7 * NP, 0, 0))
+    cross = swap_cross(cross, count)
+    pack = pl.pallas_call(
+        stage_kernel,
+        out_shape=jax.ShapeDtypeStruct(pack.shape, jnp.float32),
+        in_specs=[pl.BlockSpec(memory_space=pltpu.HBM)],
+        out_specs=pl.BlockSpec(memory_space=pltpu.VMEM),
+        scratch_shapes=[pltpu.SemaphoreType.DMA(())],
+        compiler_params=PARAMS,
+    )(pack)
+    (own,) = call(pair_kernel, [(7 * NP + 4, NP, LANES)], pack, cross)
     mate = swap_inner(own, count)
     div, op, level, cross = call(
         divergence_kernel,
         [chip, (2, 4) + field, (NP, LANES), (EDGE + 1, NP, LANES)],
-        own, mate, t["ds"], t["dq"],
+        own, mate, t["ds"], t["qright_t"],
     )
     solve = (t["sleft"], t["sright"], t["srback"], t["sback"])
     tables = (op, t["ds"], t["qright"], t["qright_t"])
@@ -656,6 +740,7 @@
         first_smooth_kernel,
         [half_shape, (2 * MODES, ES * (NP + 2)), edge],
         div, swap_cross(cross, count), level, t["spread"], t["lam"], *solve,
+        scratch=SMOOTH_SCRATCH,
     )
     vectors, locals_, images = [], [], []
     for step in STEPS:
@@ -666,25 +751,27 @@
             functools.partial(smooth_kernel, step),
             [field, half_shape, edge],
             half, local, swap_cross(cross, count), inv, *solve,
+            scratch=SMOOTH_SCRATCH,
         )
         vectors.append(v)
         locals_.append(local)
         images.append(image)
-    own, face, sums = call(
+    residual, parts = call(
+        early_kernel, [chip, (5, NP, LANES)], t["ws"], div, *vectors, *locals_
+    )
+    v, local, face, sums = call(
         last_operator_kernel,
-        [(5,) + field, (NP, LANES), (count // 2, LANES)],
-        part, swap_inner(part, count), *tables, t["ws"], div, half, *vectors, *locals_,
+        [chip, chip, (NP, LANES), (count // 2, LANES)],
+        part, swap_inner(part, count), *tables, t["ws"], residual, parts, *vectors,
     )
     sums = lax.all_to_all(sums, "dom", 0, 0, tiled=True, axis_index_groups=team_groups(count))
-    face = swap_cross(face, count)
-    return tuple(
-        call(
-            combine_kernel,
-            [(NP, 896), (NP, 896)],
-            sums, face, own, *images, t["order"],
-            scratch=[pltpu.VMEM((NP * NP, LANES), jnp.float32)] * 2,
-        )
+    (fields,) = call(
+        layout_kernel,
+        [(7, NP, 896)],
+        swap_cross(face, count), *vectors, v, half, *images, local, t["order"],
+        scratch=[pltpu.VMEM((7, NP * NP, LANES), jnp.float32)],
     )
+    return tuple(call(combine_kernel, [(NP, 896), (NP, 896)], sums, fields))
 
 
 def solution(mesh):

time: 104 us -> 101 us (0.971)
  waiting for transfers between devices: 25.7 us -> 23.6 us
    ppermute x5, waiting for transfers between devices: 14.7 us -> 13.5 us  [swap_cross(): return lax.ppermute(x, 'dom', pairs)]
    pallas_call x8 -> x11, Pallas kernels: 7.67 us -> 7.27 us  [call(): pl.pallas_call(kernel, out_shape=[jax.ShapeDtypeStruct(shape, jnp.float32...]
  transfers between devices with their start and end apart: 10 -> 10, of which waited for: 10 -> 10; matrix products, arithmetic and copies ran while one was open for 0% -> 0% of each run, Pallas kernels for 0% -> 1%
where the time goes in v5:
time: 101 us; the launch traced here: 100 us
  starting transfers between devices  63.2 us (63%)
  waiting for transfers between devices  23.6 us (23%)
  Pallas kernels  11.8 us (12%)
    ppermute x4, starting transfers between devices, swap_inner(): return lax.ppermute(x, 'dom', [(i, i ^ 1) for i in range(count)])  37.5 us
    ppermute x5, waiting for transfers between devices, swap_cross(): return lax.ppermute(x, 'dom', pairs)  13.5 us
    all_to_all x1, starting transfers between devices, shards(): lax.all_to_all(sums, 'dom', 0, 0, tiled=True, axis_index_groups=team_grou...  13.1 us
    ppermute x5, starting transfers between devices, swap_cross(): return lax.ppermute(x, 'dom', pairs)  12.6 us
    pallas_call x11, Pallas kernels, call(): pl.pallas_call(kernel, out_shape=[jax.ShapeDtypeStruct(shape, jnp.float32...  7.27 us
    all_to_all x1, waiting for transfers between devices, shards(): lax.all_to_all(sums, 'dom', 0, 0, tiled=True, axis_index_groups=team_grou...  6.51 us
    pallas_call x1, Pallas kernels, call_forcing(): pl.pallas_call(forcing_kernel, out_shape=[jax.ShapeDtypeStruct(shape, jnp...  4.28 us
    ppermute x4, waiting for transfers between devices, swap_inner(): return lax.ppermute(x, 'dom', [(i, i ^ 1) for i in range(count)])  3.59 us
  transfers between devices with their start and end apart: 10, of which 10 were waited for; matrix products, arithmetic and copies ran while one was open for 0% of the time, Pallas kernels for 1%

profile of v5, /device:TPU:1, one launch (start us, length us, event | category | flops | bytes accessed | tf_op | source)
XLA Modules:
  0.0 100.5 jit_solution(13617887358042292857)
XLA Ops:
  0.6 4.3 %shard_map.266 = (f32[56,8,128]{2,1,0:T(8,128)}, f32[4,8,128]{2,1,0:T(8,128)}) custom-call(s32[16]{0:T(128)} %slot_in.1, f32[3,3,16,512]{3,2,1,0:T(8,128)} %vel_in.1, f32[2,3,16,512]{3,2,1,0:T(8,128)} %past_in.1, f32[3,16,512]{2,1,0:T(8,128)} %metric_in.1, f32[16,512]{1,0:T(8,128)} %jac_in.1, f32[1,512]{1,0:T(1,128)} %constant.48.clone.w3_in, ...), custom_call_target="tpu_custom_call" | custom-call | tf_op jit(solution)/shard_map/pallas_call | solution.py:694
  4.9 4.6 %collective-permute-start = (f32[4,8,128]{2,1,0:T(8,128)}, f32[4,8,128]{2,1,0:T(8,128)S(1)}, u32[]{:S(2)}, u32[]{:S(2)}) collective-permute-start(f32[4,8,128]{2,1,0:T(8,128)} %get-tuple-element.30), channel_id=1, source_target_pairs={{0,511},{1,2},{2,1},{3,4},{4,3},{5,6},{6,5},{7,8},{8,7},{9,10},{10... | collective-permute-start | bytes 49160 | tf_op jit(solution)/shard_map/ppermute | solution.py:330
  9.5 0.0 copy-start.8
  9.5 0.9 copy-done.8
  10.5 0.0 copy-start.9
  10.5 0.3 shard_map.267.pack_ref
  10.8 0.0 copy-start.1
  10.8 0.0 copy-start.2
  10.8 0.4 collective-permute-done.cross_in
  11.1 0.0 copy-start.7
  11.2 0.0 copy-start
  11.2 0.0 copy-start.3
  11.2 0.0 copy-start.4
  11.2 0.0 copy-start.6
  11.2 14.4 %collective-permute-start.1 = (f32[60,8,128]{2,1,0:T(8,128)S(1)}, f32[60,8,128]{2,1,0:T(8,128)S(1)}, u32[]{:S(2)}, u32[]{:S(2)}) collective-permute-start(f32[60,8,128]{2,1,0:T(8,128)S(1)} %shard_map.268.own_ref), channel_id=1, source_target_pairs={{0,1},{1,0},{2,3},{3,2},{4,5},{5,4},{6,7},{7,6},{8,9},{9,8},{10,11... | collective-permute-start | bytes 737288 | tf_op jit(solution)/shard_map/ppermute | solution.py:325
  25.7 1.1 %collective-permute-done.1.mate_ref = f32[60,8,128]{2,1,0:T(8,128)S(1)} collective-permute-done((f32[60,8,128]{2,1,0:T(8,128)S(1)}, f32[60,8,128]{2,1,0:T(8,128)S(1)}, u32[]{:S(2)}, u32[]{:S(2)}) %collective-permute-start.1) | collective-permute-done | bytes 245792 | tf_op jit(solution)/shard_map/ppermute | solution.py:325
  26.8 0.0 copy-done.1
  26.8 0.0 copy-done.2
  26.8 0.3 shard_map.269
  27.1 1.9 %collective-permute-start.2 = (f32[10,8,128]{2,1,0:T(8,128)S(1)}, f32[10,8,128]{2,1,0:T(8,128)S(1)}, u32[]{:S(2)}, u32[]{:S(2)}) collective-permute-start(f32[10,8,128]{2,1,0:T(8,128)S(1)} %get-tuple-element.32), channel_id=1, source_target_pairs={{0,511},{1,2},{2,1},{3,4},{4,3},{5,6},{6,5},{7,8},{8,7},{9,10},{10... | collective-permute-start | bytes 122888 | tf_op jit(solution)/shard_map/ppermute | solution.py:330
  29.1 3.4 %collective-permute-done.2.received_ref = f32[10,8,128]{2,1,0:T(8,128)S(1)} collective-permute-done((f32[10,8,128]{2,1,0:T(8,128)S(1)}, f32[10,8,128]{2,1,0:T(8,128)S(1)}, u32[]{:S(2)}, u32[]{:S(2)}) %collective-permute-start.2) | collective-permute-done | bytes 40992 | tf_op jit(solution)/shard_map/ppermute | solution.py:330
  32.5 0.0 copy-done.9
  32.5 0.0 copy-done.7
  32.5 0.0 copy-done
  32.5 0.0 copy-done.3
  32.5 0.0 copy-done.4
  32.5 0.0 copy-done.6
  32.5 0.0 copy-start.5
  32.5 1.0 %shard_map.270 = (f32[17,8,128]{2,1,0:T(8,128)S(1)}, f32[224,160]{1,0:T(8,128)S(1)}, f32[9,8,128]{2,1,0:T(8,128)S(1)}) custom-call(f32[15,8,128]{2,1,0:T(8,128)S(1)} %get-tuple-element.31.div_ref, f32[10,8,128]{2,1,0:T(8,128)S(1)} %collective-permute-done.2.received_ref, f32[8,128]{1,0:T(8,128)S(1)} %get-tuple-element.33.level_ref, ...), custom_call_target="tpu_custom_call" | custom-call | tf_op jit(solution)/shard_map/pallas_call | solution.py:673
  33.5 7.7 %collective-permute-start.3 = (f32[9,8,128]{2,1,0:T(8,128)S(1)}, f32[9,8,128]{2,1,0:T(8,128)S(1)}, u32[]{:S(2)}, u32[]{:S(2)}) collective-permute-start(f32[9,8,128]{2,1,0:T(8,128)S(1)} %get-tuple-element.35.part_ref), channel_id=1, source_target_pairs={{0,1},{1,0},{2,3},{3,2},{4,5},{5,4},{6,7},{7,6},{8,9},{9,8},{10,11... | collective-permute-start | bytes 110600 | tf_op jit(solution)/shard_map/ppermute | solution.py:325
  41.3 0.8 collective-permute-done.3.mate_ref
  42.1 0.0 copy-done.5
  42.1 0.4 shard_map.271
  42.5 1.9 %collective-permute-start.4 = (f32[9,8,128]{2,1,0:T(8,128)S(1)}, f32[9,8,128]{2,1,0:T(8,128)S(1)}, u32[]{:S(2)}, u32[]{:S(2)}) collective-permute-start(f32[9,8,128]{2,1,0:T(8,128)S(1)} %get-tuple-element.38), channel_id=1, source_target_pairs={{0,511},{1,2},{2,1},{3,4},{4,3},{5,6},{6,5},{7,8},{8,7},{9,10},{10... | collective-permute-start | bytes 110600 | tf_op jit(solution)/shard_map/ppermute | solution.py:330
  44.5 3.3 %collective-permute-done.4.received_ref = f32[9,8,128]{2,1,0:T(8,128)S(1)} collective-permute-done((f32[9,8,128]{2,1,0:T(8,128)S(1)}, f32[9,8,128]{2,1,0:T(8,128)S(1)}, u32[]{:S(2)}, u32[]{:S(2)}) %collective-permute-start.4) | collective-permute-done | bytes 36896 | tf_op jit(solution)/shard_map/ppermute | solution.py:330
  47.8 1.0 shard_map.272
  48.8 7.7 %collective-permute-start.5 = (f32[9,8,128]{2,1,0:T(8,128)S(1)}, f32[9,8,128]{2,1,0:T(8,128)S(1)}, u32[]{:S(2)}, u32[]{:S(2)}) collective-permute-start(f32[9,8,128]{2,1,0:T(8,128)S(1)} %get-tuple-element.41.part_ref), channel_id=1, source_target_pairs={{0,1},{1,0},{2,3},{3,2},{4,5},{5,4},{6,7},{7,6},{8,9},{9,8},{10,11... | collective-permute-start | bytes 110600 | tf_op jit(solution)/shard_map/ppermute | solution.py:325
  56.5 0.8 collective-permute-done.5.mate_ref
  57.4 0.4 shard_map.273
  57.8 1.9 %collective-permute-start.6 = (f32[9,8,128]{2,1,0:T(8,128)S(1)}, f32[9,8,128]{2,1,0:T(8,128)S(1)}, u32[]{:S(2)}, u32[]{:S(2)}) collective-permute-start(f32[9,8,128]{2,1,0:T(8,128)S(1)} %get-tuple-element.43), channel_id=1, source_target_pairs={{0,511},{1,2},{2,1},{3,4},{4,3},{5,6},{6,5},{7,8},{8,7},{9,10},{10... | collective-permute-start | bytes 110600 | tf_op jit(solution)/shard_map/ppermute | solution.py:330
  59.7 3.3 %collective-permute-done.6.received_ref = f32[9,8,128]{2,1,0:T(8,128)S(1)} collective-permute-done((f32[9,8,128]{2,1,0:T(8,128)S(1)}, f32[9,8,128]{2,1,0:T(8,128)S(1)}, u32[]{:S(2)}, u32[]{:S(2)}) %collective-permute-start.6) | collective-permute-done | bytes 36896 | tf_op jit(solution)/shard_map/ppermute | solution.py:330
  63.1 1.0 shard_map.274
  64.1 0.0 copy-start.11
  64.1 7.7 %collective-permute-start.7 = (f32[9,8,128]{2,1,0:T(8,128)S(1)}, f32[9,8,128]{2,1,0:T(8,128)S(1)}, u32[]{:S(2)}, u32[]{:S(2)}) collective-permute-start(f32[9,8,128]{2,1,0:T(8,128)S(1)} %get-tuple-element.44.part_ref), channel_id=1, source_target_pairs={{0,1},{1,0},{2,3},{3,2},{4,5},{5,4},{6,7},{7,6},{8,9},{9,8},{10,11... | collective-permute-start | bytes 110600 | tf_op jit(solution)/shard_map/ppermute | solution.py:325
  71.8 0.0 copy-done.11
  71.8 0.8 collective-permute-done.7.mate_ref
  72.6 1.4 %shard_map.276 = (f32[15,8,128]{2,1,0:T(8,128)S(1)}, f32[15,8,128]{2,1,0:T(8,128)S(1)}, f32[8,128]{1,0:T(8,128)S(1)}, f32[256,128]{1,0:T(8,128)}) custom-call(f32[9,8,128]{2,1,0:T(8,128)S(1)} %get-tuple-element.44.part_ref, f32[9,8,128]{2,1,0:T(8,128)S(1)} %collective-permute-done.7.mate_ref, f32[2,4,8,8,128]{4,3,2,1,0:T(8,128)S(1)} %get-tuple-element.36.op_ref, ...), custom_call_target="tpu_custom_call" | custom-call | tf_op jit(solution)/shard_map/pallas_call | solution.py:673
  74.0 0.0 copy-start.10
  74.0 13.1 %all-to-all-start = ((f32[256,1,128]{2,1,0:T(1,128)}), f32[256,1,128]{2,1,0:T(1,128)S(1)}, u32[]{:S(2)}, u32[]{:S(2)}) async-start(f32[256,1,128]{2,1,0:T(1,128)} %bitcast.1), calls=%async_computation | async-start | bytes 262144 | tf_op jit(solution)/shard_map/all_to_all | solution.py:767
  87.1 2.2 %collective-permute-start.8 = (f32[8,128]{1,0:T(8,128)S(1)}, f32[8,128]{1,0:T(8,128)S(1)}, u32[]{:S(2)}, u32[]{:S(2)}) collective-permute-start(f32[8,128]{1,0:T(8,128)S(1)} %get-tuple-element.50), channel_id=1, source_target_pairs={{0,511},{1,2},{2,1},{3,4},{4,3},{5,6},{6,5},{7,8},{8,7},{9,10},{10... | collective-permute-start | bytes 12296 | tf_op jit(solution)/shard_map/ppermute | solution.py:330
  89.4 3.0 %collective-permute-done.8.face_ref = f32[8,128]{1,0:T(8,128)S(1)} collective-permute-done((f32[8,128]{1,0:T(8,128)S(1)}, f32[8,128]{1,0:T(8,128)S(1)}, u32[]{:S(2)}, u32[]{:S(2)}) %collective-permute-start.8) | collective-permute-done | bytes 4128 | tf_op jit(solution)/shard_map/ppermute | solution.py:330
  92.4 0.0 copy-done.10
  92.4 0.6 shard_map.277.fields_ref
  93.0 6.5 %all-to-all-done = f32[256,1,128]{2,1,0:T(1,128)S(1)} async-done(((f32[256,1,128]{2,1,0:T(1,128)}), f32[256,1,128]{2,1,0:T(1,128)S(1)}, u32[]{:S(2)}, u32[]{:S(2)}) %all-to-all-start) | async-done | bytes 131104 | tf_op jit(solution)/shard_map/all_to_all | solution.py:767
  99.5 1.0 shard_map.278
  (2 shorter events, 0.1 us)
Async XLA Ops:
  4.9 6.2 %collective-permute-start = (f32[4,8,128]{2,1,0:T(8,128)}, f32[4,8,128]{2,1,0:T(8,128)S(1)}, u32[]{:S(2)}, u32[]{:S(2)}) collective-permute-start(f32[4,8,128]{2,1,0:T(8,128)} %get-tuple-element.30), channel_id=1, source_target_pairs={{0,511},{1,2},{2,1},{3,4},{4,3},{5,6},{6,5},{7,8},{8,7},{9,10},{10... | collective-permute-start | bytes 49160 | tf_op jit(solution)/shard_map/ppermute | solution.py:330
  9.5 0.9 copy-start.8
  10.5 22.0 %copy-start.9 = (f32[128,160]{1,0:T(8,128)S(1)}, f32[128,160]{1,0:T(8,128)}, u32[]{:S(2)}) copy-start(f32[128,160]{1,0:T(8,128)} %constant.63.clone.spread_ref) | copy-start | bytes 245764
  10.8 16.0 %copy-start.1 = (f32[2,8,8,128]{3,2,1,0:T(8,128)S(1)}, f32[2,8,8,128]{3,2,1,0:T(8,128)}, u32[]{:S(2)}) copy-start(f32[2,8,8,128]{3,2,1,0:T(8,128)} %constant.44.clone.ds_in.ds_ref) | copy-start | bytes 196612
  10.8 16.0 %copy-start.2 = (bf16[384,128]{1,0:T(8,128)(2,1)S(1)}, bf16[384,128]{1,0:T(8,128)(2,1)}, u32[]{:S(2)}) copy-start(bf16[384,128]{1,0:T(8,128)(2,1)} %constant.47.clone.qright_t_ref) | copy-start | bytes 294916
  11.1 21.3 %copy-start.7 = (f32[3,112,160]{2,1,0:T(8,128)S(1)}, f32[3,112,160]{2,1,0:T(8,128)}, u32[]{:S(2)}) copy-start(f32[3,112,160]{2,1,0:T(8,128)} %constant.64.clone.lam_ref) | copy-start | bytes 645124
  11.2 21.3 %copy-start = (bf16[384,160]{1,0:T(8,128)(2,1)S(1)}, bf16[384,160]{1,0:T(8,128)(2,1)}, u32[]{:S(2)}) copy-start(bf16[384,160]{1,0:T(8,128)(2,1)} %constant.61.clone.sright_ref) | copy-start | bytes 368644
  11.2 21.3 %copy-start.3 = (bf16[480,128]{1,0:T(8,128)(2,1)S(1)}, bf16[480,128]{1,0:T(8,128)(2,1)}, u32[]{:S(2)}) copy-start(bf16[480,128]{1,0:T(8,128)(2,1)} %constant.62.clone.srback_ref) | copy-start | bytes 368644
  11.2 21.3 %copy-start.4 = (bf16[144,336]{1,0:T(8,128)(2,1)S(1)}, bf16[144,336]{1,0:T(8,128)(2,1)}, u32[]{:S(2)}) copy-start(bf16[144,336]{1,0:T(8,128)(2,1)} %constant.60.clone.sback_ref) | copy-start | bytes 290308
  11.2 21.3 %copy-start.6 = (bf16[112,336]{1,0:T(8,128)(2,1)S(1)}, bf16[112,336]{1,0:T(8,128)(2,1)}, u32[]{:S(2)}) copy-start(bf16[112,336]{1,0:T(8,128)(2,1)} %constant.59.clone.sleft_ref) | copy-start | bytes 225796
  11.2 15.6 %collective-permute-start.1 = (f32[60,8,128]{2,1,0:T(8,128)S(1)}, f32[60,8,128]{2,1,0:T(8,128)S(1)}, u32[]{:S(2)}, u32[]{:S(2)}) collective-permute-start(f32[60,8,128]{2,1,0:T(8,128)S(1)} %shard_map.268.own_ref), channel_id=1, source_target_pairs={{0,1},{1,0},{2,3},{3,2},{4,5},{5,4},{6,7},{7,6},{8,9},{9,8},{10,11... | collective-permute-start | bytes 737288 | tf_op jit(solution)/shard_map/ppermute | solution.py:325
  27.1 5.3 %collective-permute-start.2 = (f32[10,8,128]{2,1,0:T(8,128)S(1)}, f32[10,8,128]{2,1,0:T(8,128)S(1)}, u32[]{:S(2)}, u32[]{:S(2)}) collective-permute-start(f32[10,8,128]{2,1,0:T(8,128)S(1)} %get-tuple-element.32), channel_id=1, source_target_pairs={{0,511},{1,2},{2,1},{3,4},{4,3},{5,6},{6,5},{7,8},{8,7},{9,10},{10... | collective-permute-start | bytes 122888 | tf_op jit(solution)/shard_map/ppermute | solution.py:330
  32.5 9.6 %copy-start.5 = (bf16[384,128]{1,0:T(8,128)(2,1)S(1)}, bf16[384,128]{1,0:T(8,128)(2,1)}, u32[]{:S(2)}) copy-start(bf16[384,128]{1,0:T(8,128)(2,1)} %constant.46.clone.qright_ref) | copy-start | bytes 294916
  33.5 8.6 %collective-permute-start.3 = (f32[9,8,128]{2,1,0:T(8,128)S(1)}, f32[9,8,128]{2,1,0:T(8,128)S(1)}, u32[]{:S(2)}, u32[]{:S(2)}) collective-permute-start(f32[9,8,128]{2,1,0:T(8,128)S(1)} %get-tuple-element.35.part_ref), channel_id=1, source_target_pairs={{0,1},{1,0},{2,3},{3,2},{4,5},{5,4},{6,7},{7,6},{8,9},{9,8},{10,11... | collective-permute-start | bytes 110600 | tf_op jit(solution)/shard_map/ppermute | solution.py:325
  42.5 5.3 %collective-permute-start.4 = (f32[9,8,128]{2,1,0:T(8,128)S(1)}, f32[9,8,128]{2,1,0:T(8,128)S(1)}, u32[]{:S(2)}, u32[]{:S(2)}) collective-permute-start(f32[9,8,128]{2,1,0:T(8,128)S(1)} %get-tuple-element.38), channel_id=1, source_target_pairs={{0,511},{1,2},{2,1},{3,4},{4,3},{5,6},{6,5},{7,8},{8,7},{9,10},{10... | collective-permute-start | bytes 110600 | tf_op jit(solution)/shard_map/ppermute | solution.py:330
  48.8 8.5 %collective-permute-start.5 = (f32[9,8,128]{2,1,0:T(8,128)S(1)}, f32[9,8,128]{2,1,0:T(8,128)S(1)}, u32[]{:S(2)}, u32[]{:S(2)}) collective-permute-start(f32[9,8,128]{2,1,0:T(8,128)S(1)} %get-tuple-element.41.part_ref), channel_id=1, source_target_pairs={{0,1},{1,0},{2,3},{3,2},{4,5},{5,4},{6,7},{7,6},{8,9},{9,8},{10,11... | collective-permute-start | bytes 110600 | tf_op jit(solution)/shard_map/ppermute | solution.py:325
  57.8 5.3 %collective-permute-start.6 = (f32[9,8,128]{2,1,0:T(8,128)S(1)}, f32[9,8,128]{2,1,0:T(8,128)S(1)}, u32[]{:S(2)}, u32[]{:S(2)}) collective-permute-start(f32[9,8,128]{2,1,0:T(8,128)S(1)} %get-tuple-element.43), channel_id=1, source_target_pairs={{0,511},{1,2},{2,1},{3,4},{4,3},{5,6},{6,5},{7,8},{8,7},{9,10},{10... | collective-permute-start | bytes 110600 | tf_op jit(solution)/shard_map/ppermute | solution.py:330
  64.1 7.7 %copy-start.11 = (f32[8,128]{1,0:T(8,128)S(1)}, f32[8,128]{1,0:T(8,128)}, u32[]{:S(2)}) copy-start(f32[8,128]{1,0:T(8,128)} %constant.65.clone.ws_ref) | copy-start | bytes 12292
  64.1 8.5 %collective-permute-start.7 = (f32[9,8,128]{2,1,0:T(8,128)S(1)}, f32[9,8,128]{2,1,0:T(8,128)S(1)}, u32[]{:S(2)}, u32[]{:S(2)}) collective-permute-start(f32[9,8,128]{2,1,0:T(8,128)S(1)} %get-tuple-element.44.part_ref), channel_id=1, source_target_pairs={{0,1},{1,0},{2,3},{3,2},{4,5},{5,4},{6,7},{7,6},{8,9},{9,8},{10,11... | collective-permute-start | bytes 110600 | tf_op jit(solution)/shard_map/ppermute | solution.py:325
  74.0 18.4 %copy-start.10 = (s32[2,7,8,128]{3,2,1,0:T(8,128)S(1)}, s32[2,7,8,128]{3,2,1,0:T(8,128)}, u32[]{:S(2)}) copy-start(s32[2,7,8,128]{3,2,1,0:T(8,128)} %constant.58.clone.order_ref) | copy-start | bytes 172036
  74.0 25.5 %all-to-all-start = ((f32[256,1,128]{2,1,0:T(1,128)}), f32[256,1,128]{2,1,0:T(1,128)S(1)}, u32[]{:S(2)}, u32[]{:S(2)}) async-start(f32[256,1,128]{2,1,0:T(1,128)} %bitcast.1), calls=%async_computation | async-start | bytes 262144 | tf_op jit(solution)/shard_map/all_to_all | solution.py:767
  87.1 5.2 %collective-permute-start.8 = (f32[8,128]{1,0:T(8,128)S(1)}, f32[8,128]{1,0:T(8,128)S(1)}, u32[]{:S(2)}, u32[]{:S(2)}) collective-permute-start(f32[8,128]{1,0:T(8,128)S(1)} %get-tuple-element.50), channel_id=1, source_target_pairs={{0,511},{1,2},{2,1},{3,4},{4,3},{5,6},{6,5},{7,8},{8,7},{9,10},{10... | collective-permute-start | bytes 12296 | tf_op jit(solution)/shard_map/ppermute | solution.py:330

commit v6 on v5

--- a/solution.py
+++ b/solution.py
@@ -517,14 +517,14 @@
         after = roll(scratch_ref[pl.ds(at + 1, wide, stride=NP), :], -NP, 1)
         own = half[(NP - 1) * layer : (NP - 1) * layer + wide].reshape(wide * NP, LANES)
         columns.append(jnp.concatenate([own, before, none, after, none], axis=0))
-    spectra = left_dot(sleft_ref, jnp.concatenate(columns, axis=1))
-    spectra = jnp.concatenate([spectra[:, LANES * k : LANES * k + LANES] for k in range(2)], axis=0)
-    spectra = modes_dot(right_dot(spectra, sright_ref) * inv_ref[...], srback_ref)
-    spectra = jnp.concatenate([spectra[MODES * k : MODES * k + MODES] for k in range(2)], axis=1)
-    blocks = left_dot(sback_ref, spectra)
+    spectra = [left_dot(sleft_ref, x) for x in columns]
+    spectra = [right_dot(x, sright_ref) for x in spectra]
+    spectra = [x * inv_ref[MODES * k : MODES * k + MODES] for k, x in enumerate(spectra)]
+    spectra = [modes_dot(x, srback_ref) for x in spectra]
+    blocks = [left_dot(sback_ref, x) for x in spectra]
     z = []
     for layer in range(2):
-        part = blocks[:, LANES * layer : LANES * layer + LANES]
+        part = blocks[layer]
         sum_ref[layer] = part[:80]
         for block, (s, shift) in enumerate(((NP - 2, -NP), (NP - 1, -NP), (0, NP), (1, NP))):
             rows_at = pl.ds(s, wide, stride=NP)
@@ -606,20 +606,32 @@
         parts_ref[k] = jnp.sum(left * right, axis=0) * ws
 
 
-def last_operator_kernel(part_ref, mate_ref, op_ref, ds_ref, qright_ref, qright_t_ref, ws_ref, residual_ref, parts_ref, v0_ref, v1_ref, v_ref, local_ref, face_ref, sums_ref):
+def last_sums_kernel(part_ref, mate_ref, op_ref, ds_ref, qright_ref, parts_ref, l0_ref, l1_ref, residual_ref, ws_ref, v_ref, sums_ref):
     even = parity() == 0
     v = join_sides(even, part_ref[...], mate_ref[...])
     v_ref[...] = v
-    local = operate(v, op_ref, ds_ref, qright_ref, qright_t_ref)
-    local_ref[...] = local
-    face_ref[...] = jnp.where(even, local[0], local[-1])
+    layers = [v[(NP - 1) * k : (NP - 1) * k + NP] for k in range(2)]
+    gq = right_dot(jnp.concatenate([rows(x) for x in layers], axis=0), qright_ref)
+    energy = None
+    for k, x in enumerate(layers):
+        ga, gs, gq_k = d_a(x, False), d_s(x, ds_ref[0]), planes(gq[64 * k : 64 * k + 64])
+        part = op_ref[k, 0] * ga * ga + op_ref[k, 1] * gs * gs + op_ref[k, 2] * gq_k * gq_k + op_ref[k, 3] * x * x
+        part = jnp.sum(part, axis=0)
+        energy = part if energy is None else energy + part
     ws = ws_ref[...]
-    new = [jnp.sum(x * y, axis=0) * ws for x, y in ((v0_ref[...], local), (v1_ref[...], local), (v, local), (v, residual_ref[...]))]
+    new = [jnp.sum(x[...] * v, axis=0) * ws for x in (l0_ref, l1_ref, residual_ref)]
     p = [parts_ref[k] for k in range(5)]
-    folded = fold([p[0], p[1], new[0], p[2], new[1], new[2], p[3], p[4], new[3]])
+    folded = fold([p[0], p[1], new[0], p[2], new[1], energy, p[3], p[4], new[2]])
     line = jnp.broadcast_to(jnp.sum(folded, axis=0, keepdims=True), (NP, LANES))
     for k in range(sums_ref.shape[0] // NP):
         sums_ref[NP * k : NP * k + NP] = line
+
+
+def last_operator_kernel(v_ref, op_ref, ds_ref, qright_ref, qright_t_ref, local_ref, face_ref):
+    even = parity() == 0
+    local = operate(v_ref[...], op_ref, ds_ref, qright_ref, qright_t_ref)
+    local_ref[...] = local
+    face_ref[...] = jnp.where(even, local[0], local[-1])
 
 
 def to_output(x, order_ref, scratch_ref, slot):
@@ -759,12 +771,13 @@
     residual, parts = call(
         early_kernel, [chip, (5, NP, LANES)], t["ws"], div, *vectors, *locals_
     )
-    v, local, face, sums = call(
-        last_operator_kernel,
-        [chip, chip, (NP, LANES), (count // 2, LANES)],
-        part, swap_inner(part, count), *tables, t["ws"], residual, parts, *vectors,
+    v, sums = call(
+        last_sums_kernel,
+        [chip, (count // 2, LANES)],
+        part, swap_inner(part, count), op, t["ds"], t["qright"], parts, *locals_, residual, t["ws"],
     )
     sums = lax.all_to_all(sums, "dom", 0, 0, tiled=True, axis_index_groups=team_groups(count))
+    local, face = call(last_operator_kernel, [chip, (NP, LANES)], v, *tables)
     (fields,) = call(
         layout_kernel,
         [(7, NP, 896)],

time: 101 us -> 100 us (0.990)
    pallas_call x11 -> x12, Pallas kernels: 7.27 us -> 7.19 us  [call(): pl.pallas_call(kernel, out_shape=[jax.ShapeDtypeStruct(shape, jnp.float32...]
where the time goes in v6:
time: 100 us; the launch traced here: 99.8 us
  starting transfers between devices  63.1 us (63%)
  waiting for transfers between devices  23.1 us (23%)
  Pallas kernels  11.8 us (12%)
  local copies, waits for them, and re-layouts  1 us (1%)
    ppermute x4, starting transfers between devices, swap_inner(): return lax.ppermute(x, 'dom', [(i, i ^ 1) for i in range(count)])  37.5 us
    ppermute x5, waiting for transfers between devices, swap_cross(): return lax.ppermute(x, 'dom', pairs)  13.5 us
    all_to_all x1, starting transfers between devices, shards(): lax.all_to_all(sums, 'dom', 0, 0, tiled=True, axis_index_groups=team_grou...  13 us
    ppermute x5, starting transfers between devices, swap_cross(): return lax.ppermute(x, 'dom', pairs)  12.6 us
    pallas_call x12, Pallas kernels, call(): pl.pallas_call(kernel, out_shape=[jax.ShapeDtypeStruct(shape, jnp.float32...  7.19 us
    all_to_all x1, waiting for transfers between devices, shards(): lax.all_to_all(sums, 'dom', 0, 0, tiled=True, axis_index_groups=team_grou...  6.05 us
    pallas_call x1, Pallas kernels, call_forcing(): pl.pallas_call(forcing_kernel, out_shape=[jax.ShapeDtypeStruct(shape, jnp...  4.28 us
    ppermute x4, waiting for transfers between devices, swap_inner(): return lax.ppermute(x, 'dom', [(i, i ^ 1) for i in range(count)])  3.59 us
  transfers between devices with their start and end apart: 10, of which 10 were waited for; matrix products, arithmetic and copies ran while one was open for 0% of the time, Pallas kernels for 1%

profile of v6, /device:TPU:1, one launch (start us, length us, event | category | flops | bytes accessed | tf_op | source)
XLA Modules:
  0.0 99.8 jit_solution(7267705035633580259)
XLA Ops:
  0.6 4.3 %shard_map.266 = (f32[56,8,128]{2,1,0:T(8,128)}, f32[4,8,128]{2,1,0:T(8,128)}) custom-call(s32[16]{0:T(128)} %slot_in.1, f32[3,3,16,512]{3,2,1,0:T(8,128)} %vel_in.1, f32[2,3,16,512]{3,2,1,0:T(8,128)} %past_in.1, f32[3,16,512]{2,1,0:T(8,128)} %metric_in.1, f32[16,512]{1,0:T(8,128)} %jac_in.1, f32[1,512]{1,0:T(1,128)} %constant.48.clone.w3_in, ...), custom_call_target="tpu_custom_call" | custom-call | tf_op jit(solution)/shard_map/pallas_call | solution.py:706
  4.9 4.6 %collective-permute-start = (f32[4,8,128]{2,1,0:T(8,128)}, f32[4,8,128]{2,1,0:T(8,128)S(1)}, u32[]{:S(2)}, u32[]{:S(2)}) collective-permute-start(f32[4,8,128]{2,1,0:T(8,128)} %get-tuple-element.30), channel_id=1, source_target_pairs={{0,511},{1,2},{2,1},{3,4},{4,3},{5,6},{6,5},{7,8},{8,7},{9,10},{10... | collective-permute-start | bytes 49160 | tf_op jit(solution)/shard_map/ppermute | solution.py:330
  9.5 0.0 copy-start.8
  9.5 0.9 copy-done.8
  10.5 0.0 copy-start.9
  10.5 0.3 shard_map.267.pack_ref
  10.8 0.0 copy-start
  10.8 0.0 copy-start.2
  10.8 0.4 collective-permute-done.cross_in
  11.1 0.0 copy-start.7
  11.2 0.0 copy-start.1
  11.2 0.0 copy-start.4
  11.2 0.0 copy-start.5
  11.2 0.0 copy-start.6
  11.2 14.4 %collective-permute-start.1 = (f32[60,8,128]{2,1,0:T(8,128)S(1)}, f32[60,8,128]{2,1,0:T(8,128)S(1)}, u32[]{:S(2)}, u32[]{:S(2)}) collective-permute-start(f32[60,8,128]{2,1,0:T(8,128)S(1)} %shard_map.268.own_ref), channel_id=1, source_target_pairs={{0,1},{1,0},{2,3},{3,2},{4,5},{5,4},{6,7},{7,6},{8,9},{9,8},{10,11... | collective-permute-start | bytes 737288 | tf_op jit(solution)/shard_map/ppermute | solution.py:325
  25.7 1.1 %collective-permute-done.1.mate_ref = f32[60,8,128]{2,1,0:T(8,128)S(1)} collective-permute-done((f32[60,8,128]{2,1,0:T(8,128)S(1)}, f32[60,8,128]{2,1,0:T(8,128)S(1)}, u32[]{:S(2)}, u32[]{:S(2)}) %collective-permute-start.1) | collective-permute-done | bytes 245792 | tf_op jit(solution)/shard_map/ppermute | solution.py:325
  26.8 0.0 copy-done
  26.8 0.0 copy-done.2
  26.8 0.3 shard_map.269
  27.1 1.9 %collective-permute-start.2 = (f32[10,8,128]{2,1,0:T(8,128)S(1)}, f32[10,8,128]{2,1,0:T(8,128)S(1)}, u32[]{:S(2)}, u32[]{:S(2)}) collective-permute-start(f32[10,8,128]{2,1,0:T(8,128)S(1)} %get-tuple-element.32), channel_id=1, source_target_pairs={{0,511},{1,2},{2,1},{3,4},{4,3},{5,6},{6,5},{7,8},{8,7},{9,10},{10... | collective-permute-start | bytes 122888 | tf_op jit(solution)/shard_map/ppermute | solution.py:330
  29.1 3.4 %collective-permute-done.2.received_ref = f32[10,8,128]{2,1,0:T(8,128)S(1)} collective-permute-done((f32[10,8,128]{2,1,0:T(8,128)S(1)}, f32[10,8,128]{2,1,0:T(8,128)S(1)}, u32[]{:S(2)}, u32[]{:S(2)}) %collective-permute-start.2) | collective-permute-done | bytes 40992 | tf_op jit(solution)/shard_map/ppermute | solution.py:330
  32.5 0.0 copy-done.9
  32.5 0.0 copy-done.7
  32.5 0.0 copy-done.1
  32.5 0.0 copy-done.4
  32.5 0.0 copy-done.5
  32.5 0.0 copy-done.6
  32.5 0.0 copy-start.3
  32.5 0.9 shard_map.270
  33.4 7.7 %collective-permute-start.3 = (f32[9,8,128]{2,1,0:T(8,128)S(1)}, f32[9,8,128]{2,1,0:T(8,128)S(1)}, u32[]{:S(2)}, u32[]{:S(2)}) collective-permute-start(f32[9,8,128]{2,1,0:T(8,128)S(1)} %get-tuple-element.35.part_ref), channel_id=1, source_target_pairs={{0,1},{1,0},{2,3},{3,2},{4,5},{5,4},{6,7},{7,6},{8,9},{9,8},{10,11... | collective-permute-start | bytes 110600 | tf_op jit(solution)/shard_map/ppermute | solution.py:325
  41.2 0.8 collective-permute-done.3.mate_ref
  42.0 0.0 copy-done.3
  42.0 0.4 shard_map.271
  42.4 1.9 %collective-permute-start.4 = (f32[9,8,128]{2,1,0:T(8,128)S(1)}, f32[9,8,128]{2,1,0:T(8,128)S(1)}, u32[]{:S(2)}, u32[]{:S(2)}) collective-permute-start(f32[9,8,128]{2,1,0:T(8,128)S(1)} %get-tuple-element.38), channel_id=1, source_target_pairs={{0,511},{1,2},{2,1},{3,4},{4,3},{5,6},{6,5},{7,8},{8,7},{9,10},{10... | collective-permute-start | bytes 110600 | tf_op jit(solution)/shard_map/ppermute | solution.py:330
  44.4 3.3 %collective-permute-done.4.received_ref = f32[9,8,128]{2,1,0:T(8,128)S(1)} collective-permute-done((f32[9,8,128]{2,1,0:T(8,128)S(1)}, f32[9,8,128]{2,1,0:T(8,128)S(1)}, u32[]{:S(2)}, u32[]{:S(2)}) %collective-permute-start.4) | collective-permute-done | bytes 36896 | tf_op jit(solution)/shard_map/ppermute | solution.py:330
  47.7 0.9 shard_map.272
  48.6 7.7 %collective-permute-start.5 = (f32[9,8,128]{2,1,0:T(8,128)S(1)}, f32[9,8,128]{2,1,0:T(8,128)S(1)}, u32[]{:S(2)}, u32[]{:S(2)}) collective-permute-start(f32[9,8,128]{2,1,0:T(8,128)S(1)} %get-tuple-element.41.part_ref), channel_id=1, source_target_pairs={{0,1},{1,0},{2,3},{3,2},{4,5},{5,4},{6,7},{7,6},{8,9},{9,8},{10,11... | collective-permute-start | bytes 110600 | tf_op jit(solution)/shard_map/ppermute | solution.py:325
  56.3 0.8 collective-permute-done.5.mate_ref
  57.2 0.4 shard_map.273
  57.6 1.9 %collective-permute-start.6 = (f32[9,8,128]{2,1,0:T(8,128)S(1)}, f32[9,8,128]{2,1,0:T(8,128)S(1)}, u32[]{:S(2)}, u32[]{:S(2)}) collective-permute-start(f32[9,8,128]{2,1,0:T(8,128)S(1)} %get-tuple-element.43), channel_id=1, source_target_pairs={{0,511},{1,2},{2,1},{3,4},{4,3},{5,6},{6,5},{7,8},{8,7},{9,10},{10... | collective-permute-start | bytes 110600 | tf_op jit(solution)/shard_map/ppermute | solution.py:330
  59.5 3.3 %collective-permute-done.6.received_ref = f32[9,8,128]{2,1,0:T(8,128)S(1)} collective-permute-done((f32[9,8,128]{2,1,0:T(8,128)S(1)}, f32[9,8,128]{2,1,0:T(8,128)S(1)}, u32[]{:S(2)}, u32[]{:S(2)}) %collective-permute-start.6) | collective-permute-done | bytes 36896 | tf_op jit(solution)/shard_map/ppermute | solution.py:330
  62.9 0.9 shard_map.274
  63.8 0.0 copy-start.11
  63.8 7.7 %collective-permute-start.7 = (f32[9,8,128]{2,1,0:T(8,128)S(1)}, f32[9,8,128]{2,1,0:T(8,128)S(1)}, u32[]{:S(2)}, u32[]{:S(2)}) collective-permute-start(f32[9,8,128]{2,1,0:T(8,128)S(1)} %get-tuple-element.44.part_ref), channel_id=1, source_target_pairs={{0,1},{1,0},{2,3},{3,2},{4,5},{5,4},{6,7},{7,6},{8,9},{9,8},{10,11... | collective-permute-start | bytes 110600 | tf_op jit(solution)/shard_map/ppermute | solution.py:325
  71.5 0.0 copy-done.11
  71.5 0.8 collective-permute-done.7.mate_ref
  72.3 1.2 %shard_map.276 = (f32[15,8,128]{2,1,0:T(8,128)S(1)}, f32[256,128]{1,0:T(8,128)}) custom-call(f32[9,8,128]{2,1,0:T(8,128)S(1)} %get-tuple-element.44.part_ref, f32[9,8,128]{2,1,0:T(8,128)S(1)} %collective-permute-done.7.mate_ref, f32[2,4,8,8,128]{4,3,2,1,0:T(8,128)S(1)} %get-tuple-element.36.op_ref, f32[2,8,8,128]{3,2,1,0:T(8,128)S(1)} %copy-done, ...), custom_call_target="tpu_custom_call" | custom-call | tf_op jit(solution)/shard_map/pallas_call | solution.py:685
  73.5 13.0 %all-to-all-start = ((f32[256,1,128]{2,1,0:T(1,128)}), f32[256,1,128]{2,1,0:T(1,128)S(1)}, u32[]{:S(2)}, u32[]{:S(2)}) async-start(f32[256,1,128]{2,1,0:T(1,128)} %bitcast.1), calls=%async_computation | async-start | bytes 262144 | tf_op jit(solution)/shard_map/all_to_all | solution.py:779
  86.5 0.0 copy-start.10
  86.5 0.4 shard_map.277
  87.0 2.2 %collective-permute-start.8 = (f32[8,128]{1,0:T(8,128)S(1)}, f32[8,128]{1,0:T(8,128)S(1)}, u32[]{:S(2)}, u32[]{:S(2)}) collective-permute-start(f32[8,128]{1,0:T(8,128)S(1)} %get-tuple-element.51), channel_id=1, source_target_pairs={{0,511},{1,2},{2,1},{3,4},{4,3},{5,6},{6,5},{7,8},{8,7},{9,10},{10... | collective-permute-start | bytes 12296 | tf_op jit(solution)/shard_map/ppermute | solution.py:330
  89.2 3.0 %collective-permute-done.8.face_ref = f32[8,128]{1,0:T(8,128)S(1)} collective-permute-done((f32[8,128]{1,0:T(8,128)S(1)}, f32[8,128]{1,0:T(8,128)S(1)}, u32[]{:S(2)}, u32[]{:S(2)}) %collective-permute-start.8) | collective-permute-done | bytes 4128 | tf_op jit(solution)/shard_map/ppermute | solution.py:330
  92.2 0.0 copy-done.10
  92.2 0.6 shard_map.278.fields_ref
  92.8 6.0 %all-to-all-done = f32[256,1,128]{2,1,0:T(1,128)S(1)} async-done(((f32[256,1,128]{2,1,0:T(1,128)}), f32[256,1,128]{2,1,0:T(1,128)S(1)}, u32[]{:S(2)}, u32[]{:S(2)}) %all-to-all-start) | async-done | bytes 131104 | tf_op jit(solution)/shard_map/all_to_all | solution.py:779
  98.8 1.0 shard_map.279
  (2 shorter events, 0.1 us)
Async XLA Ops:
  4.9 6.2 %collective-permute-start = (f32[4,8,128]{2,1,0:T(8,128)}, f32[4,8,128]{2,1,0:T(8,128)S(1)}, u32[]{:S(2)}, u32[]{:S(2)}) collective-permute-start(f32[4,8,128]{2,1,0:T(8,128)} %get-tuple-element.30), channel_id=1, source_target_pairs={{0,511},{1,2},{2,1},{3,4},{4,3},{5,6},{6,5},{7,8},{8,7},{9,10},{10... | collective-permute-start | bytes 49160 | tf_op jit(solution)/shard_map/ppermute | solution.py:330
  9.5 0.9 copy-start.8
  10.5 22.0 %copy-start.9 = (f32[128,160]{1,0:T(8,128)S(1)}, f32[128,160]{1,0:T(8,128)}, u32[]{:S(2)}) copy-start(f32[128,160]{1,0:T(8,128)} %constant.63.clone.spread_ref) | copy-start | bytes 245764
  10.8 16.0 %copy-start = (f32[2,8,8,128]{3,2,1,0:T(8,128)S(1)}, f32[2,8,8,128]{3,2,1,0:T(8,128)}, u32[]{:S(2)}) copy-start(f32[2,8,8,128]{3,2,1,0:T(8,128)} %constant.44.clone.ds_in.ds_ref) | copy-start | bytes 196612
  10.8 16.0 %copy-start.2 = (bf16[384,128]{1,0:T(8,128)(2,1)S(1)}, bf16[384,128]{1,0:T(8,128)(2,1)}, u32[]{:S(2)}) copy-start(bf16[384,128]{1,0:T(8,128)(2,1)} %constant.47.clone.qright_t_ref) | copy-start | bytes 294916
  11.1 21.3 %copy-start.7 = (f32[3,112,160]{2,1,0:T(8,128)S(1)}, f32[3,112,160]{2,1,0:T(8,128)}, u32[]{:S(2)}) copy-start(f32[3,112,160]{2,1,0:T(8,128)} %constant.64.clone.lam_ref) | copy-start | bytes 645124
  11.2 21.3 %copy-start.1 = (bf16[384,160]{1,0:T(8,128)(2,1)S(1)}, bf16[384,160]{1,0:T(8,128)(2,1)}, u32[]{:S(2)}) copy-start(bf16[384,160]{1,0:T(8,128)(2,1)} %constant.61.clone.sright_ref) | copy-start | bytes 368644
  11.2 21.3 %copy-start.4 = (bf16[480,128]{1,0:T(8,128)(2,1)S(1)}, bf16[480,128]{1,0:T(8,128)(2,1)}, u32[]{:S(2)}) copy-start(bf16[480,128]{1,0:T(8,128)(2,1)} %constant.62.clone.srback_ref) | copy-start | bytes 368644
  11.2 21.3 %copy-start.5 = (bf16[144,336]{1,0:T(8,128)(2,1)S(1)}, bf16[144,336]{1,0:T(8,128)(2,1)}, u32[]{:S(2)}) copy-start(bf16[144,336]{1,0:T(8,128)(2,1)} %constant.60.clone.sback_ref) | copy-start | bytes 290308
  11.2 21.3 %copy-start.6 = (bf16[112,336]{1,0:T(8,128)(2,1)S(1)}, bf16[112,336]{1,0:T(8,128)(2,1)}, u32[]{:S(2)}) copy-start(bf16[112,336]{1,0:T(8,128)(2,1)} %constant.59.clone.sleft_ref) | copy-start | bytes 225796
  11.2 15.6 %collective-permute-start.1 = (f32[60,8,128]{2,1,0:T(8,128)S(1)}, f32[60,8,128]{2,1,0:T(8,128)S(1)}, u32[]{:S(2)}, u32[]{:S(2)}) collective-permute-start(f32[60,8,128]{2,1,0:T(8,128)S(1)} %shard_map.268.own_ref), channel_id=1, source_target_pairs={{0,1},{1,0},{2,3},{3,2},{4,5},{5,4},{6,7},{7,6},{8,9},{9,8},{10,11... | collective-permute-start | bytes 737288 | tf_op jit(solution)/shard_map/ppermute | solution.py:325
  27.1 5.3 %collective-permute-start.2 = (f32[10,8,128]{2,1,0:T(8,128)S(1)}, f32[10,8,128]{2,1,0:T(8,128)S(1)}, u32[]{:S(2)}, u32[]{:S(2)}) collective-permute-start(f32[10,8,128]{2,1,0:T(8,128)S(1)} %get-tuple-element.32), channel_id=1, source_target_pairs={{0,511},{1,2},{2,1},{3,4},{4,3},{5,6},{6,5},{7,8},{8,7},{9,10},{10... | collective-permute-start | bytes 122888 | tf_op jit(solution)/shard_map/ppermute | solution.py:330
  32.5 9.5 %copy-start.3 = (bf16[384,128]{1,0:T(8,128)(2,1)S(1)}, bf16[384,128]{1,0:T(8,128)(2,1)}, u32[]{:S(2)}) copy-start(bf16[384,128]{1,0:T(8,128)(2,1)} %constant.46.clone.qright_ref) | copy-start | bytes 294916
  33.4 8.6 %collective-permute-start.3 = (f32[9,8,128]{2,1,0:T(8,128)S(1)}, f32[9,8,128]{2,1,0:T(8,128)S(1)}, u32[]{:S(2)}, u32[]{:S(2)}) collective-permute-start(f32[9,8,128]{2,1,0:T(8,128)S(1)} %get-tuple-element.35.part_ref), channel_id=1, source_target_pairs={{0,1},{1,0},{2,3},{3,2},{4,5},{5,4},{6,7},{7,6},{8,9},{9,8},{10,11... | collective-permute-start | bytes 110600 | tf_op jit(solution)/shard_map/ppermute | solution.py:325
  42.4 5.3 %collective-permute-start.4 = (f32[9,8,128]{2,1,0:T(8,128)S(1)}, f32[9,8,128]{2,1,0:T(8,128)S(1)}, u32[]{:S(2)}, u32[]{:S(2)}) collective-permute-start(f32[9,8,128]{2,1,0:T(8,128)S(1)} %get-tuple-element.38), channel_id=1, source_target_pairs={{0,511},{1,2},{2,1},{3,4},{4,3},{5,6},{6,5},{7,8},{8,7},{9,10},{10... | collective-permute-start | bytes 110600 | tf_op jit(solution)/shard_map/ppermute | solution.py:330
  48.6 8.5 %collective-permute-start.5 = (f32[9,8,128]{2,1,0:T(8,128)S(1)}, f32[9,8,128]{2,1,0:T(8,128)S(1)}, u32[]{:S(2)}, u32[]{:S(2)}) collective-permute-start(f32[9,8,128]{2,1,0:T(8,128)S(1)} %get-tuple-element.41.part_ref), channel_id=1, source_target_pairs={{0,1},{1,0},{2,3},{3,2},{4,5},{5,4},{6,7},{7,6},{8,9},{9,8},{10,11... | collective-permute-start | bytes 110600 | tf_op jit(solution)/shard_map/ppermute | solution.py:325
  57.6 5.3 %collective-permute-start.6 = (f32[9,8,128]{2,1,0:T(8,128)S(1)}, f32[9,8,128]{2,1,0:T(8,128)S(1)}, u32[]{:S(2)}, u32[]{:S(2)}) collective-permute-start(f32[9,8,128]{2,1,0:T(8,128)S(1)} %get-tuple-element.43), channel_id=1, source_target_pairs={{0,511},{1,2},{2,1},{3,4},{4,3},{5,6},{6,5},{7,8},{8,7},{9,10},{10... | collective-permute-start | bytes 110600 | tf_op jit(solution)/shard_map/ppermute | solution.py:330
  63.8 7.7 %copy-start.11 = (f32[8,128]{1,0:T(8,128)S(1)}, f32[8,128]{1,0:T(8,128)}, u32[]{:S(2)}) copy-start(f32[8,128]{1,0:T(8,128)} %constant.65.clone.ws_ref) | copy-start | bytes 12292
  63.8 8.5 %collective-permute-start.7 = (f32[9,8,128]{2,1,0:T(8,128)S(1)}, f32[9,8,128]{2,1,0:T(8,128)S(1)}, u32[]{:S(2)}, u32[]{:S(2)}) collective-permute-start(f32[9,8,128]{2,1,0:T(8,128)S(1)} %get-tuple-element.44.part_ref), channel_id=1, source_target_pairs={{0,1},{1,0},{2,3},{3,2},{4,5},{5,4},{6,7},{7,6},{8,9},{9,8},{10,11... | collective-permute-start | bytes 110600 | tf_op jit(solution)/shard_map/ppermute | solution.py:325
  73.5 25.4 %all-to-all-start = ((f32[256,1,128]{2,1,0:T(1,128)}), f32[256,1,128]{2,1,0:T(1,128)S(1)}, u32[]{:S(2)}, u32[]{:S(2)}) async-start(f32[256,1,128]{2,1,0:T(1,128)} %bitcast.1), calls=%async_computation | async-start | bytes 262144 | tf_op jit(solution)/shard_map/all_to_all | solution.py:779
  86.5 5.7 %copy-start.10 = (s32[2,7,8,128]{3,2,1,0:T(8,128)S(1)}, s32[2,7,8,128]{3,2,1,0:T(8,128)}, u32[]{:S(2)}) copy-start(s32[2,7,8,128]{3,2,1,0:T(8,128)} %constant.58.clone.order_ref) | copy-start | bytes 172036
  87.0 5.2 %collective-permute-start.8 = (f32[8,128]{1,0:T(8,128)S(1)}, f32[8,128]{1,0:T(8,128)S(1)}, u32[]{:S(2)}, u32[]{:S(2)}) collective-permute-start(f32[8,128]{1,0:T(8,128)S(1)} %get-tuple-element.51), channel_id=1, source_target_pairs={{0,511},{1,2},{2,1},{3,4},{4,3},{5,6},{6,5},{7,8},{8,7},{9,10},{10... | collective-permute-start | bytes 12296 | tf_op jit(solution)/shard_map/ppermute | solution.py:330

commit v7 on v6

--- a/solution.py
+++ b/solution.py
@@ -140,9 +140,28 @@
 
 
 def by_modes_right(value):
-    high, rest = halves(by_modes(value, 0))
-    parts = (high, rest, high)
+    a, b, c = thirds(by_modes(value, 0))
+    parts = (c, b, a, b, a, a)
     return np.concatenate([x[:LANES] for x in parts] + [x[LANES:] for x in parts])
+
+
+def thirds(value):
+    value = np.asarray(value, dtype=np.float32)
+    pieces = []
+    for k in range(3):
+        pieces.append(value.astype(jnp.bfloat16))
+        value = value - pieces[-1].astype(np.float32)
+    return pieces
+
+
+def for_right_full(value):
+    a, b, c = thirds(value)
+    return np.concatenate([c, b, a, b, a, a], axis=0)
+
+
+def for_left_full(value):
+    a, b, c = thirds(value)
+    return np.concatenate([c, b, a, b, a, a], axis=1)
 
 
 def pair(value):
@@ -178,21 +197,21 @@
 
     out["ds"] = np.stack([sublane(deriv), sublane(deriv.T)])
     out["dq"] = np.stack([lane(deriv), lane(deriv.T)])
-    out["qright"] = for_right(np.kron(np.eye(ES), deriv.T))
-    out["qright_t"] = for_right(np.kron(np.eye(ES), deriv))
+    out["qright"] = for_right_full(np.kron(np.eye(ES), deriv.T))
+    out["qright_t"] = for_right_full(np.kron(np.eye(ES), deriv))
     out["w3"] = f32(np.einsum("a,s,q->asq", w, w, w).reshape(1, 512))
     out["wmass"] = f32(np.tile(np.einsum("a,s,q->asq", w, w, w), (1, 1, ES)))
     both = interp @ deriv
     pad = np.zeros((16 - NF, NP))
     line = np.concatenate([interp, pad])
     slope = np.concatenate([both, pad])
-    out["jright"] = for_right(np.kron(np.eye(ES), line.T))
-    out["jslope"] = for_right(np.kron(np.eye(ES), slope.T))
-    out["jright_t"] = pair(np.kron(np.eye(ES), line))
-    out["jleft"] = for_left(np.kron(interp, interp))
-    out["jleft_a"] = for_left(np.kron(both, interp))
-    out["jleft_s"] = for_left(np.kron(interp, both))
-    out["jleft_t"] = for_left(np.kron(interp, interp).T)
+    out["jright"] = for_right_full(np.kron(np.eye(ES), line.T))
+    out["jslope"] = for_right_full(np.kron(np.eye(ES), slope.T))
+    out["jright_t"] = for_right_full(np.kron(np.eye(ES), line))
+    out["jleft"] = for_left_full(np.kron(interp, interp))
+    out["jleft_a"] = for_left_full(np.kron(both, interp))
+    out["jleft_s"] = for_left_full(np.kron(interp, both))
+    out["jleft_t"] = for_left_full(np.kron(interp, interp).T)
     wide_wf = np.concatenate([wf, np.zeros(16 - NF)])
     out["wfine"] = f32(np.kron(np.kron(wf, wf)[:, None], np.tile(wide_wf, ES)[None, :]))
     at = np.arange(7 * LANES)
@@ -213,9 +232,9 @@
             back[:80, row] = inside
             for block, s in enumerate((0, 1, wide - 2, wide - 1)):
                 back[80 + 16 * block + at, row] = solve[:, i] * solve[s, j]
-    out["sleft"] = for_left(left)
-    out["sback"] = for_left(back)
-    out["sright"] = for_right(by_modes(np.kron(np.eye(ES), solve[1:-1, :]), 1))
+    out["sleft"] = for_left_full(left)
+    out["sback"] = for_left_full(back)
+    out["sright"] = for_right_full(by_modes(np.kron(np.eye(ES), solve[1:-1, :]), 1))
     out["srback"] = by_modes_right(np.kron(np.eye(ES), solve[1:-1, :].T))
     out["spread"] = f32(by_modes(np.kron(np.eye(ES), np.ones((NP, wide))), 1) / 8.0)
     lam_a = np.zeros((MODES, 1))
@@ -244,6 +263,11 @@
     return jnp.dot(left, right, preferred_element_type=jnp.float32)
 
 
+def split_once(x):
+    high = x.astype(jnp.bfloat16)
+    return high, x - high.astype(jnp.float32)
+
+
 def split(x):
     high = x.astype(jnp.bfloat16)
     return high, (x - high.astype(jnp.float32)).astype(jnp.bfloat16)
@@ -259,9 +283,23 @@
     return short_dot(jnp.concatenate([high, high, rest], axis=1), table_ref[...])
 
 
+def full_pieces(x):
+    a, rest = split_once(x)
+    b, rest = split_once(rest)
+    c = rest.astype(jnp.bfloat16)
+    return [a, b, c, a, b, a]
+
+
+def full_right_dot(x, table_ref):
+    return short_dot(jnp.concatenate(full_pieces(x), axis=1), table_ref[...])
+
+
+def full_left_dot(table_ref, x):
+    return short_dot(table_ref[...], jnp.concatenate(full_pieces(x), axis=0))
+
+
 def modes_dot(x, table_ref):
-    high, rest = split(x)
-    parts = (high, high, rest)
+    parts = full_pieces(x)
     whole = [y[:, :LANES] for y in parts] + [y[:, LANES:] for y in parts]
     return short_dot(jnp.concatenate(whole, axis=1), table_ref[...])
 
@@ -386,18 +424,18 @@
     ds, dq = ds_ref[...], dq_ref[...]
     moved = [rows(new[i]) for i in range(3)]
     plain = moved + [rows(jac)] + [rows(new[d] * metric[d]) for d in range(3)]
-    wide = right_dot(jnp.concatenate(plain, axis=0), jright_ref)
-    slope = right_dot(jnp.concatenate(moved, axis=0), jslope_ref)
-    scale = left_dot(jleft_ref, wide[192:256]) * wfine_ref[...]
-    carry = [left_dot(jleft_ref, wide[256 + 64 * d : 320 + 64 * d]) for d in range(3)]
+    wide = full_right_dot(jnp.concatenate(plain, axis=0), jright_ref)
+    slope = full_right_dot(jnp.concatenate(moved, axis=0), jslope_ref)
+    scale = full_left_dot(jleft_ref, wide[192:256]) * wfine_ref[...]
+    carry = [full_left_dot(jleft_ref, wide[256 + 64 * d : 320 + 64 * d]) for d in range(3)]
     products = []
     for i in range(3):
         part = wide[64 * i : 64 * i + 64]
-        total = carry[0] * left_dot(jleft_a_ref, part) + carry[1] * left_dot(jleft_s_ref, part)
-        total = total + carry[2] * left_dot(jleft_ref, slope[64 * i : 64 * i + 64])
+        total = carry[0] * full_left_dot(jleft_a_ref, part) + carry[1] * full_left_dot(jleft_s_ref, part)
+        total = total + carry[2] * full_left_dot(jleft_ref, slope[64 * i : 64 * i + 64])
         products.append(scale * total)
-    coarse = left_dot(jleft_t_ref, jnp.concatenate(products, axis=1))
-    coarse = pair_dot(jnp.concatenate([coarse[:, 256 * i : 256 * i + 256] for i in range(3)], axis=0), jright_t_ref)
+    coarse = full_left_dot(jleft_t_ref, jnp.concatenate(products, axis=1))
+    coarse = full_right_dot(jnp.concatenate([coarse[:, 256 * i : 256 * i + 256] for i in range(3)], axis=0), jright_t_ref)
     mass = jac * wmass_ref[...]
     factor = [mass * metric[d] * metric[d] for d in range(3)]
     result = []
@@ -476,7 +514,7 @@
         levels.append(jnp.concatenate(sums, axis=0))
         div.append(d_a(terms[0], True) + d_s(terms[1], ds_ref[1]))
         last.append(rows(terms[2]))
-    last = right_dot(jnp.concatenate(last, axis=0), qright_t_ref)
+    last = full_right_dot(jnp.concatenate(last, axis=0), qright_t_ref)
     div = [join_s(x + planes(last[64 * k : 64 * k + 64])) for k, x in enumerate(div)]
     whole = chip_rows(div[0], div[1])
     div_ref[...] = whole
@@ -517,11 +555,11 @@
         after = roll(scratch_ref[pl.ds(at + 1, wide, stride=NP), :], -NP, 1)
         own = half[(NP - 1) * layer : (NP - 1) * layer + wide].reshape(wide * NP, LANES)
         columns.append(jnp.concatenate([own, before, none, after, none], axis=0))
-    spectra = [left_dot(sleft_ref, x) for x in columns]
-    spectra = [right_dot(x, sright_ref) for x in spectra]
+    spectra = [full_left_dot(sleft_ref, x) for x in columns]
+    spectra = [full_right_dot(x, sright_ref) for x in spectra]
     spectra = [x * inv_ref[MODES * k : MODES * k + MODES] for k, x in enumerate(spectra)]
     spectra = [modes_dot(x, srback_ref) for x in spectra]
-    blocks = [left_dot(sback_ref, x) for x in spectra]
+    blocks = [full_left_dot(sback_ref, x) for x in spectra]
     z = []
     for layer in range(2):
         part = blocks[layer]
@@ -544,9 +582,9 @@
 def operate(v, op_ref, ds_ref, qright_ref, qright_t_ref):
     ds = ds_ref[...]
     layers = [v[(NP - 1) * k : (NP - 1) * k + NP] for k in range(2)]
-    gq = right_dot(jnp.concatenate([rows(x) for x in layers], axis=0), qright_ref)
+    gq = full_right_dot(jnp.concatenate([rows(x) for x in layers], axis=0), qright_ref)
     hq = [op_ref[k, 2] * planes(gq[64 * k : 64 * k + 64]) for k in range(2)]
-    back = right_dot(jnp.concatenate([rows(x) for x in hq], axis=0), qright_t_ref)
+    back = full_right_dot(jnp.concatenate([rows(x) for x in hq], axis=0), qright_t_ref)
     parts = []
     for k, x in enumerate(layers):
         local = d_a(op_ref[k, 0] * d_a(x, False), True) + d_s(op_ref[k, 1] * d_s(x, ds[0]), ds[1])
@@ -611,7 +649,7 @@
     v = join_sides(even, part_ref[...], mate_ref[...])
     v_ref[...] = v
     layers = [v[(NP - 1) * k : (NP - 1) * k + NP] for k in range(2)]
-    gq = right_dot(jnp.concatenate([rows(x) for x in layers], axis=0), qright_ref)
+    gq = full_right_dot(jnp.concatenate([rows(x) for x in layers], axis=0), qright_ref)
     energy = None
     for k, x in enumerate(layers):
         ga, gs, gq_k = d_a(x, False), d_s(x, ds_ref[0]), planes(gq[64 * k : 64 * k + 64])

time: 100 us -> 102 us (1.020)
  Pallas kernels: 11.8 us -> 13.2 us
where the time goes in v7:
time: 102 us; the launch traced here: 101 us
  starting transfers between devices  63.1 us (62%)
  waiting for transfers between devices  23 us (23%)
  Pallas kernels  13.2 us (13%)
    ppermute x4, starting transfers between devices, swap_inner(): return lax.ppermute(x, 'dom', [(i, i ^ 1) for i in range(count)])  37.5 us
    ppermute x5, waiting for transfers between devices, swap_cross(): return lax.ppermute(x, 'dom', pairs)  13.4 us
    all_to_all x1, starting transfers between devices, shards(): lax.all_to_all(sums, 'dom', 0, 0, tiled=True, axis_index_groups=team_grou...  13 us
    ppermute x5, starting transfers between devices, swap_cross(): return lax.ppermute(x, 'dom', pairs)  12.6 us
    pallas_call x12, Pallas kernels, call(): pl.pallas_call(kernel, out_shape=[jax.ShapeDtypeStruct(shape, jnp.float32...  8.04 us
    all_to_all x1, waiting for transfers between devices, shards(): lax.all_to_all(sums, 'dom', 0, 0, tiled=True, axis_index_groups=team_grou...  5.96 us
    pallas_call x1, Pallas kernels, call_forcing(): pl.pallas_call(forcing_kernel, out_shape=[jax.ShapeDtypeStruct(shape, jnp...  4.86 us
    ppermute x4, waiting for transfers between devices, swap_inner(): return lax.ppermute(x, 'dom', [(i, i ^ 1) for i in range(count)])  3.59 us
  transfers between devices with their start and end apart: 10, of which 10 were waited for; matrix products, arithmetic and copies ran while one was open for 0% of the time, Pallas kernels for 1%

profile of v7, /device:TPU:1, one launch (start us, length us, event | category | flops | bytes accessed | tf_op | source)
XLA Modules:
  0.0 101.1 jit_solution(15807477868732482578)
XLA Ops:
  0.6 0.0 copy-start.9
  0.6 4.9 %shard_map.266 = (f32[56,8,128]{2,1,0:T(8,128)}, f32[4,8,128]{2,1,0:T(8,128)}) custom-call(s32[16]{0:T(128)} %slot_in.1, f32[3,3,16,512]{3,2,1,0:T(8,128)} %vel_in.1, f32[2,3,16,512]{3,2,1,0:T(8,128)} %past_in.1, f32[3,16,512]{2,1,0:T(8,128)} %metric_in.1, f32[16,512]{1,0:T(8,128)} %jac_in.1, f32[1,512]{1,0:T(1,128)} %constant.48.clone.w3_in, ...), custom_call_target="tpu_custom_call" | custom-call | tf_op jit(solution)/shard_map/pallas_call | solution.py:744
  5.5 4.6 %collective-permute-start = (f32[4,8,128]{2,1,0:T(8,128)}, f32[4,8,128]{2,1,0:T(8,128)S(1)}, u32[]{:S(2)}, u32[]{:S(2)}) collective-permute-start(f32[4,8,128]{2,1,0:T(8,128)} %get-tuple-element.30), channel_id=1, source_target_pairs={{0,511},{1,2},{2,1},{3,4},{4,3},{5,6},{6,5},{7,8},{8,7},{9,10},{10... | collective-permute-start | bytes 49160 | tf_op jit(solution)/shard_map/ppermute | solution.py:368
  10.1 0.0 copy-start.8
  10.1 0.9 copy-done.8
  11.0 0.0 copy-start.6
  11.0 0.0 copy-start.7
  11.0 0.3 shard_map.267.pack_ref
  11.3 0.0 copy-start.1
  11.4 0.0 copy-start.3
  11.4 0.4 collective-permute-done.cross_in
  11.7 0.0 copy-start.5
  11.7 0.0 copy-start
  11.8 0.0 copy-start.4
  11.8 14.4 %collective-permute-start.1 = (f32[60,8,128]{2,1,0:T(8,128)S(1)}, f32[60,8,128]{2,1,0:T(8,128)S(1)}, u32[]{:S(2)}, u32[]{:S(2)}) collective-permute-start(f32[60,8,128]{2,1,0:T(8,128)S(1)} %shard_map.268.own_ref), channel_id=1, source_target_pairs={{0,1},{1,0},{2,3},{3,2},{4,5},{5,4},{6,7},{7,6},{8,9},{9,8},{10,11... | collective-permute-start | bytes 737288 | tf_op jit(solution)/shard_map/ppermute | solution.py:363
  26.2 1.1 %collective-permute-done.1.mate_ref = f32[60,8,128]{2,1,0:T(8,128)S(1)} collective-permute-done((f32[60,8,128]{2,1,0:T(8,128)S(1)}, f32[60,8,128]{2,1,0:T(8,128)S(1)}, u32[]{:S(2)}, u32[]{:S(2)}) %collective-permute-start.1) | collective-permute-done | bytes 245792 | tf_op jit(solution)/shard_map/ppermute | solution.py:363
  27.3 0.0 copy-done.1
  27.3 0.0 copy-done.3
  27.4 0.4 shard_map.269
  27.7 1.9 %collective-permute-start.2 = (f32[10,8,128]{2,1,0:T(8,128)S(1)}, f32[10,8,128]{2,1,0:T(8,128)S(1)}, u32[]{:S(2)}, u32[]{:S(2)}) collective-permute-start(f32[10,8,128]{2,1,0:T(8,128)S(1)} %get-tuple-element.32), channel_id=1, source_target_pairs={{0,511},{1,2},{2,1},{3,4},{4,3},{5,6},{6,5},{7,8},{8,7},{9,10},{10... | collective-permute-start | bytes 122888 | tf_op jit(solution)/shard_map/ppermute | solution.py:368
  29.6 3.4 %collective-permute-done.2.received_ref = f32[10,8,128]{2,1,0:T(8,128)S(1)} collective-permute-done((f32[10,8,128]{2,1,0:T(8,128)S(1)}, f32[10,8,128]{2,1,0:T(8,128)S(1)}, u32[]{:S(2)}, u32[]{:S(2)}) %collective-permute-start.2) | collective-permute-done | bytes 40992 | tf_op jit(solution)/shard_map/ppermute | solution.py:368
  33.0 0.0 copy-done.9
  33.0 0.0 copy-done.6
  33.0 0.0 copy-done.7
  33.1 0.0 copy-done.5
  33.1 0.0 copy-done
  33.1 0.0 copy-done.4
  33.1 0.0 copy-start.2
  33.1 1.1 %shard_map.270 = (f32[17,8,128]{2,1,0:T(8,128)S(1)}, f32[224,160]{1,0:T(8,128)S(1)}, f32[9,8,128]{2,1,0:T(8,128)S(1)}) custom-call(f32[15,8,128]{2,1,0:T(8,128)S(1)} %get-tuple-element.31.div_ref, f32[10,8,128]{2,1,0:T(8,128)S(1)} %collective-permute-done.2.received_ref, f32[8,128]{1,0:T(8,128)S(1)} %get-tuple-element.33.level_ref, ...), custom_call_target="tpu_custom_call" | custom-call | tf_op jit(solution)/shard_map/pallas_call | solution.py:723
  34.2 7.7 %collective-permute-start.3 = (f32[9,8,128]{2,1,0:T(8,128)S(1)}, f32[9,8,128]{2,1,0:T(8,128)S(1)}, u32[]{:S(2)}, u32[]{:S(2)}) collective-permute-start(f32[9,8,128]{2,1,0:T(8,128)S(1)} %get-tuple-element.35.part_ref), channel_id=1, source_target_pairs={{0,1},{1,0},{2,3},{3,2},{4,5},{5,4},{6,7},{7,6},{8,9},{9,8},{10,11... | collective-permute-start | bytes 110600 | tf_op jit(solution)/shard_map/ppermute | solution.py:363
  41.9 0.8 collective-permute-done.3.mate_ref
  42.8 0.0 copy-done.2
  42.8 0.5 shard_map.271
  43.3 1.9 %collective-permute-start.4 = (f32[9,8,128]{2,1,0:T(8,128)S(1)}, f32[9,8,128]{2,1,0:T(8,128)S(1)}, u32[]{:S(2)}, u32[]{:S(2)}) collective-permute-start(f32[9,8,128]{2,1,0:T(8,128)S(1)} %get-tuple-element.38), channel_id=1, source_target_pairs={{0,511},{1,2},{2,1},{3,4},{4,3},{5,6},{6,5},{7,8},{8,7},{9,10},{10... | collective-permute-start | bytes 110600 | tf_op jit(solution)/shard_map/ppermute | solution.py:368
  45.2 3.3 %collective-permute-done.4.received_ref = f32[9,8,128]{2,1,0:T(8,128)S(1)} collective-permute-done((f32[9,8,128]{2,1,0:T(8,128)S(1)}, f32[9,8,128]{2,1,0:T(8,128)S(1)}, u32[]{:S(2)}, u32[]{:S(2)}) %collective-permute-start.4) | collective-permute-done | bytes 36896 | tf_op jit(solution)/shard_map/ppermute | solution.py:368
  48.6 1.1 %shard_map.272 = (f32[8,8,128]{2,1,0:T(8,128)S(1)}, f32[17,8,128]{2,1,0:T(8,128)S(1)}, f32[9,8,128]{2,1,0:T(8,128)S(1)}) custom-call(f32[17,8,128]{2,1,0:T(8,128)S(1)} %get-tuple-element.34.before_ref, f32[15,8,128]{2,1,0:T(8,128)S(1)} %get-tuple-element.37.local_ref.l0_ref, f32[9,8,128]{2,1,0:T(8,128)S(1)} %collective-permute-done.4.received_ref, ...), custom_call_target="tpu_custom_call" | custom-call | tf_op jit(solution)/shard_map/pallas_call | solution.py:723
  49.7 7.7 %collective-permute-start.5 = (f32[9,8,128]{2,1,0:T(8,128)S(1)}, f32[9,8,128]{2,1,0:T(8,128)S(1)}, u32[]{:S(2)}, u32[]{:S(2)}) collective-permute-start(f32[9,8,128]{2,1,0:T(8,128)S(1)} %get-tuple-element.41.part_ref), channel_id=1, source_target_pairs={{0,1},{1,0},{2,3},{3,2},{4,5},{5,4},{6,7},{7,6},{8,9},{9,8},{10,11... | collective-permute-start | bytes 110600 | tf_op jit(solution)/shard_map/ppermute | solution.py:363
  57.3 0.8 collective-permute-done.5.mate_ref
  58.2 0.5 shard_map.273
  58.7 1.9 %collective-permute-start.6 = (f32[9,8,128]{2,1,0:T(8,128)S(1)}, f32[9,8,128]{2,1,0:T(8,128)S(1)}, u32[]{:S(2)}, u32[]{:S(2)}) collective-permute-start(f32[9,8,128]{2,1,0:T(8,128)S(1)} %get-tuple-element.43), channel_id=1, source_target_pairs={{0,511},{1,2},{2,1},{3,4},{4,3},{5,6},{6,5},{7,8},{8,7},{9,10},{10... | collective-permute-start | bytes 110600 | tf_op jit(solution)/shard_map/ppermute | solution.py:368
  60.7 3.3 %collective-permute-done.6.received_ref = f32[9,8,128]{2,1,0:T(8,128)S(1)} collective-permute-done((f32[9,8,128]{2,1,0:T(8,128)S(1)}, f32[9,8,128]{2,1,0:T(8,128)S(1)}, u32[]{:S(2)}, u32[]{:S(2)}) %collective-permute-start.6) | collective-permute-done | bytes 36896 | tf_op jit(solution)/shard_map/ppermute | solution.py:368
  64.0 1.1 %shard_map.274 = (f32[8,8,128]{2,1,0:T(8,128)S(1)}, f32[17,8,128]{2,1,0:T(8,128)S(1)}, f32[9,8,128]{2,1,0:T(8,128)S(1)}) custom-call(f32[17,8,128]{2,1,0:T(8,128)S(1)} %get-tuple-element.40.before_ref, f32[15,8,128]{2,1,0:T(8,128)S(1)} %get-tuple-element.42.local_ref.l1_ref, f32[9,8,128]{2,1,0:T(8,128)S(1)} %collective-permute-done.6.received_ref, ...), custom_call_target="tpu_custom_call" | custom-call | tf_op jit(solution)/shard_map/pallas_call | solution.py:723
  65.1 0.0 copy-start.11
  65.1 7.7 %collective-permute-start.7 = (f32[9,8,128]{2,1,0:T(8,128)S(1)}, f32[9,8,128]{2,1,0:T(8,128)S(1)}, u32[]{:S(2)}, u32[]{:S(2)}) collective-permute-start(f32[9,8,128]{2,1,0:T(8,128)S(1)} %get-tuple-element.44.part_ref), channel_id=1, source_target_pairs={{0,1},{1,0},{2,3},{3,2},{4,5},{5,4},{6,7},{7,6},{8,9},{9,8},{10,11... | collective-permute-start | bytes 110600 | tf_op jit(solution)/shard_map/ppermute | solution.py:363
  72.8 0.0 copy-done.11
  72.8 0.8 collective-permute-done.7.mate_ref
  73.6 1.2 %shard_map.276 = (f32[15,8,128]{2,1,0:T(8,128)S(1)}, f32[256,128]{1,0:T(8,128)}) custom-call(f32[9,8,128]{2,1,0:T(8,128)S(1)} %get-tuple-element.44.part_ref, f32[9,8,128]{2,1,0:T(8,128)S(1)} %collective-permute-done.7.mate_ref, f32[2,4,8,8,128]{4,3,2,1,0:T(8,128)S(1)} %get-tuple-element.36.op_ref, f32[2,8,8,128]{3,2,1,0:T(8,128)S(1)} %copy-done.3, ...), custom_call_target="tpu_custom_call" | custom-call | tf_op jit(solution)/shard_map/pallas_call | solution.py:723
  74.8 13.0 %all-to-all-start = ((f32[256,1,128]{2,1,0:T(1,128)}), f32[256,1,128]{2,1,0:T(1,128)S(1)}, u32[]{:S(2)}, u32[]{:S(2)}) async-start(f32[256,1,128]{2,1,0:T(1,128)} %bitcast.1), calls=%async_computation | async-start | bytes 262144 | tf_op jit(solution)/shard_map/all_to_all | solution.py:817
  87.8 0.0 copy-start.10
  87.8 0.5 shard_map.277
  88.4 2.2 %collective-permute-start.8 = (f32[8,128]{1,0:T(8,128)S(1)}, f32[8,128]{1,0:T(8,128)S(1)}, u32[]{:S(2)}, u32[]{:S(2)}) collective-permute-start(f32[8,128]{1,0:T(8,128)S(1)} %get-tuple-element.51), channel_id=1, source_target_pairs={{0,511},{1,2},{2,1},{3,4},{4,3},{5,6},{6,5},{7,8},{8,7},{9,10},{10... | collective-permute-start | bytes 12296 | tf_op jit(solution)/shard_map/ppermute | solution.py:368
  90.6 3.0 %collective-permute-done.8.face_ref = f32[8,128]{1,0:T(8,128)S(1)} collective-permute-done((f32[8,128]{1,0:T(8,128)S(1)}, f32[8,128]{1,0:T(8,128)S(1)}, u32[]{:S(2)}, u32[]{:S(2)}) %collective-permute-start.8) | collective-permute-done | bytes 4128 | tf_op jit(solution)/shard_map/ppermute | solution.py:368
  93.6 0.0 copy-done.10
  93.6 0.6 shard_map.278.fields_ref
  94.2 6.0 %all-to-all-done = f32[256,1,128]{2,1,0:T(1,128)S(1)} async-done(((f32[256,1,128]{2,1,0:T(1,128)}), f32[256,1,128]{2,1,0:T(1,128)S(1)}, u32[]{:S(2)}, u32[]{:S(2)}) %all-to-all-start) | async-done | bytes 131104 | tf_op jit(solution)/shard_map/all_to_all | solution.py:817
  100.1 1.0 shard_map.279
  (2 shorter events, 0.1 us)
Async XLA Ops:
  0.6 32.4 %copy-start.9 = (f32[128,160]{1,0:T(8,128)S(1)}, f32[128,160]{1,0:T(8,128)}, u32[]{:S(2)}) copy-start(f32[128,160]{1,0:T(8,128)} %constant.63.clone.spread_ref) | copy-start | bytes 245764
  5.5 6.2 %collective-permute-start = (f32[4,8,128]{2,1,0:T(8,128)}, f32[4,8,128]{2,1,0:T(8,128)S(1)}, u32[]{:S(2)}, u32[]{:S(2)}) collective-permute-start(f32[4,8,128]{2,1,0:T(8,128)} %get-tuple-element.30), channel_id=1, source_target_pairs={{0,511},{1,2},{2,1},{3,4},{4,3},{5,6},{6,5},{7,8},{8,7},{9,10},{10... | collective-permute-start | bytes 49160 | tf_op jit(solution)/shard_map/ppermute | solution.py:368
  10.1 0.9 copy-start.8
  11.0 22.0 %copy-start.6 = (bf16[112,672]{1,0:T(8,128)(2,1)S(1)}, bf16[112,672]{1,0:T(8,128)(2,1)}, u32[]{:S(2)}) copy-start(bf16[112,672]{1,0:T(8,128)(2,1)} %constant.59.clone.sleft_ref) | copy-start | bytes 451588
  11.0 22.0 %copy-start.7 = (f32[3,112,160]{2,1,0:T(8,128)S(1)}, f32[3,112,160]{2,1,0:T(8,128)}, u32[]{:S(2)}) copy-start(f32[3,112,160]{2,1,0:T(8,128)} %constant.64.clone.lam_ref) | copy-start | bytes 645124
  11.3 16.0 %copy-start.1 = (bf16[768,128]{1,0:T(8,128)(2,1)S(1)}, bf16[768,128]{1,0:T(8,128)(2,1)}, u32[]{:S(2)}) copy-start(bf16[768,128]{1,0:T(8,128)(2,1)} %constant.47.clone.qright_t_ref) | copy-start | bytes 589828
  11.4 16.0 %copy-start.3 = (f32[2,8,8,128]{3,2,1,0:T(8,128)S(1)}, f32[2,8,8,128]{3,2,1,0:T(8,128)}, u32[]{:S(2)}) copy-start(f32[2,8,8,128]{3,2,1,0:T(8,128)} %constant.44.clone.ds_in.ds_ref) | copy-start | bytes 196612
  11.7 21.3 %copy-start.5 = (bf16[144,672]{1,0:T(8,128)(2,1)S(1)}, bf16[144,672]{1,0:T(8,128)(2,1)}, u32[]{:S(2)}) copy-start(bf16[144,672]{1,0:T(8,128)(2,1)} %constant.60.clone.sback_ref) | copy-start | bytes 580612
  11.7 21.3 %copy-start = (bf16[768,160]{1,0:T(8,128)(2,1)S(1)}, bf16[768,160]{1,0:T(8,128)(2,1)}, u32[]{:S(2)}) copy-start(bf16[768,160]{1,0:T(8,128)(2,1)} %constant.61.clone.sright_ref) | copy-start | bytes 737284
  11.8 21.3 %copy-start.4 = (bf16[960,128]{1,0:T(8,128)(2,1)S(1)}, bf16[960,128]{1,0:T(8,128)(2,1)}, u32[]{:S(2)}) copy-start(bf16[960,128]{1,0:T(8,128)(2,1)} %constant.62.clone.srback_ref) | copy-start | bytes 737284
  11.8 15.6 %collective-permute-start.1 = (f32[60,8,128]{2,1,0:T(8,128)S(1)}, f32[60,8,128]{2,1,0:T(8,128)S(1)}, u32[]{:S(2)}, u32[]{:S(2)}) collective-permute-start(f32[60,8,128]{2,1,0:T(8,128)S(1)} %shard_map.268.own_ref), channel_id=1, source_target_pairs={{0,1},{1,0},{2,3},{3,2},{4,5},{5,4},{6,7},{7,6},{8,9},{9,8},{10,11... | collective-permute-start | bytes 737288 | tf_op jit(solution)/shard_map/ppermute | solution.py:363
  27.7 5.3 %collective-permute-start.2 = (f32[10,8,128]{2,1,0:T(8,128)S(1)}, f32[10,8,128]{2,1,0:T(8,128)S(1)}, u32[]{:S(2)}, u32[]{:S(2)}) collective-permute-start(f32[10,8,128]{2,1,0:T(8,128)S(1)} %get-tuple-element.32), channel_id=1, source_target_pairs={{0,511},{1,2},{2,1},{3,4},{4,3},{5,6},{6,5},{7,8},{8,7},{9,10},{10... | collective-permute-start | bytes 122888 | tf_op jit(solution)/shard_map/ppermute | solution.py:368
  33.1 9.7 %copy-start.2 = (bf16[768,128]{1,0:T(8,128)(2,1)S(1)}, bf16[768,128]{1,0:T(8,128)(2,1)}, u32[]{:S(2)}) copy-start(bf16[768,128]{1,0:T(8,128)(2,1)} %constant.46.clone.qright_ref) | copy-start | bytes 589828
  34.2 8.6 %collective-permute-start.3 = (f32[9,8,128]{2,1,0:T(8,128)S(1)}, f32[9,8,128]{2,1,0:T(8,128)S(1)}, u32[]{:S(2)}, u32[]{:S(2)}) collective-permute-start(f32[9,8,128]{2,1,0:T(8,128)S(1)} %get-tuple-element.35.part_ref), channel_id=1, source_target_pairs={{0,1},{1,0},{2,3},{3,2},{4,5},{5,4},{6,7},{7,6},{8,9},{9,8},{10,11... | collective-permute-start | bytes 110600 | tf_op jit(solution)/shard_map/ppermute | solution.py:363
  43.3 5.3 %collective-permute-start.4 = (f32[9,8,128]{2,1,0:T(8,128)S(1)}, f32[9,8,128]{2,1,0:T(8,128)S(1)}, u32[]{:S(2)}, u32[]{:S(2)}) collective-permute-start(f32[9,8,128]{2,1,0:T(8,128)S(1)} %get-tuple-element.38), channel_id=1, source_target_pairs={{0,511},{1,2},{2,1},{3,4},{4,3},{5,6},{6,5},{7,8},{8,7},{9,10},{10... | collective-permute-start | bytes 110600 | tf_op jit(solution)/shard_map/ppermute | solution.py:368
  49.7 8.5 %collective-permute-start.5 = (f32[9,8,128]{2,1,0:T(8,128)S(1)}, f32[9,8,128]{2,1,0:T(8,128)S(1)}, u32[]{:S(2)}, u32[]{:S(2)}) collective-permute-start(f32[9,8,128]{2,1,0:T(8,128)S(1)} %get-tuple-element.41.part_ref), channel_id=1, source_target_pairs={{0,1},{1,0},{2,3},{3,2},{4,5},{5,4},{6,7},{7,6},{8,9},{9,8},{10,11... | collective-permute-start | bytes 110600 | tf_op jit(solution)/shard_map/ppermute | solution.py:363
  58.7 5.3 %collective-permute-start.6 = (f32[9,8,128]{2,1,0:T(8,128)S(1)}, f32[9,8,128]{2,1,0:T(8,128)S(1)}, u32[]{:S(2)}, u32[]{:S(2)}) collective-permute-start(f32[9,8,128]{2,1,0:T(8,128)S(1)} %get-tuple-element.43), channel_id=1, source_target_pairs={{0,511},{1,2},{2,1},{3,4},{4,3},{5,6},{6,5},{7,8},{8,7},{9,10},{10... | collective-permute-start | bytes 110600 | tf_op jit(solution)/shard_map/ppermute | solution.py:368
  65.1 7.7 %copy-start.11 = (f32[8,128]{1,0:T(8,128)S(1)}, f32[8,128]{1,0:T(8,128)}, u32[]{:S(2)}) copy-start(f32[8,128]{1,0:T(8,128)} %constant.65.clone.ws_ref) | copy-start | bytes 12292
  65.1 8.5 %collective-permute-start.7 = (f32[9,8,128]{2,1,0:T(8,128)S(1)}, f32[9,8,128]{2,1,0:T(8,128)S(1)}, u32[]{:S(2)}, u32[]{:S(2)}) collective-permute-start(f32[9,8,128]{2,1,0:T(8,128)S(1)} %get-tuple-element.44.part_ref), channel_id=1, source_target_pairs={{0,1},{1,0},{2,3},{3,2},{4,5},{5,4},{6,7},{7,6},{8,9},{9,8},{10,11... | collective-permute-start | bytes 110600 | tf_op jit(solution)/shard_map/ppermute | solution.py:363
  74.8 25.3 %all-to-all-start = ((f32[256,1,128]{2,1,0:T(1,128)}), f32[256,1,128]{2,1,0:T(1,128)S(1)}, u32[]{:S(2)}, u32[]{:S(2)}) async-start(f32[256,1,128]{2,1,0:T(1,128)} %bitcast.1), calls=%async_computation | async-start | bytes 262144 | tf_op jit(solution)/shard_map/all_to_all | solution.py:817
  87.8 5.8 %copy-start.10 = (s32[2,7,8,128]{3,2,1,0:T(8,128)S(1)}, s32[2,7,8,128]{3,2,1,0:T(8,128)}, u32[]{:S(2)}) copy-start(s32[2,7,8,128]{3,2,1,0:T(8,128)} %constant.58.clone.order_ref) | copy-start | bytes 172036
  88.4 5.2 %collective-permute-start.8 = (f32[8,128]{1,0:T(8,128)S(1)}, f32[8,128]{1,0:T(8,128)S(1)}, u32[]{:S(2)}, u32[]{:S(2)}) collective-permute-start(f32[8,128]{1,0:T(8,128)S(1)} %get-tuple-element.51), channel_id=1, source_target_pairs={{0,511},{1,2},{2,1},{3,4},{4,3},{5,6},{6,5},{7,8},{8,7},{9,10},{10... | collective-permute-start | bytes 12296 | tf_op jit(solution)/shard_map/ppermute | solution.py:368

commit v8 on v6

--- a/solution.py
+++ b/solution.py
@@ -167,14 +167,8 @@
         return f32(np.broadcast_to(np.stack(rows)[:, :, None], (NP, NP, LANES)))
 
     def lane(matrix):
-        rows = []
-        for shift in range(-(NP - 1), NP):
-            row = np.zeros(NP)
-            for q in range(NP):
-                if 0 <= q + shift < NP:
-                    row[q] = matrix[q, q + shift]
-            rows.append(np.tile(row, ES))
-        return f32(np.broadcast_to(np.stack(rows)[:, None, :], (2 * NP - 1, NP, LANES)))
+        rows = [np.tile(matrix[index, (index + shift) % NP], ES) for shift in range(NP)]
+        return f32(np.broadcast_to(np.stack(rows)[:, None, :], (NP, NP, LANES)))
 
     out["ds"] = np.stack([sublane(deriv), sublane(deriv.T)])
     out["dq"] = np.stack([lane(deriv), lane(deriv.T)])
@@ -294,10 +288,12 @@
 
 
 def d_q(x, coef):
-    total = coef[NP - 1][None] * x
+    flat = x.reshape(-1, LANES)
+    lane = lax.broadcasted_iota(jnp.int32, flat.shape, 1)
+    total = coef[0][None] * x
     for shift in range(1, NP):
-        total = total + coef[NP - 1 + shift][None] * roll(x, -shift, 2)
-        total = total + coef[NP - 1 - shift][None] * roll(x, shift, 2)
+        index = (lane & (LANES - NP)) | ((lane + shift) & (NP - 1))
+        total = total + coef[shift][None] * jnp.take_along_axis(flat, index, axis=1).reshape(x.shape)
     return total
 
 
@@ -346,9 +342,13 @@
         step = 1 << bit
         in_sub = (sub & step) != 0
         in_lane = (lane & (step * 8)) != 0
-        up = roll(roll(y, -step, 1), step * 8, 2)
-        down = roll(roll(y, step, 1), -step * 8, 2)
-        y = jnp.where(in_sub == in_lane, y, jnp.where(in_lane, up, down))
+        flat = y.reshape(-1, LANES)
+        swapped = jnp.take_along_axis(flat, lane.reshape(-1, LANES) ^ (step * 8), axis=1).reshape(y.shape)
+        if step == 4:
+            moved = roll(swapped, step, 1)
+        else:
+            moved = jnp.where(in_sub, roll(swapped, step, 1), roll(swapped, -step, 1))
+        y = jnp.where(in_sub == in_lane, y, moved)
     return y.reshape(x.shape[0], NP, NP, LANES)
 
 

time: 100 us -> 99.9 us (level)
  no operation moved by 1% of the time
where the time goes in v8:
time: 99.9 us; the launch traced here: 99.4 us
  starting transfers between devices  63.1 us (63%)
  waiting for transfers between devices  23.1 us (23%)
  Pallas kernels  11.3 us (11%)
  local copies, waits for them, and re-layouts  1 us (1%)
    ppermute x4, starting transfers between devices, swap_inner(): return lax.ppermute(x, 'dom', [(i, i ^ 1) for i in range(count)])  37.5 us
    ppermute x5, waiting for transfers between devices, swap_cross(): return lax.ppermute(x, 'dom', pairs)  13.5 us
    all_to_all x1, starting transfers between devices, shards(): lax.all_to_all(sums, 'dom', 0, 0, tiled=True, axis_index_groups=team_grou...  13 us
    ppermute x5, starting transfers between devices, swap_cross(): return lax.ppermute(x, 'dom', pairs)  12.6 us
    pallas_call x12, Pallas kernels, call(): pl.pallas_call(kernel, out_shape=[jax.ShapeDtypeStruct(shape, jnp.float32...  7.19 us
    all_to_all x1, waiting for transfers between devices, shards(): lax.all_to_all(sums, 'dom', 0, 0, tiled=True, axis_index_groups=team_grou...  6.05 us
    pallas_call x1, Pallas kernels, call_forcing(): pl.pallas_call(forcing_kernel, out_shape=[jax.ShapeDtypeStruct(shape, jnp...  3.88 us
    ppermute x4, waiting for transfers between devices, swap_inner(): return lax.ppermute(x, 'dom', [(i, i ^ 1) for i in range(count)])  3.59 us
  transfers between devices with their start and end apart: 10, of which 10 were waited for; matrix products, arithmetic and copies ran while one was open for 0% of the time, Pallas kernels for 1%

profile of v8, /device:TPU:1, one launch (start us, length us, event | category | flops | bytes accessed | tf_op | source)
XLA Modules:
  0.0 99.4 jit_solution(14244957145565329310)
XLA Ops:
  0.6 3.9 %shard_map.266 = (f32[56,8,128]{2,1,0:T(8,128)}, f32[4,8,128]{2,1,0:T(8,128)}) custom-call(s32[16]{0:T(128)} %slot_in.1, f32[3,3,16,512]{3,2,1,0:T(8,128)} %vel_in.1, f32[2,3,16,512]{3,2,1,0:T(8,128)} %past_in.1, f32[3,16,512]{2,1,0:T(8,128)} %metric_in.1, f32[16,512]{1,0:T(8,128)} %jac_in.1, f32[1,512]{1,0:T(1,128)} %constant.48.clone.w3_in, ...), custom_call_target="tpu_custom_call" | custom-call | tf_op jit(solution)/shard_map/pallas_call | solution.py:706
  4.5 4.6 %collective-permute-start = (f32[4,8,128]{2,1,0:T(8,128)}, f32[4,8,128]{2,1,0:T(8,128)S(1)}, u32[]{:S(2)}, u32[]{:S(2)}) collective-permute-start(f32[4,8,128]{2,1,0:T(8,128)} %get-tuple-element.30), channel_id=1, source_target_pairs={{0,511},{1,2},{2,1},{3,4},{4,3},{5,6},{6,5},{7,8},{8,7},{9,10},{10... | collective-permute-start | bytes 49160 | tf_op jit(solution)/shard_map/ppermute | solution.py:326
  9.1 0.0 copy-start.8
  9.1 0.9 copy-done.8
  10.1 0.0 copy-start.9
  10.1 0.3 shard_map.267.pack_ref
  10.4 0.0 copy-start
  10.4 0.0 copy-start.2
  10.4 0.4 collective-permute-done.cross_in
  10.7 0.0 copy-start.7
  10.8 0.0 copy-start.1
  10.8 0.0 copy-start.4
  10.8 0.0 copy-start.5
  10.8 0.0 copy-start.6
  10.8 14.5 %collective-permute-start.1 = (f32[60,8,128]{2,1,0:T(8,128)S(1)}, f32[60,8,128]{2,1,0:T(8,128)S(1)}, u32[]{:S(2)}, u32[]{:S(2)}) collective-permute-start(f32[60,8,128]{2,1,0:T(8,128)S(1)} %shard_map.268.own_ref), channel_id=1, source_target_pairs={{0,1},{1,0},{2,3},{3,2},{4,5},{5,4},{6,7},{7,6},{8,9},{9,8},{10,11... | collective-permute-start | bytes 737288 | tf_op jit(solution)/shard_map/ppermute | solution.py:321
  25.3 1.1 %collective-permute-done.1.mate_ref = f32[60,8,128]{2,1,0:T(8,128)S(1)} collective-permute-done((f32[60,8,128]{2,1,0:T(8,128)S(1)}, f32[60,8,128]{2,1,0:T(8,128)S(1)}, u32[]{:S(2)}, u32[]{:S(2)}) %collective-permute-start.1) | collective-permute-done | bytes 245792 | tf_op jit(solution)/shard_map/ppermute | solution.py:321
  26.4 0.0 copy-done
  26.4 0.0 copy-done.2
  26.4 0.3 shard_map.269
  26.7 1.9 %collective-permute-start.2 = (f32[10,8,128]{2,1,0:T(8,128)S(1)}, f32[10,8,128]{2,1,0:T(8,128)S(1)}, u32[]{:S(2)}, u32[]{:S(2)}) collective-permute-start(f32[10,8,128]{2,1,0:T(8,128)S(1)} %get-tuple-element.32), channel_id=1, source_target_pairs={{0,511},{1,2},{2,1},{3,4},{4,3},{5,6},{6,5},{7,8},{8,7},{9,10},{10... | collective-permute-start | bytes 122888 | tf_op jit(solution)/shard_map/ppermute | solution.py:326
  28.7 3.4 %collective-permute-done.2.received_ref = f32[10,8,128]{2,1,0:T(8,128)S(1)} collective-permute-done((f32[10,8,128]{2,1,0:T(8,128)S(1)}, f32[10,8,128]{2,1,0:T(8,128)S(1)}, u32[]{:S(2)}, u32[]{:S(2)}) %collective-permute-start.2) | collective-permute-done | bytes 40992 | tf_op jit(solution)/shard_map/ppermute | solution.py:326
  32.1 0.0 copy-done.9
  32.1 0.0 copy-done.7
  32.1 0.0 copy-done.1
  32.1 0.0 copy-done.4
  32.1 0.0 copy-done.5
  32.1 0.0 copy-done.6
  32.1 0.0 copy-start.3
  32.1 0.9 shard_map.270
  33.0 7.7 %collective-permute-start.3 = (f32[9,8,128]{2,1,0:T(8,128)S(1)}, f32[9,8,128]{2,1,0:T(8,128)S(1)}, u32[]{:S(2)}, u32[]{:S(2)}) collective-permute-start(f32[9,8,128]{2,1,0:T(8,128)S(1)} %get-tuple-element.35.part_ref), channel_id=1, source_target_pairs={{0,1},{1,0},{2,3},{3,2},{4,5},{5,4},{6,7},{7,6},{8,9},{9,8},{10,11... | collective-permute-start | bytes 110600 | tf_op jit(solution)/shard_map/ppermute | solution.py:321
  40.8 0.8 collective-permute-done.3.mate_ref
  41.6 0.0 copy-done.3
  41.6 0.4 shard_map.271
  42.1 1.9 %collective-permute-start.4 = (f32[9,8,128]{2,1,0:T(8,128)S(1)}, f32[9,8,128]{2,1,0:T(8,128)S(1)}, u32[]{:S(2)}, u32[]{:S(2)}) collective-permute-start(f32[9,8,128]{2,1,0:T(8,128)S(1)} %get-tuple-element.38), channel_id=1, source_target_pairs={{0,511},{1,2},{2,1},{3,4},{4,3},{5,6},{6,5},{7,8},{8,7},{9,10},{10... | collective-permute-start | bytes 110600 | tf_op jit(solution)/shard_map/ppermute | solution.py:326
  44.0 3.3 %collective-permute-done.4.received_ref = f32[9,8,128]{2,1,0:T(8,128)S(1)} collective-permute-done((f32[9,8,128]{2,1,0:T(8,128)S(1)}, f32[9,8,128]{2,1,0:T(8,128)S(1)}, u32[]{:S(2)}, u32[]{:S(2)}) %collective-permute-start.4) | collective-permute-done | bytes 36896 | tf_op jit(solution)/shard_map/ppermute | solution.py:326
  47.3 0.9 shard_map.272
  48.2 7.7 %collective-permute-start.5 = (f32[9,8,128]{2,1,0:T(8,128)S(1)}, f32[9,8,128]{2,1,0:T(8,128)S(1)}, u32[]{:S(2)}, u32[]{:S(2)}) collective-permute-start(f32[9,8,128]{2,1,0:T(8,128)S(1)} %get-tuple-element.41.part_ref), channel_id=1, source_target_pairs={{0,1},{1,0},{2,3},{3,2},{4,5},{5,4},{6,7},{7,6},{8,9},{9,8},{10,11... | collective-permute-start | bytes 110600 | tf_op jit(solution)/shard_map/ppermute | solution.py:321
  55.9 0.8 collective-permute-done.5.mate_ref
  56.8 0.4 shard_map.273
  57.2 1.9 %collective-permute-start.6 = (f32[9,8,128]{2,1,0:T(8,128)S(1)}, f32[9,8,128]{2,1,0:T(8,128)S(1)}, u32[]{:S(2)}, u32[]{:S(2)}) collective-permute-start(f32[9,8,128]{2,1,0:T(8,128)S(1)} %get-tuple-element.43), channel_id=1, source_target_pairs={{0,511},{1,2},{2,1},{3,4},{4,3},{5,6},{6,5},{7,8},{8,7},{9,10},{10... | collective-permute-start | bytes 110600 | tf_op jit(solution)/shard_map/ppermute | solution.py:326
  59.1 3.3 %collective-permute-done.6.received_ref = f32[9,8,128]{2,1,0:T(8,128)S(1)} collective-permute-done((f32[9,8,128]{2,1,0:T(8,128)S(1)}, f32[9,8,128]{2,1,0:T(8,128)S(1)}, u32[]{:S(2)}, u32[]{:S(2)}) %collective-permute-start.6) | collective-permute-done | bytes 36896 | tf_op jit(solution)/shard_map/ppermute | solution.py:326
  62.5 0.9 shard_map.274
  63.4 0.0 copy-start.11
  63.4 7.7 %collective-permute-start.7 = (f32[9,8,128]{2,1,0:T(8,128)S(1)}, f32[9,8,128]{2,1,0:T(8,128)S(1)}, u32[]{:S(2)}, u32[]{:S(2)}) collective-permute-start(f32[9,8,128]{2,1,0:T(8,128)S(1)} %get-tuple-element.44.part_ref), channel_id=1, source_target_pairs={{0,1},{1,0},{2,3},{3,2},{4,5},{5,4},{6,7},{7,6},{8,9},{9,8},{10,11... | collective-permute-start | bytes 110600 | tf_op jit(solution)/shard_map/ppermute | solution.py:321
  71.1 0.0 copy-done.11
  71.2 0.8 collective-permute-done.7.mate_ref
  71.9 1.2 %shard_map.276 = (f32[15,8,128]{2,1,0:T(8,128)S(1)}, f32[256,128]{1,0:T(8,128)}) custom-call(f32[9,8,128]{2,1,0:T(8,128)S(1)} %get-tuple-element.44.part_ref, f32[9,8,128]{2,1,0:T(8,128)S(1)} %collective-permute-done.7.mate_ref, f32[2,4,8,8,128]{4,3,2,1,0:T(8,128)S(1)} %get-tuple-element.36.op_ref, f32[2,8,8,128]{3,2,1,0:T(8,128)S(1)} %copy-done, ...), custom_call_target="tpu_custom_call" | custom-call | tf_op jit(solution)/shard_map/pallas_call | solution.py:685
  73.1 13.0 %all-to-all-start = ((f32[256,1,128]{2,1,0:T(1,128)}), f32[256,1,128]{2,1,0:T(1,128)S(1)}, u32[]{:S(2)}, u32[]{:S(2)}) async-start(f32[256,1,128]{2,1,0:T(1,128)} %bitcast.1), calls=%async_computation | async-start | bytes 262144 | tf_op jit(solution)/shard_map/all_to_all | solution.py:779
  86.1 0.0 copy-start.10
  86.1 0.4 shard_map.277
  86.6 2.2 %collective-permute-start.8 = (f32[8,128]{1,0:T(8,128)S(1)}, f32[8,128]{1,0:T(8,128)S(1)}, u32[]{:S(2)}, u32[]{:S(2)}) collective-permute-start(f32[8,128]{1,0:T(8,128)S(1)} %get-tuple-element.51), channel_id=1, source_target_pairs={{0,511},{1,2},{2,1},{3,4},{4,3},{5,6},{6,5},{7,8},{8,7},{9,10},{10... | collective-permute-start | bytes 12296 | tf_op jit(solution)/shard_map/ppermute | solution.py:326
  88.8 3.0 %collective-permute-done.8.face_ref = f32[8,128]{1,0:T(8,128)S(1)} collective-permute-done((f32[8,128]{1,0:T(8,128)S(1)}, f32[8,128]{1,0:T(8,128)S(1)}, u32[]{:S(2)}, u32[]{:S(2)}) %collective-permute-start.8) | collective-permute-done | bytes 4128 | tf_op jit(solution)/shard_map/ppermute | solution.py:326
  91.8 0.0 copy-done.10
  91.8 0.6 shard_map.278.fields_ref
  92.4 6.0 %all-to-all-done = f32[256,1,128]{2,1,0:T(1,128)S(1)} async-done(((f32[256,1,128]{2,1,0:T(1,128)}), f32[256,1,128]{2,1,0:T(1,128)S(1)}, u32[]{:S(2)}, u32[]{:S(2)}) %all-to-all-start) | async-done | bytes 131104 | tf_op jit(solution)/shard_map/all_to_all | solution.py:779
  98.4 1.0 %shard_map.279 = (f32[8,896]{1,0:T(8,128)}, f32[8,896]{1,0:T(8,128)}) custom-call(f32[256,128]{1,0:T(8,128)S(1)} %bitcast.4, f32[7,8,896]{2,1,0:T(8,128)S(1)} %shard_map.278.fields_ref), custom_call_target="tpu_custom_call" | custom-call | tf_op jit(solution)/shard_map/pallas_call | solution.py:685
  (2 shorter events, 0.1 us)
Async XLA Ops:
  4.5 6.2 %collective-permute-start = (f32[4,8,128]{2,1,0:T(8,128)}, f32[4,8,128]{2,1,0:T(8,128)S(1)}, u32[]{:S(2)}, u32[]{:S(2)}) collective-permute-start(f32[4,8,128]{2,1,0:T(8,128)} %get-tuple-element.30), channel_id=1, source_target_pairs={{0,511},{1,2},{2,1},{3,4},{4,3},{5,6},{6,5},{7,8},{8,7},{9,10},{10... | collective-permute-start | bytes 49160 | tf_op jit(solution)/shard_map/ppermute | solution.py:326
  9.1 0.9 copy-start.8
  10.1 22.0 %copy-start.9 = (f32[128,160]{1,0:T(8,128)S(1)}, f32[128,160]{1,0:T(8,128)}, u32[]{:S(2)}) copy-start(f32[128,160]{1,0:T(8,128)} %constant.63.clone.spread_ref) | copy-start | bytes 245764
  10.4 16.0 %copy-start = (f32[2,8,8,128]{3,2,1,0:T(8,128)S(1)}, f32[2,8,8,128]{3,2,1,0:T(8,128)}, u32[]{:S(2)}) copy-start(f32[2,8,8,128]{3,2,1,0:T(8,128)} %constant.44.clone.ds_in.ds_ref) | copy-start | bytes 196612
  10.4 16.0 %copy-start.2 = (bf16[384,128]{1,0:T(8,128)(2,1)S(1)}, bf16[384,128]{1,0:T(8,128)(2,1)}, u32[]{:S(2)}) copy-start(bf16[384,128]{1,0:T(8,128)(2,1)} %constant.47.clone.qright_t_ref) | copy-start | bytes 294916
  10.7 21.3 %copy-start.7 = (f32[3,112,160]{2,1,0:T(8,128)S(1)}, f32[3,112,160]{2,1,0:T(8,128)}, u32[]{:S(2)}) copy-start(f32[3,112,160]{2,1,0:T(8,128)} %constant.64.clone.lam_ref) | copy-start | bytes 645124
  10.8 21.3 %copy-start.1 = (bf16[384,160]{1,0:T(8,128)(2,1)S(1)}, bf16[384,160]{1,0:T(8,128)(2,1)}, u32[]{:S(2)}) copy-start(bf16[384,160]{1,0:T(8,128)(2,1)} %constant.61.clone.sright_ref) | copy-start | bytes 368644
  10.8 21.3 %copy-start.4 = (bf16[480,128]{1,0:T(8,128)(2,1)S(1)}, bf16[480,128]{1,0:T(8,128)(2,1)}, u32[]{:S(2)}) copy-start(bf16[480,128]{1,0:T(8,128)(2,1)} %constant.62.clone.srback_ref) | copy-start | bytes 368644
  10.8 21.3 %copy-start.5 = (bf16[144,336]{1,0:T(8,128)(2,1)S(1)}, bf16[144,336]{1,0:T(8,128)(2,1)}, u32[]{:S(2)}) copy-start(bf16[144,336]{1,0:T(8,128)(2,1)} %constant.60.clone.sback_ref) | copy-start | bytes 290308
  10.8 21.3 %copy-start.6 = (bf16[112,336]{1,0:T(8,128)(2,1)S(1)}, bf16[112,336]{1,0:T(8,128)(2,1)}, u32[]{:S(2)}) copy-start(bf16[112,336]{1,0:T(8,128)(2,1)} %constant.59.clone.sleft_ref) | copy-start | bytes 225796
  10.8 15.6 %collective-permute-start.1 = (f32[60,8,128]{2,1,0:T(8,128)S(1)}, f32[60,8,128]{2,1,0:T(8,128)S(1)}, u32[]{:S(2)}, u32[]{:S(2)}) collective-permute-start(f32[60,8,128]{2,1,0:T(8,128)S(1)} %shard_map.268.own_ref), channel_id=1, source_target_pairs={{0,1},{1,0},{2,3},{3,2},{4,5},{5,4},{6,7},{7,6},{8,9},{9,8},{10,11... | collective-permute-start | bytes 737288 | tf_op jit(solution)/shard_map/ppermute | solution.py:321
  26.7 5.3 %collective-permute-start.2 = (f32[10,8,128]{2,1,0:T(8,128)S(1)}, f32[10,8,128]{2,1,0:T(8,128)S(1)}, u32[]{:S(2)}, u32[]{:S(2)}) collective-permute-start(f32[10,8,128]{2,1,0:T(8,128)S(1)} %get-tuple-element.32), channel_id=1, source_target_pairs={{0,511},{1,2},{2,1},{3,4},{4,3},{5,6},{6,5},{7,8},{8,7},{9,10},{10... | collective-permute-start | bytes 122888 | tf_op jit(solution)/shard_map/ppermute | solution.py:326
  32.1 9.5 %copy-start.3 = (bf16[384,128]{1,0:T(8,128)(2,1)S(1)}, bf16[384,128]{1,0:T(8,128)(2,1)}, u32[]{:S(2)}) copy-start(bf16[384,128]{1,0:T(8,128)(2,1)} %constant.46.clone.qright_ref) | copy-start | bytes 294916
  33.0 8.6 %collective-permute-start.3 = (f32[9,8,128]{2,1,0:T(8,128)S(1)}, f32[9,8,128]{2,1,0:T(8,128)S(1)}, u32[]{:S(2)}, u32[]{:S(2)}) collective-permute-start(f32[9,8,128]{2,1,0:T(8,128)S(1)} %get-tuple-element.35.part_ref), channel_id=1, source_target_pairs={{0,1},{1,0},{2,3},{3,2},{4,5},{5,4},{6,7},{7,6},{8,9},{9,8},{10,11... | collective-permute-start | bytes 110600 | tf_op jit(solution)/shard_map/ppermute | solution.py:321
  42.1 5.3 %collective-permute-start.4 = (f32[9,8,128]{2,1,0:T(8,128)S(1)}, f32[9,8,128]{2,1,0:T(8,128)S(1)}, u32[]{:S(2)}, u32[]{:S(2)}) collective-permute-start(f32[9,8,128]{2,1,0:T(8,128)S(1)} %get-tuple-element.38), channel_id=1, source_target_pairs={{0,511},{1,2},{2,1},{3,4},{4,3},{5,6},{6,5},{7,8},{8,7},{9,10},{10... | collective-permute-start | bytes 110600 | tf_op jit(solution)/shard_map/ppermute | solution.py:326
  48.2 8.5 %collective-permute-start.5 = (f32[9,8,128]{2,1,0:T(8,128)S(1)}, f32[9,8,128]{2,1,0:T(8,128)S(1)}, u32[]{:S(2)}, u32[]{:S(2)}) collective-permute-start(f32[9,8,128]{2,1,0:T(8,128)S(1)} %get-tuple-element.41.part_ref), channel_id=1, source_target_pairs={{0,1},{1,0},{2,3},{3,2},{4,5},{5,4},{6,7},{7,6},{8,9},{9,8},{10,11... | collective-permute-start | bytes 110600 | tf_op jit(solution)/shard_map/ppermute | solution.py:321
  57.2 5.3 %collective-permute-start.6 = (f32[9,8,128]{2,1,0:T(8,128)S(1)}, f32[9,8,128]{2,1,0:T(8,128)S(1)}, u32[]{:S(2)}, u32[]{:S(2)}) collective-permute-start(f32[9,8,128]{2,1,0:T(8,128)S(1)} %get-tuple-element.43), channel_id=1, source_target_pairs={{0,511},{1,2},{2,1},{3,4},{4,3},{5,6},{6,5},{7,8},{8,7},{9,10},{10... | collective-permute-start | bytes 110600 | tf_op jit(solution)/shard_map/ppermute | solution.py:326
  63.4 7.7 %copy-start.11 = (f32[8,128]{1,0:T(8,128)S(1)}, f32[8,128]{1,0:T(8,128)}, u32[]{:S(2)}) copy-start(f32[8,128]{1,0:T(8,128)} %constant.65.clone.ws_ref) | copy-start | bytes 12292
  63.4 8.5 %collective-permute-start.7 = (f32[9,8,128]{2,1,0:T(8,128)S(1)}, f32[9,8,128]{2,1,0:T(8,128)S(1)}, u32[]{:S(2)}, u32[]{:S(2)}) collective-permute-start(f32[9,8,128]{2,1,0:T(8,128)S(1)} %get-tuple-element.44.part_ref), channel_id=1, source_target_pairs={{0,1},{1,0},{2,3},{3,2},{4,5},{5,4},{6,7},{7,6},{8,9},{9,8},{10,11... | collective-permute-start | bytes 110600 | tf_op jit(solution)/shard_map/ppermute | solution.py:321
  73.1 25.3 %all-to-all-start = ((f32[256,1,128]{2,1,0:T(1,128)}), f32[256,1,128]{2,1,0:T(1,128)S(1)}, u32[]{:S(2)}, u32[]{:S(2)}) async-start(f32[256,1,128]{2,1,0:T(1,128)} %bitcast.1), calls=%async_computation | async-start | bytes 262144 | tf_op jit(solution)/shard_map/all_to_all | solution.py:779
  86.1 5.7 %copy-start.10 = (s32[2,7,8,128]{3,2,1,0:T(8,128)S(1)}, s32[2,7,8,128]{3,2,1,0:T(8,128)}, u32[]{:S(2)}) copy-start(s32[2,7,8,128]{3,2,1,0:T(8,128)} %constant.58.clone.order_ref) | copy-start | bytes 172036
  86.6 5.2 %collective-permute-start.8 = (f32[8,128]{1,0:T(8,128)S(1)}, f32[8,128]{1,0:T(8,128)S(1)}, u32[]{:S(2)}, u32[]{:S(2)}) collective-permute-start(f32[8,128]{1,0:T(8,128)S(1)} %get-tuple-element.51), channel_id=1, source_target_pairs={{0,511},{1,2},{2,1},{3,4},{4,3},{5,6},{6,5},{7,8},{8,7},{9,10},{10... | collective-permute-start | bytes 12296 | tf_op jit(solution)/shard_map/ppermute | solution.py:326

commit v9 on v7

--- a/solution.py
+++ b/solution.py
@@ -186,14 +186,8 @@
         return f32(np.broadcast_to(np.stack(rows)[:, :, None], (NP, NP, LANES)))
 
     def lane(matrix):
-        rows = []
-        for shift in range(-(NP - 1), NP):
-            row = np.zeros(NP)
-            for q in range(NP):
-                if 0 <= q + shift < NP:
-                    row[q] = matrix[q, q + shift]
-            rows.append(np.tile(row, ES))
-        return f32(np.broadcast_to(np.stack(rows)[:, None, :], (2 * NP - 1, NP, LANES)))
+        rows = [np.tile(matrix[index, (index + shift) % NP], ES) for shift in range(NP)]
+        return f32(np.broadcast_to(np.stack(rows)[:, None, :], (NP, NP, LANES)))
 
     out["ds"] = np.stack([sublane(deriv), sublane(deriv.T)])
     out["dq"] = np.stack([lane(deriv), lane(deriv.T)])
@@ -332,10 +326,12 @@
 
 
 def d_q(x, coef):
-    total = coef[NP - 1][None] * x
+    flat = x.reshape(-1, LANES)
+    lane = lax.broadcasted_iota(jnp.int32, flat.shape, 1)
+    total = coef[0][None] * x
     for shift in range(1, NP):
-        total = total + coef[NP - 1 + shift][None] * roll(x, -shift, 2)
-        total = total + coef[NP - 1 - shift][None] * roll(x, shift, 2)
+        index = (lane & (LANES - NP)) | ((lane + shift) & (NP - 1))
+        total = total + coef[shift][None] * jnp.take_along_axis(flat, index, axis=1).reshape(x.shape)
     return total
 
 
@@ -384,9 +380,13 @@
         step = 1 << bit
         in_sub = (sub & step) != 0
         in_lane = (lane & (step * 8)) != 0
-        up = roll(roll(y, -step, 1), step * 8, 2)
-        down = roll(roll(y, step, 1), -step * 8, 2)
-        y = jnp.where(in_sub == in_lane, y, jnp.where(in_lane, up, down))
+        flat = y.reshape(-1, LANES)
+        swapped = jnp.take_along_axis(flat, lane.reshape(-1, LANES) ^ (step * 8), axis=1).reshape(y.shape)
+        if step == 4:
+            moved = roll(swapped, step, 1)
+        else:
+            moved = jnp.where(in_sub, roll(swapped, step, 1), roll(swapped, -step, 1))
+        y = jnp.where(in_sub == in_lane, y, moved)
     return y.reshape(x.shape[0], NP, NP, LANES)
 
 

time: 102 us -> 101 us (level)
  no operation moved by 1% of the time
where the time goes in v9:
time: 101 us
  starting transfers between devices  63.1 us (62%)
  waiting for transfers between devices  23 us (23%)
  Pallas kernels  12.9 us (13%)
    ppermute x4, starting transfers between devices, swap_inner(): return lax.ppermute(x, 'dom', [(i, i ^ 1) for i in range(count)])  37.5 us
    ppermute x5, waiting for transfers between devices, swap_cross(): return lax.ppermute(x, 'dom', pairs)  13.4 us
    all_to_all x1, starting transfers between devices, shards(): lax.all_to_all(sums, 'dom', 0, 0, tiled=True, axis_index_groups=team_grou...  13 us
    ppermute x5, starting transfers between devices, swap_cross(): return lax.ppermute(x, 'dom', pairs)  12.6 us
    pallas_call x12, Pallas kernels, call(): pl.pallas_call(kernel, out_shape=[jax.ShapeDtypeStruct(shape, jnp.float32...  8.04 us
    all_to_all x1, waiting for transfers between devices, shards(): lax.all_to_all(sums, 'dom', 0, 0, tiled=True, axis_index_groups=team_grou...  5.96 us
    pallas_call x1, Pallas kernels, call_forcing(): pl.pallas_call(forcing_kernel, out_shape=[jax.ShapeDtypeStruct(shape, jnp...  4.58 us
    ppermute x4, waiting for transfers between devices, swap_inner(): return lax.ppermute(x, 'dom', [(i, i ^ 1) for i in range(count)])  3.59 us
  transfers between devices with their start and end apart: 10, of which 10 were waited for; matrix products, arithmetic and copies ran while one was open for 0% of the time, Pallas kernels for 1%

profile of v9, /device:TPU:1, one launch (start us, length us, event | category | flops | bytes accessed | tf_op | source)
XLA Modules:
  0.0 100.9 jit_solution(6944310030217558994)
XLA Ops:
  0.6 0.0 copy-start.9
  0.6 4.6 %shard_map.266 = (f32[56,8,128]{2,1,0:T(8,128)}, f32[4,8,128]{2,1,0:T(8,128)}) custom-call(s32[16]{0:T(128)} %slot_in.1, f32[3,3,16,512]{3,2,1,0:T(8,128)} %vel_in.1, f32[2,3,16,512]{3,2,1,0:T(8,128)} %past_in.1, f32[3,16,512]{2,1,0:T(8,128)} %metric_in.1, f32[16,512]{1,0:T(8,128)} %jac_in.1, f32[1,512]{1,0:T(1,128)} %constant.48.clone.w3_in, ...), custom_call_target="tpu_custom_call" | custom-call | tf_op jit(solution)/shard_map/pallas_call | solution.py:744
  5.2 4.6 %collective-permute-start = (f32[4,8,128]{2,1,0:T(8,128)}, f32[4,8,128]{2,1,0:T(8,128)S(1)}, u32[]{:S(2)}, u32[]{:S(2)}) collective-permute-start(f32[4,8,128]{2,1,0:T(8,128)} %get-tuple-element.30), channel_id=1, source_target_pairs={{0,511},{1,2},{2,1},{3,4},{4,3},{5,6},{6,5},{7,8},{8,7},{9,10},{10... | collective-permute-start | bytes 49160 | tf_op jit(solution)/shard_map/ppermute | solution.py:364
  9.8 0.0 copy-start.8
  9.8 0.9 copy-done.8
  10.8 0.0 copy-start.6
  10.8 0.0 copy-start.7
  10.8 0.3 shard_map.267.pack_ref
  11.1 0.0 copy-start.1
  11.1 0.0 copy-start.3
  11.1 0.4 collective-permute-done.cross_in
  11.4 0.0 copy-start.5
  11.5 0.0 copy-start
  11.5 0.0 copy-start.4
  11.5 14.5 %collective-permute-start.1 = (f32[60,8,128]{2,1,0:T(8,128)S(1)}, f32[60,8,128]{2,1,0:T(8,128)S(1)}, u32[]{:S(2)}, u32[]{:S(2)}) collective-permute-start(f32[60,8,128]{2,1,0:T(8,128)S(1)} %shard_map.268.own_ref), channel_id=1, source_target_pairs={{0,1},{1,0},{2,3},{3,2},{4,5},{5,4},{6,7},{7,6},{8,9},{9,8},{10,11... | collective-permute-start | bytes 737288 | tf_op jit(solution)/shard_map/ppermute | solution.py:359
  26.0 1.1 %collective-permute-done.1.mate_ref = f32[60,8,128]{2,1,0:T(8,128)S(1)} collective-permute-done((f32[60,8,128]{2,1,0:T(8,128)S(1)}, f32[60,8,128]{2,1,0:T(8,128)S(1)}, u32[]{:S(2)}, u32[]{:S(2)}) %collective-permute-start.1) | collective-permute-done | bytes 245792 | tf_op jit(solution)/shard_map/ppermute | solution.py:359
  27.1 0.0 copy-done.1
  27.1 0.0 copy-done.3
  27.1 0.4 shard_map.269
  27.4 1.9 %collective-permute-start.2 = (f32[10,8,128]{2,1,0:T(8,128)S(1)}, f32[10,8,128]{2,1,0:T(8,128)S(1)}, u32[]{:S(2)}, u32[]{:S(2)}) collective-permute-start(f32[10,8,128]{2,1,0:T(8,128)S(1)} %get-tuple-element.32), channel_id=1, source_target_pairs={{0,511},{1,2},{2,1},{3,4},{4,3},{5,6},{6,5},{7,8},{8,7},{9,10},{10... | collective-permute-start | bytes 122888 | tf_op jit(solution)/shard_map/ppermute | solution.py:364
  29.4 3.4 %collective-permute-done.2.received_ref = f32[10,8,128]{2,1,0:T(8,128)S(1)} collective-permute-done((f32[10,8,128]{2,1,0:T(8,128)S(1)}, f32[10,8,128]{2,1,0:T(8,128)S(1)}, u32[]{:S(2)}, u32[]{:S(2)}) %collective-permute-start.2) | collective-permute-done | bytes 40992 | tf_op jit(solution)/shard_map/ppermute | solution.py:364
  32.8 0.0 copy-done.9
  32.8 0.0 copy-done.6
  32.8 0.0 copy-done.7
  32.8 0.0 copy-done.5
  32.8 0.0 copy-done
  32.8 0.0 copy-done.4
  32.8 0.0 copy-start.2
  32.8 1.1 %shard_map.270 = (f32[17,8,128]{2,1,0:T(8,128)S(1)}, f32[224,160]{1,0:T(8,128)S(1)}, f32[9,8,128]{2,1,0:T(8,128)S(1)}) custom-call(f32[15,8,128]{2,1,0:T(8,128)S(1)} %get-tuple-element.31.div_ref, f32[10,8,128]{2,1,0:T(8,128)S(1)} %collective-permute-done.2.received_ref, f32[8,128]{1,0:T(8,128)S(1)} %get-tuple-element.33.level_ref, ...), custom_call_target="tpu_custom_call" | custom-call | tf_op jit(solution)/shard_map/pallas_call | solution.py:723
  33.9 7.7 %collective-permute-start.3 = (f32[9,8,128]{2,1,0:T(8,128)S(1)}, f32[9,8,128]{2,1,0:T(8,128)S(1)}, u32[]{:S(2)}, u32[]{:S(2)}) collective-permute-start(f32[9,8,128]{2,1,0:T(8,128)S(1)} %get-tuple-element.35.part_ref), channel_id=1, source_target_pairs={{0,1},{1,0},{2,3},{3,2},{4,5},{5,4},{6,7},{7,6},{8,9},{9,8},{10,11... | collective-permute-start | bytes 110600 | tf_op jit(solution)/shard_map/ppermute | solution.py:359
  41.6 0.8 collective-permute-done.3.mate_ref
  42.5 0.0 copy-done.2
  42.5 0.5 shard_map.271
  43.0 1.9 %collective-permute-start.4 = (f32[9,8,128]{2,1,0:T(8,128)S(1)}, f32[9,8,128]{2,1,0:T(8,128)S(1)}, u32[]{:S(2)}, u32[]{:S(2)}) collective-permute-start(f32[9,8,128]{2,1,0:T(8,128)S(1)} %get-tuple-element.38), channel_id=1, source_target_pairs={{0,511},{1,2},{2,1},{3,4},{4,3},{5,6},{6,5},{7,8},{8,7},{9,10},{10... | collective-permute-start | bytes 110600 | tf_op jit(solution)/shard_map/ppermute | solution.py:364
  44.9 3.3 %collective-permute-done.4.received_ref = f32[9,8,128]{2,1,0:T(8,128)S(1)} collective-permute-done((f32[9,8,128]{2,1,0:T(8,128)S(1)}, f32[9,8,128]{2,1,0:T(8,128)S(1)}, u32[]{:S(2)}, u32[]{:S(2)}) %collective-permute-start.4) | collective-permute-done | bytes 36896 | tf_op jit(solution)/shard_map/ppermute | solution.py:364
  48.3 1.1 %shard_map.272 = (f32[8,8,128]{2,1,0:T(8,128)S(1)}, f32[17,8,128]{2,1,0:T(8,128)S(1)}, f32[9,8,128]{2,1,0:T(8,128)S(1)}) custom-call(f32[17,8,128]{2,1,0:T(8,128)S(1)} %get-tuple-element.34.before_ref, f32[15,8,128]{2,1,0:T(8,128)S(1)} %get-tuple-element.37.local_ref.l0_ref, f32[9,8,128]{2,1,0:T(8,128)S(1)} %collective-permute-done.4.received_ref, ...), custom_call_target="tpu_custom_call" | custom-call | tf_op jit(solution)/shard_map/pallas_call | solution.py:723
  49.4 7.7 %collective-permute-start.5 = (f32[9,8,128]{2,1,0:T(8,128)S(1)}, f32[9,8,128]{2,1,0:T(8,128)S(1)}, u32[]{:S(2)}, u32[]{:S(2)}) collective-permute-start(f32[9,8,128]{2,1,0:T(8,128)S(1)} %get-tuple-element.41.part_ref), channel_id=1, source_target_pairs={{0,1},{1,0},{2,3},{3,2},{4,5},{5,4},{6,7},{7,6},{8,9},{9,8},{10,11... | collective-permute-start | bytes 110600 | tf_op jit(solution)/shard_map/ppermute | solution.py:359
  57.1 0.8 collective-permute-done.5.mate_ref
  57.9 0.5 shard_map.273
  58.4 1.9 %collective-permute-start.6 = (f32[9,8,128]{2,1,0:T(8,128)S(1)}, f32[9,8,128]{2,1,0:T(8,128)S(1)}, u32[]{:S(2)}, u32[]{:S(2)}) collective-permute-start(f32[9,8,128]{2,1,0:T(8,128)S(1)} %get-tuple-element.43), channel_id=1, source_target_pairs={{0,511},{1,2},{2,1},{3,4},{4,3},{5,6},{6,5},{7,8},{8,7},{9,10},{10... | collective-permute-start | bytes 110600 | tf_op jit(solution)/shard_map/ppermute | solution.py:364
  60.4 3.3 %collective-permute-done.6.received_ref = f32[9,8,128]{2,1,0:T(8,128)S(1)} collective-permute-done((f32[9,8,128]{2,1,0:T(8,128)S(1)}, f32[9,8,128]{2,1,0:T(8,128)S(1)}, u32[]{:S(2)}, u32[]{:S(2)}) %collective-permute-start.6) | collective-permute-done | bytes 36896 | tf_op jit(solution)/shard_map/ppermute | solution.py:364
  63.7 1.1 %shard_map.274 = (f32[8,8,128]{2,1,0:T(8,128)S(1)}, f32[17,8,128]{2,1,0:T(8,128)S(1)}, f32[9,8,128]{2,1,0:T(8,128)S(1)}) custom-call(f32[17,8,128]{2,1,0:T(8,128)S(1)} %get-tuple-element.40.before_ref, f32[15,8,128]{2,1,0:T(8,128)S(1)} %get-tuple-element.42.local_ref.l1_ref, f32[9,8,128]{2,1,0:T(8,128)S(1)} %collective-permute-done.6.received_ref, ...), custom_call_target="tpu_custom_call" | custom-call | tf_op jit(solution)/shard_map/pallas_call | solution.py:723
  64.8 0.0 copy-start.11
  64.8 7.7 %collective-permute-start.7 = (f32[9,8,128]{2,1,0:T(8,128)S(1)}, f32[9,8,128]{2,1,0:T(8,128)S(1)}, u32[]{:S(2)}, u32[]{:S(2)}) collective-permute-start(f32[9,8,128]{2,1,0:T(8,128)S(1)} %get-tuple-element.44.part_ref), channel_id=1, source_target_pairs={{0,1},{1,0},{2,3},{3,2},{4,5},{5,4},{6,7},{7,6},{8,9},{9,8},{10,11... | collective-permute-start | bytes 110600 | tf_op jit(solution)/shard_map/ppermute | solution.py:359
  72.5 0.0 copy-done.11
  72.6 0.8 collective-permute-done.7.mate_ref
  73.3 1.2 %shard_map.276 = (f32[15,8,128]{2,1,0:T(8,128)S(1)}, f32[256,128]{1,0:T(8,128)}) custom-call(f32[9,8,128]{2,1,0:T(8,128)S(1)} %get-tuple-element.44.part_ref, f32[9,8,128]{2,1,0:T(8,128)S(1)} %collective-permute-done.7.mate_ref, f32[2,4,8,8,128]{4,3,2,1,0:T(8,128)S(1)} %get-tuple-element.36.op_ref, f32[2,8,8,128]{3,2,1,0:T(8,128)S(1)} %copy-done.3, ...), custom_call_target="tpu_custom_call" | custom-call | tf_op jit(solution)/shard_map/pallas_call | solution.py:723
  74.5 13.0 %all-to-all-start = ((f32[256,1,128]{2,1,0:T(1,128)}), f32[256,1,128]{2,1,0:T(1,128)S(1)}, u32[]{:S(2)}, u32[]{:S(2)}) async-start(f32[256,1,128]{2,1,0:T(1,128)} %bitcast.1), calls=%async_computation | async-start | bytes 262144 | tf_op jit(solution)/shard_map/all_to_all | solution.py:817
  87.5 0.0 copy-start.10
  87.5 0.5 shard_map.277
  88.1 2.2 %collective-permute-start.8 = (f32[8,128]{1,0:T(8,128)S(1)}, f32[8,128]{1,0:T(8,128)S(1)}, u32[]{:S(2)}, u32[]{:S(2)}) collective-permute-start(f32[8,128]{1,0:T(8,128)S(1)} %get-tuple-element.51), channel_id=1, source_target_pairs={{0,511},{1,2},{2,1},{3,4},{4,3},{5,6},{6,5},{7,8},{8,7},{9,10},{10... | collective-permute-start | bytes 12296 | tf_op jit(solution)/shard_map/ppermute | solution.py:364
  90.3 3.0 %collective-permute-done.8.face_ref = f32[8,128]{1,0:T(8,128)S(1)} collective-permute-done((f32[8,128]{1,0:T(8,128)S(1)}, f32[8,128]{1,0:T(8,128)S(1)}, u32[]{:S(2)}, u32[]{:S(2)}) %collective-permute-start.8) | collective-permute-done | bytes 4128 | tf_op jit(solution)/shard_map/ppermute | solution.py:364
  93.3 0.0 copy-done.10
  93.3 0.6 shard_map.278.fields_ref
  93.9 6.0 %all-to-all-done = f32[256,1,128]{2,1,0:T(1,128)S(1)} async-done(((f32[256,1,128]{2,1,0:T(1,128)}), f32[256,1,128]{2,1,0:T(1,128)S(1)}, u32[]{:S(2)}, u32[]{:S(2)}) %all-to-all-start) | async-done | bytes 131104 | tf_op jit(solution)/shard_map/all_to_all | solution.py:817
  99.9 1.0 shard_map.279
  (2 shorter events, 0.1 us)
Async XLA Ops:
  0.6 32.1 %copy-start.9 = (f32[128,160]{1,0:T(8,128)S(1)}, f32[128,160]{1,0:T(8,128)}, u32[]{:S(2)}) copy-start(f32[128,160]{1,0:T(8,128)} %constant.63.clone.spread_ref) | copy-start | bytes 245764
  5.2 6.2 %collective-permute-start = (f32[4,8,128]{2,1,0:T(8,128)}, f32[4,8,128]{2,1,0:T(8,128)S(1)}, u32[]{:S(2)}, u32[]{:S(2)}) collective-permute-start(f32[4,8,128]{2,1,0:T(8,128)} %get-tuple-element.30), channel_id=1, source_target_pairs={{0,511},{1,2},{2,1},{3,4},{4,3},{5,6},{6,5},{7,8},{8,7},{9,10},{10... | collective-permute-start | bytes 49160 | tf_op jit(solution)/shard_map/ppermute | solution.py:364
  9.8 0.9 copy-start.8
  10.8 22.0 %copy-start.6 = (bf16[112,672]{1,0:T(8,128)(2,1)S(1)}, bf16[112,672]{1,0:T(8,128)(2,1)}, u32[]{:S(2)}) copy-start(bf16[112,672]{1,0:T(8,128)(2,1)} %constant.59.clone.sleft_ref) | copy-start | bytes 451588
  10.8 22.0 %copy-start.7 = (f32[3,112,160]{2,1,0:T(8,128)S(1)}, f32[3,112,160]{2,1,0:T(8,128)}, u32[]{:S(2)}) copy-start(f32[3,112,160]{2,1,0:T(8,128)} %constant.64.clone.lam_ref) | copy-start | bytes 645124
  11.1 16.0 %copy-start.1 = (bf16[768,128]{1,0:T(8,128)(2,1)S(1)}, bf16[768,128]{1,0:T(8,128)(2,1)}, u32[]{:S(2)}) copy-start(bf16[768,128]{1,0:T(8,128)(2,1)} %constant.47.clone.qright_t_ref) | copy-start | bytes 589828
  11.1 16.0 %copy-start.3 = (f32[2,8,8,128]{3,2,1,0:T(8,128)S(1)}, f32[2,8,8,128]{3,2,1,0:T(8,128)}, u32[]{:S(2)}) copy-start(f32[2,8,8,128]{3,2,1,0:T(8,128)} %constant.44.clone.ds_in.ds_ref) | copy-start | bytes 196612
  11.4 21.3 %copy-start.5 = (bf16[144,672]{1,0:T(8,128)(2,1)S(1)}, bf16[144,672]{1,0:T(8,128)(2,1)}, u32[]{:S(2)}) copy-start(bf16[144,672]{1,0:T(8,128)(2,1)} %constant.60.clone.sback_ref) | copy-start | bytes 580612
  11.5 21.3 %copy-start = (bf16[768,160]{1,0:T(8,128)(2,1)S(1)}, bf16[768,160]{1,0:T(8,128)(2,1)}, u32[]{:S(2)}) copy-start(bf16[768,160]{1,0:T(8,128)(2,1)} %constant.61.clone.sright_ref) | copy-start | bytes 737284
  11.5 21.3 %copy-start.4 = (bf16[960,128]{1,0:T(8,128)(2,1)S(1)}, bf16[960,128]{1,0:T(8,128)(2,1)}, u32[]{:S(2)}) copy-start(bf16[960,128]{1,0:T(8,128)(2,1)} %constant.62.clone.srback_ref) | copy-start | bytes 737284
  11.5 15.6 %collective-permute-start.1 = (f32[60,8,128]{2,1,0:T(8,128)S(1)}, f32[60,8,128]{2,1,0:T(8,128)S(1)}, u32[]{:S(2)}, u32[]{:S(2)}) collective-permute-start(f32[60,8,128]{2,1,0:T(8,128)S(1)} %shard_map.268.own_ref), channel_id=1, source_target_pairs={{0,1},{1,0},{2,3},{3,2},{4,5},{5,4},{6,7},{7,6},{8,9},{9,8},{10,11... | collective-permute-start | bytes 737288 | tf_op jit(solution)/shard_map/ppermute | solution.py:359
  27.4 5.3 %collective-permute-start.2 = (f32[10,8,128]{2,1,0:T(8,128)S(1)}, f32[10,8,128]{2,1,0:T(8,128)S(1)}, u32[]{:S(2)}, u32[]{:S(2)}) collective-permute-start(f32[10,8,128]{2,1,0:T(8,128)S(1)} %get-tuple-element.32), channel_id=1, source_target_pairs={{0,511},{1,2},{2,1},{3,4},{4,3},{5,6},{6,5},{7,8},{8,7},{9,10},{10... | collective-permute-start | bytes 122888 | tf_op jit(solution)/shard_map/ppermute | solution.py:364
  32.8 9.7 %copy-start.2 = (bf16[768,128]{1,0:T(8,128)(2,1)S(1)}, bf16[768,128]{1,0:T(8,128)(2,1)}, u32[]{:S(2)}) copy-start(bf16[768,128]{1,0:T(8,128)(2,1)} %constant.46.clone.qright_ref) | copy-start | bytes 589828
  33.9 8.6 %collective-permute-start.3 = (f32[9,8,128]{2,1,0:T(8,128)S(1)}, f32[9,8,128]{2,1,0:T(8,128)S(1)}, u32[]{:S(2)}, u32[]{:S(2)}) collective-permute-start(f32[9,8,128]{2,1,0:T(8,128)S(1)} %get-tuple-element.35.part_ref), channel_id=1, source_target_pairs={{0,1},{1,0},{2,3},{3,2},{4,5},{5,4},{6,7},{7,6},{8,9},{9,8},{10,11... | collective-permute-start | bytes 110600 | tf_op jit(solution)/shard_map/ppermute | solution.py:359
  43.0 5.3 %collective-permute-start.4 = (f32[9,8,128]{2,1,0:T(8,128)S(1)}, f32[9,8,128]{2,1,0:T(8,128)S(1)}, u32[]{:S(2)}, u32[]{:S(2)}) collective-permute-start(f32[9,8,128]{2,1,0:T(8,128)S(1)} %get-tuple-element.38), channel_id=1, source_target_pairs={{0,511},{1,2},{2,1},{3,4},{4,3},{5,6},{6,5},{7,8},{8,7},{9,10},{10... | collective-permute-start | bytes 110600 | tf_op jit(solution)/shard_map/ppermute | solution.py:364
  49.4 8.5 %collective-permute-start.5 = (f32[9,8,128]{2,1,0:T(8,128)S(1)}, f32[9,8,128]{2,1,0:T(8,128)S(1)}, u32[]{:S(2)}, u32[]{:S(2)}) collective-permute-start(f32[9,8,128]{2,1,0:T(8,128)S(1)} %get-tuple-element.41.part_ref), channel_id=1, source_target_pairs={{0,1},{1,0},{2,3},{3,2},{4,5},{5,4},{6,7},{7,6},{8,9},{9,8},{10,11... | collective-permute-start | bytes 110600 | tf_op jit(solution)/shard_map/ppermute | solution.py:359
  58.4 5.3 %collective-permute-start.6 = (f32[9,8,128]{2,1,0:T(8,128)S(1)}, f32[9,8,128]{2,1,0:T(8,128)S(1)}, u32[]{:S(2)}, u32[]{:S(2)}) collective-permute-start(f32[9,8,128]{2,1,0:T(8,128)S(1)} %get-tuple-element.43), channel_id=1, source_target_pairs={{0,511},{1,2},{2,1},{3,4},{4,3},{5,6},{6,5},{7,8},{8,7},{9,10},{10... | collective-permute-start | bytes 110600 | tf_op jit(solution)/shard_map/ppermute | solution.py:364
  64.8 7.7 %copy-start.11 = (f32[8,128]{1,0:T(8,128)S(1)}, f32[8,128]{1,0:T(8,128)}, u32[]{:S(2)}) copy-start(f32[8,128]{1,0:T(8,128)} %constant.65.clone.ws_ref) | copy-start | bytes 12292
  64.8 8.5 %collective-permute-start.7 = (f32[9,8,128]{2,1,0:T(8,128)S(1)}, f32[9,8,128]{2,1,0:T(8,128)S(1)}, u32[]{:S(2)}, u32[]{:S(2)}) collective-permute-start(f32[9,8,128]{2,1,0:T(8,128)S(1)} %get-tuple-element.44.part_ref), channel_id=1, source_target_pairs={{0,1},{1,0},{2,3},{3,2},{4,5},{5,4},{6,7},{7,6},{8,9},{9,8},{10,11... | collective-permute-start | bytes 110600 | tf_op jit(solution)/shard_map/ppermute | solution.py:359
  74.5 25.4 %all-to-all-start = ((f32[256,1,128]{2,1,0:T(1,128)}), f32[256,1,128]{2,1,0:T(1,128)S(1)}, u32[]{:S(2)}, u32[]{:S(2)}) async-start(f32[256,1,128]{2,1,0:T(1,128)} %bitcast.1), calls=%async_computation | async-start | bytes 262144 | tf_op jit(solution)/shard_map/all_to_all | solution.py:817
  87.5 5.8 %copy-start.10 = (s32[2,7,8,128]{3,2,1,0:T(8,128)S(1)}, s32[2,7,8,128]{3,2,1,0:T(8,128)}, u32[]{:S(2)}) copy-start(s32[2,7,8,128]{3,2,1,0:T(8,128)} %constant.58.clone.order_ref) | copy-start | bytes 172036
  88.1 5.2 %collective-permute-start.8 = (f32[8,128]{1,0:T(8,128)S(1)}, f32[8,128]{1,0:T(8,128)S(1)}, u32[]{:S(2)}, u32[]{:S(2)}) collective-permute-start(f32[8,128]{1,0:T(8,128)S(1)} %get-tuple-element.51), channel_id=1, source_target_pairs={{0,511},{1,2},{2,1},{3,4},{4,3},{5,6},{6,5},{7,8},{8,7},{9,10},{10... | collective-permute-start | bytes 12296 | tf_op jit(solution)/shard_map/ppermute | solution.py:364

commit v10 on v8

--- a/solution.py
+++ b/solution.py
@@ -366,7 +366,7 @@
     return jnp.take_along_axis(flat, tiled, axis=1).reshape(x.shape)
 
 
-def forcing_kernel(slot_in, vel_in, past_in, metric_in, jac_in, w3_in, wmass_in, ds_in, dq_in, jright_in, jslope_in, jright_t_in, jleft_in, jleft_a_in, jleft_s_in, jleft_t_in, wfine_in, pack_ref, cross_ref, slot_ref, vel_ref, past_ref, metric_ref, jac_ref, w3_ref, wmass_ref, ds_ref, dq_ref, jright_ref, jslope_ref, jright_t_ref, jleft_ref, jleft_a_ref, jleft_s_ref, jleft_t_ref, wfine_ref, sems):
+def forcing_kernel(slot_in, vel_in, past_in, metric_in, jac_in, w3_in, wmass_in, ds_in, dq_in, jright_in, jslope_in, jright_t_in, jleft_in, jleft_a_in, jleft_s_in, jleft_t_in, wfine_in, pack_out, cross_out, slot_ref, vel_ref, past_ref, metric_ref, jac_ref, w3_ref, wmass_ref, ds_ref, dq_ref, jright_ref, jslope_ref, jright_t_ref, jleft_ref, jleft_a_ref, jleft_s_ref, jleft_t_ref, wfine_ref, pack_ref, cross_ref, sems, out_sems):
     sources = (slot_in, vel_in, past_in, metric_in, jac_in, w3_in, wmass_in, ds_in, dq_in, jright_in, jslope_in, jright_t_in, jleft_in, jleft_a_in, jleft_s_in, jleft_t_in, wfine_in)
     targets = (slot_ref, vel_ref, past_ref, metric_ref, jac_ref, w3_ref, wmass_ref, ds_ref, dq_ref, jright_ref, jslope_ref, jright_t_ref, jleft_ref, jleft_a_ref, jleft_s_ref, jleft_t_ref, wfine_ref)
     copies = [pltpu.make_async_copy(x, y, sems.at[k]) for k, (x, y) in enumerate(zip(sources, targets))]
@@ -381,8 +381,29 @@
     direct = (jac * w3_ref[...])[None] * (-10.0 * new + 16.0 * mid - 6.0 * old) + 3.0 * past_ref[0] - past_ref[1]
     lanes = to_lanes(jnp.concatenate([new, guess, direct, metric_ref[...], jac[None]], axis=0))
     new, guess, direct, metric, jac = lanes[0:3], lanes[3:6], lanes[6:9], lanes[9:12], lanes[12]
+    leaving = []
+
+    def send(k, value):
+        at = pl.ds(NP * k, NP)
+        pack_ref[at] = value
+        copy = pltpu.make_async_copy(pack_ref.at[at], pack_out.at[at], out_sems.at[k])
+        copy.start()
+        leaving.append(copy)
+
     for copy in copies[6:]:
         copy.wait()
+    mass = jac * wmass_ref[...]
+    lane = lax.broadcasted_iota(jnp.int32, (NP, LANES), 1)
+    index = jnp.zeros((NP, LANES), jnp.int32)
+    for e in range(ES):
+        index = jnp.where((lane >> 3) == slot_ref[e], e * NP, index)
+    index = index + (lane & 7)
+    sorted_mass = take_lanes(mass, index)
+    joined = join_s(sorted_mass)
+    cross_ref[3] = jnp.where(even, joined[0], joined[NP - 1])
+    send(3, sorted_mass)
+    for k in range(3):
+        send(4 + k, take_lanes(metric[k], index))
     ds, dq = ds_ref[...], dq_ref[...]
     moved = [rows(new[i]) for i in range(3)]
     plain = moved + [rows(jac)] + [rows(new[d] * metric[d]) for d in range(3)]
@@ -398,26 +419,20 @@
         products.append(scale * total)
     coarse = left_dot(jleft_t_ref, jnp.concatenate(products, axis=1))
     coarse = pair_dot(jnp.concatenate([coarse[:, 256 * i : 256 * i + 256] for i in range(3)], axis=0), jright_t_ref)
-    mass = jac * wmass_ref[...]
     factor = [mass * metric[d] * metric[d] for d in range(3)]
     result = []
     for i in range(3):
         ga, gs, gq = gradient(guess[i], ds, dq)
         stiff = gradient_t(factor[0] * ga, factor[1] * gs, factor[2] * gq, ds, dq)
         result.append(direct[i] - 3.0 * planes(coarse[64 * i : 64 * i + 64]) - viscosity * stiff)
-    result.extend([mass, metric[0], metric[1], metric[2]])
-    lane = lax.broadcasted_iota(jnp.int32, (NP, LANES), 1)
-    index = jnp.zeros((NP, LANES), jnp.int32)
-    for e in range(ES):
-        index = jnp.where((lane >> 3) == slot_ref[e], e * NP, index)
-    index = index + (lane & 7)
-    result = [take_lanes(x, index) for x in result]
-    for k in range(4):
-        joined = join_s(result[k])
+    for k in range(3):
+        joined = join_s(take_lanes(result[k], index))
         cross_ref[k] = jnp.where(even, joined[0], joined[NP - 1])
-        pack_ref[NP * k : NP * k + NP] = joined if k < 3 else result[k]
-    for k in range(4, 7):
-        pack_ref[NP * k : NP * k + NP] = result[k]
+        send(k, joined)
+    copy = pltpu.make_async_copy(cross_ref, cross_out, out_sems.at[7])
+    copy.start()
+    for copy in leaving + [copy]:
+        copy.wait()
 
 
 def stage_kernel(pack_ref, out_ref, sem):
@@ -702,12 +717,14 @@
     shapes = [(7 * NP, NP, LANES), (4, NP, LANES)]
     scratch = [pltpu.SMEM(args[0].shape, jnp.int32)]
     scratch.extend(pltpu.VMEM(x.shape, x.dtype) for x in args[1:])
+    scratch.extend(pltpu.VMEM(shape, jnp.float32) for shape in shapes)
     scratch.append(pltpu.SemaphoreType.DMA((len(args),)))
+    scratch.append(pltpu.SemaphoreType.DMA((8,)))
     return pl.pallas_call(
         forcing_kernel,
         out_shape=[jax.ShapeDtypeStruct(shape, jnp.float32) for shape in shapes],
         in_specs=[pl.BlockSpec(memory_space=pltpu.HBM)] * len(args),
-        out_specs=[pl.BlockSpec(memory_space=pltpu.VMEM)] * len(shapes),
+        out_specs=[pl.BlockSpec(memory_space=pltpu.HBM)] * len(shapes),
         scratch_shapes=scratch,
         compiler_params=pltpu.CompilerParams(vmem_limit_bytes=FORCING_VMEM),
     )(*args)

time: 99.9 us -> 99.9 us (level)
  no operation moved by 1% of the time
where the time goes in v10:
time: 99.9 us; the launch traced here: 99.4 us
  starting transfers between devices  63.1 us (63%)
  waiting for transfers between devices  23.1 us (23%)
  Pallas kernels  11.4 us (11%)
  local copies, waits for them, and re-layouts  1 us (1%)
    ppermute x4, starting transfers between devices, swap_inner(): return lax.ppermute(x, 'dom', [(i, i ^ 1) for i in range(count)])  37.5 us
    ppermute x5, waiting for transfers between devices, swap_cross(): return lax.ppermute(x, 'dom', pairs)  13.5 us
    all_to_all x1, starting transfers between devices, shards(): lax.all_to_all(sums, 'dom', 0, 0, tiled=True, axis_index_groups=team_grou...  13 us
    ppermute x5, starting transfers between devices, swap_cross(): return lax.ppermute(x, 'dom', pairs)  12.6 us
    pallas_call x12, Pallas kernels, call(): pl.pallas_call(kernel, out_shape=[jax.ShapeDtypeStruct(shape, jnp.float32...  7.19 us
    all_to_all x1, waiting for transfers between devices, shards(): lax.all_to_all(sums, 'dom', 0, 0, tiled=True, axis_index_groups=team_grou...  6.05 us
    pallas_call x1, Pallas kernels, call_forcing(): pl.pallas_call(forcing_kernel, out_shape=[jax.ShapeDtypeStruct(shape, jnp...  3.88 us
    ppermute x4, waiting for transfers between devices, swap_inner(): return lax.ppermute(x, 'dom', [(i, i ^ 1) for i in range(count)])  3.59 us
  transfers between devices with their start and end apart: 10, of which 10 were waited for; matrix products, arithmetic and copies ran while one was open for 0% of the time, Pallas kernels for 1%

profile of v10, /device:TPU:1, one launch (start us, length us, event | category | flops | bytes accessed | tf_op | source)
XLA Modules:
  0.0 99.4 jit_solution(12562154464936965958)
XLA Ops:
  0.6 3.9 %shard_map.266 = (f32[56,8,128]{2,1,0:T(8,128)}, f32[4,8,128]{2,1,0:T(8,128)}) custom-call(s32[16]{0:T(128)} %slot_in.1, f32[3,3,16,512]{3,2,1,0:T(8,128)} %vel_in.1, f32[2,3,16,512]{3,2,1,0:T(8,128)} %past_in.1, f32[3,16,512]{2,1,0:T(8,128)} %metric_in.1, f32[16,512]{1,0:T(8,128)} %jac_in.1, f32[1,512]{1,0:T(1,128)} %constant.48.clone.w3_in, ...), custom_call_target="tpu_custom_call" | custom-call | tf_op jit(solution)/shard_map/pallas_call | solution.py:723
  4.5 4.6 %collective-permute-start = (f32[4,8,128]{2,1,0:T(8,128)}, f32[4,8,128]{2,1,0:T(8,128)S(1)}, u32[]{:S(2)}, u32[]{:S(2)}) collective-permute-start(f32[4,8,128]{2,1,0:T(8,128)} %get-tuple-element.30), channel_id=1, source_target_pairs={{0,511},{1,2},{2,1},{3,4},{4,3},{5,6},{6,5},{7,8},{8,7},{9,10},{10... | collective-permute-start | bytes 49160 | tf_op jit(solution)/shard_map/ppermute | solution.py:326
  9.1 0.0 copy-start.8
  9.1 0.9 copy-done.8
  10.1 0.0 copy-start.9
  10.1 0.3 shard_map.267.pack_ref
  10.4 0.0 copy-start
  10.4 0.0 copy-start.2
  10.4 0.4 collective-permute-done.cross_in
  10.7 0.0 copy-start.7
  10.8 0.0 copy-start.1
  10.8 0.0 copy-start.4
  10.8 0.0 copy-start.5
  10.8 0.0 copy-start.6
  10.8 14.5 %collective-permute-start.1 = (f32[60,8,128]{2,1,0:T(8,128)S(1)}, f32[60,8,128]{2,1,0:T(8,128)S(1)}, u32[]{:S(2)}, u32[]{:S(2)}) collective-permute-start(f32[60,8,128]{2,1,0:T(8,128)S(1)} %shard_map.268.own_ref), channel_id=1, source_target_pairs={{0,1},{1,0},{2,3},{3,2},{4,5},{5,4},{6,7},{7,6},{8,9},{9,8},{10,11... | collective-permute-start | bytes 737288 | tf_op jit(solution)/shard_map/ppermute | solution.py:321
  25.3 1.1 %collective-permute-done.1.mate_ref = f32[60,8,128]{2,1,0:T(8,128)S(1)} collective-permute-done((f32[60,8,128]{2,1,0:T(8,128)S(1)}, f32[60,8,128]{2,1,0:T(8,128)S(1)}, u32[]{:S(2)}, u32[]{:S(2)}) %collective-permute-start.1) | collective-permute-done | bytes 245792 | tf_op jit(solution)/shard_map/ppermute | solution.py:321
  26.4 0.0 copy-done
  26.4 0.0 copy-done.2
  26.4 0.3 shard_map.269
  26.7 1.9 %collective-permute-start.2 = (f32[10,8,128]{2,1,0:T(8,128)S(1)}, f32[10,8,128]{2,1,0:T(8,128)S(1)}, u32[]{:S(2)}, u32[]{:S(2)}) collective-permute-start(f32[10,8,128]{2,1,0:T(8,128)S(1)} %get-tuple-element.32), channel_id=1, source_target_pairs={{0,511},{1,2},{2,1},{3,4},{4,3},{5,6},{6,5},{7,8},{8,7},{9,10},{10... | collective-permute-start | bytes 122888 | tf_op jit(solution)/shard_map/ppermute | solution.py:326
  28.7 3.4 %collective-permute-done.2.received_ref = f32[10,8,128]{2,1,0:T(8,128)S(1)} collective-permute-done((f32[10,8,128]{2,1,0:T(8,128)S(1)}, f32[10,8,128]{2,1,0:T(8,128)S(1)}, u32[]{:S(2)}, u32[]{:S(2)}) %collective-permute-start.2) | collective-permute-done | bytes 40992 | tf_op jit(solution)/shard_map/ppermute | solution.py:326
  32.1 0.0 copy-done.9
  32.1 0.0 copy-done.7
  32.1 0.0 copy-done.1
  32.1 0.0 copy-done.4
  32.1 0.0 copy-done.5
  32.1 0.0 copy-done.6
  32.1 0.0 copy-start.3
  32.1 0.9 shard_map.270
  33.0 7.7 %collective-permute-start.3 = (f32[9,8,128]{2,1,0:T(8,128)S(1)}, f32[9,8,128]{2,1,0:T(8,128)S(1)}, u32[]{:S(2)}, u32[]{:S(2)}) collective-permute-start(f32[9,8,128]{2,1,0:T(8,128)S(1)} %get-tuple-element.35.part_ref), channel_id=1, source_target_pairs={{0,1},{1,0},{2,3},{3,2},{4,5},{5,4},{6,7},{7,6},{8,9},{9,8},{10,11... | collective-permute-start | bytes 110600 | tf_op jit(solution)/shard_map/ppermute | solution.py:321
  40.8 0.8 collective-permute-done.3.mate_ref
  41.6 0.0 copy-done.3
  41.6 0.4 shard_map.271
  42.1 1.9 %collective-permute-start.4 = (f32[9,8,128]{2,1,0:T(8,128)S(1)}, f32[9,8,128]{2,1,0:T(8,128)S(1)}, u32[]{:S(2)}, u32[]{:S(2)}) collective-permute-start(f32[9,8,128]{2,1,0:T(8,128)S(1)} %get-tuple-element.38), channel_id=1, source_target_pairs={{0,511},{1,2},{2,1},{3,4},{4,3},{5,6},{6,5},{7,8},{8,7},{9,10},{10... | collective-permute-start | bytes 110600 | tf_op jit(solution)/shard_map/ppermute | solution.py:326
  44.0 3.3 %collective-permute-done.4.received_ref = f32[9,8,128]{2,1,0:T(8,128)S(1)} collective-permute-done((f32[9,8,128]{2,1,0:T(8,128)S(1)}, f32[9,8,128]{2,1,0:T(8,128)S(1)}, u32[]{:S(2)}, u32[]{:S(2)}) %collective-permute-start.4) | collective-permute-done | bytes 36896 | tf_op jit(solution)/shard_map/ppermute | solution.py:326
  47.3 0.9 shard_map.272
  48.2 7.7 %collective-permute-start.5 = (f32[9,8,128]{2,1,0:T(8,128)S(1)}, f32[9,8,128]{2,1,0:T(8,128)S(1)}, u32[]{:S(2)}, u32[]{:S(2)}) collective-permute-start(f32[9,8,128]{2,1,0:T(8,128)S(1)} %get-tuple-element.41.part_ref), channel_id=1, source_target_pairs={{0,1},{1,0},{2,3},{3,2},{4,5},{5,4},{6,7},{7,6},{8,9},{9,8},{10,11... | collective-permute-start | bytes 110600 | tf_op jit(solution)/shard_map/ppermute | solution.py:321
  55.9 0.8 collective-permute-done.5.mate_ref
  56.8 0.4 shard_map.273
  57.2 1.9 %collective-permute-start.6 = (f32[9,8,128]{2,1,0:T(8,128)S(1)}, f32[9,8,128]{2,1,0:T(8,128)S(1)}, u32[]{:S(2)}, u32[]{:S(2)}) collective-permute-start(f32[9,8,128]{2,1,0:T(8,128)S(1)} %get-tuple-element.43), channel_id=1, source_target_pairs={{0,511},{1,2},{2,1},{3,4},{4,3},{5,6},{6,5},{7,8},{8,7},{9,10},{10... | collective-permute-start | bytes 110600 | tf_op jit(solution)/shard_map/ppermute | solution.py:326
  59.1 3.3 %collective-permute-done.6.received_ref = f32[9,8,128]{2,1,0:T(8,128)S(1)} collective-permute-done((f32[9,8,128]{2,1,0:T(8,128)S(1)}, f32[9,8,128]{2,1,0:T(8,128)S(1)}, u32[]{:S(2)}, u32[]{:S(2)}) %collective-permute-start.6) | collective-permute-done | bytes 36896 | tf_op jit(solution)/shard_map/ppermute | solution.py:326
  62.5 0.9 shard_map.274
  63.4 0.0 copy-start.11
  63.4 7.7 %collective-permute-start.7 = (f32[9,8,128]{2,1,0:T(8,128)S(1)}, f32[9,8,128]{2,1,0:T(8,128)S(1)}, u32[]{:S(2)}, u32[]{:S(2)}) collective-permute-start(f32[9,8,128]{2,1,0:T(8,128)S(1)} %get-tuple-element.44.part_ref), channel_id=1, source_target_pairs={{0,1},{1,0},{2,3},{3,2},{4,5},{5,4},{6,7},{7,6},{8,9},{9,8},{10,11... | collective-permute-start | bytes 110600 | tf_op jit(solution)/shard_map/ppermute | solution.py:321
  71.1 0.0 copy-done.11
  71.2 0.8 collective-permute-done.7.mate_ref
  71.9 1.2 %shard_map.276 = (f32[15,8,128]{2,1,0:T(8,128)S(1)}, f32[256,128]{1,0:T(8,128)}) custom-call(f32[9,8,128]{2,1,0:T(8,128)S(1)} %get-tuple-element.44.part_ref, f32[9,8,128]{2,1,0:T(8,128)S(1)} %collective-permute-done.7.mate_ref, f32[2,4,8,8,128]{4,3,2,1,0:T(8,128)S(1)} %get-tuple-element.36.op_ref, f32[2,8,8,128]{3,2,1,0:T(8,128)S(1)} %copy-done, ...), custom_call_target="tpu_custom_call" | custom-call | tf_op jit(solution)/shard_map/pallas_call | solution.py:700
  73.1 13.0 %all-to-all-start = ((f32[256,1,128]{2,1,0:T(1,128)}), f32[256,1,128]{2,1,0:T(1,128)S(1)}, u32[]{:S(2)}, u32[]{:S(2)}) async-start(f32[256,1,128]{2,1,0:T(1,128)} %bitcast.1), calls=%async_computation | async-start | bytes 262144 | tf_op jit(solution)/shard_map/all_to_all | solution.py:796
  86.1 0.0 copy-start.10
  86.1 0.4 shard_map.277
  86.6 2.2 %collective-permute-start.8 = (f32[8,128]{1,0:T(8,128)S(1)}, f32[8,128]{1,0:T(8,128)S(1)}, u32[]{:S(2)}, u32[]{:S(2)}) collective-permute-start(f32[8,128]{1,0:T(8,128)S(1)} %get-tuple-element.51), channel_id=1, source_target_pairs={{0,511},{1,2},{2,1},{3,4},{4,3},{5,6},{6,5},{7,8},{8,7},{9,10},{10... | collective-permute-start | bytes 12296 | tf_op jit(solution)/shard_map/ppermute | solution.py:326
  88.8 3.0 %collective-permute-done.8.face_ref = f32[8,128]{1,0:T(8,128)S(1)} collective-permute-done((f32[8,128]{1,0:T(8,128)S(1)}, f32[8,128]{1,0:T(8,128)S(1)}, u32[]{:S(2)}, u32[]{:S(2)}) %collective-permute-start.8) | collective-permute-done | bytes 4128 | tf_op jit(solution)/shard_map/ppermute | solution.py:326
  91.8 0.0 copy-done.10
  91.8 0.6 shard_map.278.fields_ref
  92.4 6.0 %all-to-all-done = f32[256,1,128]{2,1,0:T(1,128)S(1)} async-done(((f32[256,1,128]{2,1,0:T(1,128)}), f32[256,1,128]{2,1,0:T(1,128)S(1)}, u32[]{:S(2)}, u32[]{:S(2)}) %all-to-all-start) | async-done | bytes 131104 | tf_op jit(solution)/shard_map/all_to_all | solution.py:796
  98.4 1.0 %shard_map.279 = (f32[8,896]{1,0:T(8,128)}, f32[8,896]{1,0:T(8,128)}) custom-call(f32[256,128]{1,0:T(8,128)S(1)} %bitcast.4, f32[7,8,896]{2,1,0:T(8,128)S(1)} %shard_map.278.fields_ref), custom_call_target="tpu_custom_call" | custom-call | tf_op jit(solution)/shard_map/pallas_call | solution.py:700
  (2 shorter events, 0.1 us)
Async XLA Ops:
  4.5 6.2 %collective-permute-start = (f32[4,8,128]{2,1,0:T(8,128)}, f32[4,8,128]{2,1,0:T(8,128)S(1)}, u32[]{:S(2)}, u32[]{:S(2)}) collective-permute-start(f32[4,8,128]{2,1,0:T(8,128)} %get-tuple-element.30), channel_id=1, source_target_pairs={{0,511},{1,2},{2,1},{3,4},{4,3},{5,6},{6,5},{7,8},{8,7},{9,10},{10... | collective-permute-start | bytes 49160 | tf_op jit(solution)/shard_map/ppermute | solution.py:326
  9.1 0.9 copy-start.8
  10.1 22.0 %copy-start.9 = (f32[128,160]{1,0:T(8,128)S(1)}, f32[128,160]{1,0:T(8,128)}, u32[]{:S(2)}) copy-start(f32[128,160]{1,0:T(8,128)} %constant.63.clone.spread_ref) | copy-start | bytes 245764
  10.4 16.0 %copy-start = (f32[2,8,8,128]{3,2,1,0:T(8,128)S(1)}, f32[2,8,8,128]{3,2,1,0:T(8,128)}, u32[]{:S(2)}) copy-start(f32[2,8,8,128]{3,2,1,0:T(8,128)} %constant.44.clone.ds_in.ds_ref) | copy-start | bytes 196612
  10.4 16.0 %copy-start.2 = (bf16[384,128]{1,0:T(8,128)(2,1)S(1)}, bf16[384,128]{1,0:T(8,128)(2,1)}, u32[]{:S(2)}) copy-start(bf16[384,128]{1,0:T(8,128)(2,1)} %constant.47.clone.qright_t_ref) | copy-start | bytes 294916
  10.7 21.3 %copy-start.7 = (f32[3,112,160]{2,1,0:T(8,128)S(1)}, f32[3,112,160]{2,1,0:T(8,128)}, u32[]{:S(2)}) copy-start(f32[3,112,160]{2,1,0:T(8,128)} %constant.64.clone.lam_ref) | copy-start | bytes 645124
  10.8 21.3 %copy-start.1 = (bf16[384,160]{1,0:T(8,128)(2,1)S(1)}, bf16[384,160]{1,0:T(8,128)(2,1)}, u32[]{:S(2)}) copy-start(bf16[384,160]{1,0:T(8,128)(2,1)} %constant.61.clone.sright_ref) | copy-start | bytes 368644
  10.8 21.3 %copy-start.4 = (bf16[480,128]{1,0:T(8,128)(2,1)S(1)}, bf16[480,128]{1,0:T(8,128)(2,1)}, u32[]{:S(2)}) copy-start(bf16[480,128]{1,0:T(8,128)(2,1)} %constant.62.clone.srback_ref) | copy-start | bytes 368644
  10.8 21.3 %copy-start.5 = (bf16[144,336]{1,0:T(8,128)(2,1)S(1)}, bf16[144,336]{1,0:T(8,128)(2,1)}, u32[]{:S(2)}) copy-start(bf16[144,336]{1,0:T(8,128)(2,1)} %constant.60.clone.sback_ref) | copy-start | bytes 290308
  10.8 21.3 %copy-start.6 = (bf16[112,336]{1,0:T(8,128)(2,1)S(1)}, bf16[112,336]{1,0:T(8,128)(2,1)}, u32[]{:S(2)}) copy-start(bf16[112,336]{1,0:T(8,128)(2,1)} %constant.59.clone.sleft_ref) | copy-start | bytes 225796
  10.8 15.6 %collective-permute-start.1 = (f32[60,8,128]{2,1,0:T(8,128)S(1)}, f32[60,8,128]{2,1,0:T(8,128)S(1)}, u32[]{:S(2)}, u32[]{:S(2)}) collective-permute-start(f32[60,8,128]{2,1,0:T(8,128)S(1)} %shard_map.268.own_ref), channel_id=1, source_target_pairs={{0,1},{1,0},{2,3},{3,2},{4,5},{5,4},{6,7},{7,6},{8,9},{9,8},{10,11... | collective-permute-start | bytes 737288 | tf_op jit(solution)/shard_map/ppermute | solution.py:321
  26.7 5.3 %collective-permute-start.2 = (f32[10,8,128]{2,1,0:T(8,128)S(1)}, f32[10,8,128]{2,1,0:T(8,128)S(1)}, u32[]{:S(2)}, u32[]{:S(2)}) collective-permute-start(f32[10,8,128]{2,1,0:T(8,128)S(1)} %get-tuple-element.32), channel_id=1, source_target_pairs={{0,511},{1,2},{2,1},{3,4},{4,3},{5,6},{6,5},{7,8},{8,7},{9,10},{10... | collective-permute-start | bytes 122888 | tf_op jit(solution)/shard_map/ppermute | solution.py:326
  32.1 9.5 %copy-start.3 = (bf16[384,128]{1,0:T(8,128)(2,1)S(1)}, bf16[384,128]{1,0:T(8,128)(2,1)}, u32[]{:S(2)}) copy-start(bf16[384,128]{1,0:T(8,128)(2,1)} %constant.46.clone.qright_ref) | copy-start | bytes 294916
  33.0 8.6 %collective-permute-start.3 = (f32[9,8,128]{2,1,0:T(8,128)S(1)}, f32[9,8,128]{2,1,0:T(8,128)S(1)}, u32[]{:S(2)}, u32[]{:S(2)}) collective-permute-start(f32[9,8,128]{2,1,0:T(8,128)S(1)} %get-tuple-element.35.part_ref), channel_id=1, source_target_pairs={{0,1},{1,0},{2,3},{3,2},{4,5},{5,4},{6,7},{7,6},{8,9},{9,8},{10,11... | collective-permute-start | bytes 110600 | tf_op jit(solution)/shard_map/ppermute | solution.py:321
  42.1 5.3 %collective-permute-start.4 = (f32[9,8,128]{2,1,0:T(8,128)S(1)}, f32[9,8,128]{2,1,0:T(8,128)S(1)}, u32[]{:S(2)}, u32[]{:S(2)}) collective-permute-start(f32[9,8,128]{2,1,0:T(8,128)S(1)} %get-tuple-element.38), channel_id=1, source_target_pairs={{0,511},{1,2},{2,1},{3,4},{4,3},{5,6},{6,5},{7,8},{8,7},{9,10},{10... | collective-permute-start | bytes 110600 | tf_op jit(solution)/shard_map/ppermute | solution.py:326
  48.2 8.5 %collective-permute-start.5 = (f32[9,8,128]{2,1,0:T(8,128)S(1)}, f32[9,8,128]{2,1,0:T(8,128)S(1)}, u32[]{:S(2)}, u32[]{:S(2)}) collective-permute-start(f32[9,8,128]{2,1,0:T(8,128)S(1)} %get-tuple-element.41.part_ref), channel_id=1, source_target_pairs={{0,1},{1,0},{2,3},{3,2},{4,5},{5,4},{6,7},{7,6},{8,9},{9,8},{10,11... | collective-permute-start | bytes 110600 | tf_op jit(solution)/shard_map/ppermute | solution.py:321
  57.2 5.3 %collective-permute-start.6 = (f32[9,8,128]{2,1,0:T(8,128)S(1)}, f32[9,8,128]{2,1,0:T(8,128)S(1)}, u32[]{:S(2)}, u32[]{:S(2)}) collective-permute-start(f32[9,8,128]{2,1,0:T(8,128)S(1)} %get-tuple-element.43), channel_id=1, source_target_pairs={{0,511},{1,2},{2,1},{3,4},{4,3},{5,6},{6,5},{7,8},{8,7},{9,10},{10... | collective-permute-start | bytes 110600 | tf_op jit(solution)/shard_map/ppermute | solution.py:326
  63.4 7.7 %copy-start.11 = (f32[8,128]{1,0:T(8,128)S(1)}, f32[8,128]{1,0:T(8,128)}, u32[]{:S(2)}) copy-start(f32[8,128]{1,0:T(8,128)} %constant.65.clone.ws_ref) | copy-start | bytes 12292
  63.4 8.5 %collective-permute-start.7 = (f32[9,8,128]{2,1,0:T(8,128)S(1)}, f32[9,8,128]{2,1,0:T(8,128)S(1)}, u32[]{:S(2)}, u32[]{:S(2)}) collective-permute-start(f32[9,8,128]{2,1,0:T(8,128)S(1)} %get-tuple-element.44.part_ref), channel_id=1, source_target_pairs={{0,1},{1,0},{2,3},{3,2},{4,5},{5,4},{6,7},{7,6},{8,9},{9,8},{10,11... | collective-permute-start | bytes 110600 | tf_op jit(solution)/shard_map/ppermute | solution.py:321
  73.1 25.3 %all-to-all-start = ((f32[256,1,128]{2,1,0:T(1,128)}), f32[256,1,128]{2,1,0:T(1,128)S(1)}, u32[]{:S(2)}, u32[]{:S(2)}) async-start(f32[256,1,128]{2,1,0:T(1,128)} %bitcast.1), calls=%async_computation | async-start | bytes 262144 | tf_op jit(solution)/shard_map/all_to_all | solution.py:796
  86.1 5.7 %copy-start.10 = (s32[2,7,8,128]{3,2,1,0:T(8,128)S(1)}, s32[2,7,8,128]{3,2,1,0:T(8,128)}, u32[]{:S(2)}) copy-start(s32[2,7,8,128]{3,2,1,0:T(8,128)} %constant.58.clone.order_ref) | copy-start | bytes 172036
  86.6 5.2 %collective-permute-start.8 = (f32[8,128]{1,0:T(8,128)S(1)}, f32[8,128]{1,0:T(8,128)S(1)}, u32[]{:S(2)}, u32[]{:S(2)}) collective-permute-start(f32[8,128]{1,0:T(8,128)S(1)} %get-tuple-element.51), channel_id=1, source_target_pairs={{0,511},{1,2},{2,1},{3,4},{4,3},{5,6},{6,5},{7,8},{8,7},{9,10},{10... | collective-permute-start | bytes 12296 | tf_op jit(solution)/shard_map/ppermute | solution.py:326
